TPU v7x, 32 devices: a whole 2x2x4 slice. The times are simulated.
32 devices in a mesh: dp: 4 (over y, x), ctx: 8 (over z, core).
Axes of the slice: x: 2, y: 2, z: 4, core: 2. Of those that a mesh axis runs over, the one named last changes fastest.
Arguments:
- segment_ids: int32 [8192], P(('dp', 'ctx')), parts along dimension 0, may hold values from 0 to 7, never falling along the last dimension, each value on 1 to 1024 neighbouring positions
- attn_query: bfloat16 [8192, 2048], P(('dp', 'ctx')), parts along dimension 0, may hold values from -96 to 96
- attention_keys: bfloat16 [8192, 256], P(('dp', 'ctx')), parts along dimension 0, may hold values from -8 to 8
- attention_values: bfloat16 [8192, 256], P(('dp', 'ctx')), parts along dimension 0, may hold values from -6 to 6
- attn_gate: bfloat16 [8192, 2048], P(('dp', 'ctx')), parts along dimension 0, may hold values from -8 to 8
- delta_query: bfloat16 [8192, 1024], P(('dp', 'ctx')), parts along dimension 0, may hold values from -400 to 400
- delta_key: bfloat16 [8192, 1024], P(('dp', 'ctx')), parts along dimension 0, may hold values from -400 to 400
- update_rule_payload: bfloat16 [8192, 2048], P(('dp', 'ctx')), parts along dimension 0, may hold values from -400 to 400
- delta_beta: float32 [8192, 16], P(('dp', 'ctx')), parts along dimension 0, may hold values from 0.1 to 0.9
- delta_decay: float32 [8192, 16], P(('dp', 'ctx')), parts along dimension 0, may hold values from -1 to 0
- delta_gate: bfloat16 [8192, 2048], P(('dp', 'ctx')), parts along dimension 0, may hold values from -8 to 8
- norm_gain: float32 [128], replicated, may hold values from 0.5 to 1.5
Outputs:
- attn_mixed: bfloat16 [8192, 2048], P(('dp', 'ctx')), parts along dimension 0
- delta_mixed: bfloat16 [8192, 2048], P(('dp', 'ctx')), parts along dimension 0
There are 4 independent parts, one for each index of `dp`. A program takes and returns all parts, laid end to end along the dimension named above; an argument that names none is the same for every part. Nothing has to cross between parts.
Inputs may be any that keep to these rules, and one draw needn't show every extreme that they name: `segment_ids`: segment ids never fall along the sequence; each of the 8 documents holds 1 to 1024 positions, and one holds exactly 1024.
All inputs are finite; a program needn't handle non-finite values.
Results may differ from a plain program's by a relative error of at most 0.0085.
Values may be sent and summed in bfloat16 or wider, within the bound.
No kernel may reach another device: no remote copies, remote signals or barrier semaphores. Data moves between devices by JAX's collectives and lax.ppermute only.
A program may use at most 256 MiB of HBM per device.

v0:
```python
from functools import partial

import jax
import jax.numpy as jnp
from jax import lax
from jax.sharding import PartitionSpec as P

HEAD_WIDTH = 256
ROTARY_ENTRIES = 64
DK = 128
DV = 128
STRETCH = 128
DOCS = 8


rope_theta = 10000000.0
highest_value = lax.Precision.HIGHEST


def shifted(value, axis, steps):
    count = lax.axis_size(axis)
    initial, last = (max(0, -steps), min(count, count - steps))
    return lax.ppermute(value, axis, [(source, source + steps) for source in range(initial, last)])


def apply_rotary(field, shift_amount):
    half = ROTARY_ENTRIES // 2
    index = jnp.arange(half).astype(jnp.float32)
    freq = rope_theta ** (-2.0 * index / ROTARY_ENTRIES)
    angle = shift_amount.astype(jnp.float32)[:, None, None] * freq[None, None, :]
    angular_cos_table = jnp.cos(angle)
    sine = jnp.sin(angle)
    first = field[..., :half]
    second = field[..., half:ROTARY_ENTRIES]
    return jnp.concatenate(
        [
            first * angular_cos_table - second * sine,
            second * angular_cos_table + first * sine,
            field[..., ROTARY_ENTRIES:],
        ],
        axis=-1,
    )


def normalize(field):
    return field * lax.rsqrt(jnp.sum(field * field, axis=-1, keepdims=True) + 1e-06)


def starts_of(slot_number, first_rows):
    return jnp.max(
        jnp.where(first_rows[None, :] <= slot_number[:, None], first_rows[None, :], 0), axis=1
    )


def attend_half(
    query_vector, query_pos, query_start, key_rows, value_matrix, key_pos, recurrent_state
):
    best, total, accum = recurrent_state
    scores = jnp.einsum(
        "qngd,knd->ngqk", query_vector, key_rows, preferred_element_type=jnp.float32
    ) * HEAD_WIDTH ** (-0.5)
    allowed = (key_pos[None, :] <= query_pos[:, None]) & (key_pos[None, :] >= query_start[:, None])
    scores = jnp.where(allowed[None, None], scores, -jnp.inf)
    rising = jnp.max(scores, axis=-1)
    anchor = jnp.where(jnp.isfinite(rising), rising, 0.0)
    weights = jnp.where(allowed[None, None], jnp.exp(scores - anchor[..., None]), 0.0)
    factor = jnp.exp(best - anchor)
    accum = factor[..., None] * accum + jnp.einsum(
        "ngqk,knd->ngqd",
        weights.astype(jnp.bfloat16),
        value_matrix,
        preferred_element_type=jnp.float32,
    )
    total = factor * total + jnp.sum(weights, axis=-1)
    return (rising, total, accum)


def unchanged(recurrent_state):
    return recurrent_state


def per_device(
    segment_ids,
    attn_query,
    attention_keys,
    attention_values,
    attn_gate,
    delta_query,
    delta_key,
    update_rule_payload,
    delta_beta,
    delta_decay,
    delta_gate,
    norm_gain,
):
    ranks = lax.axis_size("ctx")
    rank = lax.axis_index("ctx")
    rows = segment_ids.shape[0]
    half = rows // 2
    documents = jnp.arange(DOCS, dtype=jnp.int32)
    counts = jnp.sum((segment_ids[:, None] == documents[None, :]).astype(jnp.int32), axis=0)
    totals = lax.psum(counts, "ctx")
    first_rows = jnp.cumsum(totals) - totals
    slot_number = rank * rows + jnp.arange(rows, dtype=jnp.int32)
    starts = starts_of(slot_number, first_rows)
    shift_amount = slot_number - starts
    heads_q = attn_query.shape[1] // HEAD_WIDTH
    heads_kv = attention_keys.shape[1] // HEAD_WIDTH
    shared_portion = heads_q // heads_kv
    query_vector = (
        apply_rotary(
            attn_query.astype(jnp.float32).reshape(rows, heads_q, HEAD_WIDTH), shift_amount
        )
        .astype(jnp.bfloat16)
        .reshape(rows, heads_q * HEAD_WIDTH)
    )
    key_rows = (
        apply_rotary(
            attention_keys.astype(jnp.float32).reshape(rows, heads_kv, HEAD_WIDTH), shift_amount
        )
        .astype(jnp.bfloat16)
        .reshape(rows, heads_kv * HEAD_WIDTH)
    )
    query_sets = query_vector.reshape(2, half, heads_kv, shared_portion, HEAD_WIDTH)
    gate_sets = attn_gate.reshape(2, half, heads_q * HEAD_WIDTH)
    pos_sets = slot_number.reshape(2, half)
    start_sets = starts.reshape(2, half)
    initial = (
        jnp.full((2, heads_kv, shared_portion, half), -jnp.inf, jnp.float32),
        jnp.zeros((2, heads_kv, shared_portion, half), jnp.float32),
        jnp.zeros((2, heads_kv, shared_portion, half, HEAD_WIDTH), jnp.float32),
    )
    start = jnp.int32(0)
    key_piece = lax.all_gather(key_rows, "ctx", axis=0, tiled=True)
    value_piece = lax.all_gather(attention_values, "ctx", axis=0, tiled=True)
    count = key_piece.shape[0]
    key_pos = jnp.arange(count, dtype=jnp.int32)
    key_piece = key_piece.reshape(count, heads_kv, HEAD_WIDTH)
    value_piece = value_piece.reshape(count, heads_kv, HEAD_WIDTH)
    bests = []
    sums = []
    accums = []
    for part in range(2):
        recurrent_state = (initial[0][part], initial[1][part], initial[2][part])
        active = (start <= jnp.max(pos_sets[part])) & (
            start + count - 1 >= jnp.min(start_sets[part])
        )
        work = partial(
            attend_half,
            query_sets[part],
            pos_sets[part],
            start_sets[part],
            key_piece,
            value_piece,
            key_pos,
        )
        recurrent_state = lax.cond(active, work, unchanged, recurrent_state)
        bests.append(recurrent_state[0])
        sums.append(recurrent_state[1])
        accums.append(recurrent_state[2])
    total = jnp.stack(sums)
    accum = jnp.stack(accums)
    mixed = accum / total[..., None]
    mixed = jnp.transpose(mixed, (0, 3, 1, 2, 4)).reshape(2, half, heads_q * HEAD_WIDTH)
    gated = (mixed * jax.nn.sigmoid(gate_sets.astype(jnp.float32))).astype(jnp.bfloat16)
    attn_mixed = gated.reshape(rows, heads_q * HEAD_WIDTH)
    heads_k = delta_query.shape[1] // DK
    heads_v = update_rule_payload.shape[1] // DV
    group = heads_v // heads_k
    unit_query = jnp.repeat(
        normalize(delta_query.astype(jnp.float32).reshape(rows, heads_k, DK)) * DK ** (-0.5),
        group,
        axis=1,
    )
    unit_key = jnp.repeat(
        normalize(delta_key.astype(jnp.float32).reshape(rows, heads_k, DK)), group, axis=1
    )
    value_rows = update_rule_payload.astype(jnp.float32).reshape(rows, heads_v, DV)
    stretches = rows // STRETCH

    def blocked(field):
        return jnp.transpose(
            field.reshape(stretches, STRETCH, heads_v, field.shape[-1]), (0, 2, 1, 3)
        )

    stretch_query = blocked(unit_query)
    stretch_key = blocked(unit_key)
    stretch_value = blocked(value_rows)
    beta = jnp.transpose(delta_beta.reshape(stretches, STRETCH, heads_v), (0, 2, 1))
    decay_log = jnp.transpose(delta_decay.reshape(stretches, STRETCH, heads_v), (0, 2, 1))
    fresh = (shift_amount == 0).astype(jnp.int32).reshape(stretches, STRETCH)
    resets = jnp.cumsum(fresh, axis=1)
    cumulative = jnp.cumsum(decay_log, axis=-1)
    steps_index = jnp.arange(STRETCH)
    inclusive = steps_index[:, None] >= steps_index[None, :]
    strict = steps_index[:, None] > steps_index[None, :]
    same = (resets[:, :, None] == resets[:, None, :]) & inclusive[None]
    span = jnp.where(
        same[:, None],
        jnp.exp(jnp.minimum(cumulative[..., :, None] - cumulative[..., None, :], 0.0)),
        0.0,
    )
    entry = jnp.where(resets == 0, 1.0, 0.0)[:, None, :] * jnp.exp(cumulative)
    gram = jnp.einsum("chtk,chsk->chts", stretch_key, stretch_key, precision=highest_value)
    system = jnp.eye(STRETCH, dtype=jnp.float32) + jnp.where(
        strict, beta[..., None] * span * gram, 0.0
    )
    right_hand = jnp.concatenate(
        [(beta * entry)[..., None] * stretch_key, beta[..., None] * stretch_value], axis=-1
    )
    solved = jax.scipy.linalg.solve_triangular(system, right_hand, lower=True, unit_diagonal=True)
    wide_keys = solved[..., :DK]
    base_values = solved[..., DK:]
    probe = (
        jnp.einsum("chtk,chsk->chts", stretch_query, stretch_key, precision=highest_value) * span
    )
    intra = jnp.einsum("chts,chsv->chtv", probe, base_values, precision=highest_value)
    reach = entry[..., None] * stretch_query - jnp.einsum(
        "chts,chsk->chtk", probe, wide_keys, precision=highest_value
    )
    weighted = span[..., -1, :][..., None] * stretch_key
    identity_map = jnp.eye(DK, dtype=jnp.float32)
    stretch_maps = entry[..., -1][..., None, None] * identity_map - jnp.einsum(
        "chsa,chsb->chab", weighted, wide_keys, precision=highest_value
    )
    stretch_adds = jnp.einsum("chsa,chsv->chav", weighted, base_values, precision=highest_value)

    def compose(carry, item):
        total_map, total_add = carry
        stretch_map, stretch_add = item
        new_map = jnp.einsum("hab,hbc->hac", stretch_map, total_map, precision=highest_value)
        new_add = (
            jnp.einsum("hab,hbv->hav", stretch_map, total_add, precision=highest_value)
            + stretch_add
        )
        return ((new_map, new_add), None)

    start_map = jnp.tile(identity_map[None], (heads_v, 1, 1))
    empty_state = jnp.zeros((heads_v, DK, DV), jnp.float32)
    (processor_layout, device_add), unused_maps = lax.scan(
        compose, (start_map, empty_state), (stretch_maps, stretch_adds)
    )

    def relay(step, recurrent_state):
        leaving = (
            jnp.einsum("hab,hbv->hav", processor_layout, recurrent_state, precision=highest_value)
            + device_add
        )
        return shifted(leaving.astype(jnp.bfloat16), "ctx", 1).astype(leaving.dtype)

    incoming = lax.fori_loop(0, ranks - 1, relay, empty_state)

    def emit(recurrent_state, item):
        stretch_map, stretch_add, reachable_rows, inside_rows = item
        mixed_output = inside_rows + jnp.einsum(
            "yul,ylf->yuf", reachable_rows, recurrent_state, precision=highest_value
        )
        following = (
            jnp.einsum("hab,hbv->hav", stretch_map, recurrent_state, precision=highest_value)
            + stretch_add
        )
        return (following, mixed_output)

    final_state, outputs = lax.scan(emit, incoming, (stretch_maps, stretch_adds, reach, intra))
    outputs = jnp.transpose(outputs, (0, 2, 1, 3)).reshape(rows, heads_v, DV)
    spread = lax.rsqrt(jnp.mean(outputs * outputs, axis=-1, keepdims=True) + 1e-06)
    gate_rows = jax.nn.silu(delta_gate.astype(jnp.float32).reshape(rows, heads_v, DV))
    delta_mixed = (
        (outputs * spread * norm_gain * gate_rows).reshape(rows, heads_v * DV).astype(jnp.bfloat16)
    )
    return (attn_mixed, delta_mixed)


def solution(mesh):
    return jax.shard_map(
        per_device,
        mesh=mesh,
        in_specs=(
            P(("dp", "ctx")),
            P(("dp", "ctx"), None),
            P(("dp", "ctx"), None),
            P(("dp", "ctx"), None),
            P(("dp", "ctx"), None),
            P(("dp", "ctx"), None),
            P(("dp", "ctx"), None),
            P(("dp", "ctx"), None),
            P(("dp", "ctx"), None),
            P(("dp", "ctx"), None),
            P(("dp", "ctx"), None),
            P(),
        ),
        out_specs=(P(("dp", "ctx"), None), P(("dp", "ctx"), None)),
        check_vma=False,
    )
```

profile of v0, /device:TPU:9, one launch (start us, length us, event | category | flops | bytes accessed | tf_op | source)
XLA Modules:
  0.0 566.0 jit_solution(11906175830048067618)
XLA Ops:
  8.0 6.5 %psum.7 = s32[8]{0:T(128)S(1)} all-reduce(s32[8]{0:T(128)S(1)} %convert_reduce_fusion), channel_id=1, replica_groups=mesh['dp'=4,'ctx'=8] {'ctx'}, use_global_device_ids=true, to_apply=%region_2.0 | all-reduce | flops 8 | bytes 64 | tf_op jit(solution)/shard_map/psum | solution.py:102
  23.2 6.0 %add_bitcast_fusion = f32[2,16,1,128,128]{4,3,2,1,0:T(8,128)} fusion(f32[2,128,16,128]{3,1,0,2:T(8,128)S(1)} %bitcast.260, f32[128,128]{1,0:T(8,128)S(1)} %get-tuple-element.319, f32[2,16,128]{2,1,0:T(8,128)S(1)} %bitcast_bitcast_fusion, f32[2,16,128]{2,1,0:T(8,128)S(1)} %reduce_window_sum.30, f32[128,128]{1,0:T(8,128)S(1)} %get-tuple-element.318, ...), kind=kOutput, calls=%fused_computation.105 | convolution fusion | flops 810024960 | bytes 4423680 | tf_op jit(solution)/shard_map/chtk,chsk->chts/dot_general | solution.py:204
  29.2 316.0 %custom-call.4 = f32[2,16,1,128,128]{3,4,2,1,0:T(8,128)} custom-call(f32[2,16,1,128,128]{4,3,2,1,0:T(8,128)} %add_bitcast_fusion), custom_call_target="InvertDiagBlocksLowerTriangular" | custom-call | tf_op jit(solution)/shard_map/jit(_solve_triangular)/vmap(vmap())/triangular_solve | solution.py:211
  348.0 4.5 fusion.103
  354.0 3.8 fusion.72
  357.8 4.1 fusion.84
  362.0 3.5 fusion.92
  370.4 5.6 fusion.90
  376.0 6.0 %multiply_subtract_fusion = f32[2,16,128,128]{3,2,1,0:T(8,128)S(1)} fusion(f32[2,16,128,256]{3,2,1,0:T(8,128)S(1)} %copy-done.6, f32[2,128,16,128]{3,1,0,2:T(8,128)} %bitcast.264, f32[2,16,128]{2,1,0:T(8,128)S(1)} %bitcast.280, f32[128,128]{1,0:T(8,128)S(1)} %get-tuple-element.318, f32[2,16]{1,0:T(2,128)S(1)} %slice_reduce_fusion), kind=kOutput, calls=%fused_computation.107 | convolution fusion | flops 806879232 | bytes 6374400 | tf_op jit(solution)/shard_map/chsa,chsb->chab/dot_general | solution.py:223
  382.1 10.8 %while.40 = (s32[]{:T(128)}, f32[16,128,128]{2,1,0:T(8,128)S(1)}, f32[16,128,128]{2,1,0:T(8,128)}, f32[2,16,128,128]{3,2,1,0:T(8,128)S(1)}, f32[2,16,128,128]{3,2,1,0:T(8,128)}) while((s32[]{:T(128)}, f32[16,128,128]{2,1,0:T(8,128)S(1)}, f32[16,128,128]{2,1,0:T(8,128)}, f32[2,16,128,128]{3,2,1,0:T(8,128)S(1)}, ...), condition=%wide.region_20.21_spmd.clone.clone, body=%wide.region_19.20_spmd.clone.sunk.clone | while | flops 805830656 | bytes 19924072 | solution.py:240
  392.9 114.5 %while.41 = (s32[]{:T(128)}, f32[16,128,128]{2,1,0:T(8,128)}, f32[16,128,128]{2,1,0:T(8,128)S(1)}, f32[16,128,128]{2,1,0:T(8,128)}) while((s32[]{:T(128)}, f32[16,128,128]{2,1,0:T(8,128)}, f32[16,128,128]{2,1,0:T(8,128)S(1)}, f32[16,128,128]{2,1,0:T(8,128)}) %tuple.131), condition=%wide.region_22.23_spmd.clone.clone, body=%wide.region_21.22_spmd.clone.sunk.clone | while | flops 403701760 | bytes 7340135 | solution.py:251
  396.1 4.2 collective-permute-start
  400.3 6.4 %collective-permute-done = bf16[16,128,128]{2,1,0:T(8,128)(2,1)} collective-permute-done((bf16[16,128,128]{2,1,0:T(8,128)(2,1)}, bf16[16,128,128]{2,1,0:T(8,128)(2,1)}, u32[]{:S(2)}, u32[]{:S(2)}) %collective-permute-start) | collective-permute-done | bytes 524320 | tf_op jit(solution)/shard_map/while/body/eval_jaxpr/ppermute | solution.py:23
  408.8 3.5 fusion.177
  412.3 4.4 collective-permute-start
  416.7 6.4 %collective-permute-done = bf16[16,128,128]{2,1,0:T(8,128)(2,1)} collective-permute-done((bf16[16,128,128]{2,1,0:T(8,128)(2,1)}, bf16[16,128,128]{2,1,0:T(8,128)(2,1)}, u32[]{:S(2)}, u32[]{:S(2)}) %collective-permute-start) | collective-permute-done | bytes 524320 | tf_op jit(solution)/shard_map/while/body/eval_jaxpr/ppermute | solution.py:23
  425.3 3.5 fusion.177
  428.8 4.4 collective-permute-start
  433.2 6.4 %collective-permute-done = bf16[16,128,128]{2,1,0:T(8,128)(2,1)} collective-permute-done((bf16[16,128,128]{2,1,0:T(8,128)(2,1)}, bf16[16,128,128]{2,1,0:T(8,128)(2,1)}, u32[]{:S(2)}, u32[]{:S(2)}) %collective-permute-start) | collective-permute-done | bytes 524320 | tf_op jit(solution)/shard_map/while/body/eval_jaxpr/ppermute | solution.py:23
  445.2 4.4 collective-permute-start
  449.6 6.4 %collective-permute-done = bf16[16,128,128]{2,1,0:T(8,128)(2,1)} collective-permute-done((bf16[16,128,128]{2,1,0:T(8,128)(2,1)}, bf16[16,128,128]{2,1,0:T(8,128)(2,1)}, u32[]{:S(2)}, u32[]{:S(2)}) %collective-permute-start) | collective-permute-done | bytes 524320 | tf_op jit(solution)/shard_map/while/body/eval_jaxpr/ppermute | solution.py:23
  461.6 4.4 collective-permute-start
  466.0 6.4 %collective-permute-done = bf16[16,128,128]{2,1,0:T(8,128)(2,1)} collective-permute-done((bf16[16,128,128]{2,1,0:T(8,128)(2,1)}, bf16[16,128,128]{2,1,0:T(8,128)(2,1)}, u32[]{:S(2)}, u32[]{:S(2)}) %collective-permute-start) | collective-permute-done | bytes 524320 | tf_op jit(solution)/shard_map/while/body/eval_jaxpr/ppermute | solution.py:23
  478.1 4.4 collective-permute-start
  482.5 6.4 %collective-permute-done = bf16[16,128,128]{2,1,0:T(8,128)(2,1)} collective-permute-done((bf16[16,128,128]{2,1,0:T(8,128)(2,1)}, bf16[16,128,128]{2,1,0:T(8,128)(2,1)}, u32[]{:S(2)}, u32[]{:S(2)}) %collective-permute-start) | collective-permute-done | bytes 524320 | tf_op jit(solution)/shard_map/while/body/eval_jaxpr/ppermute | solution.py:23
  494.5 4.4 collective-permute-start
  498.9 6.4 %collective-permute-done = bf16[16,128,128]{2,1,0:T(8,128)(2,1)} collective-permute-done((bf16[16,128,128]{2,1,0:T(8,128)(2,1)}, bf16[16,128,128]{2,1,0:T(8,128)(2,1)}, u32[]{:S(2)}, u32[]{:S(2)}) %collective-permute-start) | collective-permute-done | bytes 524320 | tf_op jit(solution)/shard_map/while/body/eval_jaxpr/ppermute | solution.py:23
  507.4 15.3 %while.39 = (s32[]{:T(128)}, f32[16,128,128]{2,1,0:T(8,128)}, f32[2,16,128,128]{3,2,1,0:T(8,128)}, f32[2,16,128,128]{3,2,1,0:T(8,128)S(1)}, f32[2,16,128,128]{3,...) while((s32[]{:T(128)}, f32[16,128,128]{2,1,0:T(8,128)}, ...), condition=%wide.region_25.26_spmd.clone, body=%wide.region_24.25_spmd.sunk.clone | while | flops 805830656 | bytes 27265156 | solution.py:264
  509.3 3.6 fusion.169
  517.0 3.5 fusion.169
  537.1 8.5 %conditional.2 = (f32[1,1,8,128]{3,2,1,0:T(8,128)S(1)}, f32[1,1,8,128,256]{4,3,2,1,0:T(8,128)S(1)}) conditional(s32[]{:T(128)} %convert_element_type.84, () %tuple.44, (s32[2048]{0:T(1024)S(1)}, s32[2048]{0:T(1024)S(1)}, s32[128]{0:T(128)S(1)}, s32[128]{0:T(128)S(1)}, bf16[2048,1,256]{0,2,1:T(8,128)(2,1)}, ...), branch_computations={%region_6.7_spmd, %region_7.10_spmd} | conditional | flops 2175802368 | bytes 40432712 | solution.py:157
  545.6 9.0 %conditional.3 = (f32[1,1,8,128]{3,2,1,0:T(8,128)S(1)}, f32[1,1,8,128,256]{4,3,2,1,0:T(8,128)S(1)}) conditional(s32[]{:T(128)} %convert_element_type.87, () %tuple.46, (s32[2048]{0:T(1024)S(1)}, s32[2048]{0:T(1024)S(1)}, s32[128]{0:T(128)S(1)}, s32[128]{0:T(128)S(1)}, bf16[2048,1,256]{0,2,1:T(8,128)(2,1)}, ...), branch_computations={%region_12.13_spmd, %region_13.16_spmd} | conditional | flops 2175802368 | bytes 36238380 | solution.py:157
  (161 shorter events, 102.5 us)
Async XLA Ops:
  7.2 13.5 %copy-start = (f32[256,16]{0,1:T(8,128)S(1)}, f32[256,16]{0,1:T(8,128)}, u32[]{:S(2)}) copy-start(f32[256,16]{0,1:T(8,128)} %param.30) | copy-start | bytes 49156
  7.2 529.9 %all-gather.3.cloned.1.call-start = ((), (), s32[]{:S(2)}) async-start(), calls=%async_computation | async-start | bytes 1179648 | tf_op jit(solution)/shard_map/all_gather | solution.py:134
  16.8 520.3 %all-gather.5.cloned.1.call-start = ((), (), s32[]{:S(2)}) async-start(), calls=%async_computation.1 | async-start | bytes 1179648 | tf_op jit(solution)/shard_map/all_gather | solution.py:135
  23.2 347.2 %copy-start.4 = (f32[256,8,2,128]{3,0,2,1:T(8,128)}, f32[256,8,2,128]{3,0,2,1:T(8,128)S(1)}, u32[]{:S(2)}) copy-start(f32[256,8,2,128]{3,0,2,1:T(8,128)S(1)} %broadcast_in_dim.138) | copy-start | bytes 6291460
  23.2 322.0 %copy-start.12 = (bf16[256,2048]{1,0:T(8,128)(2,1)S(1)}, bf16[256,2048]{1,0:T(8,128)(2,1)}, u32[]{:S(2)}) copy-start(bf16[256,2048]{1,0:T(8,128)(2,1)} %param.29) | copy-start | bytes 3145732
  345.4 1.0 copy-start.15
  352.4 1.6 copy-start.11
  357.8 4.2 copy-start.5
  367.0 3.4 copy-start.6
  382.3 1.9 copy-start.2
  387.6 1.9 copy-start.2
  396.1 10.6 %collective-permute-start = (bf16[16,128,128]{2,1,0:T(8,128)(2,1)}, bf16[16,128,128]{2,1,0:T(8,128)(2,1)}, u32[]{:S(2)}, u32[]{:S(2)}) collective-permute-start(bf16[16,128,128]{2,1,0:T(8,128)(2,1)} %fusion.177), channel_id=1, source_target_pairs={{0,1},{1,2},{2,3},{3,4},{4,5},{5,6},{6,7},{8,9},{9,10},{10,11},{11... | collective-permute-start | bytes 1572872 | tf_op jit(solution)/shard_map/while/body/eval_jaxpr/ppermute | solution.py:23
  412.3 10.8 %collective-permute-start = (bf16[16,128,128]{2,1,0:T(8,128)(2,1)}, bf16[16,128,128]{2,1,0:T(8,128)(2,1)}, u32[]{:S(2)}, u32[]{:S(2)}) collective-permute-start(bf16[16,128,128]{2,1,0:T(8,128)(2,1)} %fusion.177), channel_id=1, source_target_pairs={{0,1},{1,2},{2,3},{3,4},{4,5},{5,6},{6,7},{8,9},{9,10},{10,11},{11... | collective-permute-start | bytes 1572872 | tf_op jit(solution)/shard_map/while/body/eval_jaxpr/ppermute | solution.py:23
  428.8 10.8 %collective-permute-start = (bf16[16,128,128]{2,1,0:T(8,128)(2,1)}, bf16[16,128,128]{2,1,0:T(8,128)(2,1)}, u32[]{:S(2)}, u32[]{:S(2)}) collective-permute-start(bf16[16,128,128]{2,1,0:T(8,128)(2,1)} %fusion.177), channel_id=1, source_target_pairs={{0,1},{1,2},{2,3},{3,4},{4,5},{5,6},{6,7},{8,9},{9,10},{10,11},{11... | collective-permute-start | bytes 1572872 | tf_op jit(solution)/shard_map/while/body/eval_jaxpr/ppermute | solution.py:23
  445.2 10.8 %collective-permute-start = (bf16[16,128,128]{2,1,0:T(8,128)(2,1)}, bf16[16,128,128]{2,1,0:T(8,128)(2,1)}, u32[]{:S(2)}, u32[]{:S(2)}) collective-permute-start(bf16[16,128,128]{2,1,0:T(8,128)(2,1)} %fusion.177), channel_id=1, source_target_pairs={{0,1},{1,2},{2,3},{3,4},{4,5},{5,6},{6,7},{8,9},{9,10},{10,11},{11... | collective-permute-start | bytes 1572872 | tf_op jit(solution)/shard_map/while/body/eval_jaxpr/ppermute | solution.py:23
  461.6 10.8 %collective-permute-start = (bf16[16,128,128]{2,1,0:T(8,128)(2,1)}, bf16[16,128,128]{2,1,0:T(8,128)(2,1)}, u32[]{:S(2)}, u32[]{:S(2)}) collective-permute-start(bf16[16,128,128]{2,1,0:T(8,128)(2,1)} %fusion.177), channel_id=1, source_target_pairs={{0,1},{1,2},{2,3},{3,4},{4,5},{5,6},{6,7},{8,9},{9,10},{10,11},{11... | collective-permute-start | bytes 1572872 | tf_op jit(solution)/shard_map/while/body/eval_jaxpr/ppermute | solution.py:23
  478.1 10.8 %collective-permute-start = (bf16[16,128,128]{2,1,0:T(8,128)(2,1)}, bf16[16,128,128]{2,1,0:T(8,128)(2,1)}, u32[]{:S(2)}, u32[]{:S(2)}) collective-permute-start(bf16[16,128,128]{2,1,0:T(8,128)(2,1)} %fusion.177), channel_id=1, source_target_pairs={{0,1},{1,2},{2,3},{3,4},{4,5},{5,6},{6,7},{8,9},{9,10},{10,11},{11... | collective-permute-start | bytes 1572872 | tf_op jit(solution)/shard_map/while/body/eval_jaxpr/ppermute | solution.py:23
  494.5 10.8 %collective-permute-start = (bf16[16,128,128]{2,1,0:T(8,128)(2,1)}, bf16[16,128,128]{2,1,0:T(8,128)(2,1)}, u32[]{:S(2)}, u32[]{:S(2)}) collective-permute-start(bf16[16,128,128]{2,1,0:T(8,128)(2,1)} %fusion.177), channel_id=1, source_target_pairs={{0,1},{1,2},{2,3},{3,4},{4,5},{5,6},{6,7},{8,9},{9,10},{10,11},{11... | collective-permute-start | bytes 1572872 | tf_op jit(solution)/shard_map/while/body/eval_jaxpr/ppermute | solution.py:23
  507.4 1.9 copy-start.7
  509.3 3.6 copy-start.3
  515.1 1.9 copy-start.7
  517.0 3.6 copy-start.3
  522.7 2.5 copy-start.8
  525.2 7.1 %copy-start.10 = (bf16[256,8,192]{0,2,1:T(8,128)(2,1)S(1)}, bf16[256,8,192]{0,2,1:T(8,128)(2,1)}, u32[]{:S(2)}) copy-start(bf16[256,8,192]{0,2,1:T(8,128)(2,1)} %slice.89) | copy-start | bytes 2359300
  527.7 4.7 copy-start.17
  532.3 1.6 copy-start.9
  532.3 1.8 copy-start.13
  538.4 1.2 copy-start.18
  539.7 1.4 copy-start.19
  547.5 2.7 copy-start.20
  556.2 1.2 copy-start.14
  557.1 1.8 copy-start.1
  (1 other events, 0.7 us)
Sparse Core Ops, SparseCore 0:
  16.9 26.6 all-gather.2
  45.2 20.6 all-gather.4
where the time goes:
time: 574 us; the launch traced here: 566 us
  other arithmetic  357 us (62%)
  matrix products  84.4 us (15%)
  waiting for transfers between devices  45.7 us (8%)
  starting transfers between devices  30.5 us (5%)
  local copies, waits for them, and re-layouts  23.6 us (4%)
  between operations  17.3 us (3%)
  blocking collectives  6.51 us (1%)
    another operation x2, other arithmetic, per_device(): jax.scipy.linalg.solve_triangular(system, right_hand, lower=True, unit_di...  316 us
    ppermute x7, waiting for transfers between devices, shifted(): lax.ppermute(value, axis, [(source, source + steps) for source in range(i...  44.9 us
    ppermute x7, starting transfers between devices, shifted(): lax.ppermute(value, axis, [(source, source + steps) for source in range(i...  30.4 us
    dot_general x7, matrix products, relay(): jnp.einsum('hab,hbv->hav', processor_layout, recurrent_state, precision=h...  24.3 us
    convert_element_type x7, other arithmetic, relay(): return shifted(leaving.astype(jnp.bfloat16), 'ctx', 1).astype(leaving.dtype)  14.8 us
  transfers between devices with their start and end apart: 9, of which 7 were waited for; matrix products, arithmetic and copies ran while one was open for 77% of the time, Pallas kernels for 0%

commit v1 on v0

v1 whole, which is shorter than its diff:
```python
from functools import partial

import jax
import jax.numpy as jnp
from jax import lax
from jax.experimental import pallas as pl
from jax.experimental.pallas import tpu as pltpu
from jax.sharding import PartitionSpec as P

HEAD_WIDTH = 256
ROTARY_ENTRIES = 64
DK = 128
DV = 128
DOCS = 8
ROPE_THETA = 10000000.0
LOG2E = 1.4426950408889634
MASKED = -1e30
EPS = 1e-6
LEVELS = 7
TILE = 128
KEYS_PER_STEP = 2
VMEM_LIMIT = 48 * 1024 * 1024

f32 = jnp.float32
bf16 = jnp.bfloat16


def dot(a, b, precision=None):
    return jnp.dot(a, b, preferred_element_type=f32, precision=precision)


def params():
    return pltpu.CompilerParams(vmem_limit_bytes=VMEM_LIMIT)


def cost(flops, nbytes, exps=0):
    return pl.CostEstimate(flops=flops, bytes_accessed=nbytes, transcendentals=exps)


def delta_local_kernel(
    half_ref,
    seg_ref,
    q_ref,
    k_ref,
    v_ref,
    beta_ref,
    decay_ref,
    map_add_ref,
    reach_ref,
    inner_ref,
    mask_ref,
    level_ref,
    crow_ref,
    ccol_ref,
    bcol_ref,
    first_ref,
):
    rows = q_ref.shape[0]
    step = pl.program_id(0)
    heads = 2 * KEYS_PER_STEP

    @pl.when(step == 0)
    def _():
        seg_row = seg_ref[...]
        seg_col = jnp.transpose(jnp.broadcast_to(seg_row, (TILE, rows)))
        seg_cols = jnp.concatenate([seg_col] * (rows // TILE), axis=1)
        r = lax.broadcasted_iota(jnp.int32, (rows, rows), 0)
        c = lax.broadcasted_iota(jnp.int32, (rows, rows), 1)
        mask_ref[...] = jnp.where((seg_cols == seg_row) & (r >= c), 0.0, MASKED)
        first_ref[...] = jnp.where(seg_col == seg_row[:, :1], 1.0, 0.0)
        r = lax.broadcasted_iota(jnp.int32, (TILE, TILE), 0)
        c = lax.broadcasted_iota(jnp.int32, (TILE, TILE), 1)
        top = jnp.bitwise_xor(r, c)
        for level in range(LEVELS):
            inside = (r > c) & (lax.shift_right_logical(top, level) == 1)
            level_ref[level] = jnp.where(inside, 1.0, 0.0).astype(bf16)
        all_heads = decay_ref.shape[1]
        base = half_ref[0] * (all_heads // 2)
        er = lax.broadcasted_iota(jnp.int32, (all_heads, TILE), 0)
        ec = lax.broadcasted_iota(jnp.int32, (all_heads, TILE), 1)
        pick = jnp.where(er - ec == base, 1.0, 0.0)
        tr = lax.broadcasted_iota(jnp.int32, (rows, rows), 0)
        tc = lax.broadcasted_iota(jnp.int32, (rows, rows), 1)
        tril = jnp.where(tr >= tc, 1.0, 0.0)
        decay = dot(decay_ref[...], pick, lax.Precision.HIGHEST) * LOG2E
        cumulative = dot(tril, decay, lax.Precision.HIGHEST)
        ccol_ref[...] = cumulative
        crow_ref[...] = jnp.transpose(cumulative)
        bcol_ref[...] = dot(beta_ref[...], pick, lax.Precision.HIGHEST)

    shift = lax.rem(TILE - step * heads, TILE)
    ccol = pltpu.roll(ccol_ref[...], shift, 1)
    bcol = pltpu.roll(bcol_ref[...], shift, 1)
    first = first_ref[...]
    eye = jnp.where(
        lax.broadcasted_iota(jnp.int32, (TILE, TILE), 0)
        == lax.broadcasted_iota(jnp.int32, (TILE, TILE), 1),
        1.0,
        0.0,
    )
    work = []
    for kk in range(KEYS_PER_STEP):
        cols = slice(kk * DK, (kk + 1) * DK)
        k_raw = k_ref[:, cols]
        q_raw = q_ref[:, cols]
        kf = k_raw.astype(f32)
        qf = q_raw.astype(f32)
        rk_col = lax.rsqrt(jnp.sum(kf * kf, axis=1, keepdims=True) + EPS)
        rq_col = lax.rsqrt(jnp.sum(qf * qf, axis=1, keepdims=True) + EPS) * DK**-0.5
        kt = jnp.transpose(kf)
        rk_row = lax.rsqrt(jnp.sum(kt * kt, axis=0, keepdims=True) + EPS)
        ktb = kt.astype(bf16)
        upper = dot(jnp.concatenate([k_raw[:TILE], q_raw[:TILE]], axis=0), ktb[:, :TILE])
        lower = dot(jnp.concatenate([k_raw[TILE:], q_raw[TILE:]], axis=0), ktb)
        gram1 = upper[:TILE] * rk_row[:, :TILE]
        probe1 = upper[TILE:] * rk_row[:, :TILE] * rq_col[:TILE]
        gram2 = lower[:TILE] * rk_row
        probe2 = lower[TILE:] * rk_row * rq_col[TILE:]
        kn = kf * rk_col
        qn = qf * rq_col
        for j in range(2):
            h = 2 * kk + j
            cc = ccol[:, h : h + 1]
            bt = bcol[:, h : h + 1]
            cr = crow_ref[pl.ds(step * heads + h, 1), :]
            span1 = jnp.exp2(cc[:TILE] - cr[:, :TILE] + mask_ref[:TILE, :TILE])
            span2 = jnp.exp2(cc[TILE:] - cr + mask_ref[TILE:, :])
            scale = -bt * rk_col
            d11 = (span1 * scale[:TILE] * gram1).astype(bf16)
            d2 = (span2 * scale[TILE:] * gram2).astype(bf16)
            p11 = (span1 * probe1).astype(bf16)
            p2 = (span2 * probe2).astype(bf16)
            entry = jnp.exp2(cc) * first
            right = jnp.concatenate(
                [bt * entry * kn, bt * v_ref[:, h * DV : (h + 1) * DV].astype(f32)], axis=1
            )
            kd = (kt * (rk_row * span2[TILE - 1 : TILE, :])).astype(bf16)
            work.append(
                dict(h=h, d=[d11, d2[:, TILE:]], d21=d2[:, :TILE], p11=p11, p2=p2, kd=kd,
                     right=right, reach=entry * qn, last=entry[rows - 1 : rows, :])
            )
    mats = [m for w in work for m in w["d"]]
    inverses = [m * level_ref[0] for m in mats]
    for level in range(1, LEVELS):
        keep = level_ref[level]
        picked = [m * keep for m in mats]
        ys = [
            (p.astype(f32) + dot(p, x)).astype(bf16) for p, x in zip(picked, inverses)
        ]
        inverses = [
            x + (y.astype(f32) + dot(x, y)).astype(bf16) for x, y in zip(inverses, ys)
        ]
    for i, w in enumerate(work):
        x1, x2 = inverses[2 * i], inverses[2 * i + 1]
        h = w["h"]
        r1 = w["right"][:TILE]
        u1 = (r1 + dot(x1, r1.astype(bf16))).astype(bf16)
        r2 = w["right"][TILE:] + dot(w["d21"], u1)
        u2 = (r2 + dot(x2, r2.astype(bf16))).astype(bf16)
        u = jnp.concatenate([u1, u2], axis=0)
        pu = jnp.concatenate([dot(w["p11"], u1), dot(w["p2"], u)], axis=0)
        ma = dot(w["kd"], u)
        map_add_ref[h] = jnp.concatenate(
            [w["last"] * eye - ma[:, :DK], ma[:, DK:]], axis=1
        ).astype(bf16)
        reach_ref[:, h * DK : (h + 1) * DK] = (w["reach"] - pu[:, :DK]).astype(bf16)
        inner_ref[:, h * DV : (h + 1) * DV] = pu[:, DK:].astype(inner_ref.dtype)


def delta_local(half, seg_row, query, key, value, beta, decay):
    rows = query.shape[0]
    heads = 2 * KEYS_PER_STEP
    n = value.shape[1] // DV // 2
    steps = n // heads
    kw = KEYS_PER_STEP * DK
    vw = heads * DV

    def at_half(i, s):
        return (0, s[0] * steps + i)

    def whole(i, s):
        return (0, 0)

    return pl.pallas_call(
        delta_local_kernel,
        grid_spec=pltpu.PrefetchScalarGridSpec(
            num_scalar_prefetch=1,
            grid=(steps,),
            in_specs=[
                pl.BlockSpec((1, rows), whole),
                pl.BlockSpec((rows, kw), at_half),
                pl.BlockSpec((rows, kw), at_half),
                pl.BlockSpec((rows, vw), at_half),
                pl.BlockSpec(beta.shape, whole),
                pl.BlockSpec(decay.shape, whole),
            ],
            out_specs=[
                pl.BlockSpec((heads, DK, DK + DV), lambda i, s: (i, 0, 0)),
                pl.BlockSpec((rows, heads * DK), lambda i, s: (0, i)),
                pl.BlockSpec((rows, vw), lambda i, s: (0, i)),
            ],
            scratch_shapes=[
                pltpu.VMEM((rows, rows), f32),
                pltpu.VMEM((LEVELS, TILE, TILE), bf16),
                pltpu.VMEM((TILE, rows), f32),
                pltpu.VMEM((rows, TILE), f32),
                pltpu.VMEM((rows, TILE), f32),
                pltpu.VMEM((rows, TILE), f32),
            ],
        ),
        out_shape=[
            jax.ShapeDtypeStruct((n, DK, DK + DV), bf16),
            jax.ShapeDtypeStruct((rows, n * DK), bf16),
            jax.ShapeDtypeStruct((rows, n * DV), f32),
        ],
        compiler_params=params(),
        cost_estimate=cost(6 * 10**9, 3 * 2**20),
        name="delta_local",
    )(half, seg_row, query, key, value, beta, decay)


def flag(flags_ref, i):
    return flags_ref[i].astype(f32)


def ordered(flags_ref, mine, other):
    odd = flags_ref[0] == 1
    return jnp.where(odd, other, mine), jnp.where(odd, mine, other)


def compose_kernel(flags_ref, mine_ref, other_ref, map_ref, add_ref):
    into, across = flag(flags_ref, 1), flag(flags_ref, 2)
    for h in range(mine_ref.shape[0]):
        early, late = ordered(flags_ref, mine_ref[h], other_ref[h])
        both = dot(late[:, :DK], early) * across
        map_ref[h] = (both[:, :DK] * into).astype(bf16)
        add_ref[h] = (both[:, DK:] + late[:, DK:].astype(f32)).astype(bf16)


def relay_kernel(map_ref, add_ref, state_ref, out_ref):
    for h in range(map_ref.shape[0]):
        out_ref[h] = (dot(map_ref[h], state_ref[h]) + add_ref[h].astype(f32)).astype(bf16)


def arrive_kernel(flags_ref, mine_ref, other_ref, state_ref, keep_ref, give_ref):
    into, across = flag(flags_ref, 1), flag(flags_ref, 2)
    odd = flags_ref[0] == 1
    for h in range(mine_ref.shape[0]):
        early, _ = ordered(flags_ref, mine_ref[h], other_ref[h])
        first = state_ref[h] * into.astype(bf16)
        second = (
            (dot(early[:, :DK], first) + early[:, DK:].astype(f32)) * across
        ).astype(bf16)
        keep_ref[h] = jnp.where(odd, second, first)
        give_ref[h] = jnp.where(odd, first, second)


SMEM = pl.BlockSpec(memory_space=pltpu.SMEM)
VMEM = pl.BlockSpec(memory_space=pltpu.VMEM)


def small_call(kernel, name, outs, *args, scalars=0):
    return pl.pallas_call(
        kernel,
        in_specs=[SMEM] * scalars + [VMEM] * (len(args) - scalars),
        out_specs=[VMEM] * len(outs),
        out_shape=outs,
        compiler_params=params(),
        cost_estimate=cost(10**8, 2**20),
        name=name,
    )(*args)


def delta_out_kernel(half_ref, reach_ref, inner_ref, state_ref, gate_ref, gain_ref, *rest):
    out_ref = rest[-1]
    gain = gain_ref[...]
    for h in range(state_ref.shape[0]):
        cols = slice(h * DV, (h + 1) * DV)
        out = inner_ref[:, cols] + dot(reach_ref[:, cols], state_ref[h])
        spread = lax.rsqrt(jnp.mean(out * out, axis=1, keepdims=True) + EPS)
        gate = gate_ref[:, cols].astype(f32)
        gate = gate * jax.nn.sigmoid(gate)
        out_ref[:, cols] = (out * spread * gain * gate).astype(bf16)


def delta_out(half, reach, inner, state, gate, gain, partial_out=None):
    rows = reach.shape[0]
    n = state.shape[0]
    heads = 4
    steps = n // heads

    def at_half(i, s):
        return (0, s[0] * steps + i)

    in_specs = [
        pl.BlockSpec((rows, heads * DK), lambda i, s: (0, i)),
        pl.BlockSpec((rows, heads * DV), lambda i, s: (0, i)),
        pl.BlockSpec((heads, DK, DV), lambda i, s: (i, 0, 0)),
        pl.BlockSpec((rows, heads * DV), at_half),
        pl.BlockSpec((1, DV), lambda i, s: (0, 0)),
    ]
    args = [half, reach, inner, state, gate, gain]
    aliases = {}
    if partial_out is not None:
        in_specs.append(pl.BlockSpec(memory_space=pl.ANY))
        args.append(partial_out)
        aliases = {6: 0}
    return pl.pallas_call(
        delta_out_kernel,
        grid_spec=pltpu.PrefetchScalarGridSpec(
            num_scalar_prefetch=1,
            grid=(steps,),
            in_specs=in_specs,
            out_specs=pl.BlockSpec((rows, heads * DV), at_half),
        ),
        out_shape=jax.ShapeDtypeStruct(gate.shape, bf16),
        input_output_aliases=aliases,
        compiler_params=params(),
        cost_estimate=cost(10**8, 3 * 2**20),
        name="delta_out",
    )(*args)


def attention_kernel(ids_ref, freq_ref, q_ref, gate_ref, *rest):
    *pieces, out_ref, kt_ref, v_ref, mask_ref, cos_ref, sin_ref = rest
    rows = q_ref.shape[0]
    window = ids_ref.shape[1]
    half = ROTARY_ENTRIES // 2

    @pl.when(pl.program_id(0) == 0)
    def _():
        ids = jnp.broadcast_to(ids_ref[...], (DOCS, window))
        docs = lax.broadcasted_iota(jnp.int32, (DOCS, window), 0).astype(f32)
        before = jnp.sum(jnp.where(ids < docs, 1.0, 0.0), axis=1, keepdims=True)
        start = jnp.sum(jnp.where(ids == docs, before, 0.0), axis=0, keepdims=True)
        place = lax.broadcasted_iota(jnp.int32, (1, window), 1).astype(f32)
        angle = freq_ref[:, :1] * (place - start)
        cosine = jnp.cos(angle)
        sine = jnp.sin(angle)
        for b, (ref, index) in enumerate(blocks_of(pieces)):
            cols = slice(b * rows, (b + 1) * rows)
            piece = ref[...] if index is None else ref[index]
            kt = jnp.transpose(piece[:, :HEAD_WIDTH].astype(f32))
            one, two = kt[:half], kt[half:ROTARY_ENTRIES]
            cb, sb = cosine[:, cols], sine[:, cols]
            kt_ref[:half, cols] = (one * cb - two * sb).astype(bf16)
            kt_ref[half:ROTARY_ENTRIES, cols] = (two * cb + one * sb).astype(bf16)
            kt_ref[ROTARY_ENTRIES:, cols] = kt[ROTARY_ENTRIES:].astype(bf16)
            v_ref[cols, :] = piece[:, HEAD_WIDTH:]
        cq, sq = cosine[:, window - rows :], sine[:, window - rows :]
        rest_rows = TILE - ROTARY_ENTRIES
        cos_ref[...] = jnp.transpose(
            jnp.concatenate([cq, cq, jnp.ones((rest_rows, rows), f32)], axis=0)
        )
        sin_ref[...] = jnp.transpose(
            jnp.concatenate([-sq, sq, jnp.zeros((rest_rows, rows), f32)], axis=0)
        )
        own = ids_ref[:, window - rows :]
        own_col = jnp.transpose(jnp.broadcast_to(own, (TILE, rows)))
        own_cols = jnp.concatenate([own_col] * (window // TILE), axis=1)
        r = lax.broadcasted_iota(jnp.int32, (rows, window), 0) + (window - rows)
        c = lax.broadcasted_iota(jnp.int32, (rows, window), 1)
        mask_ref[...] = jnp.where((own_cols == ids_ref[...]) & (c <= r), 0.0, MASKED)

    scaling = HEAD_WIDTH**-0.5
    lane = lax.broadcasted_iota(jnp.int32, (rows, TILE), 1)
    for h in range(q_ref.shape[1] // HEAD_WIDTH):
        base = h * HEAD_WIDTH
        x = q_ref[:, base : base + TILE].astype(f32)
        swapped = jnp.where(lane < half, pltpu.roll(x, TILE - half, 1), pltpu.roll(x, half, 1))
        rotated = ((x * cos_ref[...] + swapped * sin_ref[...]) * scaling).astype(bf16)
        tail = q_ref[:, base + TILE : base + HEAD_WIDTH] * jnp.asarray(scaling, bf16)
        scores = dot(jnp.concatenate([rotated, tail], axis=1), kt_ref[...]) + mask_ref[...]
        best = jnp.max(scores, axis=1, keepdims=True)
        weights = jnp.exp(scores - best)
        total = jnp.sum(weights, axis=1, keepdims=True)
        mixed = dot(weights.astype(bf16), v_ref[...])
        gate = jax.nn.sigmoid(gate_ref[:, base : base + HEAD_WIDTH].astype(f32))
        out_ref[:, base : base + HEAD_WIDTH] = (mixed / total * gate).astype(bf16)


def blocks_of(pieces):
    own, *same, other = pieces
    order = [(own, None)]
    for i, ref in enumerate(same):
        order += [(other, i), (ref, None)]
    return order[::-1]


def attention(ids, freq, query, gate, own, same, other):
    rows = query.shape[0]
    window = ids.shape[1]
    heads = 2
    width = heads * HEAD_WIDTH
    pieces = [own, *same, other]
    whole = [pl.BlockSpec(p.shape, lambda i, n=p.ndim: (0,) * n) for p in pieces]
    return pl.pallas_call(
        attention_kernel,
        grid=(query.shape[1] // width,),
        in_specs=[
            pl.BlockSpec(ids.shape, lambda i: (0, 0)),
            pl.BlockSpec(freq.shape, lambda i: (0, 0)),
            pl.BlockSpec((rows, width), lambda i: (0, i)),
            pl.BlockSpec((rows, width), lambda i: (0, i)),
            *whole,
        ],
        out_specs=pl.BlockSpec((rows, width), lambda i: (0, i)),
        out_shape=jax.ShapeDtypeStruct(query.shape, bf16),
        scratch_shapes=[
            pltpu.VMEM((HEAD_WIDTH, window), bf16),
            pltpu.VMEM((window, HEAD_WIDTH), bf16),
            pltpu.VMEM((rows, window), f32),
            pltpu.VMEM((rows, TILE), f32),
            pltpu.VMEM((rows, TILE), f32),
        ],
        compiler_params=params(),
        cost_estimate=cost(6 * 10**9, 5 * 2**20, 3 * 10**6),
        name="attention",
    )(ids, freq, query, gate, *pieces)


def up_chip(value, ranks):
    return lax.ppermute(value, "ctx", [(i, i + 2) for i in range(ranks - 2)])


def swap_cores(value, ranks):
    return lax.ppermute(value, "ctx", [(i, i ^ 1) for i in range(ranks)])


def per_device(
    segment_ids,
    attn_query,
    attention_keys,
    attention_values,
    attn_gate,
    delta_query,
    delta_key,
    update_rule_payload,
    delta_beta,
    delta_decay,
    delta_gate,
    norm_gain,
):
    ranks = lax.axis_size("ctx")
    rank = lax.axis_index("ctx")
    rows = segment_ids.shape[0]
    hops = ranks // 4
    core = rank % 2
    odd = core == 1

    ids = lax.all_gather(segment_ids, "ctx", axis=0, tiled=True)

    own = jnp.concatenate([attention_keys, attention_values], axis=1)
    same = []
    for _ in range(hops):
        same.append(up_chip(same[-1] if same else own, ranks))
    chain = [own, *same]
    other = swap_cores(
        jnp.stack([jnp.where(odd, chain[i + 1], chain[i]) for i in range(hops)]), ranks
    )

    seg_row = segment_ids.astype(f32).reshape(1, rows)
    keep_half = core.reshape(1).astype(jnp.int32)
    give_half = 1 - keep_half
    local = partial(
        delta_local,
        seg_row=seg_row,
        query=delta_query,
        key=delta_key,
        value=update_rule_payload,
        beta=delta_beta,
        decay=delta_decay,
    )
    give_ma, give_reach, give_inner = local(give_half)
    other_ma = swap_cores(give_ma, ranks)
    keep_ma, keep_reach, keep_inner = local(keep_half)

    chip_first = (rank - core) * rows
    into = (rank > 1) & (ids[jnp.maximum(chip_first - 1, 0)] == ids[chip_first])
    across = ids[chip_first + rows - 1] == ids[chip_first + rows]
    flags = jnp.stack([core, into, across]).astype(jnp.int32)

    n = keep_ma.shape[0]
    state_like = jax.ShapeDtypeStruct((n, DK, DV), bf16)
    chip_map, chip_add = small_call(
        compose_kernel, "compose", [state_like] * 2, flags, keep_ma, other_ma, scalars=1
    )
    state = up_chip(chip_add, ranks)
    for _ in range(hops - 1):
        (leaving,) = small_call(relay_kernel, "relay", [state_like], chip_map, chip_add, state)
        state = up_chip(leaving, ranks)
    keep_state, pass_state = small_call(
        arrive_kernel, "arrive", [state_like] * 2, flags, keep_ma, other_ma, state, scalars=1
    )
    give_state = swap_cores(pass_state, ranks)

    window = (2 * hops + 1) * rows
    padded = jnp.concatenate([jnp.full((window - rows,), -1, jnp.int32), ids]).astype(f32)
    window_ids = lax.dynamic_slice(padded, (rank * rows,), (window,)).reshape(1, window)
    index = jnp.arange(ROTARY_ENTRIES // 2).astype(f32)
    freq = ROPE_THETA ** (-2.0 * index / ROTARY_ENTRIES)
    freq = jnp.broadcast_to(freq[:, None], (ROTARY_ENTRIES // 2, TILE))
    attn_mixed = attention(window_ids, freq, attn_query, attn_gate, own, same, other)

    gain = norm_gain.reshape(1, DV)
    delta_mixed = delta_out(keep_half, keep_reach, keep_inner, keep_state, delta_gate, gain)
    delta_mixed = delta_out(
        give_half, give_reach, give_inner, give_state, delta_gate, gain, delta_mixed
    )
    return (attn_mixed, delta_mixed)


def solution(mesh):
    rows = P(("dp", "ctx"))
    wide = P(("dp", "ctx"), None)
    return jax.shard_map(
        per_device,
        mesh=mesh,
        in_specs=(rows,) + (wide,) * 10 + (P(),),
        out_specs=(wide, wide),
        check_vma=False,
    )
```

time: 574 us -> 89.1 us (0.16); the launches traced: 566 us -> 88.6 us
  other arithmetic: 357 us -> 2.09 us
  matrix products: 84.4 us -> 0 us
  Pallas kernels: 0 us -> 37.8 us
  waiting for transfers between devices: 45.7 us -> 12.1 us
  starting transfers between devices: 30.5 us -> 13.8 us
  between operations: 17.3 us -> 3.31 us
  local copies, waits for them, and re-layouts: 23.6 us -> 9.86 us
    another operation x7 -> x3, other arithmetic: 318 us -> 2 us  [the longest x2 1.92 us: per_device(): jnp.stack([jnp.where(odd, chain[i + 1], chain[i]) for i in range(hops)])]
    dot_general x25 -> x0, matrix products: 80.6 us -> none  [the longest x7 24.3 us: relay(): jnp.einsum('hab,hbv->hav', processor_layout, recurrent_state, precision=h...]
    pallas_call x0 -> x8, Pallas kernels: none -> 37.8 us  [the longest x2 21.7 us: delta_local(): pl.pallas_call(delta_local_kernel, grid_spec=pltpu.PrefetchScalarGridSpec...]
    ppermute x7, waiting for transfers between devices: 44.9 us -> 12.1 us  [the longest x4 12.1 us: up_chip(): return lax.ppermute(value, 'ctx', [(i, i + 2) for i in range(ranks - 2)])]
    convert_element_type x12 -> x2, other arithmetic: 19.3 us -> 0.09 us  [the longest x1 0.08 us: per_device(): jnp.concatenate([jnp.full((window - rows,), -1, jnp.int32), ids])]
    ppermute x7, starting transfers between devices: 30.4 us -> 13.8 us  [the longest x4 10.7 us: up_chip(): return lax.ppermute(value, 'ctx', [(i, i + 2) for i in range(ranks - 2)])]
    all_gather x0 -> x1, blocking collectives: none -> 9.59 us  [per_device(): ids = lax.all_gather(segment_ids, 'ctx', axis=0, tiled=True)]
    reduce_sum x6 -> x0, other arithmetic: 7.85 us -> none  [the longest x2 4.03 us: attend_half(): total = factor * total + jnp.sum(weights, axis=-1)]
  transfers between devices with their start and end apart: 9 -> 7, of which waited for: 7 -> 2; matrix products, arithmetic and copies ran while one was open for 77% -> 3% of each run, Pallas kernels for 0% -> 41%
where the time goes in v1:
time: 89.1 us; the launch traced here: 88.6 us
  Pallas kernels  37.8 us (42%)
  starting transfers between devices  13.8 us (15%)
  waiting for transfers between devices  12.1 us (14%)
  local copies, waits for them, and re-layouts  9.86 us (11%)
  blocking collectives  9.59 us (11%)
  between operations  3.31 us (4%)
  other arithmetic  2.09 us (2%)
    pallas_call x2, Pallas kernels, delta_local(): pl.pallas_call(delta_local_kernel, grid_spec=pltpu.PrefetchScalarGridSpec...  21.7 us
    ppermute x4, waiting for transfers between devices, up_chip(): return lax.ppermute(value, 'ctx', [(i, i + 2) for i in range(ranks - 2)])  12.1 us
    ppermute x4, starting transfers between devices, up_chip(): return lax.ppermute(value, 'ctx', [(i, i + 2) for i in range(ranks - 2)])  10.7 us
    pallas_call x1, Pallas kernels, attention(): pl.pallas_call(attention_kernel, grid=(query.shape[1] // width,), in_spec...  9.67 us
    all_gather x1, blocking collectives, per_device(): ids = lax.all_gather(segment_ids, 'ctx', axis=0, tiled=True)  9.59 us
    unnamed x41, local copies, waits for them, and re-layouts  9.11 us
    pallas_call x2, Pallas kernels, delta_out(): pl.pallas_call(delta_out_kernel, grid_spec=pltpu.PrefetchScalarGridSpec(n...  3.41 us
    ppermute x3, starting transfers between devices, swap_cores(): return lax.ppermute(value, 'ctx', [(i, i ^ 1) for i in range(ranks)])  3.05 us
  transfers between devices with their start and end apart: 7, of which 2 were waited for; matrix products, arithmetic and copies ran while one was open for 3% of the time, Pallas kernels for 41%

profile of v1, /device:TPU:9, one launch (start us, length us, event | category | flops | bytes accessed | tf_op | source)
XLA Modules:
  0.0 88.6 jit_solution(6954317876470264237)
XLA Ops:
  0.7 1.0 %constant_dynamic-update-slice_fusion.1 = bf16[256,512]{1,0:T(8,128)(2,1)S(1)} fusion(bf16[256,256]{1,0:T(8,128)(2,1)} %param.14), kind=kLoop, calls=%fused_computation.6 | loop fusion | bytes 262144
  1.7 3.2 %collective-permute-start = (bf16[256,512]{1,0:T(8,128)(2,1)S(1)}, bf16[256,512]{1,0:T(8,128)(2,1)}, u32[]{:S(2)}, u32[]{:S(2)}) collective-permute-start(bf16[256,512]{1,0:T(8,128)(2,1)S(1)} %constant_dynamic-update-slice_fusion.rest_0_), channel_id=1, source_target_pairs={{0,2},{1,3},{2,4},{3,5},{4,6},{5,7},{8,10},{9,11},{10,12},{11,13},... | collective-permute-start | bytes 786440 | tf_op jit(solution)/shard_map/ppermute | solution.py:423
  4.9 0.1 copy.19.beta_ref
  5.0 0.6 copy-done.17
  5.7 0.6 copy-done.18
  6.3 1.3 %copy-done.8 = bf16[256,2048]{1,0:T(8,128)(2,1)S(1)} copy-done((bf16[256,2048]{1,0:T(8,128)(2,1)S(1)}, bf16[256,2048]{1,0:T(8,128)(2,1)}, u32[]{:S(2)}) %copy-start.8) | copy-done | bytes 1048600
  7.6 1.0 %copy-done.14 = bf16[256,1024]{1,0:T(8,128)(2,1)S(1)} copy-done((bf16[256,1024]{1,0:T(8,128)(2,1)S(1)}, bf16[256,1024]{1,0:T(8,128)(2,1)}, u32[]{:S(2)}) %copy-start.14) | copy-done | bytes 524312
  8.6 11.2 %delta_local.2 = (bf16[8,128,256]{2,1,0:T(8,128)(2,1)}, bf16[256,1024]{1,0:T(8,128)(2,1)S(1)}, f32[256,1024]{1,0:T(8,128)S(1)}) custom-call(s32[1]{0:T(128)S(6)} %sub.12.half_ref, f32[1,256]{1,0:T(1,128)S(1)} %bitcast.13, bf16[256,1024]{1,0:T(8,128)(2,1)S(1)} %copy-done.12, bf16[256,1024]{1,0:T(8,128)(2,1)S(1)} %copy-done.14, ...), custom_call_target="tpu_custom_call" | custom-call | flops 6000000000 | bytes 3145728 | tf_op jit(solution)/shard_map/delta_local/pallas_call | solution.py:184
  19.8 0.8 copy-done.3
  20.6 1.0 %collective-permute-start.3 = (bf16[8,128,256]{2,1,0:T(8,128)(2,1)}, bf16[8,128,256]{2,1,0:T(8,128)(2,1)S(1)}, u32[]{:S(2)}, u32[]{:S(2)}) collective-permute-start(bf16[8,128,256]{2,1,0:T(8,128)(2,1)} %get-tuple-element.15), channel_id=1, source_target_pairs={{0,1},{1,0},{2,3},{3,2},{4,5},{5,4},{6,7},{7,6},{8,9},{9,8},{10,11... | collective-permute-start | bytes 1572872 | tf_op jit(solution)/shard_map/ppermute | solution.py:427
  21.6 3.2 %collective-permute-start.1 = (bf16[256,512]{1,0:T(8,128)(2,1)}, bf16[256,512]{1,0:T(8,128)(2,1)}, u32[]{:S(2)}, u32[]{:S(2)}) collective-permute-start(bf16[256,512]{1,0:T(8,128)(2,1)} %collective-permute-done.rest_1_), channel_id=1, source_target_pairs={{0,2},{1,3},{2,4},{3,5},{4,6},{5,7},{8,10},{9,11},{10,12},{11,13},... | collective-permute-start | bytes 786440 | tf_op jit(solution)/shard_map/ppermute | solution.py:423
  24.8 0.9 %copy-done.6 = f32[256,16]{1,0:T(8,128)S(1)} copy-done((f32[256,16]{1,0:T(8,128)S(1)}, f32[256,16]{1,0:T(8,128)}, u32[]{:S(2)}) %copy-start.6) | copy-done | bytes 16408
  25.7 10.6 %delta_local.3 = (bf16[8,128,256]{2,1,0:T(8,128)(2,1)S(1)}, bf16[256,1024]{1,0:T(8,128)(2,1)S(1)}, f32[256,1024]{1,0:T(8,128)S(1)}) custom-call(s32[1]{0:T(128)} %bitcast.4.half_ref, f32[1,256]{1,0:T(1,128)S(1)} %bitcast.14, bf16[256,1024]{1,0:T(8,128)(2,1)S(1)} %copy-done.13, bf16[256,1024]{1,0:T(8,128)(2,1)S(1)} %copy-done.14, ...), custom_call_target="tpu_custom_call" | custom-call | flops 6000000000 | bytes 3145728 | tf_op jit(solution)/shard_map/delta_local/pallas_call | solution.py:184
  36.3 0.8 copy-done.1
  37.1 9.6 %all-gather = s32[8,1,256]{2,1,0:T(1,128)S(1)} all-gather(s32[1,1,256]{2,1,0:T(1,128)S(1)} %bitcast.17), channel_id=1, replica_groups=mesh['dp'=4,'ctx'=8] {'ctx'}, dimensions={0}, use_global_device_ids=true | all-gather | bytes 9216 | tf_op jit(solution)/shard_map/all_gather | solution.py:451
  46.7 0.7 fusion.1
  49.9 0.8 compose.1
  50.7 1.9 %collective-permute-start.4 = (bf16[8,128,128]{2,1,0:T(8,128)(2,1)S(1)}, bf16[8,128,128]{2,1,0:T(8,128)(2,1)S(1)}, u32[]{:S(2)}, u32[]{:S(2)}) collective-permute-start(bf16[8,128,128]{2,1,0:T(8,128)(2,1)S(1)} %get-tuple-element.17.add_ref), channel_id=1, source_target_pairs={{0,2},{1,3},{2,4},{3,5},{4,6},{5,7},{8,10},{9,11},{10,12},{11,13},... | collective-permute-start | bytes 786440 | tf_op jit(solution)/shard_map/ppermute | solution.py:423
  52.7 1.1 %select_bitcast_fusion.1 = (bf16[1,256,512]{2,1,0:T(8,128)(2,1)S(1)}, bf16[1,256,512]{2,1,0:T(8,128)(2,1)S(1)}) fusion(bf16[256,512]{1,0:T(8,128)(2,1)} %collective-permute-done.rest_1_, bf16[256,512]{1,0:T(8,128)(2,1)S(1)} %constant_dynamic-update-slice_fusion.rest_0_, pred[]{:T(512)S(6)} %eq.15, bf16[256,512]{1,0:T(8,128)(2,1)} %collective-permute-done.1.rest_2_), kind=kLoop, calls=%fused_computation.2 | loop fusion | flops 262144 | bytes 1310721 | tf_op jit(solution)/shard_map/stack | solution.py:459
  53.8 0.8 pad_maximum_fusion
  54.6 0.1 collective-permute-start.2
  54.7 5.6 %collective-permute-done.4.state_ref = bf16[8,128,128]{2,1,0:T(8,128)(2,1)S(1)} collective-permute-done((bf16[8,128,128]{2,1,0:T(8,128)(2,1)S(1)}, bf16[8,128,128]{2,1,0:T(8,128)(2,1)S(1)}, u32[]{:S(2)}, u32[]{:S(2)}) %collective-permute-start.4) | collective-permute-done | bytes 262176 | tf_op jit(solution)/shard_map/ppermute | solution.py:423
  60.4 0.9 %relay.1 = bf16[8,128,128]{2,1,0:T(8,128)(2,1)} custom-call(bf16[8,128,128]{2,1,0:T(8,128)(2,1)S(1)} %get-tuple-element.16.map_ref, bf16[8,128,128]{2,1,0:T(8,128)(2,1)S(1)} %get-tuple-element.17.add_ref, bf16[8,128,128]{2,1,0:T(8,128)(2,1)S(1)} %collective-permute-done.4.state_ref), custom_call_target="tpu_custom_call" | custom-call | flops 100000000 | bytes 1048576 | tf_op jit(solution)/shard_map/relay/pallas_call | solution.py:263
  61.3 2.4 %collective-permute-start.5 = (bf16[8,128,128]{2,1,0:T(8,128)(2,1)}, bf16[8,128,128]{2,1,0:T(8,128)(2,1)}, u32[]{:S(2)}, u32[]{:S(2)}) collective-permute-start(bf16[8,128,128]{2,1,0:T(8,128)(2,1)} %relay.1), channel_id=1, source_target_pairs={{0,2},{1,3},{2,4},{3,5},{4,6},{5,7},{8,10},{9,11},{10,12},{11,13},... | collective-permute-start | bytes 786440 | tf_op jit(solution)/shard_map/ppermute | solution.py:423
  63.8 6.5 %collective-permute-done.5.state_ref = bf16[8,128,128]{2,1,0:T(8,128)(2,1)} collective-permute-done((bf16[8,128,128]{2,1,0:T(8,128)(2,1)}, bf16[8,128,128]{2,1,0:T(8,128)(2,1)}, u32[]{:S(2)}, u32[]{:S(2)}) %collective-permute-start.5) | collective-permute-done | bytes 262176 | tf_op jit(solution)/shard_map/ppermute | solution.py:423
  70.3 1.2 %arrive.1 = (bf16[8,128,128]{2,1,0:T(8,128)(2,1)S(1)}, bf16[8,128,128]{2,1,0:T(8,128)(2,1)S(1)}) custom-call(s32[3]{0:T(128)S(1)} %pad_add_fusion.flags_ref, bf16[8,128,256]{2,1,0:T(8,128)(2,1)S(1)} %get-tuple-element.14.mine_ref, bf16[8,128,256]{2,1,0:T(8,128)(2,1)S(1)} %collective-permute-done.3.other_ref, ...), custom_call_target="tpu_custom_call" | custom-call | flops 100000000 | bytes 1048576 | tf_op jit(solution)/shard_map/arrive/pallas_call | solution.py:263
  71.5 2.0 %collective-permute-start.6 = (bf16[8,128,128]{2,1,0:T(8,128)(2,1)S(1)}, bf16[8,128,128]{2,1,0:T(8,128)(2,1)S(1)}, u32[]{:S(2)}, u32[]{:S(2)}) collective-permute-start(bf16[8,128,128]{2,1,0:T(8,128)(2,1)S(1)} %get-tuple-element.18), channel_id=1, source_target_pairs={{0,1},{1,0},{2,3},{3,2},{4,5},{5,4},{6,7},{7,6},{8,9},{9,8},{10,11... | collective-permute-start | bytes 786440 | tf_op jit(solution)/shard_map/ppermute | solution.py:427
  73.6 1.2 %copy-done.11 = bf16[256,2048]{1,0:T(8,128)(2,1)S(1)} copy-done((bf16[256,2048]{1,0:T(8,128)(2,1)S(1)}, bf16[256,2048]{1,0:T(8,128)(2,1)}, u32[]{:S(2)}) %copy-start.11) | copy-done | bytes 1048600
  74.8 9.7 %attention.1 = bf16[256,2048]{1,0:T(8,128)(2,1)} custom-call(f32[1,1280]{1,0:T(1,128)S(1)} %reshape.26.ids_ref, f32[32,128]{1,0:T(8,128)S(1)} %broadcast_in_dim.2.freq_ref, bf16[256,2048]{1,0:T(8,128)(2,1)S(1)} %copy-done.10, bf16[256,2048]{1,0:T(8,128)(2,1)S(1)} %copy-done.11, bf16[256,512]{1,0:T(8,128)(2,1)S(1)} %constant_dynamic-update-slice_fusion.rest_0_, ...), custom_call_target="tpu_custom_call" | custom-call | flops 6000000000 | bytes 5242880 | tf_op jit(solution)/shard_map/attention/pallas_call | solution.py:397
  84.5 0.6 copy-done.7
  85.2 1.7 %delta_out.2.rest_0_ = bf16[256,2048]{1,0:T(8,128)(2,1)} custom-call(s32[1]{0:T(128)} %bitcast.4.half_ref, bf16[256,1024]{1,0:T(8,128)(2,1)S(1)} %copy-done.2, f32[256,1024]{1,0:T(8,128)S(1)} %get-tuple-element.20.inner_ref, bf16[8,128,128]{2,1,0:T(8,128)(2,1)S(1)} %get-tuple-element.21.state_ref, bf16[256,2048]{1,0:T(8,128)(2,1)S(1)} %copy-done, ...), custom_call_target="tpu_custom_call" | custom-call | flops 100000000 | bytes 3145728 | tf_op jit(solution)/shard_map/delta_out/pallas_call | solution.py:308
  86.9 1.7 %delta_out.3 = bf16[256,2048]{1,0:T(8,128)(2,1)} custom-call(s32[1]{0:T(128)S(6)} %sub.12.half_ref, bf16[256,1024]{1,0:T(8,128)(2,1)S(1)} %copy-done.4, f32[256,1024]{1,0:T(8,128)S(1)} %get-tuple-element.13.inner_ref, bf16[8,128,128]{2,1,0:T(8,128)(2,1)S(1)} %collective-permute-done.6.state_ref, ...), custom_call_target="tpu_custom_call", output_to_operand_aliasing={{}: (6, {})} | custom-call | flops 100000000 | bytes 3145728 | tf_op jit(solution)/shard_map/delta_out/pallas_call | solution.py:308
  (42 shorter events, 0.4 us)
Async XLA Ops:
  0.6 1.0 %copy-start.15 = (bf16[256,256]{1,0:T(8,128)(2,1)S(1)}, bf16[256,256]{1,0:T(8,128)(2,1)}, u32[]{:S(2)}) copy-start(bf16[256,256]{1,0:T(8,128)(2,1)} %param.15) | copy-start | bytes 393220
  0.6 4.3 %copy-start.16 = (f32[256,16]{0,1:T(8,128)S(1)}, f32[256,16]{0,1:T(8,128)}, u32[]{:S(2)}) copy-start(f32[256,16]{0,1:T(8,128)} %param.20) | copy-start | bytes 49156
  0.7 5.7 %copy-start.12 = (bf16[256,1024]{1,0:T(8,128)(2,1)S(1)}, bf16[256,1024]{1,0:T(8,128)(2,1)}, u32[]{:S(2)}) copy-start(bf16[256,1024]{1,0:T(8,128)(2,1)} %q_ref.5) | copy-start | bytes 1572868
  1.7 19.9 %collective-permute-start = (bf16[256,512]{1,0:T(8,128)(2,1)S(1)}, bf16[256,512]{1,0:T(8,128)(2,1)}, u32[]{:S(2)}, u32[]{:S(2)}) collective-permute-start(bf16[256,512]{1,0:T(8,128)(2,1)S(1)} %constant_dynamic-update-slice_fusion.rest_0_), channel_id=1, source_target_pairs={{0,2},{1,3},{2,4},{3,5},{4,6},{5,7},{8,10},{9,11},{10,12},{11,13},... | collective-permute-start | bytes 786440 | tf_op jit(solution)/shard_map/ppermute | solution.py:423
  4.9 0.7 copy-start.17
  5.6 0.7 copy-start.18
  6.3 13.5 %copy-start.5 = (f32[256,16]{1,0:T(8,128)}, f32[256,16]{1,0:T(8,128)S(1)}, u32[]{:S(2)}) copy-start(f32[256,16]{1,0:T(8,128)S(1)} %copy.20.decay_ref) | copy-start | bytes 49156
  6.3 1.3 %copy-start.8 = (bf16[256,2048]{1,0:T(8,128)(2,1)S(1)}, bf16[256,2048]{1,0:T(8,128)(2,1)}, u32[]{:S(2)}) copy-start(bf16[256,2048]{1,0:T(8,128)(2,1)} %v_ref.3) | copy-start | bytes 3145732
  7.6 1.0 %copy-start.14 = (bf16[256,1024]{1,0:T(8,128)(2,1)S(1)}, bf16[256,1024]{1,0:T(8,128)(2,1)}, u32[]{:S(2)}) copy-start(bf16[256,1024]{1,0:T(8,128)(2,1)} %k_ref.3) | copy-start | bytes 1572868
  8.6 16.2 %copy-start.9 = (bf16[256,2048]{1,0:T(8,128)(2,1)S(1)}, bf16[256,2048]{1,0:T(8,128)(2,1)}, u32[]{:S(2)}) copy-start(bf16[256,2048]{1,0:T(8,128)(2,1)} %v_ref.3) | copy-start | bytes 3145732
  8.6 16.2 %copy-start.13 = (bf16[256,1024]{1,0:T(8,128)(2,1)S(1)}, bf16[256,1024]{1,0:T(8,128)(2,1)}, u32[]{:S(2)}) copy-start(bf16[256,1024]{1,0:T(8,128)(2,1)} %q_ref.5) | copy-start | bytes 1572868
  19.8 0.8 copy-start.3
  20.6 29.3 %collective-permute-start.3 = (bf16[8,128,256]{2,1,0:T(8,128)(2,1)}, bf16[8,128,256]{2,1,0:T(8,128)(2,1)S(1)}, u32[]{:S(2)}, u32[]{:S(2)}) collective-permute-start(bf16[8,128,256]{2,1,0:T(8,128)(2,1)} %get-tuple-element.15), channel_id=1, source_target_pairs={{0,1},{1,0},{2,3},{3,2},{4,5},{5,4},{6,7},{7,6},{8,9},{9,8},{10,11... | collective-permute-start | bytes 1572872 | tf_op jit(solution)/shard_map/ppermute | solution.py:427
  21.6 31.1 %collective-permute-start.1 = (bf16[256,512]{1,0:T(8,128)(2,1)}, bf16[256,512]{1,0:T(8,128)(2,1)}, u32[]{:S(2)}, u32[]{:S(2)}) collective-permute-start(bf16[256,512]{1,0:T(8,128)(2,1)} %collective-permute-done.rest_1_), channel_id=1, source_target_pairs={{0,2},{1,3},{2,4},{3,5},{4,6},{5,7},{8,10},{9,11},{10,12},{11,13},... | collective-permute-start | bytes 786440 | tf_op jit(solution)/shard_map/ppermute | solution.py:423
  24.8 0.9 %copy-start.6 = (f32[256,16]{1,0:T(8,128)S(1)}, f32[256,16]{1,0:T(8,128)}, u32[]{:S(2)}) copy-start(f32[256,16]{1,0:T(8,128)} %copy-done.5) | copy-start | bytes 49156
  36.3 0.8 copy-start.1
  50.7 9.6 %collective-permute-start.4 = (bf16[8,128,128]{2,1,0:T(8,128)(2,1)S(1)}, bf16[8,128,128]{2,1,0:T(8,128)(2,1)S(1)}, u32[]{:S(2)}, u32[]{:S(2)}) collective-permute-start(bf16[8,128,128]{2,1,0:T(8,128)(2,1)S(1)} %get-tuple-element.17.add_ref), channel_id=1, source_target_pairs={{0,2},{1,3},{2,4},{3,5},{4,6},{5,7},{8,10},{9,11},{10,12},{11,13},... | collective-permute-start | bytes 786440 | tf_op jit(solution)/shard_map/ppermute | solution.py:423
  54.6 18.9 %collective-permute-start.2 = (bf16[2,256,512]{2,1,0:T(8,128)(2,1)}, bf16[2,256,512]{2,1,0:T(8,128)(2,1)}, u32[]{:S(2)}, u32[]{:S(2)}) collective-permute-start(bf16[2,256,512]{2,1,0:T(8,128)(2,1)} %pad_maximum_fusion), channel_id=1, source_target_pairs={{0,1},{1,0},{2,3},{3,2},{4,5},{5,4},{6,7},{7,6},{8,9},{9,8},{10,11... | collective-permute-start | bytes 1572872 | tf_op jit(solution)/shard_map/ppermute | solution.py:427
  61.3 9.0 %collective-permute-start.5 = (bf16[8,128,128]{2,1,0:T(8,128)(2,1)}, bf16[8,128,128]{2,1,0:T(8,128)(2,1)}, u32[]{:S(2)}, u32[]{:S(2)}) collective-permute-start(bf16[8,128,128]{2,1,0:T(8,128)(2,1)} %relay.1), channel_id=1, source_target_pairs={{0,2},{1,3},{2,4},{3,5},{4,6},{5,7},{8,10},{9,11},{10,12},{11,13},... | collective-permute-start | bytes 786440 | tf_op jit(solution)/shard_map/ppermute | solution.py:423
  63.7 9.9 %copy-start.10 = (bf16[256,2048]{1,0:T(8,128)(2,1)S(1)}, bf16[256,2048]{1,0:T(8,128)(2,1)}, u32[]{:S(2)}) copy-start(bf16[256,2048]{1,0:T(8,128)(2,1)} %q_ref.3) | copy-start | bytes 3145732
  71.5 15.3 %collective-permute-start.6 = (bf16[8,128,128]{2,1,0:T(8,128)(2,1)S(1)}, bf16[8,128,128]{2,1,0:T(8,128)(2,1)S(1)}, u32[]{:S(2)}, u32[]{:S(2)}) collective-permute-start(bf16[8,128,128]{2,1,0:T(8,128)(2,1)S(1)} %get-tuple-element.18), channel_id=1, source_target_pairs={{0,1},{1,0},{2,3},{3,2},{4,5},{5,4},{6,7},{7,6},{8,9},{9,8},{10,11... | collective-permute-start | bytes 786440 | tf_op jit(solution)/shard_map/ppermute | solution.py:427
  73.6 1.2 %copy-start.11 = (bf16[256,2048]{1,0:T(8,128)(2,1)S(1)}, bf16[256,2048]{1,0:T(8,128)(2,1)}, u32[]{:S(2)}) copy-start(bf16[256,2048]{1,0:T(8,128)(2,1)} %gate_ref.3) | copy-start | bytes 3145732
  74.8 9.7 %copy-start = (bf16[256,2048]{1,0:T(8,128)(2,1)S(1)}, bf16[256,2048]{1,0:T(8,128)(2,1)}, u32[]{:S(2)}) copy-start(bf16[256,2048]{1,0:T(8,128)(2,1)} %gate_ref.5) | copy-start | bytes 3145732
  74.8 9.7 %copy-start.2 = (bf16[256,1024]{1,0:T(8,128)(2,1)S(1)}, bf16[256,1024]{1,0:T(8,128)(2,1)}, u32[]{:S(2)}) copy-start(bf16[256,1024]{1,0:T(8,128)(2,1)} %copy-done.1) | copy-start | bytes 1572868
  84.5 0.7 copy-start.7
  85.2 1.7 %copy-start.4 = (bf16[256,1024]{1,0:T(8,128)(2,1)S(1)}, bf16[256,1024]{1,0:T(8,128)(2,1)}, u32[]{:S(2)}) copy-start(bf16[256,1024]{1,0:T(8,128)(2,1)} %copy-done.3) | copy-start | bytes 1572868

commit v2 on v1

--- a/solution.py
+++ b/solution.py
@@ -16,10 +16,9 @@
 LOG2E = 1.4426950408889634
 MASKED = -1e30
 EPS = 1e-6
-LEVELS = 7
 TILE = 128
 KEYS_PER_STEP = 2
-VMEM_LIMIT = 48 * 1024 * 1024
+VMEM_LIMIT = 60 * 1024 * 1024
 
 f32 = jnp.float32
 bf16 = jnp.bfloat16
@@ -35,6 +34,57 @@
 
 def cost(flops, nbytes, exps=0):
     return pl.CostEstimate(flops=flops, bytes_accessed=nbytes, transcendentals=exps)
+
+
+BLOCK = 16
+MERGES = 3
+
+
+def odd_rows(m, b):
+    return jnp.concatenate([m[i + b : i + 2 * b] for i in range(0, TILE, 2 * b)], axis=0)
+
+
+def interleave(even, odd, b):
+    parts = []
+    for i in range(0, TILE // 2, b):
+        parts += [even[i : i + b], odd[i : i + b]]
+    return jnp.concatenate(parts, axis=0)
+
+
+def even_rows(m, b):
+    return jnp.concatenate([m[i : i + b] for i in range(0, TILE, 2 * b)], axis=0)
+
+
+def block_inverses(mats):
+    row = lax.broadcasted_iota(jnp.int32, (BLOCK, TILE), 0)
+    lane = lax.broadcasted_iota(jnp.int32, (BLOCK, TILE), 1)
+    within = lax.rem(lane, BLOCK)
+    group = lane // BLOCK
+    folded = []
+    for m in mats:
+        z = jnp.where(group == 0, m[:BLOCK], 0.0)
+        for r in range(1, TILE // BLOCK):
+            z = jnp.where(group == r, m[r * BLOCK : (r + 1) * BLOCK], z)
+        folded.append(jnp.where(row > within, z, 0.0))
+    xs = [jnp.where(row == within, 1.0, 0.0)] * len(mats)
+    small = 8
+    for k in range(BLOCK - 1):
+        low = 0 if k < small - 1 else small
+        at = (group * BLOCK + k)[low:]
+        for i, z in enumerate(folded):
+            spread = jnp.take_along_axis(z[low:], at, axis=1)
+            x = xs[i]
+            new = x[low:] + spread * x[k : k + 1]
+            xs[i] = new if low == 0 else jnp.concatenate([x[:low], new], axis=0)
+    out = []
+    for x in xs:
+        x = jnp.where(row > within, x, 0.0)
+        out.append(
+            jnp.concatenate(
+                [jnp.where(group == r, x, 0.0) for r in range(TILE // BLOCK)], axis=0
+            ).astype(bf16)
+        )
+    return out
 
 
 def delta_local_kernel(
@@ -70,10 +120,10 @@
         first_ref[...] = jnp.where(seg_col == seg_row[:, :1], 1.0, 0.0)
         r = lax.broadcasted_iota(jnp.int32, (TILE, TILE), 0)
         c = lax.broadcasted_iota(jnp.int32, (TILE, TILE), 1)
-        top = jnp.bitwise_xor(r, c)
-        for level in range(LEVELS):
-            inside = (r > c) & (lax.shift_right_logical(top, level) == 1)
-            level_ref[level] = jnp.where(inside, 1.0, 0.0).astype(bf16)
+        for level in range(MERGES):
+            b = BLOCK << level
+            sibling = jnp.where(r // b == c // b + 1, 1.0, 0.0)
+            level_ref[level] = odd_rows(sibling, b).astype(bf16)
         all_heads = decay_ref.shape[1]
         base = half_ref[0] * (all_heads // 2)
         er = lax.broadcasted_iota(jnp.int32, (all_heads, TILE), 0)
@@ -87,6 +137,8 @@
         ccol_ref[...] = cumulative
         crow_ref[...] = jnp.transpose(cumulative)
         bcol_ref[...] = dot(beta_ref[...], pick, lax.Precision.HIGHEST)
+        end = map_add_ref.shape[0] - BLOCK
+        map_add_ref[end:, :] = jnp.broadcast_to(seg_row, (BLOCK, rows)).astype(bf16)
 
     shift = lax.rem(TILE - step * heads, TILE)
     ccol = pltpu.roll(ccol_ref[...], shift, 1)
@@ -126,8 +178,8 @@
             span1 = jnp.exp2(cc[:TILE] - cr[:, :TILE] + mask_ref[:TILE, :TILE])
             span2 = jnp.exp2(cc[TILE:] - cr + mask_ref[TILE:, :])
             scale = -bt * rk_col
-            d11 = (span1 * scale[:TILE] * gram1).astype(bf16)
-            d2 = (span2 * scale[TILE:] * gram2).astype(bf16)
+            d11 = span1 * scale[:TILE] * gram1
+            d2 = span2 * scale[TILE:] * gram2
             p11 = (span1 * probe1).astype(bf16)
             p2 = (span2 * probe2).astype(bf16)
             entry = jnp.exp2(cc) * first
@@ -136,20 +188,24 @@
             )
             kd = (kt * (rk_row * span2[TILE - 1 : TILE, :])).astype(bf16)
             work.append(
-                dict(h=h, d=[d11, d2[:, TILE:]], d21=d2[:, :TILE], p11=p11, p2=p2, kd=kd,
-                     right=right, reach=entry * qn, last=entry[rows - 1 : rows, :])
+                dict(h=h, d=[d11, d2[:, TILE:]], d21=d2[:, :TILE].astype(bf16), p11=p11, p2=p2,
+                     kd=kd, right=right, reach=entry * qn, last=entry[rows - 1 : rows, :])
             )
     mats = [m for w in work for m in w["d"]]
-    inverses = [m * level_ref[0] for m in mats]
-    for level in range(1, LEVELS):
+    inverses = block_inverses(mats)
+    mats = [m.astype(bf16) for m in mats]
+    zeros = jnp.zeros((TILE // 2, TILE), bf16)
+    for level in range(MERGES):
+        b = BLOCK << level
         keep = level_ref[level]
-        picked = [m * keep for m in mats]
-        ys = [
-            (p.astype(f32) + dot(p, x)).astype(bf16) for p, x in zip(picked, inverses)
+        picked = [odd_rows(m, b) * keep for m in mats]
+        ys = [(p.astype(f32) + dot(p, x)).astype(bf16) for p, x in zip(picked, inverses)]
+        odds = [odd_rows(x, b) for x in inverses]
+        odds = [
+            x + (y.astype(f32) + dot(x, interleave(zeros, y, b))).astype(bf16)
+            for x, y in zip(odds, ys)
         ]
-        inverses = [
-            x + (y.astype(f32) + dot(x, y)).astype(bf16) for x, y in zip(inverses, ys)
-        ]
+        inverses = [interleave(even_rows(x, b), o, b) for x, o in zip(inverses, odds)]
     for i, w in enumerate(work):
         x1, x2 = inverses[2 * i], inverses[2 * i + 1]
         h = w["h"]
@@ -160,7 +216,8 @@
         u = jnp.concatenate([u1, u2], axis=0)
         pu = jnp.concatenate([dot(w["p11"], u1), dot(w["p2"], u)], axis=0)
         ma = dot(w["kd"], u)
-        map_add_ref[h] = jnp.concatenate(
+        at = pl.multiple_of((step * heads + h) * DK, DK)
+        map_add_ref[pl.ds(at, DK), :] = jnp.concatenate(
             [w["last"] * eye - ma[:, :DK], ma[:, DK:]], axis=1
         ).astype(bf16)
         reach_ref[:, h * DK : (h + 1) * DK] = (w["reach"] - pu[:, :DK]).astype(bf16)
@@ -174,6 +231,7 @@
     steps = n // heads
     kw = KEYS_PER_STEP * DK
     vw = heads * DV
+    tall = n * DK + BLOCK
 
     def at_half(i, s):
         return (0, s[0] * steps + i)
@@ -195,13 +253,13 @@
                 pl.BlockSpec(decay.shape, whole),
             ],
             out_specs=[
-                pl.BlockSpec((heads, DK, DK + DV), lambda i, s: (i, 0, 0)),
+                pl.BlockSpec((tall, DK + DV), whole),
                 pl.BlockSpec((rows, heads * DK), lambda i, s: (0, i)),
                 pl.BlockSpec((rows, vw), lambda i, s: (0, i)),
             ],
             scratch_shapes=[
                 pltpu.VMEM((rows, rows), f32),
-                pltpu.VMEM((LEVELS, TILE, TILE), bf16),
+                pltpu.VMEM((MERGES, TILE // 2, TILE), bf16),
                 pltpu.VMEM((TILE, rows), f32),
                 pltpu.VMEM((rows, TILE), f32),
                 pltpu.VMEM((rows, TILE), f32),
@@ -209,7 +267,7 @@
             ],
         ),
         out_shape=[
-            jax.ShapeDtypeStruct((n, DK, DK + DV), bf16),
+            jax.ShapeDtypeStruct((tall, DK + DV), bf16),
             jax.ShapeDtypeStruct((rows, n * DK), bf16),
             jax.ShapeDtypeStruct((rows, n * DV), f32),
         ],
@@ -219,40 +277,61 @@
     )(half, seg_row, query, key, value, beta, decay)
 
 
-def flag(flags_ref, i):
-    return flags_ref[i].astype(f32)
-
-
-def ordered(flags_ref, mine, other):
-    odd = flags_ref[0] == 1
-    return jnp.where(odd, other, mine), jnp.where(odd, mine, other)
-
-
-def compose_kernel(flags_ref, mine_ref, other_ref, map_ref, add_ref):
-    into, across = flag(flags_ref, 1), flag(flags_ref, 2)
-    for h in range(mine_ref.shape[0]):
-        early, late = ordered(flags_ref, mine_ref[h], other_ref[h])
+def ids_of(ref):
+    end = ref.shape[0] - BLOCK
+    return ref[end : end + BLOCK, :].astype(f32)[:1]
+
+
+def put_id(ref, value):
+    end = ref.shape[0] - BLOCK
+    ref[end:, :] = jnp.broadcast_to(value, (BLOCK, ref.shape[1])).astype(bf16)
+
+
+def matching(a, b):
+    return jnp.where(a == b, 1.0, 0.0)
+
+
+def compose_kernel(core_ref, mine_ref, other_ref, map_ref, add_ref):
+    odd = core_ref[0] == 1
+    mine_ids, other_ids = ids_of(mine_ref), ids_of(other_ref)
+    early_ids = jnp.where(odd, other_ids, mine_ids)
+    late_ids = jnp.where(odd, mine_ids, other_ids)
+    across = matching(early_ids[:, -1:], late_ids[:, :1])
+    put_id(map_ref, early_ids[:, :1])
+    put_id(add_ref, late_ids[:, -1:])
+    for h in range(mine_ref.shape[0] // DK):
+        at = slice(h * DK, (h + 1) * DK)
+        mine, other = mine_ref[at], other_ref[at]
+        early, late = jnp.where(odd, other, mine), jnp.where(odd, mine, other)
         both = dot(late[:, :DK], early) * across
-        map_ref[h] = (both[:, :DK] * into).astype(bf16)
-        add_ref[h] = (both[:, DK:] + late[:, DK:].astype(f32)).astype(bf16)
+        map_ref[at] = both[:, :DK].astype(bf16)
+        add_ref[at] = (both[:, DK:] + late[:, DK:].astype(f32)).astype(bf16)
 
 
 def relay_kernel(map_ref, add_ref, state_ref, out_ref):
-    for h in range(map_ref.shape[0]):
-        out_ref[h] = (dot(map_ref[h], state_ref[h]) + add_ref[h].astype(f32)).astype(bf16)
-
-
-def arrive_kernel(flags_ref, mine_ref, other_ref, state_ref, keep_ref, give_ref):
-    into, across = flag(flags_ref, 1), flag(flags_ref, 2)
-    odd = flags_ref[0] == 1
-    for h in range(mine_ref.shape[0]):
-        early, _ = ordered(flags_ref, mine_ref[h], other_ref[h])
-        first = state_ref[h] * into.astype(bf16)
+    into = matching(ids_of(state_ref), ids_of(map_ref))
+    put_id(out_ref, ids_of(add_ref))
+    for h in range(map_ref.shape[0] // DK):
+        at = slice(h * DK, (h + 1) * DK)
+        out_ref[at] = (dot(map_ref[at], state_ref[at]) * into + add_ref[at].astype(f32)).astype(bf16)
+
+
+def arrive_kernel(core_ref, mine_ref, other_ref, state_ref, keep_ref, give_ref):
+    odd = core_ref[0] == 1
+    mine_ids, other_ids = ids_of(mine_ref), ids_of(other_ref)
+    early_ids = jnp.where(odd, other_ids, mine_ids)
+    late_ids = jnp.where(odd, mine_ids, other_ids)
+    across = matching(early_ids[:, -1:], late_ids[:, :1])
+    into = matching(ids_of(state_ref), early_ids[:, :1])
+    for h in range(keep_ref.shape[0] // DK):
+        at = slice(h * DK, (h + 1) * DK)
+        early = jnp.where(odd, other_ref[at], mine_ref[at])
+        first = (state_ref[at].astype(f32) * into).astype(bf16)
         second = (
             (dot(early[:, :DK], first) + early[:, DK:].astype(f32)) * across
         ).astype(bf16)
-        keep_ref[h] = jnp.where(odd, second, first)
-        give_ref[h] = jnp.where(odd, first, second)
+        keep_ref[at] = jnp.where(odd, second, first)
+        give_ref[at] = jnp.where(odd, first, second)
 
 
 SMEM = pl.BlockSpec(memory_space=pltpu.SMEM)
@@ -274,9 +353,10 @@
 def delta_out_kernel(half_ref, reach_ref, inner_ref, state_ref, gate_ref, gain_ref, *rest):
     out_ref = rest[-1]
     gain = gain_ref[...]
-    for h in range(state_ref.shape[0]):
+    for h in range(state_ref.shape[0] // DK):
         cols = slice(h * DV, (h + 1) * DV)
-        out = inner_ref[:, cols] + dot(reach_ref[:, cols], state_ref[h])
+        state = state_ref[h * DK : (h + 1) * DK]
+        out = inner_ref[:, cols].astype(f32) + dot(reach_ref[:, cols], state)
         spread = lax.rsqrt(jnp.mean(out * out, axis=1, keepdims=True) + EPS)
         gate = gate_ref[:, cols].astype(f32)
         gate = gate * jax.nn.sigmoid(gate)
@@ -285,7 +365,7 @@
 
 def delta_out(half, reach, inner, state, gate, gain, partial_out=None):
     rows = reach.shape[0]
-    n = state.shape[0]
+    n = state.shape[0] // DK
     heads = 4
     steps = n // heads
 
@@ -295,7 +375,7 @@
     in_specs = [
         pl.BlockSpec((rows, heads * DK), lambda i, s: (0, i)),
         pl.BlockSpec((rows, heads * DV), lambda i, s: (0, i)),
-        pl.BlockSpec((heads, DK, DV), lambda i, s: (i, 0, 0)),
+        pl.BlockSpec((heads * DK, DV), lambda i, s: (i, 0)),
         pl.BlockSpec((rows, heads * DV), at_half),
         pl.BlockSpec((1, DV), lambda i, s: (0, 0)),
     ]
@@ -321,40 +401,59 @@
     )(*args)
 
 
-def attention_kernel(ids_ref, freq_ref, q_ref, gate_ref, *rest):
-    *pieces, out_ref, kt_ref, v_ref, mask_ref, cos_ref, sin_ref = rest
+def blocks_of(pieces):
+    own, *same, other = pieces
+    order = [(own, None)]
+    for i, ref in enumerate(same):
+        order += [(other, i), (ref, None)]
+    return order[::-1]
+
+
+def window_kernel(freq_ref, *rest):
+    *pieces, kt_ref, v_ref, ids_ref, cos_ref, sin_ref = rest
+    rows = cos_ref.shape[0]
+    window = ids_ref.shape[1]
+    half = ROTARY_ENTRIES // 2
+    blocks = [ref if index is None else ref.at[index] for ref, index in blocks_of(pieces)]
+    row_ids = jnp.concatenate(
+        [ref[rows : rows + BLOCK, :rows].astype(f32)[:1] for ref in blocks], axis=1
+    )
+    ids_ref[...] = row_ids
+    ids = jnp.broadcast_to(row_ids, (DOCS, window))
+    docs = lax.broadcasted_iota(jnp.int32, (DOCS, window), 0).astype(f32) + 1.0
+    before = jnp.sum(jnp.where(ids < docs, 1.0, 0.0), axis=1, keepdims=True)
+    start = jnp.sum(jnp.where(ids == docs, before, 0.0), axis=0, keepdims=True)
+    place = lax.broadcasted_iota(jnp.int32, (1, window), 1).astype(f32)
+    angle = freq_ref[:, :1] * (place - start)
+    cosine = jnp.cos(angle)
+    sine = jnp.sin(angle)
+    for b, ref in enumerate(blocks):
+        cols = slice(b * rows, (b + 1) * rows)
+        kt = jnp.transpose(ref[:rows, :HEAD_WIDTH].astype(f32))
+        one, two = kt[:half], kt[half:ROTARY_ENTRIES]
+        cb, sb = cosine[:, cols], sine[:, cols]
+        kt_ref[:half, cols] = (one * cb - two * sb).astype(bf16)
+        kt_ref[half:ROTARY_ENTRIES, cols] = (two * cb + one * sb).astype(bf16)
+        kt_ref[ROTARY_ENTRIES:, cols] = kt[ROTARY_ENTRIES:].astype(bf16)
+        v_ref[cols, :] = ref[:rows, HEAD_WIDTH:]
+    cq, sq = cosine[:, window - rows :], sine[:, window - rows :]
+    rest_rows = TILE - ROTARY_ENTRIES
+    cos_ref[...] = jnp.transpose(
+        jnp.concatenate([cq, cq, jnp.ones((rest_rows, rows), f32)], axis=0)
+    )
+    sin_ref[...] = jnp.transpose(
+        jnp.concatenate([-sq, sq, jnp.zeros((rest_rows, rows), f32)], axis=0)
+    )
+
+
+def attention_kernel(ids_ref, cos_ref, sin_ref, kt_ref, v_ref, q_ref, gate_ref, *rest):
+    out_ref, mask_ref = rest[-2:]
     rows = q_ref.shape[0]
     window = ids_ref.shape[1]
     half = ROTARY_ENTRIES // 2
 
     @pl.when(pl.program_id(0) == 0)
     def _():
-        ids = jnp.broadcast_to(ids_ref[...], (DOCS, window))
-        docs = lax.broadcasted_iota(jnp.int32, (DOCS, window), 0).astype(f32)
-        before = jnp.sum(jnp.where(ids < docs, 1.0, 0.0), axis=1, keepdims=True)
-        start = jnp.sum(jnp.where(ids == docs, before, 0.0), axis=0, keepdims=True)
-        place = lax.broadcasted_iota(jnp.int32, (1, window), 1).astype(f32)
-        angle = freq_ref[:, :1] * (place - start)
-        cosine = jnp.cos(angle)
-        sine = jnp.sin(angle)
-        for b, (ref, index) in enumerate(blocks_of(pieces)):
-            cols = slice(b * rows, (b + 1) * rows)
-            piece = ref[...] if index is None else ref[index]
-            kt = jnp.transpose(piece[:, :HEAD_WIDTH].astype(f32))
-            one, two = kt[:half], kt[half:ROTARY_ENTRIES]
-            cb, sb = cosine[:, cols], sine[:, cols]
-            kt_ref[:half, cols] = (one * cb - two * sb).astype(bf16)
-            kt_ref[half:ROTARY_ENTRIES, cols] = (two * cb + one * sb).astype(bf16)
-            kt_ref[ROTARY_ENTRIES:, cols] = kt[ROTARY_ENTRIES:].astype(bf16)
-            v_ref[cols, :] = piece[:, HEAD_WIDTH:]
-        cq, sq = cosine[:, window - rows :], sine[:, window - rows :]
-        rest_rows = TILE - ROTARY_ENTRIES
-        cos_ref[...] = jnp.transpose(
-            jnp.concatenate([cq, cq, jnp.ones((rest_rows, rows), f32)], axis=0)
-        )
-        sin_ref[...] = jnp.transpose(
-            jnp.concatenate([-sq, sq, jnp.zeros((rest_rows, rows), f32)], axis=0)
-        )
         own = ids_ref[:, window - rows :]
         own_col = jnp.transpose(jnp.broadcast_to(own, (TILE, rows)))
         own_cols = jnp.concatenate([own_col] * (window // TILE), axis=1)
@@ -379,44 +478,36 @@
         out_ref[:, base : base + HEAD_WIDTH] = (mixed / total * gate).astype(bf16)
 
 
-def blocks_of(pieces):
-    own, *same, other = pieces
-    order = [(own, None)]
-    for i, ref in enumerate(same):
-        order += [(other, i), (ref, None)]
-    return order[::-1]
-
-
-def attention(ids, freq, query, gate, own, same, other):
+def attention_half(part, window_arrays, query, gate, partial_out=None):
     rows = query.shape[0]
-    window = ids.shape[1]
+    window = window_arrays[0].shape[1]
     heads = 2
     width = heads * HEAD_WIDTH
-    pieces = [own, *same, other]
-    whole = [pl.BlockSpec(p.shape, lambda i, n=p.ndim: (0,) * n) for p in pieces]
+    steps = query.shape[1] // width // 2
+
+    def at_part(i):
+        return (0, part * steps + i)
+
+    in_specs = [pl.BlockSpec(a.shape, lambda i: (0, 0)) for a in window_arrays]
+    in_specs += [pl.BlockSpec((rows, width), at_part)] * 2
+    args = [*window_arrays, query, gate]
+    aliases = {}
+    if partial_out is not None:
+        aliases = {len(args): 0}
+        in_specs.append(pl.BlockSpec(memory_space=pl.ANY))
+        args.append(partial_out)
     return pl.pallas_call(
         attention_kernel,
-        grid=(query.shape[1] // width,),
-        in_specs=[
-            pl.BlockSpec(ids.shape, lambda i: (0, 0)),
-            pl.BlockSpec(freq.shape, lambda i: (0, 0)),
-            pl.BlockSpec((rows, width), lambda i: (0, i)),
-            pl.BlockSpec((rows, width), lambda i: (0, i)),
-            *whole,
-        ],
-        out_specs=pl.BlockSpec((rows, width), lambda i: (0, i)),
+        grid=(steps,),
+        in_specs=in_specs,
+        out_specs=pl.BlockSpec((rows, width), at_part),
         out_shape=jax.ShapeDtypeStruct(query.shape, bf16),
-        scratch_shapes=[
-            pltpu.VMEM((HEAD_WIDTH, window), bf16),
-            pltpu.VMEM((window, HEAD_WIDTH), bf16),
-            pltpu.VMEM((rows, window), f32),
-            pltpu.VMEM((rows, TILE), f32),
-            pltpu.VMEM((rows, TILE), f32),
-        ],
+        scratch_shapes=[pltpu.VMEM((rows, window), f32)],
+        input_output_aliases=aliases,
         compiler_params=params(),
-        cost_estimate=cost(6 * 10**9, 5 * 2**20, 3 * 10**6),
+        cost_estimate=cost(5 * 10**9, 3 * 2**20, 10**6),
         name="attention",
-    )(ids, freq, query, gate, *pieces)
+    )(*args)
 
 
 def up_chip(value, ranks):
@@ -448,9 +539,12 @@
     core = rank % 2
     odd = core == 1
 
-    ids = lax.all_gather(segment_ids, "ctx", axis=0, tiled=True)
-
-    own = jnp.concatenate([attention_keys, attention_values], axis=1)
+    ids = segment_ids.astype(f32).reshape(1, rows) + 1.0
+
+    id_rows = jnp.broadcast_to(jnp.concatenate([ids, ids], axis=1), (BLOCK, 2 * rows))
+    own = jnp.concatenate(
+        [jnp.concatenate([attention_keys, attention_values], axis=1), id_rows.astype(bf16)], axis=0
+    )
     same = []
     for _ in range(hops):
         same.append(up_chip(same[-1] if same else own, ranks))
@@ -459,12 +553,11 @@
         jnp.stack([jnp.where(odd, chain[i + 1], chain[i]) for i in range(hops)]), ranks
     )
 
-    seg_row = segment_ids.astype(f32).reshape(1, rows)
     keep_half = core.reshape(1).astype(jnp.int32)
     give_half = 1 - keep_half
     local = partial(
         delta_local,
-        seg_row=seg_row,
+        seg_row=ids,
         query=delta_query,
         key=delta_key,
         value=update_rule_payload,
@@ -475,32 +568,43 @@
     other_ma = swap_cores(give_ma, ranks)
     keep_ma, keep_reach, keep_inner = local(keep_half)
 
-    chip_first = (rank - core) * rows
-    into = (rank > 1) & (ids[jnp.maximum(chip_first - 1, 0)] == ids[chip_first])
-    across = ids[chip_first + rows - 1] == ids[chip_first + rows]
-    flags = jnp.stack([core, into, across]).astype(jnp.int32)
-
-    n = keep_ma.shape[0]
-    state_like = jax.ShapeDtypeStruct((n, DK, DV), bf16)
+    tall = keep_ma.shape[0]
+    state_like = jax.ShapeDtypeStruct((tall, DV), bf16)
     chip_map, chip_add = small_call(
-        compose_kernel, "compose", [state_like] * 2, flags, keep_ma, other_ma, scalars=1
+        compose_kernel, "compose", [state_like] * 2, keep_half, keep_ma, other_ma, scalars=1
     )
     state = up_chip(chip_add, ranks)
     for _ in range(hops - 1):
         (leaving,) = small_call(relay_kernel, "relay", [state_like], chip_map, chip_add, state)
         state = up_chip(leaving, ranks)
+    final_like = jax.ShapeDtypeStruct((tall - BLOCK, DV), bf16)
     keep_state, pass_state = small_call(
-        arrive_kernel, "arrive", [state_like] * 2, flags, keep_ma, other_ma, state, scalars=1
+        arrive_kernel, "arrive", [final_like] * 2, keep_half, keep_ma, other_ma, state, scalars=1
     )
     give_state = swap_cores(pass_state, ranks)
 
     window = (2 * hops + 1) * rows
-    padded = jnp.concatenate([jnp.full((window - rows,), -1, jnp.int32), ids]).astype(f32)
-    window_ids = lax.dynamic_slice(padded, (rank * rows,), (window,)).reshape(1, window)
     index = jnp.arange(ROTARY_ENTRIES // 2).astype(f32)
     freq = ROPE_THETA ** (-2.0 * index / ROTARY_ENTRIES)
     freq = jnp.broadcast_to(freq[:, None], (ROTARY_ENTRIES // 2, TILE))
-    attn_mixed = attention(window_ids, freq, attn_query, attn_gate, own, same, other)
+    kt, v_all, window_ids, cosine, sine = small_call(
+        window_kernel,
+        "window",
+        [
+            jax.ShapeDtypeStruct((HEAD_WIDTH, window), bf16),
+            jax.ShapeDtypeStruct((window, HEAD_WIDTH), bf16),
+            jax.ShapeDtypeStruct((1, window), f32),
+            jax.ShapeDtypeStruct((rows, TILE), f32),
+            jax.ShapeDtypeStruct((rows, TILE), f32),
+        ],
+        freq,
+        own,
+        *same,
+        other,
+    )
+    window_arrays = (window_ids, cosine, sine, kt, v_all)
+    attn_mixed = attention_half(0, window_arrays, attn_query, attn_gate)
+    attn_mixed = attention_half(1, window_arrays, attn_query, attn_gate, attn_mixed)
 
     gain = norm_gain.reshape(1, DV)
     delta_mixed = delta_out(keep_half, keep_reach, keep_inner, keep_state, delta_gate, gain)

time: 89.1 us -> 86.8 us (0.974)
  Pallas kernels: 37.8 us -> 49.8 us
  blocking collectives: 9.59 us -> 0 us
  local copies, waits for them, and re-layouts: 9.86 us -> 6.38 us
  between operations: 3.31 us -> 0.8 us
  waiting for transfers between devices: 12.1 us -> 13.1 us
    all_gather x1 -> x0, blocking collectives: 9.59 us -> none  [per_device(): ids = lax.all_gather(segment_ids, 'ctx', axis=0, tiled=True)]
    pallas_call x3 -> x4, Pallas kernels: 3.01 us -> 10.1 us  [small_call(): pl.pallas_call(kernel, in_specs=[SMEM] * scalars + [VMEM] * (len(args) -...]
    unnamed x41 -> x28, local copies, waits for them, and re-layouts: 9.11 us -> 5.61 us
    pallas_call x2, Pallas kernels: 3.41 us -> 5.6 us  [delta_out(): pl.pallas_call(delta_out_kernel, grid_spec=pltpu.PrefetchScalarGridSpec(n...]
    another operation x2, other arithmetic: 1.92 us -> 0.17 us  [per_device(): jnp.stack([jnp.where(odd, chain[i + 1], chain[i]) for i in range(hops)])]
    pallas_call x1 -> x2, Pallas kernels: 9.67 us -> 11.4 us  [attention_half(): pl.pallas_call(attention_kernel, grid=(steps,), in_specs=in_specs, out_sp...]
    concatenate x0 -> x2, other arithmetic: none -> 1.01 us  [the longest x1 0.99 us: per_device(): jnp.concatenate([jnp.concatenate([attention_keys, attention_values], axis...]
    pallas_call x2, Pallas kernels: 21.7 us -> 22.7 us  [delta_local(): pl.pallas_call(delta_local_kernel, grid_spec=pltpu.PrefetchScalarGridSpec...]
  transfers between devices with their start and end apart: 7 -> 7, of which waited for: 2 -> 2; matrix products, arithmetic and copies ran while one was open for 3% -> 3% of each run, Pallas kernels for 41% -> 54%
where the time goes in v2:
time: 86.8 us; the launch traced here: 86.2 us
  Pallas kernels  49.8 us (57%)
  starting transfers between devices  14.3 us (16%)
  waiting for transfers between devices  13.1 us (15%)
  local copies, waits for them, and re-layouts  6.38 us (7%)
  other arithmetic  1.87 us (2%)
    pallas_call x2, Pallas kernels, delta_local(): pl.pallas_call(delta_local_kernel, grid_spec=pltpu.PrefetchScalarGridSpec...  22.7 us
    ppermute x4, waiting for transfers between devices, up_chip(): return lax.ppermute(value, 'ctx', [(i, i + 2) for i in range(ranks - 2)])  13 us
    pallas_call x2, Pallas kernels, attention_half(): pl.pallas_call(attention_kernel, grid=(steps,), in_specs=in_specs, out_sp...  11.4 us
    ppermute x4, starting transfers between devices, up_chip(): return lax.ppermute(value, 'ctx', [(i, i + 2) for i in range(ranks - 2)])  10.8 us
    pallas_call x4, Pallas kernels, small_call(): pl.pallas_call(kernel, in_specs=[SMEM] * scalars + [VMEM] * (len(args) -...  10.1 us
    unnamed x28, local copies, waits for them, and re-layouts  5.61 us
    pallas_call x2, Pallas kernels, delta_out(): pl.pallas_call(delta_out_kernel, grid_spec=pltpu.PrefetchScalarGridSpec(n...  5.6 us
    ppermute x3, starting transfers between devices, swap_cores(): return lax.ppermute(value, 'ctx', [(i, i ^ 1) for i in range(ranks)])  3.47 us
  transfers between devices with their start and end apart: 7, of which 2 were waited for; matrix products, arithmetic and copies ran while one was open for 3% of the time, Pallas kernels for 54%

profile of v2, /device:TPU:9, one launch (start us, length us, event | category | flops | bytes accessed | tf_op | source)
XLA Modules:
  0.0 86.2 jit_solution(6000003194508851283)
XLA Ops:
  0.6 0.7 convert_add_fusion
  1.3 0.6 copy-done.12
  1.9 1.0 %pad_maximum_fusion.1.rest_0_ = bf16[272,512]{1,0:T(8,128)(2,1)S(1)} fusion(bf16[16,512]{1,0:T(8,128)(2,1)S(1)} %broadcast_in_dim.5, bf16[256,256]{1,0:T(8,128)(2,1)} %param.15, bf16[256,256]{1,0:T(8,128)(2,1)} %param.14), kind=kLoop, calls=%fused_computation.1 | loop fusion | flops 835584 | bytes 557056 | tf_op jit(solution)/shard_map/concatenate | solution.py:545
  2.9 3.3 %collective-permute-start = (bf16[272,512]{1,0:T(8,128)(2,1)S(1)}, bf16[272,512]{1,0:T(8,128)(2,1)S(1)}, u32[]{:S(2)}, u32[]{:S(2)}) collective-permute-start(bf16[272,512]{1,0:T(8,128)(2,1)S(1)} %pad_maximum_fusion.1.rest_0_), channel_id=1, source_target_pairs={{0,2},{1,3},{2,4},{3,5},{4,6},{5,7},{8,10},{9,11},{10,12},{11,13},... | collective-permute-start | bytes 835592 | tf_op jit(solution)/shard_map/ppermute | solution.py:514
  6.3 0.8 copy.16.beta_ref
  7.1 0.7 copy.17.decay_ref
  7.8 11.3 %delta_local.2 = (bf16[1040,256]{1,0:T(8,128)(2,1)}, bf16[256,1024]{1,0:T(8,128)(2,1)}, f32[256,1024]{1,0:T(8,128)}) custom-call(s32[1]{0:T(128)S(6)} %sub.3.half_ref, f32[1,256]{1,0:T(1,128)} %bitcast.8, bf16[256,1024]{1,0:T(8,128)(2,1)} %q_ref.7, bf16[256,1024]{1,0:T(8,128)(2,1)} %k_ref.3, bf16[256,2048]{1,0:T(8,128)(2,1)} %v_ref.3, ...), custom_call_target="tpu_custom_call" | custom-call | flops 6000000000 | bytes 3145728 | tf_op jit(solution)/shard_map/delta_local/pallas_call | solution.py:242
  19.1 1.0 %collective-permute-start.3 = (bf16[1040,256]{1,0:T(8,128)(2,1)}, bf16[1040,256]{1,0:T(8,128)(2,1)S(1)}, u32[]{:S(2)}, u32[]{:S(2)}) collective-permute-start(bf16[1040,256]{1,0:T(8,128)(2,1)} %get-tuple-element.25), channel_id=1, source_target_pairs={{0,1},{1,0},{2,3},{3,2},{4,5},{5,4},{6,7},{7,6},{8,9},{9,8},{10,11... | collective-permute-start | bytes 1597448 | tf_op jit(solution)/shard_map/ppermute | solution.py:518
  20.2 3.2 %collective-permute-start.1 = (bf16[272,512]{1,0:T(8,128)(2,1)S(1)}, bf16[272,512]{1,0:T(8,128)(2,1)S(1)}, u32[]{:S(2)}, u32[]{:S(2)}) collective-permute-start(bf16[272,512]{1,0:T(8,128)(2,1)S(1)} %collective-permute-done.rest_1_), channel_id=1, source_target_pairs={{0,2},{1,3},{2,4},{3,5},{4,6},{5,7},{8,10},{9,11},{10,12},{11,13},... | collective-permute-start | bytes 835592 | tf_op jit(solution)/shard_map/ppermute | solution.py:514
  23.4 11.4 %delta_local.3 = (bf16[1040,256]{1,0:T(8,128)(2,1)}, bf16[256,1024]{1,0:T(8,128)(2,1)}, f32[256,1024]{1,0:T(8,128)}) custom-call(s32[1]{0:T(128)} %bitcast.3.half_ref.core_ref, f32[1,256]{1,0:T(1,128)} %bitcast.9, bf16[256,1024]{1,0:T(8,128)(2,1)} %q_ref.7, bf16[256,1024]{1,0:T(8,128)(2,1)} %k_ref.3, bf16[256,2048]{1,0:T(8,128)(2,1)} %v_ref.3, ...), custom_call_target="tpu_custom_call" | custom-call | flops 6000000000 | bytes 3145728 | tf_op jit(solution)/shard_map/delta_local/pallas_call | solution.py:242
  34.7 0.8 copy-done
  35.5 2.4 %compose.1 = (bf16[1040,128]{1,0:T(8,128)(2,1)}, bf16[1040,128]{1,0:T(8,128)(2,1)}) custom-call(s32[1]{0:T(128)} %bitcast.3.half_ref.core_ref, bf16[1040,256]{1,0:T(8,128)(2,1)} %get-tuple-element.24.mine_ref, bf16[1040,256]{1,0:T(8,128)(2,1)} %copy-done), custom_call_target="tpu_custom_call" | custom-call | flops 100000000 | bytes 1048576 | tf_op jit(solution)/shard_map/compose/pallas_call | solution.py:342
  37.9 1.9 %collective-permute-start.4 = (bf16[1040,128]{1,0:T(8,128)(2,1)}, bf16[1040,128]{1,0:T(8,128)(2,1)S(1)}, u32[]{:S(2)}, u32[]{:S(2)}) collective-permute-start(bf16[1040,128]{1,0:T(8,128)(2,1)} %get-tuple-element.27.add_ref), channel_id=1, source_target_pairs={{0,2},{1,3},{2,4},{3,5},{4,6},{5,7},{8,10},{9,11},{10,12},{11,13},... | collective-permute-start | bytes 798728 | tf_op jit(solution)/shard_map/ppermute | solution.py:514
  39.9 0.1 select_bitcast_fusion.1
  40.0 0.6 copy-done.2
  40.6 0.1 pad_maximum_fusion
  40.6 0.4 collective-permute-start.2
  41.0 6.6 %collective-permute-done.4.state_ref = bf16[1040,128]{1,0:T(8,128)(2,1)S(1)} collective-permute-done((bf16[1040,128]{1,0:T(8,128)(2,1)}, bf16[1040,128]{1,0:T(8,128)(2,1)S(1)}, u32[]{:S(2)}, u32[]{:S(2)}) %collective-permute-start.4) | collective-permute-done | bytes 266272 | tf_op jit(solution)/shard_map/ppermute | solution.py:514
  47.6 0.7 copy-done.8
  48.4 2.0 %relay.1 = bf16[1040,128]{1,0:T(8,128)(2,1)} custom-call(bf16[1040,128]{1,0:T(8,128)(2,1)} %get-tuple-element.26.map_ref, bf16[1040,128]{1,0:T(8,128)(2,1)} %get-tuple-element.27.add_ref, bf16[1040,128]{1,0:T(8,128)(2,1)} %copy-done.8), custom_call_target="tpu_custom_call" | custom-call | flops 100000000 | bytes 1048576 | tf_op jit(solution)/shard_map/relay/pallas_call | solution.py:342
  50.4 2.4 %collective-permute-start.5 = (bf16[1040,128]{1,0:T(8,128)(2,1)}, bf16[1040,128]{1,0:T(8,128)(2,1)S(1)}, u32[]{:S(2)}, u32[]{:S(2)}) collective-permute-start(bf16[1040,128]{1,0:T(8,128)(2,1)} %relay.1), channel_id=1, source_target_pairs={{0,2},{1,3},{2,4},{3,5},{4,6},{5,7},{8,10},{9,11},{10,12},{11,13},... | collective-permute-start | bytes 798728 | tf_op jit(solution)/shard_map/ppermute | solution.py:514
  52.8 6.4 %collective-permute-done.5.state_ref = bf16[1040,128]{1,0:T(8,128)(2,1)S(1)} collective-permute-done((bf16[1040,128]{1,0:T(8,128)(2,1)}, bf16[1040,128]{1,0:T(8,128)(2,1)S(1)}, u32[]{:S(2)}, u32[]{:S(2)}) %collective-permute-start.5) | collective-permute-done | bytes 266272 | tf_op jit(solution)/shard_map/ppermute | solution.py:514
  59.2 0.7 copy-done.7
  59.9 2.4 %arrive.1 = (bf16[1024,128]{1,0:T(8,128)(2,1)}, bf16[1024,128]{1,0:T(8,128)(2,1)}) custom-call(s32[1]{0:T(128)} %bitcast.3.half_ref.core_ref, bf16[1040,256]{1,0:T(8,128)(2,1)} %get-tuple-element.24.mine_ref, bf16[1040,256]{1,0:T(8,128)(2,1)} %copy-done, bf16[1040,128]{1,0:T(8,128)(2,1)} %copy-done.7), custom_call_target="tpu_custom_call" | custom-call | flops 100000000 | bytes 1048576 | tf_op jit(solution)/shard_map/arrive/pallas_call | solution.py:342
  62.4 2.1 %collective-permute-start.6 = (bf16[1024,128]{1,0:T(8,128)(2,1)}, bf16[1024,128]{1,0:T(8,128)(2,1)S(1)}, u32[]{:S(2)}, u32[]{:S(2)}) collective-permute-start(bf16[1024,128]{1,0:T(8,128)(2,1)} %get-tuple-element.28), channel_id=1, source_target_pairs={{0,1},{1,0},{2,3},{3,2},{4,5},{5,4},{6,7},{7,6},{8,9},{9,8},{10,11... | collective-permute-start | bytes 786440 | tf_op jit(solution)/shard_map/ppermute | solution.py:518
  64.4 2.8 %delta_out.2.rest_0_ = bf16[256,2048]{1,0:T(8,128)(2,1)} custom-call(s32[1]{0:T(128)} %bitcast.3.half_ref.core_ref, bf16[256,1024]{1,0:T(8,128)(2,1)} %get-tuple-element.29.reach_ref, f32[256,1024]{1,0:T(8,128)} %get-tuple-element.30.inner_ref, bf16[1024,128]{1,0:T(8,128)(2,1)} %get-tuple-element.31.state_ref, bf16[256,2048]{1,0:T(8,128)(2,1)} %gate_ref.7, ...), custom_call_target="tpu_custom_call" | custom-call | flops 100000000 | bytes 3145728 | tf_op jit(solution)/shard_map/delta_out/pallas_call | solution.py:388
  67.2 0.8 broadcast_in_dim.4.freq_ref
  68.0 3.3 %window.1 = (bf16[256,1280]{1,0:T(8,128)(2,1)}, bf16[1280,256]{1,0:T(8,128)(2,1)}, f32[1,1280]{1,0:T(1,128)}, f32[256,128]{1,0:T(8,128)}, f32[256,128]{1,0:T(8,128)}) custom-call(f32[32,128]{1,0:T(8,128)} %broadcast_in_dim.4.freq_ref, bf16[272,512]{1,0:T(8,128)(2,1)} %copy-done.3, bf16[272,512]{1,0:T(8,128)(2,1)} %copy-done.1, bf16[272,512]{1,0:T(8,128)(2,1)} %copy-done.2, ...), custom_call_target="tpu_custom_call" | custom-call | flops 100000000 | bytes 1048576 | tf_op jit(solution)/shard_map/window/pallas_call | solution.py:342
  71.3 5.7 %attention.2.rest_0_ = bf16[256,2048]{1,0:T(8,128)(2,1)} custom-call(f32[1,1280]{1,0:T(1,128)} %get-tuple-element.17.ids_ref, f32[256,128]{1,0:T(8,128)} %get-tuple-element.18.cos_ref, f32[256,128]{1,0:T(8,128)} %get-tuple-element.19.sin_ref, bf16[256,1280]{1,0:T(8,128)(2,1)} %get-tuple-element.20.kt_ref, bf16[1280,256]{1,0:T(8,128)(2,1)} %get-tuple-element.21.v_ref, ...), custom_call_target="tpu_custom_call" | custom-call | flops 5000000000 | bytes 3145728 | tf_op jit(solution)/shard_map/attention/pallas_call | solution.py:499
  77.0 5.7 %attention.3 = bf16[256,2048]{1,0:T(8,128)(2,1)} custom-call(f32[1,1280]{1,0:T(1,128)} %get-tuple-element.17.ids_ref, f32[256,128]{1,0:T(8,128)} %get-tuple-element.18.cos_ref, f32[256,128]{1,0:T(8,128)} %get-tuple-element.19.sin_ref, bf16[256,1280]{1,0:T(8,128)(2,1)} %get-tuple-element.20.kt_ref, ...), custom_call_target="tpu_custom_call", output_to_operand_aliasing={{}: (7, {})} | custom-call | flops 5000000000 | bytes 3145728 | tf_op jit(solution)/shard_map/attention/pallas_call | solution.py:499
  82.7 0.7 copy-done.9
  83.4 2.8 %delta_out.3 = bf16[256,2048]{1,0:T(8,128)(2,1)} custom-call(s32[1]{0:T(128)S(6)} %sub.3.half_ref, bf16[256,1024]{1,0:T(8,128)(2,1)} %get-tuple-element.22.reach_ref, f32[256,1024]{1,0:T(8,128)} %get-tuple-element.23.inner_ref, bf16[1024,128]{1,0:T(8,128)(2,1)} %copy-done.9, bf16[256,2048]{1,0:T(8,128)(2,1)} %gate_ref.7, ...), custom_call_target="tpu_custom_call", output_to_operand_aliasing={{}: (6, {})} | custom-call | flops 100000000 | bytes 3145728 | tf_op jit(solution)/shard_map/delta_out/pallas_call | solution.py:388
  (29 shorter events, 0.1 us)
Async XLA Ops:
  1.3 0.6 copy-start.12
  2.9 16.2 %copy-start.3 = (bf16[272,512]{1,0:T(8,128)(2,1)}, bf16[272,512]{1,0:T(8,128)(2,1)S(1)}, u32[]{:S(2)}) copy-start(bf16[272,512]{1,0:T(8,128)(2,1)S(1)} %pad_maximum_fusion.1.rest_0_) | copy-start | bytes 835588
  2.9 3.4 %copy-start.10 = (f32[256,16]{0,1:T(8,128)S(1)}, f32[256,16]{0,1:T(8,128)}, u32[]{:S(2)}) copy-start(f32[256,16]{0,1:T(8,128)} %param.20) | copy-start | bytes 49156
  2.9 17.2 %collective-permute-start = (bf16[272,512]{1,0:T(8,128)(2,1)S(1)}, bf16[272,512]{1,0:T(8,128)(2,1)S(1)}, u32[]{:S(2)}, u32[]{:S(2)}) collective-permute-start(bf16[272,512]{1,0:T(8,128)(2,1)S(1)} %pad_maximum_fusion.1.rest_0_), channel_id=1, source_target_pairs={{0,2},{1,3},{2,4},{3,5},{4,6},{5,7},{8,10},{9,11},{10,12},{11,13},... | collective-permute-start | bytes 835592 | tf_op jit(solution)/shard_map/ppermute | solution.py:514
  6.3 0.8 copy-start.11
  19.1 15.6 %collective-permute-start.3 = (bf16[1040,256]{1,0:T(8,128)(2,1)}, bf16[1040,256]{1,0:T(8,128)(2,1)S(1)}, u32[]{:S(2)}, u32[]{:S(2)}) collective-permute-start(bf16[1040,256]{1,0:T(8,128)(2,1)} %get-tuple-element.25), channel_id=1, source_target_pairs={{0,1},{1,0},{2,3},{3,2},{4,5},{5,4},{6,7},{7,6},{8,9},{9,8},{10,11... | collective-permute-start | bytes 1597448 | tf_op jit(solution)/shard_map/ppermute | solution.py:518
  20.2 19.7 %copy-start.1 = (bf16[272,512]{1,0:T(8,128)(2,1)}, bf16[272,512]{1,0:T(8,128)(2,1)S(1)}, u32[]{:S(2)}) copy-start(bf16[272,512]{1,0:T(8,128)(2,1)S(1)} %collective-permute-done.rest_1_) | copy-start | bytes 835588
  20.2 19.6 %collective-permute-start.1 = (bf16[272,512]{1,0:T(8,128)(2,1)S(1)}, bf16[272,512]{1,0:T(8,128)(2,1)S(1)}, u32[]{:S(2)}, u32[]{:S(2)}) collective-permute-start(bf16[272,512]{1,0:T(8,128)(2,1)S(1)} %collective-permute-done.rest_1_), channel_id=1, source_target_pairs={{0,2},{1,3},{2,4},{3,5},{4,6},{5,7},{8,10},{9,11},{10,12},{11,13},... | collective-permute-start | bytes 835592 | tf_op jit(solution)/shard_map/ppermute | solution.py:514
  34.7 0.8 copy-start
  35.5 4.3 %copy-start.5 = (bf16[256,256]{1,0:T(8,128)(2,1)S(1)}, bf16[256,256]{1,0:T(8,128)(2,1)}, u32[]{:S(2)}) copy-start(bf16[256,256]{1,0:T(8,128)(2,1)} %param.15) | copy-start | bytes 393220
  35.5 4.3 %copy-start.6 = (bf16[256,256]{1,0:T(8,128)(2,1)S(1)}, bf16[256,256]{1,0:T(8,128)(2,1)}, u32[]{:S(2)}) copy-start(bf16[256,256]{1,0:T(8,128)(2,1)} %param.14) | copy-start | bytes 393220
  37.9 9.8 %collective-permute-start.4 = (bf16[1040,128]{1,0:T(8,128)(2,1)}, bf16[1040,128]{1,0:T(8,128)(2,1)S(1)}, u32[]{:S(2)}, u32[]{:S(2)}) collective-permute-start(bf16[1040,128]{1,0:T(8,128)(2,1)} %get-tuple-element.27.add_ref), channel_id=1, source_target_pairs={{0,2},{1,3},{2,4},{3,5},{4,6},{5,7},{8,10},{9,11},{10,12},{11,13},... | collective-permute-start | bytes 798728 | tf_op jit(solution)/shard_map/ppermute | solution.py:514
  39.8 0.7 copy-start.2
  40.6 26.6 %collective-permute-start.2 = (bf16[2,272,512]{2,1,0:T(8,128)(2,1)S(1)}, bf16[2,272,512]{2,1,0:T(8,128)(2,1)S(1)}, u32[]{:S(2)}, u32[]{:S(2)}) collective-permute-start(bf16[2,272,512]{2,1,0:T(8,128)(2,1)S(1)} %pad_maximum_fusion), channel_id=1, source_target_pairs={{0,1},{1,0},{2,3},{3,2},{4,5},{5,4},{6,7},{7,6},{8,9},{9,8},{10,11... | collective-permute-start | bytes 1671176 | tf_op jit(solution)/shard_map/ppermute | solution.py:518
  47.6 0.7 copy-start.8
  50.4 8.8 %collective-permute-start.5 = (bf16[1040,128]{1,0:T(8,128)(2,1)}, bf16[1040,128]{1,0:T(8,128)(2,1)S(1)}, u32[]{:S(2)}, u32[]{:S(2)}) collective-permute-start(bf16[1040,128]{1,0:T(8,128)(2,1)} %relay.1), channel_id=1, source_target_pairs={{0,2},{1,3},{2,4},{3,5},{4,6},{5,7},{8,10},{9,11},{10,12},{11,13},... | collective-permute-start | bytes 798728 | tf_op jit(solution)/shard_map/ppermute | solution.py:514
  59.2 0.7 copy-start.7
  62.4 20.3 %collective-permute-start.6 = (bf16[1024,128]{1,0:T(8,128)(2,1)}, bf16[1024,128]{1,0:T(8,128)(2,1)S(1)}, u32[]{:S(2)}, u32[]{:S(2)}) collective-permute-start(bf16[1024,128]{1,0:T(8,128)(2,1)} %get-tuple-element.28), channel_id=1, source_target_pairs={{0,1},{1,0},{2,3},{3,2},{4,5},{5,4},{6,7},{7,6},{8,9},{9,8},{10,11... | collective-permute-start | bytes 786440 | tf_op jit(solution)/shard_map/ppermute | solution.py:518
  67.2 0.8 copy-start.4
  82.7 0.7 copy-start.9

commit v3 on v2

--- a/solution.py
+++ b/solution.py
@@ -17,8 +17,8 @@
 MASKED = -1e30
 EPS = 1e-6
 TILE = 128
-KEYS_PER_STEP = 2
-VMEM_LIMIT = 60 * 1024 * 1024
+KEYS_PER_STEP = 1
+MIB = 1024 * 1024
 
 f32 = jnp.float32
 bf16 = jnp.bfloat16
@@ -28,8 +28,12 @@
     return jnp.dot(a, b, preferred_element_type=f32, precision=precision)
 
 
-def params():
-    return pltpu.CompilerParams(vmem_limit_bytes=VMEM_LIMIT)
+def params(mib=16):
+    return pltpu.CompilerParams(vmem_limit_bytes=mib * MIB)
+
+
+def sigmoid(x):
+    return 0.5 * jnp.tanh(0.5 * x) + 0.5
 
 
 def cost(flops, nbytes, exps=0):
@@ -102,7 +106,6 @@
     level_ref,
     crow_ref,
     ccol_ref,
-    bcol_ref,
     first_ref,
 ):
     rows = q_ref.shape[0]
@@ -111,7 +114,7 @@
 
     @pl.when(step == 0)
     def _():
-        seg_row = seg_ref[...]
+        seg_row = seg_ref[...].astype(f32) + 1.0
         seg_col = jnp.transpose(jnp.broadcast_to(seg_row, (TILE, rows)))
         seg_cols = jnp.concatenate([seg_col] * (rows // TILE), axis=1)
         r = lax.broadcasted_iota(jnp.int32, (rows, rows), 0)
@@ -124,25 +127,28 @@
             b = BLOCK << level
             sibling = jnp.where(r // b == c // b + 1, 1.0, 0.0)
             level_ref[level] = odd_rows(sibling, b).astype(bf16)
-        all_heads = decay_ref.shape[1]
-        base = half_ref[0] * (all_heads // 2)
-        er = lax.broadcasted_iota(jnp.int32, (all_heads, TILE), 0)
-        ec = lax.broadcasted_iota(jnp.int32, (all_heads, TILE), 1)
-        pick = jnp.where(er - ec == base, 1.0, 0.0)
-        tr = lax.broadcasted_iota(jnp.int32, (rows, rows), 0)
-        tc = lax.broadcasted_iota(jnp.int32, (rows, rows), 1)
-        tril = jnp.where(tr >= tc, 1.0, 0.0)
-        decay = dot(decay_ref[...], pick, lax.Precision.HIGHEST) * LOG2E
-        cumulative = dot(tril, decay, lax.Precision.HIGHEST)
-        ccol_ref[...] = cumulative
-        crow_ref[...] = jnp.transpose(cumulative)
-        bcol_ref[...] = dot(beta_ref[...], pick, lax.Precision.HIGHEST)
+        n = map_add_ref.shape[0] // DK
+        base = pl.multiple_of(half_ref[0] * n, n)
+        decay = decay_ref[pl.ds(base, n), :] * LOG2E
+        high = decay.astype(bf16)
+        rest = decay - high.astype(f32)
+        middle = rest.astype(bf16)
+        parts = [high, middle, (rest - middle.astype(f32)).astype(bf16)]
+        parts = jnp.concatenate([p.astype(f32) for p in parts], axis=0).astype(bf16)
+        r = lax.broadcasted_iota(jnp.int32, (rows, rows), 0)
+        c = lax.broadcasted_iota(jnp.int32, (rows, rows), 1)
+        sums = dot(parts, jnp.where(r <= c, 1.0, 0.0).astype(bf16))
+        cumulative = sums[:n] + sums[n : 2 * n] + sums[2 * n :]
+        crow_ref[...] = cumulative
+        fill = jnp.zeros((TILE - 2 * n, rows), f32)
+        both = jnp.concatenate([cumulative, beta_ref[pl.ds(base, n), :], fill], axis=0)
+        ccol_ref[...] = jnp.transpose(both)
         end = map_add_ref.shape[0] - BLOCK
         map_add_ref[end:, :] = jnp.broadcast_to(seg_row, (BLOCK, rows)).astype(bf16)
 
     shift = lax.rem(TILE - step * heads, TILE)
-    ccol = pltpu.roll(ccol_ref[...], shift, 1)
-    bcol = pltpu.roll(bcol_ref[...], shift, 1)
+    columns = pltpu.roll(ccol_ref[...], shift, 1)
+    n = map_add_ref.shape[0] // DK
     first = first_ref[...]
     eye = jnp.where(
         lax.broadcasted_iota(jnp.int32, (TILE, TILE), 0)
@@ -164,22 +170,21 @@
         ktb = kt.astype(bf16)
         upper = dot(jnp.concatenate([k_raw[:TILE], q_raw[:TILE]], axis=0), ktb[:, :TILE])
         lower = dot(jnp.concatenate([k_raw[TILE:], q_raw[TILE:]], axis=0), ktb)
-        gram1 = upper[:TILE] * rk_row[:, :TILE]
+        gram1 = upper[:TILE] * rk_row[:, :TILE] * -rk_col[:TILE]
         probe1 = upper[TILE:] * rk_row[:, :TILE] * rq_col[:TILE]
-        gram2 = lower[:TILE] * rk_row
+        gram2 = lower[:TILE] * rk_row * -rk_col[TILE:]
         probe2 = lower[TILE:] * rk_row * rq_col[TILE:]
         kn = kf * rk_col
         qn = qf * rq_col
         for j in range(2):
             h = 2 * kk + j
-            cc = ccol[:, h : h + 1]
-            bt = bcol[:, h : h + 1]
+            cc = columns[:, h : h + 1]
+            bt = columns[:, n + h : n + h + 1]
             cr = crow_ref[pl.ds(step * heads + h, 1), :]
             span1 = jnp.exp2(cc[:TILE] - cr[:, :TILE] + mask_ref[:TILE, :TILE])
             span2 = jnp.exp2(cc[TILE:] - cr + mask_ref[TILE:, :])
-            scale = -bt * rk_col
-            d11 = span1 * scale[:TILE] * gram1
-            d2 = span2 * scale[TILE:] * gram2
+            d11 = span1 * bt[:TILE] * gram1
+            d2 = span2 * bt[TILE:] * gram2
             p11 = (span1 * probe1).astype(bf16)
             p2 = (span2 * probe2).astype(bf16)
             entry = jnp.exp2(cc) * first
@@ -211,11 +216,13 @@
         h = w["h"]
         r1 = w["right"][:TILE]
         u1 = (r1 + dot(x1, r1.astype(bf16))).astype(bf16)
-        r2 = w["right"][TILE:] + dot(w["d21"], u1)
+        after = dot(jnp.concatenate([w["d21"], w["p11"]], axis=0), u1)
+        r2 = w["right"][TILE:] + after[:TILE]
         u2 = (r2 + dot(x2, r2.astype(bf16))).astype(bf16)
         u = jnp.concatenate([u1, u2], axis=0)
-        pu = jnp.concatenate([dot(w["p11"], u1), dot(w["p2"], u)], axis=0)
-        ma = dot(w["kd"], u)
+        last = dot(jnp.concatenate([w["p2"], w["kd"]], axis=0), u)
+        pu = jnp.concatenate([after[TILE:], last[:TILE]], axis=0)
+        ma = last[TILE:]
         at = pl.multiple_of((step * heads + h) * DK, DK)
         map_add_ref[pl.ds(at, DK), :] = jnp.concatenate(
             [w["last"] * eye - ma[:, :DK], ma[:, DK:]], axis=1
@@ -224,7 +231,7 @@
         inner_ref[:, h * DV : (h + 1) * DV] = pu[:, DK:].astype(inner_ref.dtype)
 
 
-def delta_local(half, seg_row, query, key, value, beta, decay):
+def delta_local(half, mib, seg_row, query, key, value, beta, decay):
     rows = query.shape[0]
     heads = 2 * KEYS_PER_STEP
     n = value.shape[1] // DV // 2
@@ -260,8 +267,7 @@
             scratch_shapes=[
                 pltpu.VMEM((rows, rows), f32),
                 pltpu.VMEM((MERGES, TILE // 2, TILE), bf16),
-                pltpu.VMEM((TILE, rows), f32),
-                pltpu.VMEM((rows, TILE), f32),
+                pltpu.VMEM((n, rows), f32),
                 pltpu.VMEM((rows, TILE), f32),
                 pltpu.VMEM((rows, TILE), f32),
             ],
@@ -271,7 +277,7 @@
             jax.ShapeDtypeStruct((rows, n * DK), bf16),
             jax.ShapeDtypeStruct((rows, n * DV), f32),
         ],
-        compiler_params=params(),
+        compiler_params=params(mib),
         cost_estimate=cost(6 * 10**9, 3 * 2**20),
         name="delta_local",
     )(half, seg_row, query, key, value, beta, decay)
@@ -338,13 +344,13 @@
 VMEM = pl.BlockSpec(memory_space=pltpu.VMEM)
 
 
-def small_call(kernel, name, outs, *args, scalars=0):
+def small_call(kernel, name, outs, *args, scalars=0, mib=16):
     return pl.pallas_call(
         kernel,
         in_specs=[SMEM] * scalars + [VMEM] * (len(args) - scalars),
         out_specs=[VMEM] * len(outs),
         out_shape=outs,
-        compiler_params=params(),
+        compiler_params=params(mib),
         cost_estimate=cost(10**8, 2**20),
         name=name,
     )(*args)
@@ -359,7 +365,7 @@
         out = inner_ref[:, cols].astype(f32) + dot(reach_ref[:, cols], state)
         spread = lax.rsqrt(jnp.mean(out * out, axis=1, keepdims=True) + EPS)
         gate = gate_ref[:, cols].astype(f32)
-        gate = gate * jax.nn.sigmoid(gate)
+        gate = gate * sigmoid(gate)
         out_ref[:, cols] = (out * spread * gain * gate).astype(bf16)
 
 
@@ -409,6 +415,15 @@
     return order[::-1]
 
 
+def pack_kernel(seg_ref, key_ref, value_ref, out_ref):
+    rows = key_ref.shape[0]
+    ids = seg_ref[...].astype(f32) + 1.0
+    out_ref[:rows, :HEAD_WIDTH] = key_ref[...]
+    out_ref[:rows, HEAD_WIDTH:] = value_ref[...]
+    out_ref[rows:, :rows] = jnp.broadcast_to(ids, (BLOCK, rows)).astype(bf16)
+    out_ref[rows:, rows:] = jnp.zeros((BLOCK, 2 * HEAD_WIDTH - rows), bf16)
+
+
 def window_kernel(freq_ref, *rest):
     *pieces, kt_ref, v_ref, ids_ref, cos_ref, sin_ref = rest
     rows = cos_ref.shape[0]
@@ -462,20 +477,27 @@
         mask_ref[...] = jnp.where((own_cols == ids_ref[...]) & (c <= r), 0.0, MASKED)
 
     scaling = HEAD_WIDTH**-0.5
-    lane = lax.broadcasted_iota(jnp.int32, (rows, TILE), 1)
+    lane = lax.broadcasted_iota(jnp.int32, (TILE, TILE), 1)
+    reach = window - rows + TILE
     for h in range(q_ref.shape[1] // HEAD_WIDTH):
         base = h * HEAD_WIDTH
-        x = q_ref[:, base : base + TILE].astype(f32)
-        swapped = jnp.where(lane < half, pltpu.roll(x, TILE - half, 1), pltpu.roll(x, half, 1))
-        rotated = ((x * cos_ref[...] + swapped * sin_ref[...]) * scaling).astype(bf16)
-        tail = q_ref[:, base + TILE : base + HEAD_WIDTH] * jnp.asarray(scaling, bf16)
-        scores = dot(jnp.concatenate([rotated, tail], axis=1), kt_ref[...]) + mask_ref[...]
-        best = jnp.max(scores, axis=1, keepdims=True)
-        weights = jnp.exp(scores - best)
-        total = jnp.sum(weights, axis=1, keepdims=True)
-        mixed = dot(weights.astype(bf16), v_ref[...])
-        gate = jax.nn.sigmoid(gate_ref[:, base : base + HEAD_WIDTH].astype(f32))
-        out_ref[:, base : base + HEAD_WIDTH] = (mixed / total * gate).astype(bf16)
+        for first in range(0, rows, TILE):
+            at = slice(first, first + TILE)
+            keys = slice(first, first + reach)
+            x = q_ref[at, base : base + TILE].astype(f32)
+            swapped = jnp.where(
+                lane < half, pltpu.roll(x, TILE - half, 1), pltpu.roll(x, half, 1)
+            )
+            rotated = ((x * cos_ref[at] + swapped * sin_ref[at]) * scaling).astype(bf16)
+            tail = q_ref[at, base + TILE : base + HEAD_WIDTH] * jnp.asarray(scaling, bf16)
+            scores = dot(jnp.concatenate([rotated, tail], axis=1), kt_ref[:, keys])
+            scores = scores + mask_ref[at, keys]
+            best = jnp.max(scores, axis=1, keepdims=True)
+            weights = jnp.exp(scores - best)
+            total = jnp.sum(weights, axis=1, keepdims=True)
+            mixed = dot(weights.astype(bf16), v_ref[keys, :])
+            gate = sigmoid(gate_ref[at, base : base + HEAD_WIDTH].astype(f32))
+            out_ref[at, base : base + HEAD_WIDTH] = (mixed * (1.0 / total) * gate).astype(bf16)
 
 
 def attention_half(part, window_arrays, query, gate, partial_out=None):
@@ -539,19 +561,18 @@
     core = rank % 2
     odd = core == 1
 
-    ids = segment_ids.astype(f32).reshape(1, rows) + 1.0
-
-    id_rows = jnp.broadcast_to(jnp.concatenate([ids, ids], axis=1), (BLOCK, 2 * rows))
-    own = jnp.concatenate(
-        [jnp.concatenate([attention_keys, attention_values], axis=1), id_rows.astype(bf16)], axis=0
-    )
-    same = []
-    for _ in range(hops):
-        same.append(up_chip(same[-1] if same else own, ranks))
-    chain = [own, *same]
-    other = swap_cores(
-        jnp.stack([jnp.where(odd, chain[i + 1], chain[i]) for i in range(hops)]), ranks
-    )
+    ids = segment_ids.reshape(1, rows)
+
+    (own,) = small_call(
+        pack_kernel,
+        "pack",
+        [jax.ShapeDtypeStruct((rows + BLOCK, 2 * HEAD_WIDTH), bf16)],
+        ids,
+        attention_keys,
+        attention_values,
+        mib=60,
+    )
+    nearest = up_chip(own, ranks)
 
     keep_half = core.reshape(1).astype(jnp.int32)
     give_half = 1 - keep_half
@@ -561,12 +582,21 @@
         query=delta_query,
         key=delta_key,
         value=update_rule_payload,
-        beta=delta_beta,
-        decay=delta_decay,
-    )
-    give_ma, give_reach, give_inner = local(give_half)
+        beta=delta_beta.T,
+        decay=delta_decay.T,
+    )
+    give_ma, give_reach, give_inner = local(give_half, 60)
     other_ma = swap_cores(give_ma, ranks)
-    keep_ma, keep_reach, keep_inner = local(keep_half)
+    nearest, give_ma = lax.optimization_barrier((nearest, give_ma))
+    same = [nearest]
+    for _ in range(hops - 1):
+        same.append(up_chip(same[-1], ranks))
+    keep_ma, keep_reach, keep_inner = local(keep_half, 20)
+    same, keep_ma = lax.optimization_barrier((same, keep_ma))
+    chain = [own, *same]
+    other = swap_cores(
+        jnp.stack([jnp.where(odd, chain[i + 1], chain[i]) for i in range(hops)]), ranks
+    )
 
     tall = keep_ma.shape[0]
     state_like = jax.ShapeDtypeStruct((tall, DV), bf16)
@@ -574,20 +604,12 @@
         compose_kernel, "compose", [state_like] * 2, keep_half, keep_ma, other_ma, scalars=1
     )
     state = up_chip(chip_add, ranks)
-    for _ in range(hops - 1):
-        (leaving,) = small_call(relay_kernel, "relay", [state_like], chip_map, chip_add, state)
-        state = up_chip(leaving, ranks)
-    final_like = jax.ShapeDtypeStruct((tall - BLOCK, DV), bf16)
-    keep_state, pass_state = small_call(
-        arrive_kernel, "arrive", [final_like] * 2, keep_half, keep_ma, other_ma, state, scalars=1
-    )
-    give_state = swap_cores(pass_state, ranks)
 
     window = (2 * hops + 1) * rows
     index = jnp.arange(ROTARY_ENTRIES // 2).astype(f32)
     freq = ROPE_THETA ** (-2.0 * index / ROTARY_ENTRIES)
     freq = jnp.broadcast_to(freq[:, None], (ROTARY_ENTRIES // 2, TILE))
-    kt, v_all, window_ids, cosine, sine = small_call(
+    window_arrays = small_call(
         window_kernel,
         "window",
         [
@@ -602,8 +624,20 @@
         *same,
         other,
     )
+    state, window_arrays = lax.optimization_barrier((state, window_arrays))
+    for _ in range(hops - 1):
+        (leaving,) = small_call(relay_kernel, "relay", [state_like], chip_map, chip_add, state)
+        state = up_chip(leaving, ranks)
+    kt, v_all, window_ids, cosine, sine = window_arrays
     window_arrays = (window_ids, cosine, sine, kt, v_all)
     attn_mixed = attention_half(0, window_arrays, attn_query, attn_gate)
+    state, attn_mixed = lax.optimization_barrier((state, attn_mixed))
+
+    final_like = jax.ShapeDtypeStruct((tall - BLOCK, DV), bf16)
+    keep_state, pass_state = small_call(
+        arrive_kernel, "arrive", [final_like] * 2, keep_half, keep_ma, other_ma, state, scalars=1
+    )
+    give_state = swap_cores(pass_state, ranks)
     attn_mixed = attention_half(1, window_arrays, attn_query, attn_gate, attn_mixed)
 
     gain = norm_gain.reshape(1, DV)

time: 86.8 us -> 64.4 us (0.74)
  Pallas kernels: 49.8 us -> 37.4 us
  waiting for transfers between devices: 13.1 us -> 9.04 us
  local copies, waits for them, and re-layouts: 6.38 us -> 3.03 us
  other arithmetic: 1.87 us -> 0.11 us
    pallas_call x4 -> x5, Pallas kernels: 10.1 us -> 3.54 us  [small_call(): pl.pallas_call(kernel, in_specs=[SMEM] * scalars + [VMEM] * (len(args) -...]
    ppermute x4, waiting for transfers between devices: 13 us -> 9.03 us  [up_chip(): return lax.ppermute(value, 'ctx', [(i, i + 2) for i in range(ranks - 2)])]
    unnamed x28 -> x26, local copies, waits for them, and re-layouts: 5.61 us -> 2.96 us
    pallas_call x2, Pallas kernels: 11.4 us -> 9.06 us  [attention_half(): pl.pallas_call(attention_kernel, grid=(steps,), in_specs=in_specs, out_sp...]
    pallas_call x2, Pallas kernels: 5.6 us -> 3.55 us  [delta_out(): pl.pallas_call(delta_out_kernel, grid_spec=pltpu.PrefetchScalarGridSpec(n...]
    pallas_call x2, Pallas kernels: 22.7 us -> 21.2 us  [delta_local(): pl.pallas_call(delta_local_kernel, grid_spec=pltpu.PrefetchScalarGridSpec...]
    concatenate x2 -> x0, other arithmetic: 1.01 us -> none  [the longest x1 0.99 us: per_device(): jnp.concatenate([jnp.concatenate([attention_keys, attention_values], axis...]
  transfers between devices with their start and end apart: 7 -> 7, of which waited for: 2 -> 2; matrix products, arithmetic and copies ran while one was open for 3% -> 0% of each run, Pallas kernels for 54% -> 52%
where the time goes in v3:
time: 64.4 us; the launch traced here: 64.1 us
  Pallas kernels  37.4 us (58%)
  starting transfers between devices  13.6 us (21%)
  waiting for transfers between devices  9.04 us (14%)
  local copies, waits for them, and re-layouts  3.03 us (5%)
  between operations  0.87 us (1%)
    pallas_call x2, Pallas kernels, delta_local(): pl.pallas_call(delta_local_kernel, grid_spec=pltpu.PrefetchScalarGridSpec...  21.2 us
    ppermute x4, starting transfers between devices, up_chip(): return lax.ppermute(value, 'ctx', [(i, i + 2) for i in range(ranks - 2)])  10.2 us
    pallas_call x2, Pallas kernels, attention_half(): pl.pallas_call(attention_kernel, grid=(steps,), in_specs=in_specs, out_sp...  9.06 us
    ppermute x4, waiting for transfers between devices, up_chip(): return lax.ppermute(value, 'ctx', [(i, i + 2) for i in range(ranks - 2)])  9.03 us
    pallas_call x2, Pallas kernels, delta_out(): pl.pallas_call(delta_out_kernel, grid_spec=pltpu.PrefetchScalarGridSpec(n...  3.55 us
    pallas_call x5, Pallas kernels, small_call(): pl.pallas_call(kernel, in_specs=[SMEM] * scalars + [VMEM] * (len(args) -...  3.54 us
    ppermute x3, starting transfers between devices, swap_cores(): return lax.ppermute(value, 'ctx', [(i, i ^ 1) for i in range(ranks)])  3.4 us
    unnamed x26, local copies, waits for them, and re-layouts  2.96 us
  transfers between devices with their start and end apart: 7, of which 2 were waited for; matrix products, arithmetic and copies ran while one was open for 0% of the time, Pallas kernels for 52%

profile of v3, /device:TPU:9, one launch (start us, length us, event | category | flops | bytes accessed | tf_op | source)
XLA Modules:
  0.0 64.1 jit_solution(5282662643421290554)
XLA Ops:
  0.6 1.7 %pack.1.rest_0_ = bf16[272,512]{1,0:T(8,128)(2,1)} custom-call(s32[1,256]{1,0:T(1,128)} %bitcast.11, bf16[256,256]{1,0:T(8,128)(2,1)} %key_ref.1, bf16[256,256]{1,0:T(8,128)(2,1)} %value_ref.1), custom_call_target="tpu_custom_call" | custom-call | flops 100000000 | bytes 1048576 | tf_op jit(solution)/shard_map/pack/pallas_call | solution.py:348
  2.3 3.2 %collective-permute-start = (bf16[272,512]{1,0:T(8,128)(2,1)}, bf16[272,512]{1,0:T(8,128)(2,1)S(1)}, u32[]{:S(2)}, u32[]{:S(2)}) collective-permute-start(bf16[272,512]{1,0:T(8,128)(2,1)} %pack.1.rest_0_), channel_id=1, source_target_pairs={{0,2},{1,3},{2,4},{3,5},{4,6},{5,7},{8,10},{9,11},{10,12},{11,13},... | collective-permute-start | bytes 835592 | tf_op jit(solution)/shard_map/ppermute | solution.py:536
  5.6 0.0 copy-start.9
  5.6 0.0 copy-start.11
  5.6 0.0 copy-start.12
  5.6 11.4 %delta_local.2 = (bf16[1040,256]{1,0:T(8,128)(2,1)}, bf16[256,1024]{1,0:T(8,128)(2,1)}, f32[256,1024]{1,0:T(8,128)}) custom-call(s32[1]{0:T(128)S(6)} %sub.3.half_ref, s32[1,256]{1,0:T(1,128)} %bitcast.12, bf16[256,1024]{1,0:T(8,128)(2,1)} %q_ref.5, bf16[256,1024]{1,0:T(8,128)(2,1)} %k_ref.3, bf16[256,2048]{1,0:T(8,128)(2,1)} %v_ref.3, f32[16,256]{1,0:T(8,128)} %bitcast.14, ...), custom_call_target="tpu_custom_call" | custom-call | flops 6000000000 | bytes 3145728 | tf_op jit(solution)/shard_map/delta_local/pallas_call | solution.py:249
  17.0 0.0 copy-start.5
  17.0 0.0 copy-start.1
  17.0 1.0 %collective-permute-start.2 = (bf16[1040,256]{1,0:T(8,128)(2,1)}, bf16[1040,256]{1,0:T(8,128)(2,1)S(1)}, u32[]{:S(2)}, u32[]{:S(2)}) collective-permute-start(bf16[1040,256]{1,0:T(8,128)(2,1)} %get-tuple-element.29), channel_id=1, source_target_pairs={{0,1},{1,0},{2,3},{3,2},{4,5},{5,4},{6,7},{7,6},{8,9},{9,8},{10,11... | collective-permute-start | bytes 1597448 | tf_op jit(solution)/shard_map/ppermute | solution.py:540
  18.1 3.2 %collective-permute-start.1 = (bf16[272,512]{1,0:T(8,128)(2,1)S(1)}, bf16[272,512]{1,0:T(8,128)(2,1)S(1)}, u32[]{:S(2)}, u32[]{:S(2)}) collective-permute-start(bf16[272,512]{1,0:T(8,128)(2,1)S(1)} %collective-permute-done.rest_1_), channel_id=1, source_target_pairs={{0,2},{1,3},{2,4},{3,5},{4,6},{5,7},{8,10},{9,11},{10,12},{11,13},... | collective-permute-start | bytes 835592 | tf_op jit(solution)/shard_map/ppermute | solution.py:536
  21.3 0.0 copy-start.6
  21.3 1.2 %copy-done.6 = bf16[256,2048]{1,0:T(8,128)(2,1)S(1)} copy-done((bf16[256,2048]{1,0:T(8,128)(2,1)S(1)}, bf16[256,2048]{1,0:T(8,128)(2,1)}, u32[]{:S(2)}) %copy-start.6) | copy-done | bytes 1048600
  22.5 1.0 %copy-done.10 = bf16[256,1024]{1,0:T(8,128)(2,1)S(1)} copy-done((bf16[256,1024]{1,0:T(8,128)(2,1)S(1)}, bf16[256,1024]{1,0:T(8,128)(2,1)}, u32[]{:S(2)}) %copy-start.10) | copy-done | bytes 524312
  23.6 9.8 %delta_local.3 = (bf16[1040,256]{1,0:T(8,128)(2,1)S(1)}, bf16[256,1024]{1,0:T(8,128)(2,1)S(1)}, f32[256,1024]{1,0:T(8,128)S(1)}) custom-call(s32[1]{0:T(128)} %bitcast.half_ref.core_ref, s32[1,256]{1,0:T(1,128)S(1)} %bitcast.13, bf16[256,1024]{1,0:T(8,128)(2,1)S(1)} %copy-done.9, bf16[256,1024]{1,0:T(8,128)(2,1)S(1)} %copy-done.10, ...), custom_call_target="tpu_custom_call" | custom-call | flops 6000000000 | bytes 3145728 | tf_op jit(solution)/shard_map/delta_local/pallas_call | solution.py:249
  33.4 0.1 select_bitcast_fusion.1
  33.5 0.1 pad_maximum_fusion
  33.5 0.4 collective-permute-start.4
  33.9 0.3 compose.1
  34.2 1.9 %collective-permute-start.3 = (bf16[1040,128]{1,0:T(8,128)(2,1)S(1)}, bf16[1040,128]{1,0:T(8,128)(2,1)S(1)}, u32[]{:S(2)}, u32[]{:S(2)}) collective-permute-start(bf16[1040,128]{1,0:T(8,128)(2,1)S(1)} %get-tuple-element.33.add_ref), channel_id=1, source_target_pairs={{0,2},{1,3},{2,4},{3,5},{4,6},{5,7},{8,10},{9,11},{10,12},{11,13},... | collective-permute-start | bytes 798728 | tf_op jit(solution)/shard_map/ppermute | solution.py:536
  36.2 0.1 broadcast_in_dim.2.freq_ref
  36.3 0.9 %window.1 = (bf16[256,1280]{1,0:T(8,128)(2,1)S(1)}, bf16[1280,256]{1,0:T(8,128)(2,1)S(1)}, f32[1,1280]{1,0:T(1,128)S(1)}, f32[256,128]{1,0:T(8,128)S(1)}, f32[256,128]{1,0:T(8,128)S(1)}) custom-call(f32[32,128]{1,0:T(8,128)S(1)} %broadcast_in_dim.2.freq_ref, bf16[272,512]{1,0:T(8,128)(2,1)S(1)} %copy-done.1, ...), custom_call_target="tpu_custom_call" | custom-call | flops 100000000 | bytes 1048576 | tf_op jit(solution)/shard_map/window/pallas_call | solution.py:348
  37.2 6.7 %collective-permute-done.3.state_ref = bf16[1040,128]{1,0:T(8,128)(2,1)S(1)} collective-permute-done((bf16[1040,128]{1,0:T(8,128)(2,1)S(1)}, bf16[1040,128]{1,0:T(8,128)(2,1)S(1)}, u32[]{:S(2)}, u32[]{:S(2)}) %collective-permute-start.3) | collective-permute-done | bytes 266272 | tf_op jit(solution)/shard_map/ppermute | solution.py:536
  43.9 0.2 relay.1
  44.2 1.9 %collective-permute-start.5 = (bf16[1040,128]{1,0:T(8,128)(2,1)S(1)}, bf16[1040,128]{1,0:T(8,128)(2,1)S(1)}, u32[]{:S(2)}, u32[]{:S(2)}) collective-permute-start(bf16[1040,128]{1,0:T(8,128)(2,1)S(1)} %relay.1), channel_id=1, source_target_pairs={{0,2},{1,3},{2,4},{3,5},{4,6},{5,7},{8,10},{9,11},{10,12},{11,13},... | collective-permute-start | bytes 798728 | tf_op jit(solution)/shard_map/ppermute | solution.py:536
  46.1 4.5 %attention.2.rest_0_ = bf16[256,2048]{1,0:T(8,128)(2,1)} custom-call(f32[1,1280]{1,0:T(1,128)S(1)} %get-tuple-element.41.ids_ref, f32[256,128]{1,0:T(8,128)S(1)} %get-tuple-element.42.cos_ref, f32[256,128]{1,0:T(8,128)S(1)} %get-tuple-element.43.sin_ref, bf16[256,1280]{1,0:T(8,128)(2,1)S(1)} %get-tuple-element.44.kt_ref, ...), custom_call_target="tpu_custom_call" | custom-call | flops 5000000000 | bytes 3145728 | tf_op jit(solution)/shard_map/attention/pallas_call | solution.py:521
  50.7 2.3 %collective-permute-done.5.state_ref = bf16[1040,128]{1,0:T(8,128)(2,1)S(1)} collective-permute-done((bf16[1040,128]{1,0:T(8,128)(2,1)S(1)}, bf16[1040,128]{1,0:T(8,128)(2,1)S(1)}, u32[]{:S(2)}, u32[]{:S(2)}) %collective-permute-start.5) | collective-permute-done | bytes 266272 | tf_op jit(solution)/shard_map/ppermute | solution.py:536
  53.0 0.4 arrive.1
  53.3 2.0 %collective-permute-start.6 = (bf16[1024,128]{1,0:T(8,128)(2,1)S(1)}, bf16[1024,128]{1,0:T(8,128)(2,1)S(1)}, u32[]{:S(2)}, u32[]{:S(2)}) collective-permute-start(bf16[1024,128]{1,0:T(8,128)(2,1)S(1)} %get-tuple-element.52), channel_id=1, source_target_pairs={{0,1},{1,0},{2,3},{3,2},{4,5},{5,4},{6,7},{7,6},{8,9},{9,8},{10,11... | collective-permute-start | bytes 786440 | tf_op jit(solution)/shard_map/ppermute | solution.py:540
  55.3 0.7 %copy-done.4 = f32[128]{0:T(128)S(1)} copy-done((f32[128]{0:T(128)S(1)}, f32[128]{0:T(128)}, u32[]{:S(2)}) %copy-start.4) | copy-done | bytes 536
  56.0 1.8 %delta_out.2.rest_0_ = bf16[256,2048]{1,0:T(8,128)(2,1)} custom-call(s32[1]{0:T(128)} %bitcast.half_ref.core_ref, bf16[256,1024]{1,0:T(8,128)(2,1)S(1)} %get-tuple-element.53.reach_ref, f32[256,1024]{1,0:T(8,128)S(1)} %get-tuple-element.54.inner_ref, bf16[1024,128]{1,0:T(8,128)(2,1)S(1)} %get-tuple-element.55.state_ref, bf16[256,2048]{1,0:T(8,128)(2,1)S(1)} %copy-done, ...), custom_call_target="tpu_custom_call" | custom-call | flops 100000000 | bytes 3145728 | tf_op jit(solution)/shard_map/delta_out/pallas_call | solution.py:394
  57.7 4.5 %attention.3 = bf16[256,2048]{1,0:T(8,128)(2,1)} custom-call(f32[1,1280]{1,0:T(1,128)S(1)} %get-tuple-element.41.ids_ref, f32[256,128]{1,0:T(8,128)S(1)} %get-tuple-element.42.cos_ref, f32[256,128]{1,0:T(8,128)S(1)} %get-tuple-element.43.sin_ref, bf16[256,1280]{1,0:T(8,128)(2,1)S(1)} %get-tuple-element.44.kt_ref, ...), custom_call_target="tpu_custom_call", output_to_operand_aliasing={{}: (7, {})} | custom-call | flops 5000000000 | bytes 3145728 | tf_op jit(solution)/shard_map/attention/pallas_call | solution.py:521
  62.3 1.8 %delta_out.3 = bf16[256,2048]{1,0:T(8,128)(2,1)} custom-call(s32[1]{0:T(128)S(6)} %sub.3.half_ref, bf16[256,1024]{1,0:T(8,128)(2,1)S(1)} %copy-done.3, f32[256,1024]{1,0:T(8,128)S(1)} %copy-done.2, bf16[1024,128]{1,0:T(8,128)(2,1)S(1)} %collective-permute-done.6.state_ref, bf16[256,2048]{1,0:T(8,128)(2,1)S(1)} %copy-done, ...), custom_call_target="tpu_custom_call", output_to_operand_aliasing={{}: (6, {})} | custom-call | flops 100000000 | bytes 3145728 | tf_op jit(solution)/shard_map/delta_out/pallas_call | solution.py:394
  (23 shorter events, 0.1 us)
Async XLA Ops:
  2.3 15.7 %collective-permute-start = (bf16[272,512]{1,0:T(8,128)(2,1)}, bf16[272,512]{1,0:T(8,128)(2,1)S(1)}, u32[]{:S(2)}, u32[]{:S(2)}) collective-permute-start(bf16[272,512]{1,0:T(8,128)(2,1)} %pack.1.rest_0_), channel_id=1, source_target_pairs={{0,2},{1,3},{2,4},{3,5},{4,6},{5,7},{8,10},{9,11},{10,12},{11,13},... | collective-permute-start | bytes 835592 | tf_op jit(solution)/shard_map/ppermute | solution.py:536
  5.6 15.7 %copy-start.9 = (bf16[256,1024]{1,0:T(8,128)(2,1)S(1)}, bf16[256,1024]{1,0:T(8,128)(2,1)}, u32[]{:S(2)}) copy-start(bf16[256,1024]{1,0:T(8,128)(2,1)} %q_ref.5) | copy-start | bytes 1572868
  5.6 15.7 %copy-start.11 = (f32[256,16]{0,1:T(8,128)S(1)}, f32[256,16]{0,1:T(8,128)}, u32[]{:S(2)}) copy-start(f32[256,16]{0,1:T(8,128)} %param.20) | copy-start | bytes 49156
  5.6 15.7 %copy-start.12 = (f32[256,16]{0,1:T(8,128)S(1)}, f32[256,16]{0,1:T(8,128)}, u32[]{:S(2)}) copy-start(f32[256,16]{0,1:T(8,128)} %param.21) | copy-start | bytes 49156
  17.0 4.3 %copy-start.5 = (s32[256]{0:T(256)S(1)}, s32[256]{0:T(256)}, u32[]{:S(2)}) copy-start(s32[256]{0:T(256)} %param.12) | copy-start | bytes 3076
  17.0 16.4 %copy-start.1 = (bf16[272,512]{1,0:T(8,128)(2,1)S(1)}, bf16[272,512]{1,0:T(8,128)(2,1)}, u32[]{:S(2)}) copy-start(bf16[272,512]{1,0:T(8,128)(2,1)} %pack.1.rest_0_) | copy-start | bytes 835588
  17.0 16.9 %collective-permute-start.2 = (bf16[1040,256]{1,0:T(8,128)(2,1)}, bf16[1040,256]{1,0:T(8,128)(2,1)S(1)}, u32[]{:S(2)}, u32[]{:S(2)}) collective-permute-start(bf16[1040,256]{1,0:T(8,128)(2,1)} %get-tuple-element.29), channel_id=1, source_target_pairs={{0,1},{1,0},{2,3},{3,2},{4,5},{5,4},{6,7},{7,6},{8,9},{9,8},{10,11... | collective-permute-start | bytes 1597448 | tf_op jit(solution)/shard_map/ppermute | solution.py:540
  18.1 15.3 %collective-permute-start.1 = (bf16[272,512]{1,0:T(8,128)(2,1)S(1)}, bf16[272,512]{1,0:T(8,128)(2,1)S(1)}, u32[]{:S(2)}, u32[]{:S(2)}) collective-permute-start(bf16[272,512]{1,0:T(8,128)(2,1)S(1)} %collective-permute-done.rest_1_), channel_id=1, source_target_pairs={{0,2},{1,3},{2,4},{3,5},{4,6},{5,7},{8,10},{9,11},{10,12},{11,13},... | collective-permute-start | bytes 835592 | tf_op jit(solution)/shard_map/ppermute | solution.py:536
  21.3 1.2 %copy-start.6 = (bf16[256,2048]{1,0:T(8,128)(2,1)S(1)}, bf16[256,2048]{1,0:T(8,128)(2,1)}, u32[]{:S(2)}) copy-start(bf16[256,2048]{1,0:T(8,128)(2,1)} %v_ref.3) | copy-start | bytes 3145732
  22.5 1.0 %copy-start.10 = (bf16[256,1024]{1,0:T(8,128)(2,1)S(1)}, bf16[256,1024]{1,0:T(8,128)(2,1)}, u32[]{:S(2)}) copy-start(bf16[256,1024]{1,0:T(8,128)(2,1)} %k_ref.3) | copy-start | bytes 1572868
  33.5 2.6 %collective-permute-start.4 = (bf16[2,272,512]{2,1,0:T(8,128)(2,1)S(1)}, bf16[2,272,512]{2,1,0:T(8,128)(2,1)S(1)}, u32[]{:S(2)}, u32[]{:S(2)}) collective-permute-start(bf16[2,272,512]{2,1,0:T(8,128)(2,1)S(1)} %pad_maximum_fusion), channel_id=1, source_target_pairs={{0,1},{1,0},{2,3},{3,2},{4,5},{5,4},{6,7},{7,6},{8,9},{9,8},{10,11... | collective-permute-start | bytes 1671176 | tf_op jit(solution)/shard_map/ppermute | solution.py:540
  34.2 9.7 %collective-permute-start.3 = (bf16[1040,128]{1,0:T(8,128)(2,1)S(1)}, bf16[1040,128]{1,0:T(8,128)(2,1)S(1)}, u32[]{:S(2)}, u32[]{:S(2)}) collective-permute-start(bf16[1040,128]{1,0:T(8,128)(2,1)S(1)} %get-tuple-element.33.add_ref), channel_id=1, source_target_pairs={{0,2},{1,3},{2,4},{3,5},{4,6},{5,7},{8,10},{9,11},{10,12},{11,13},... | collective-permute-start | bytes 798728 | tf_op jit(solution)/shard_map/ppermute | solution.py:536
  36.3 9.9 %copy-start.7 = (bf16[256,2048]{1,0:T(8,128)(2,1)S(1)}, bf16[256,2048]{1,0:T(8,128)(2,1)}, u32[]{:S(2)}) copy-start(bf16[256,2048]{1,0:T(8,128)(2,1)} %q_ref.7) | copy-start | bytes 3145732
  36.3 9.9 %copy-start.8 = (bf16[256,2048]{1,0:T(8,128)(2,1)S(1)}, bf16[256,2048]{1,0:T(8,128)(2,1)}, u32[]{:S(2)}) copy-start(bf16[256,2048]{1,0:T(8,128)(2,1)} %gate_ref.5) | copy-start | bytes 3145732
  44.2 8.8 %collective-permute-start.5 = (bf16[1040,128]{1,0:T(8,128)(2,1)S(1)}, bf16[1040,128]{1,0:T(8,128)(2,1)S(1)}, u32[]{:S(2)}, u32[]{:S(2)}) collective-permute-start(bf16[1040,128]{1,0:T(8,128)(2,1)S(1)} %relay.1), channel_id=1, source_target_pairs={{0,2},{1,3},{2,4},{3,5},{4,6},{5,7},{8,10},{9,11},{10,12},{11,13},... | collective-permute-start | bytes 798728 | tf_op jit(solution)/shard_map/ppermute | solution.py:536
  50.7 4.6 %copy-start = (bf16[256,2048]{1,0:T(8,128)(2,1)S(1)}, bf16[256,2048]{1,0:T(8,128)(2,1)}, u32[]{:S(2)}) copy-start(bf16[256,2048]{1,0:T(8,128)(2,1)} %gate_ref.7) | copy-start | bytes 3145732
  53.3 9.0 %collective-permute-start.6 = (bf16[1024,128]{1,0:T(8,128)(2,1)S(1)}, bf16[1024,128]{1,0:T(8,128)(2,1)S(1)}, u32[]{:S(2)}, u32[]{:S(2)}) collective-permute-start(bf16[1024,128]{1,0:T(8,128)(2,1)S(1)} %get-tuple-element.52), channel_id=1, source_target_pairs={{0,1},{1,0},{2,3},{3,2},{4,5},{5,4},{6,7},{7,6},{8,9},{9,8},{10,11... | collective-permute-start | bytes 786440 | tf_op jit(solution)/shard_map/ppermute | solution.py:540
  55.3 0.7 %copy-start.4 = (f32[128]{0:T(128)S(1)}, f32[128]{0:T(128)}, u32[]{:S(2)}) copy-start(f32[128]{0:T(128)} %param.23) | copy-start | bytes 1540
  57.7 4.5 %copy-start.2 = (f32[256,1024]{1,0:T(8,128)S(1)}, f32[256,1024]{1,0:T(8,128)}, u32[]{:S(2)}) copy-start(f32[256,1024]{1,0:T(8,128)} %get-tuple-element.50.inner_ref) | copy-start | bytes 3145732
  57.7 4.5 %copy-start.3 = (bf16[256,1024]{1,0:T(8,128)(2,1)S(1)}, bf16[256,1024]{1,0:T(8,128)(2,1)}, u32[]{:S(2)}) copy-start(bf16[256,1024]{1,0:T(8,128)(2,1)} %get-tuple-element.49.reach_ref) | copy-start | bytes 1572868

commit v4 on v3

--- a/solution.py
+++ b/solution.py
@@ -42,6 +42,8 @@
 
 BLOCK = 16
 MERGES = 3
+STRIP = 32
+FINE = 16
 
 
 def odd_rows(m, b):
@@ -76,7 +78,7 @@
         low = 0 if k < small - 1 else small
         at = (group * BLOCK + k)[low:]
         for i, z in enumerate(folded):
-            spread = jnp.take_along_axis(z[low:], at, axis=1)
+            spread = jnp.take_along_axis(z[low:], at, axis=1, mode="promise_in_bounds")
             x = xs[i]
             new = x[low:] + spread * x[k : k + 1]
             xs[i] = new if low == 0 else jnp.concatenate([x[:low], new], axis=0)
@@ -157,45 +159,62 @@
         0.0,
     )
     work = []
+    strips = [slice(i, i + STRIP) for i in range(0, rows, STRIP)]
     for kk in range(KEYS_PER_STEP):
         cols = slice(kk * DK, (kk + 1) * DK)
         k_raw = k_ref[:, cols]
         q_raw = q_ref[:, cols]
-        kf = k_raw.astype(f32)
-        qf = q_raw.astype(f32)
-        rk_col = lax.rsqrt(jnp.sum(kf * kf, axis=1, keepdims=True) + EPS)
-        rq_col = lax.rsqrt(jnp.sum(qf * qf, axis=1, keepdims=True) + EPS) * DK**-0.5
-        kt = jnp.transpose(kf)
+        kt = jnp.transpose(k_raw.astype(f32))
         rk_row = lax.rsqrt(jnp.sum(kt * kt, axis=0, keepdims=True) + EPS)
         ktb = kt.astype(bf16)
         upper = dot(jnp.concatenate([k_raw[:TILE], q_raw[:TILE]], axis=0), ktb[:, :TILE])
         lower = dot(jnp.concatenate([k_raw[TILE:], q_raw[TILE:]], axis=0), ktb)
-        gram1 = upper[:TILE] * rk_row[:, :TILE] * -rk_col[:TILE]
-        probe1 = upper[TILE:] * rk_row[:, :TILE] * rq_col[:TILE]
-        gram2 = lower[:TILE] * rk_row * -rk_col[TILE:]
-        probe2 = lower[TILE:] * rk_row * rq_col[TILE:]
-        kn = kf * rk_col
-        qn = qf * rq_col
-        for j in range(2):
-            h = 2 * kk + j
-            cc = columns[:, h : h + 1]
-            bt = columns[:, n + h : n + h + 1]
-            cr = crow_ref[pl.ds(step * heads + h, 1), :]
-            span1 = jnp.exp2(cc[:TILE] - cr[:, :TILE] + mask_ref[:TILE, :TILE])
-            span2 = jnp.exp2(cc[TILE:] - cr + mask_ref[TILE:, :])
-            d11 = span1 * bt[:TILE] * gram1
-            d2 = span2 * bt[TILE:] * gram2
-            p11 = (span1 * probe1).astype(bf16)
-            p2 = (span2 * probe2).astype(bf16)
-            entry = jnp.exp2(cc) * first
-            right = jnp.concatenate(
-                [bt * entry * kn, bt * v_ref[:, h * DV : (h + 1) * DV].astype(f32)], axis=1
-            )
-            kd = (kt * (rk_row * span2[TILE - 1 : TILE, :])).astype(bf16)
-            work.append(
-                dict(h=h, d=[d11, d2[:, TILE:]], d21=d2[:, :TILE].astype(bf16), p11=p11, p2=p2,
-                     kd=kd, right=right, reach=entry * qn, last=entry[rows - 1 : rows, :])
-            )
+        pair = [
+            dict(h=2 * kk + j, d=[], p=[], right=[], scaled=[],
+                 cr=crow_ref[pl.ds(step * heads + 2 * kk + j, 1), :])
+            for j in range(2)
+        ]
+        work += pair
+        for at in strips:
+            raw, start = (upper, at.start) if at.start < TILE else (lower, at.start - TILE)
+            wide = slice(0, raw.shape[1])
+            kf = k_raw[at].astype(f32)
+            qf = q_raw[at].astype(f32)
+            rk = lax.rsqrt(jnp.sum(kf * kf, axis=1, keepdims=True) + EPS)
+            rq = lax.rsqrt(jnp.sum(qf * qf, axis=1, keepdims=True) + EPS) * DK**-0.5
+            kn = kf * rk
+            qn = qf * rq
+            gram = raw[start : start + STRIP] * rk_row[:, wide] * -rk
+            probe = raw[TILE + start : TILE + start + STRIP] * rk_row[:, wide] * rq
+            for w in pair:
+                h = w["h"]
+                cc = jnp.broadcast_to(columns[at, h : h + 1], (STRIP, TILE))
+                bt = jnp.broadcast_to(columns[at, n + h : n + h + 1], (STRIP, TILE))
+                ccw, btw = cc, bt
+                if raw.shape[1] > TILE:
+                    ccw = jnp.concatenate([cc, cc], axis=1)
+                    btw = jnp.concatenate([bt, bt], axis=1)
+                span = jnp.exp2(ccw - w["cr"][:, wide] + mask_ref[at, wide])
+                w["d"].append(span * btw * gram)
+                w["p"].append((span * probe).astype(bf16))
+                entry = jnp.exp2(cc) * first[at]
+                value = v_ref[at, h * DV : (h + 1) * DV].astype(f32)
+                w["right"].append(
+                    jnp.concatenate([bt * entry * kn, bt * value], axis=1).astype(bf16)
+                )
+                w["scaled"].append((entry * qn).astype(bf16))
+                if at.stop == rows:
+                    w["last"] = entry[STRIP - 1 :]
+                    w["kd"] = (kt * (rk_row * span[STRIP - 1 :])).astype(bf16)
+        top = TILE // STRIP
+        for w in pair:
+            d11 = jnp.concatenate(w["d"][:top], axis=0)
+            d2 = jnp.concatenate(w["d"][top:], axis=0)
+            w["d"] = [d11, d2[:, TILE:]]
+            w["d21"] = d2[:, :TILE].astype(bf16)
+            w["p11"] = jnp.concatenate(w["p"][:top], axis=0)
+            w["p2"] = jnp.concatenate(w["p"][top:], axis=0)
+            w["right"] = jnp.concatenate(w["right"], axis=0)
     mats = [m for w in work for m in w["d"]]
     inverses = block_inverses(mats)
     mats = [m.astype(bf16) for m in mats]
@@ -215,20 +234,34 @@
         x1, x2 = inverses[2 * i], inverses[2 * i + 1]
         h = w["h"]
         r1 = w["right"][:TILE]
-        u1 = (r1 + dot(x1, r1.astype(bf16))).astype(bf16)
+        u1 = add_strips(r1, dot(x1, r1))
         after = dot(jnp.concatenate([w["d21"], w["p11"]], axis=0), u1)
-        r2 = w["right"][TILE:] + after[:TILE]
-        u2 = (r2 + dot(x2, r2.astype(bf16))).astype(bf16)
+        r2 = add_strips(w["right"][TILE:], after[:TILE])
+        u2 = add_strips(r2, dot(x2, r2))
         u = jnp.concatenate([u1, u2], axis=0)
         last = dot(jnp.concatenate([w["p2"], w["kd"]], axis=0), u)
-        pu = jnp.concatenate([after[TILE:], last[:TILE]], axis=0)
-        ma = last[TILE:]
-        at = pl.multiple_of((step * heads + h) * DK, DK)
-        map_add_ref[pl.ds(at, DK), :] = jnp.concatenate(
-            [w["last"] * eye - ma[:, :DK], ma[:, DK:]], axis=1
-        ).astype(bf16)
-        reach_ref[:, h * DK : (h + 1) * DK] = (w["reach"] - pu[:, :DK]).astype(bf16)
-        inner_ref[:, h * DV : (h + 1) * DV] = pu[:, DK:].astype(inner_ref.dtype)
+        for at, scaled in zip(strips, w["scaled"]):
+            pu = after[TILE + at.start :] if at.start < TILE else last[at.start - TILE :]
+            pu = pu[:STRIP]
+            reach_ref[at, h * DK : (h + 1) * DK] = (scaled.astype(f32) - pu[:, :DK]).astype(bf16)
+            inner_ref[at, h * DV : (h + 1) * DV] = pu[:, DK:].astype(inner_ref.dtype)
+        base = pl.multiple_of((step * heads + h) * DK, DK)
+        for start in range(0, DK, STRIP):
+            ma = last[TILE + start : TILE + start + STRIP]
+            kept = w["last"] * eye[start : start + STRIP]
+            map_add_ref[pl.ds(base + start, STRIP), :] = jnp.concatenate(
+                [kept - ma[:, :DK], ma[:, DK:]], axis=1
+            ).astype(bf16)
+
+
+def add_strips(a, b):
+    return jnp.concatenate(
+        [
+            (a[i : i + STRIP].astype(f32) + b[i : i + STRIP]).astype(bf16)
+            for i in range(0, a.shape[0], STRIP)
+        ],
+        axis=0,
+    )
 
 
 def delta_local(half, mib, seg_row, query, key, value, beta, decay):
@@ -362,11 +395,14 @@
     for h in range(state_ref.shape[0] // DK):
         cols = slice(h * DV, (h + 1) * DV)
         state = state_ref[h * DK : (h + 1) * DK]
-        out = inner_ref[:, cols].astype(f32) + dot(reach_ref[:, cols], state)
-        spread = lax.rsqrt(jnp.mean(out * out, axis=1, keepdims=True) + EPS)
-        gate = gate_ref[:, cols].astype(f32)
-        gate = gate * sigmoid(gate)
-        out_ref[:, cols] = (out * spread * gain * gate).astype(bf16)
+        carried = dot(reach_ref[:, cols], state)
+        for i in range(0, carried.shape[0], STRIP):
+            at = slice(i, i + STRIP)
+            out = inner_ref[at, cols].astype(f32) + carried[at]
+            spread = lax.rsqrt(jnp.mean(out * out, axis=1, keepdims=True) + EPS)
+            gate = gate_ref[at, cols].astype(f32)
+            gate = gate * sigmoid(gate)
+            out_ref[at, cols] = (out * spread * gain * gate).astype(bf16)
 
 
 def delta_out(half, reach, inner, state, gate, gain, partial_out=None):
@@ -491,13 +527,20 @@
             rotated = ((x * cos_ref[at] + swapped * sin_ref[at]) * scaling).astype(bf16)
             tail = q_ref[at, base + TILE : base + HEAD_WIDTH] * jnp.asarray(scaling, bf16)
             scores = dot(jnp.concatenate([rotated, tail], axis=1), kt_ref[:, keys])
-            scores = scores + mask_ref[at, keys]
-            best = jnp.max(scores, axis=1, keepdims=True)
-            weights = jnp.exp(scores - best)
-            total = jnp.sum(weights, axis=1, keepdims=True)
-            mixed = dot(weights.astype(bf16), v_ref[keys, :])
-            gate = sigmoid(gate_ref[at, base : base + HEAD_WIDTH].astype(f32))
-            out_ref[at, base : base + HEAD_WIDTH] = (mixed * (1.0 / total) * gate).astype(bf16)
+            weights = []
+            totals = []
+            for i in range(0, TILE, FINE):
+                strip = scores[i : i + FINE] + mask_ref[first + i : first + i + FINE, keys]
+                strip = jnp.exp(strip - jnp.max(strip, axis=1, keepdims=True))
+                totals.append(1.0 / jnp.sum(strip, axis=1, keepdims=True))
+                weights.append(strip.astype(bf16))
+            mixed = dot(jnp.concatenate(weights, axis=0), v_ref[keys, :])
+            for i, inverse in zip(range(0, TILE, FINE), totals):
+                rows_at = slice(first + i, first + i + FINE)
+                gate = sigmoid(gate_ref[rows_at, base : base + HEAD_WIDTH].astype(f32))
+                out_ref[rows_at, base : base + HEAD_WIDTH] = (
+                    mixed[i : i + FINE] * inverse * gate
+                ).astype(bf16)
 
 
 def attention_half(part, window_arrays, query, gate, partial_out=None):

time: 64.4 us -> 64.6 us (level)
  no operation moved by 1% of the time
where the time goes in v4:
time: 64.6 us; the launch traced here: 64.2 us
  Pallas kernels  37.5 us (58%)
  starting transfers between devices  13.6 us (21%)
  waiting for transfers between devices  9.05 us (14%)
  local copies, waits for them, and re-layouts  3.03 us (5%)
  between operations  0.87 us (1%)
    pallas_call x2, Pallas kernels, delta_local(): pl.pallas_call(delta_local_kernel, grid_spec=pltpu.PrefetchScalarGridSpec...  21.4 us
    ppermute x4, starting transfers between devices, up_chip(): return lax.ppermute(value, 'ctx', [(i, i + 2) for i in range(ranks - 2)])  10.2 us
    ppermute x4, waiting for transfers between devices, up_chip(): return lax.ppermute(value, 'ctx', [(i, i + 2) for i in range(ranks - 2)])  9.04 us
    pallas_call x2, Pallas kernels, attention_half(): pl.pallas_call(attention_kernel, grid=(steps,), in_specs=in_specs, out_sp...  9.03 us
    pallas_call x2, Pallas kernels, delta_out(): pl.pallas_call(delta_out_kernel, grid_spec=pltpu.PrefetchScalarGridSpec(n...  3.55 us
    pallas_call x5, Pallas kernels, small_call(): pl.pallas_call(kernel, in_specs=[SMEM] * scalars + [VMEM] * (len(args) -...  3.54 us
    ppermute x3, starting transfers between devices, swap_cores(): return lax.ppermute(value, 'ctx', [(i, i ^ 1) for i in range(ranks)])  3.39 us
    unnamed x26, local copies, waits for them, and re-layouts  2.96 us
  transfers between devices with their start and end apart: 7, of which 2 were waited for; matrix products, arithmetic and copies ran while one was open for 0% of the time, Pallas kernels for 52%

profile of v4, /device:TPU:9, one launch (start us, length us, event | category | flops | bytes accessed | tf_op | source)
XLA Modules:
  0.0 64.2 jit_solution(16130128876062619253)
XLA Ops:
  0.6 1.7 %pack.1.rest_0_ = bf16[272,512]{1,0:T(8,128)(2,1)} custom-call(s32[1,256]{1,0:T(1,128)} %bitcast.11, bf16[256,256]{1,0:T(8,128)(2,1)} %key_ref.1, bf16[256,256]{1,0:T(8,128)(2,1)} %value_ref.1), custom_call_target="tpu_custom_call" | custom-call | flops 100000000 | bytes 1048576 | tf_op jit(solution)/shard_map/pack/pallas_call | solution.py:381
  2.3 3.2 %collective-permute-start = (bf16[272,512]{1,0:T(8,128)(2,1)}, bf16[272,512]{1,0:T(8,128)(2,1)S(1)}, u32[]{:S(2)}, u32[]{:S(2)}) collective-permute-start(bf16[272,512]{1,0:T(8,128)(2,1)} %pack.1.rest_0_), channel_id=1, source_target_pairs={{0,2},{1,3},{2,4},{3,5},{4,6},{5,7},{8,10},{9,11},{10,12},{11,13},... | collective-permute-start | bytes 835592 | tf_op jit(solution)/shard_map/ppermute | solution.py:579
  5.6 0.0 copy-start.9
  5.6 0.0 copy-start.11
  5.6 0.0 copy-start.12
  5.6 11.5 %delta_local.2 = (bf16[1040,256]{1,0:T(8,128)(2,1)}, bf16[256,1024]{1,0:T(8,128)(2,1)}, f32[256,1024]{1,0:T(8,128)}) custom-call(s32[1]{0:T(128)S(6)} %sub.3.half_ref, s32[1,256]{1,0:T(1,128)} %bitcast.12, bf16[256,1024]{1,0:T(8,128)(2,1)} %q_ref.5, bf16[256,1024]{1,0:T(8,128)(2,1)} %k_ref.3, bf16[256,2048]{1,0:T(8,128)(2,1)} %v_ref.3, f32[16,256]{1,0:T(8,128)} %bitcast.14, ...), custom_call_target="tpu_custom_call" | custom-call | flops 6000000000 | bytes 3145728 | tf_op jit(solution)/shard_map/delta_local/pallas_call | solution.py:282
  17.1 0.0 copy-start.5
  17.1 0.0 copy-start.1
  17.1 1.0 %collective-permute-start.2 = (bf16[1040,256]{1,0:T(8,128)(2,1)}, bf16[1040,256]{1,0:T(8,128)(2,1)S(1)}, u32[]{:S(2)}, u32[]{:S(2)}) collective-permute-start(bf16[1040,256]{1,0:T(8,128)(2,1)} %get-tuple-element.29), channel_id=1, source_target_pairs={{0,1},{1,0},{2,3},{3,2},{4,5},{5,4},{6,7},{7,6},{8,9},{9,8},{10,11... | collective-permute-start | bytes 1597448 | tf_op jit(solution)/shard_map/ppermute | solution.py:583
  18.2 3.2 %collective-permute-start.1 = (bf16[272,512]{1,0:T(8,128)(2,1)S(1)}, bf16[272,512]{1,0:T(8,128)(2,1)S(1)}, u32[]{:S(2)}, u32[]{:S(2)}) collective-permute-start(bf16[272,512]{1,0:T(8,128)(2,1)S(1)} %collective-permute-done.rest_1_), channel_id=1, source_target_pairs={{0,2},{1,3},{2,4},{3,5},{4,6},{5,7},{8,10},{9,11},{10,12},{11,13},... | collective-permute-start | bytes 835592 | tf_op jit(solution)/shard_map/ppermute | solution.py:579
  21.4 0.0 copy-start.6
  21.4 1.2 %copy-done.6 = bf16[256,2048]{1,0:T(8,128)(2,1)S(1)} copy-done((bf16[256,2048]{1,0:T(8,128)(2,1)S(1)}, bf16[256,2048]{1,0:T(8,128)(2,1)}, u32[]{:S(2)}) %copy-start.6) | copy-done | bytes 1048600
  22.6 1.0 %copy-done.10 = bf16[256,1024]{1,0:T(8,128)(2,1)S(1)} copy-done((bf16[256,1024]{1,0:T(8,128)(2,1)S(1)}, bf16[256,1024]{1,0:T(8,128)(2,1)}, u32[]{:S(2)}) %copy-start.10) | copy-done | bytes 524312
  23.7 9.9 %delta_local.3 = (bf16[1040,256]{1,0:T(8,128)(2,1)S(1)}, bf16[256,1024]{1,0:T(8,128)(2,1)S(1)}, f32[256,1024]{1,0:T(8,128)S(1)}) custom-call(s32[1]{0:T(128)} %bitcast.half_ref.core_ref, s32[1,256]{1,0:T(1,128)S(1)} %bitcast.13, bf16[256,1024]{1,0:T(8,128)(2,1)S(1)} %copy-done.9, bf16[256,1024]{1,0:T(8,128)(2,1)S(1)} %copy-done.10, ...), custom_call_target="tpu_custom_call" | custom-call | flops 6000000000 | bytes 3145728 | tf_op jit(solution)/shard_map/delta_local/pallas_call | solution.py:282
  33.6 0.1 select_bitcast_fusion.1
  33.7 0.1 pad_maximum_fusion
  33.7 0.4 collective-permute-start.4
  34.1 0.3 compose.1
  34.4 1.9 %collective-permute-start.3 = (bf16[1040,128]{1,0:T(8,128)(2,1)S(1)}, bf16[1040,128]{1,0:T(8,128)(2,1)S(1)}, u32[]{:S(2)}, u32[]{:S(2)}) collective-permute-start(bf16[1040,128]{1,0:T(8,128)(2,1)S(1)} %get-tuple-element.33.add_ref), channel_id=1, source_target_pairs={{0,2},{1,3},{2,4},{3,5},{4,6},{5,7},{8,10},{9,11},{10,12},{11,13},... | collective-permute-start | bytes 798728 | tf_op jit(solution)/shard_map/ppermute | solution.py:579
  36.4 0.1 broadcast_in_dim.2.freq_ref
  36.5 0.9 %window.1 = (bf16[256,1280]{1,0:T(8,128)(2,1)S(1)}, bf16[1280,256]{1,0:T(8,128)(2,1)S(1)}, f32[1,1280]{1,0:T(1,128)S(1)}, f32[256,128]{1,0:T(8,128)S(1)}, f32[256,128]{1,0:T(8,128)S(1)}) custom-call(f32[32,128]{1,0:T(8,128)S(1)} %broadcast_in_dim.2.freq_ref, bf16[272,512]{1,0:T(8,128)(2,1)S(1)} %copy-done.1, ...), custom_call_target="tpu_custom_call" | custom-call | flops 100000000 | bytes 1048576 | tf_op jit(solution)/shard_map/window/pallas_call | solution.py:381
  37.4 6.7 %collective-permute-done.3.state_ref = bf16[1040,128]{1,0:T(8,128)(2,1)S(1)} collective-permute-done((bf16[1040,128]{1,0:T(8,128)(2,1)S(1)}, bf16[1040,128]{1,0:T(8,128)(2,1)S(1)}, u32[]{:S(2)}, u32[]{:S(2)}) %collective-permute-start.3) | collective-permute-done | bytes 266272 | tf_op jit(solution)/shard_map/ppermute | solution.py:579
  44.1 0.2 relay.1
  44.4 1.9 %collective-permute-start.5 = (bf16[1040,128]{1,0:T(8,128)(2,1)S(1)}, bf16[1040,128]{1,0:T(8,128)(2,1)S(1)}, u32[]{:S(2)}, u32[]{:S(2)}) collective-permute-start(bf16[1040,128]{1,0:T(8,128)(2,1)S(1)} %relay.1), channel_id=1, source_target_pairs={{0,2},{1,3},{2,4},{3,5},{4,6},{5,7},{8,10},{9,11},{10,12},{11,13},... | collective-permute-start | bytes 798728 | tf_op jit(solution)/shard_map/ppermute | solution.py:579
  46.3 4.5 %attention.2.rest_0_ = bf16[256,2048]{1,0:T(8,128)(2,1)} custom-call(f32[1,1280]{1,0:T(1,128)S(1)} %get-tuple-element.41.ids_ref, f32[256,128]{1,0:T(8,128)S(1)} %get-tuple-element.42.cos_ref, f32[256,128]{1,0:T(8,128)S(1)} %get-tuple-element.43.sin_ref, bf16[256,1280]{1,0:T(8,128)(2,1)S(1)} %get-tuple-element.44.kt_ref, ...), custom_call_target="tpu_custom_call" | custom-call | flops 5000000000 | bytes 3145728 | tf_op jit(solution)/shard_map/attention/pallas_call | solution.py:564
  50.8 2.3 %collective-permute-done.5.state_ref = bf16[1040,128]{1,0:T(8,128)(2,1)S(1)} collective-permute-done((bf16[1040,128]{1,0:T(8,128)(2,1)S(1)}, bf16[1040,128]{1,0:T(8,128)(2,1)S(1)}, u32[]{:S(2)}, u32[]{:S(2)}) %collective-permute-start.5) | collective-permute-done | bytes 266272 | tf_op jit(solution)/shard_map/ppermute | solution.py:579
  53.1 0.4 arrive.1
  53.5 2.0 %collective-permute-start.6 = (bf16[1024,128]{1,0:T(8,128)(2,1)S(1)}, bf16[1024,128]{1,0:T(8,128)(2,1)S(1)}, u32[]{:S(2)}, u32[]{:S(2)}) collective-permute-start(bf16[1024,128]{1,0:T(8,128)(2,1)S(1)} %get-tuple-element.52), channel_id=1, source_target_pairs={{0,1},{1,0},{2,3},{3,2},{4,5},{5,4},{6,7},{7,6},{8,9},{9,8},{10,11... | collective-permute-start | bytes 786440 | tf_op jit(solution)/shard_map/ppermute | solution.py:583
  55.5 0.7 %copy-done.4 = f32[128]{0:T(128)S(1)} copy-done((f32[128]{0:T(128)S(1)}, f32[128]{0:T(128)}, u32[]{:S(2)}) %copy-start.4) | copy-done | bytes 536
  56.1 1.8 %delta_out.2.rest_0_ = bf16[256,2048]{1,0:T(8,128)(2,1)} custom-call(s32[1]{0:T(128)} %bitcast.half_ref.core_ref, bf16[256,1024]{1,0:T(8,128)(2,1)S(1)} %get-tuple-element.53.reach_ref, f32[256,1024]{1,0:T(8,128)S(1)} %get-tuple-element.54.inner_ref, bf16[1024,128]{1,0:T(8,128)(2,1)S(1)} %get-tuple-element.55.state_ref, bf16[256,2048]{1,0:T(8,128)(2,1)S(1)} %copy-done, ...), custom_call_target="tpu_custom_call" | custom-call | flops 100000000 | bytes 3145728 | tf_op jit(solution)/shard_map/delta_out/pallas_call | solution.py:430
  57.9 4.5 %attention.3 = bf16[256,2048]{1,0:T(8,128)(2,1)} custom-call(f32[1,1280]{1,0:T(1,128)S(1)} %get-tuple-element.41.ids_ref, f32[256,128]{1,0:T(8,128)S(1)} %get-tuple-element.42.cos_ref, f32[256,128]{1,0:T(8,128)S(1)} %get-tuple-element.43.sin_ref, bf16[256,1280]{1,0:T(8,128)(2,1)S(1)} %get-tuple-element.44.kt_ref, ...), custom_call_target="tpu_custom_call", output_to_operand_aliasing={{}: (7, {})} | custom-call | flops 5000000000 | bytes 3145728 | tf_op jit(solution)/shard_map/attention/pallas_call | solution.py:564
  62.4 1.8 %delta_out.3 = bf16[256,2048]{1,0:T(8,128)(2,1)} custom-call(s32[1]{0:T(128)S(6)} %sub.3.half_ref, bf16[256,1024]{1,0:T(8,128)(2,1)S(1)} %copy-done.3, f32[256,1024]{1,0:T(8,128)S(1)} %copy-done.2, bf16[1024,128]{1,0:T(8,128)(2,1)S(1)} %collective-permute-done.6.state_ref, bf16[256,2048]{1,0:T(8,128)(2,1)S(1)} %copy-done, ...), custom_call_target="tpu_custom_call", output_to_operand_aliasing={{}: (6, {})} | custom-call | flops 100000000 | bytes 3145728 | tf_op jit(solution)/shard_map/delta_out/pallas_call | solution.py:430
  (23 shorter events, 0.1 us)
Async XLA Ops:
  2.3 15.8 %collective-permute-start = (bf16[272,512]{1,0:T(8,128)(2,1)}, bf16[272,512]{1,0:T(8,128)(2,1)S(1)}, u32[]{:S(2)}, u32[]{:S(2)}) collective-permute-start(bf16[272,512]{1,0:T(8,128)(2,1)} %pack.1.rest_0_), channel_id=1, source_target_pairs={{0,2},{1,3},{2,4},{3,5},{4,6},{5,7},{8,10},{9,11},{10,12},{11,13},... | collective-permute-start | bytes 835592 | tf_op jit(solution)/shard_map/ppermute | solution.py:579
  5.6 15.8 %copy-start.9 = (bf16[256,1024]{1,0:T(8,128)(2,1)S(1)}, bf16[256,1024]{1,0:T(8,128)(2,1)}, u32[]{:S(2)}) copy-start(bf16[256,1024]{1,0:T(8,128)(2,1)} %q_ref.5) | copy-start | bytes 1572868
  5.6 15.8 %copy-start.11 = (f32[256,16]{0,1:T(8,128)S(1)}, f32[256,16]{0,1:T(8,128)}, u32[]{:S(2)}) copy-start(f32[256,16]{0,1:T(8,128)} %param.20) | copy-start | bytes 49156
  5.6 15.8 %copy-start.12 = (f32[256,16]{0,1:T(8,128)S(1)}, f32[256,16]{0,1:T(8,128)}, u32[]{:S(2)}) copy-start(f32[256,16]{0,1:T(8,128)} %param.21) | copy-start | bytes 49156
  17.1 4.3 %copy-start.5 = (s32[256]{0:T(256)S(1)}, s32[256]{0:T(256)}, u32[]{:S(2)}) copy-start(s32[256]{0:T(256)} %param.12) | copy-start | bytes 3076
  17.1 16.5 %copy-start.1 = (bf16[272,512]{1,0:T(8,128)(2,1)S(1)}, bf16[272,512]{1,0:T(8,128)(2,1)}, u32[]{:S(2)}) copy-start(bf16[272,512]{1,0:T(8,128)(2,1)} %pack.1.rest_0_) | copy-start | bytes 835588
  17.1 17.0 %collective-permute-start.2 = (bf16[1040,256]{1,0:T(8,128)(2,1)}, bf16[1040,256]{1,0:T(8,128)(2,1)S(1)}, u32[]{:S(2)}, u32[]{:S(2)}) collective-permute-start(bf16[1040,256]{1,0:T(8,128)(2,1)} %get-tuple-element.29), channel_id=1, source_target_pairs={{0,1},{1,0},{2,3},{3,2},{4,5},{5,4},{6,7},{7,6},{8,9},{9,8},{10,11... | collective-permute-start | bytes 1597448 | tf_op jit(solution)/shard_map/ppermute | solution.py:583
  18.2 15.4 %collective-permute-start.1 = (bf16[272,512]{1,0:T(8,128)(2,1)S(1)}, bf16[272,512]{1,0:T(8,128)(2,1)S(1)}, u32[]{:S(2)}, u32[]{:S(2)}) collective-permute-start(bf16[272,512]{1,0:T(8,128)(2,1)S(1)} %collective-permute-done.rest_1_), channel_id=1, source_target_pairs={{0,2},{1,3},{2,4},{3,5},{4,6},{5,7},{8,10},{9,11},{10,12},{11,13},... | collective-permute-start | bytes 835592 | tf_op jit(solution)/shard_map/ppermute | solution.py:579
  21.4 1.2 %copy-start.6 = (bf16[256,2048]{1,0:T(8,128)(2,1)S(1)}, bf16[256,2048]{1,0:T(8,128)(2,1)}, u32[]{:S(2)}) copy-start(bf16[256,2048]{1,0:T(8,128)(2,1)} %v_ref.3) | copy-start | bytes 3145732
  22.6 1.0 %copy-start.10 = (bf16[256,1024]{1,0:T(8,128)(2,1)S(1)}, bf16[256,1024]{1,0:T(8,128)(2,1)}, u32[]{:S(2)}) copy-start(bf16[256,1024]{1,0:T(8,128)(2,1)} %k_ref.3) | copy-start | bytes 1572868
  33.7 2.6 %collective-permute-start.4 = (bf16[2,272,512]{2,1,0:T(8,128)(2,1)S(1)}, bf16[2,272,512]{2,1,0:T(8,128)(2,1)S(1)}, u32[]{:S(2)}, u32[]{:S(2)}) collective-permute-start(bf16[2,272,512]{2,1,0:T(8,128)(2,1)S(1)} %pad_maximum_fusion), channel_id=1, source_target_pairs={{0,1},{1,0},{2,3},{3,2},{4,5},{5,4},{6,7},{7,6},{8,9},{9,8},{10,11... | collective-permute-start | bytes 1671176 | tf_op jit(solution)/shard_map/ppermute | solution.py:583
  34.4 9.7 %collective-permute-start.3 = (bf16[1040,128]{1,0:T(8,128)(2,1)S(1)}, bf16[1040,128]{1,0:T(8,128)(2,1)S(1)}, u32[]{:S(2)}, u32[]{:S(2)}) collective-permute-start(bf16[1040,128]{1,0:T(8,128)(2,1)S(1)} %get-tuple-element.33.add_ref), channel_id=1, source_target_pairs={{0,2},{1,3},{2,4},{3,5},{4,6},{5,7},{8,10},{9,11},{10,12},{11,13},... | collective-permute-start | bytes 798728 | tf_op jit(solution)/shard_map/ppermute | solution.py:579
  36.5 9.8 %copy-start.7 = (bf16[256,2048]{1,0:T(8,128)(2,1)S(1)}, bf16[256,2048]{1,0:T(8,128)(2,1)}, u32[]{:S(2)}) copy-start(bf16[256,2048]{1,0:T(8,128)(2,1)} %q_ref.7) | copy-start | bytes 3145732
  36.5 9.9 %copy-start.8 = (bf16[256,2048]{1,0:T(8,128)(2,1)S(1)}, bf16[256,2048]{1,0:T(8,128)(2,1)}, u32[]{:S(2)}) copy-start(bf16[256,2048]{1,0:T(8,128)(2,1)} %gate_ref.5) | copy-start | bytes 3145732
  44.4 8.8 %collective-permute-start.5 = (bf16[1040,128]{1,0:T(8,128)(2,1)S(1)}, bf16[1040,128]{1,0:T(8,128)(2,1)S(1)}, u32[]{:S(2)}, u32[]{:S(2)}) collective-permute-start(bf16[1040,128]{1,0:T(8,128)(2,1)S(1)} %relay.1), channel_id=1, source_target_pairs={{0,2},{1,3},{2,4},{3,5},{4,6},{5,7},{8,10},{9,11},{10,12},{11,13},... | collective-permute-start | bytes 798728 | tf_op jit(solution)/shard_map/ppermute | solution.py:579
  50.8 4.7 %copy-start = (bf16[256,2048]{1,0:T(8,128)(2,1)S(1)}, bf16[256,2048]{1,0:T(8,128)(2,1)}, u32[]{:S(2)}) copy-start(bf16[256,2048]{1,0:T(8,128)(2,1)} %gate_ref.7) | copy-start | bytes 3145732
  53.5 8.9 %collective-permute-start.6 = (bf16[1024,128]{1,0:T(8,128)(2,1)S(1)}, bf16[1024,128]{1,0:T(8,128)(2,1)S(1)}, u32[]{:S(2)}, u32[]{:S(2)}) collective-permute-start(bf16[1024,128]{1,0:T(8,128)(2,1)S(1)} %get-tuple-element.52), channel_id=1, source_target_pairs={{0,1},{1,0},{2,3},{3,2},{4,5},{5,4},{6,7},{7,6},{8,9},{9,8},{10,11... | collective-permute-start | bytes 786440 | tf_op jit(solution)/shard_map/ppermute | solution.py:583
  55.5 0.7 %copy-start.4 = (f32[128]{0:T(128)S(1)}, f32[128]{0:T(128)}, u32[]{:S(2)}) copy-start(f32[128]{0:T(128)} %param.23) | copy-start | bytes 1540
  57.9 4.5 %copy-start.2 = (f32[256,1024]{1,0:T(8,128)S(1)}, f32[256,1024]{1,0:T(8,128)}, u32[]{:S(2)}) copy-start(f32[256,1024]{1,0:T(8,128)} %get-tuple-element.50.inner_ref) | copy-start | bytes 3145732
  57.9 4.5 %copy-start.3 = (bf16[256,1024]{1,0:T(8,128)(2,1)S(1)}, bf16[256,1024]{1,0:T(8,128)(2,1)}, u32[]{:S(2)}) copy-start(bf16[256,1024]{1,0:T(8,128)(2,1)} %get-tuple-element.49.reach_ref) | copy-start | bytes 1572868

commit v5 on v4

--- a/solution.py
+++ b/solution.py
@@ -17,7 +17,7 @@
 MASKED = -1e30
 EPS = 1e-6
 TILE = 128
-KEYS_PER_STEP = 1
+KEYS_PER_STEP = 4
 MIB = 1024 * 1024
 
 f32 = jnp.float32
@@ -515,38 +515,41 @@
     scaling = HEAD_WIDTH**-0.5
     lane = lax.broadcasted_iota(jnp.int32, (TILE, TILE), 1)
     reach = window - rows + TILE
-    for h in range(q_ref.shape[1] // HEAD_WIDTH):
-        base = h * HEAD_WIDTH
-        for first in range(0, rows, TILE):
-            at = slice(first, first + TILE)
-            keys = slice(first, first + reach)
+    heads = q_ref.shape[1] // HEAD_WIDTH
+    for first in range(0, rows, TILE):
+        at = slice(first, first + TILE)
+        keys = slice(first, first + reach)
+        queries = []
+        for h in range(heads):
+            base = h * HEAD_WIDTH
             x = q_ref[at, base : base + TILE].astype(f32)
             swapped = jnp.where(
                 lane < half, pltpu.roll(x, TILE - half, 1), pltpu.roll(x, half, 1)
             )
             rotated = ((x * cos_ref[at] + swapped * sin_ref[at]) * scaling).astype(bf16)
             tail = q_ref[at, base + TILE : base + HEAD_WIDTH] * jnp.asarray(scaling, bf16)
-            scores = dot(jnp.concatenate([rotated, tail], axis=1), kt_ref[:, keys])
-            weights = []
-            totals = []
-            for i in range(0, TILE, FINE):
-                strip = scores[i : i + FINE] + mask_ref[first + i : first + i + FINE, keys]
-                strip = jnp.exp(strip - jnp.max(strip, axis=1, keepdims=True))
-                totals.append(1.0 / jnp.sum(strip, axis=1, keepdims=True))
-                weights.append(strip.astype(bf16))
-            mixed = dot(jnp.concatenate(weights, axis=0), v_ref[keys, :])
-            for i, inverse in zip(range(0, TILE, FINE), totals):
-                rows_at = slice(first + i, first + i + FINE)
-                gate = sigmoid(gate_ref[rows_at, base : base + HEAD_WIDTH].astype(f32))
-                out_ref[rows_at, base : base + HEAD_WIDTH] = (
-                    mixed[i : i + FINE] * inverse * gate
-                ).astype(bf16)
+            queries.append(jnp.concatenate([rotated, tail], axis=1))
+        scores = dot(jnp.concatenate(queries, axis=0), kt_ref[:, keys])
+        weights = []
+        totals = []
+        for i in range(0, heads * TILE, FINE):
+            row = first + i % TILE
+            strip = scores[i : i + FINE] + mask_ref[row : row + FINE, keys]
+            strip = jnp.exp(strip - jnp.max(strip, axis=1, keepdims=True))
+            totals.append(1.0 / jnp.sum(strip, axis=1, keepdims=True))
+            weights.append(strip.astype(bf16))
+        mixed = dot(jnp.concatenate(weights, axis=0), v_ref[keys, :])
+        for i, inverse in zip(range(0, heads * TILE, FINE), totals):
+            rows_at = slice(first + i % TILE, first + i % TILE + FINE)
+            cols = slice(i // TILE * HEAD_WIDTH, (i // TILE + 1) * HEAD_WIDTH)
+            gate = sigmoid(gate_ref[rows_at, cols].astype(f32))
+            out_ref[rows_at, cols] = (mixed[i : i + FINE] * inverse * gate).astype(bf16)
 
 
 def attention_half(part, window_arrays, query, gate, partial_out=None):
     rows = query.shape[0]
     window = window_arrays[0].shape[1]
-    heads = 2
+    heads = 4
     width = heads * HEAD_WIDTH
     steps = query.shape[1] // width // 2
 
@@ -569,7 +572,7 @@
         out_shape=jax.ShapeDtypeStruct(query.shape, bf16),
         scratch_shapes=[pltpu.VMEM((rows, window), f32)],
         input_output_aliases=aliases,
-        compiler_params=params(),
+        compiler_params=params(28),
         cost_estimate=cost(5 * 10**9, 3 * 2**20, 10**6),
         name="attention",
     )(*args)
@@ -634,7 +637,7 @@
     same = [nearest]
     for _ in range(hops - 1):
         same.append(up_chip(same[-1], ranks))
-    keep_ma, keep_reach, keep_inner = local(keep_half, 20)
+    keep_ma, keep_reach, keep_inner = local(keep_half, 60)
     same, keep_ma = lax.optimization_barrier((same, keep_ma))
     chain = [own, *same]
     other = swap_cores(

time: 64.6 us -> 56.5 us (0.87)
  Pallas kernels: 37.5 us -> 31 us
  local copies, waits for them, and re-layouts: 3.03 us -> 1.22 us
    pallas_call x2, Pallas kernels: 21.4 us -> 16.2 us  [delta_local(): pl.pallas_call(delta_local_kernel, grid_spec=pltpu.PrefetchScalarGridSpec...]
    unnamed x26 -> x20, local copies, waits for them, and re-layouts: 2.96 us -> 1.15 us
    pallas_call x2, Pallas kernels: 9.03 us -> 7.71 us  [attention_half(): pl.pallas_call(attention_kernel, grid=(steps,), in_specs=in_specs, out_sp...]
  transfers between devices with their start and end apart: 7 -> 7, of which waited for: 2 -> 2; matrix products, arithmetic and copies ran while one was open for 0% -> 0% of each run, Pallas kernels for 52% -> 48%
where the time goes in v5:
time: 56.5 us; the launch traced here: 56.2 us
  Pallas kernels  31 us (55%)
  starting transfers between devices  14.2 us (25%)
  waiting for transfers between devices  8.94 us (16%)
  local copies, waits for them, and re-layouts  1.22 us (2%)
  between operations  0.79 us (1%)
    pallas_call x2, Pallas kernels, delta_local(): pl.pallas_call(delta_local_kernel, grid_spec=pltpu.PrefetchScalarGridSpec...  16.2 us
    ppermute x4, starting transfers between devices, up_chip(): return lax.ppermute(value, 'ctx', [(i, i + 2) for i in range(ranks - 2)])  10.4 us
    ppermute x4, waiting for transfers between devices, up_chip(): return lax.ppermute(value, 'ctx', [(i, i + 2) for i in range(ranks - 2)])  8.93 us
    pallas_call x2, Pallas kernels, attention_half(): pl.pallas_call(attention_kernel, grid=(steps,), in_specs=in_specs, out_sp...  7.71 us
    ppermute x3, starting transfers between devices, swap_cores(): return lax.ppermute(value, 'ctx', [(i, i ^ 1) for i in range(ranks)])  3.71 us
    pallas_call x5, Pallas kernels, small_call(): pl.pallas_call(kernel, in_specs=[SMEM] * scalars + [VMEM] * (len(args) -...  3.57 us
    pallas_call x2, Pallas kernels, delta_out(): pl.pallas_call(delta_out_kernel, grid_spec=pltpu.PrefetchScalarGridSpec(n...  3.54 us
    unnamed x20, local copies, waits for them, and re-layouts  1.15 us
  transfers between devices with their start and end apart: 7, of which 2 were waited for; matrix products, arithmetic and copies ran while one was open for 0% of the time, Pallas kernels for 48%

profile of v5, /device:TPU:9, one launch (start us, length us, event | category | flops | bytes accessed | tf_op | source)
XLA Modules:
  0.0 56.2 jit_solution(8099955465372677277)
XLA Ops:
  0.6 1.7 %pack.1.rest_0_ = bf16[272,512]{1,0:T(8,128)(2,1)} custom-call(s32[1,256]{1,0:T(1,128)} %bitcast.11, bf16[256,256]{1,0:T(8,128)(2,1)} %key_ref.1, bf16[256,256]{1,0:T(8,128)(2,1)} %value_ref.1), custom_call_target="tpu_custom_call" | custom-call | flops 100000000 | bytes 1048576 | tf_op jit(solution)/shard_map/pack/pallas_call | solution.py:381
  2.4 3.2 %collective-permute-start = (bf16[272,512]{1,0:T(8,128)(2,1)}, bf16[272,512]{1,0:T(8,128)(2,1)S(1)}, u32[]{:S(2)}, u32[]{:S(2)}) collective-permute-start(bf16[272,512]{1,0:T(8,128)(2,1)} %pack.1.rest_0_), channel_id=1, source_target_pairs={{0,2},{1,3},{2,4},{3,5},{4,6},{5,7},{8,10},{9,11},{10,12},{11,13},... | collective-permute-start | bytes 835592 | tf_op jit(solution)/shard_map/ppermute | solution.py:582
  5.6 8.1 %delta_local.2 = (bf16[1040,256]{1,0:T(8,128)(2,1)}, bf16[256,1024]{1,0:T(8,128)(2,1)}, f32[256,1024]{1,0:T(8,128)}) custom-call(s32[1]{0:T(128)S(6)} %sub.3.half_ref, s32[1,256]{1,0:T(1,128)} %bitcast.12, bf16[256,1024]{1,0:T(8,128)(2,1)} %q_ref.5, bf16[256,1024]{1,0:T(8,128)(2,1)} %k_ref.3, bf16[256,2048]{1,0:T(8,128)(2,1)} %v_ref.3, f32[16,256]{1,0:T(8,128)} %bitcast.14, ...), custom_call_target="tpu_custom_call" | custom-call | flops 6000000000 | bytes 3145728 | tf_op jit(solution)/shard_map/delta_local/pallas_call | solution.py:282
  13.6 1.0 %collective-permute-start.2 = (bf16[1040,256]{1,0:T(8,128)(2,1)}, bf16[1040,256]{1,0:T(8,128)(2,1)S(1)}, u32[]{:S(2)}, u32[]{:S(2)}) collective-permute-start(bf16[1040,256]{1,0:T(8,128)(2,1)} %get-tuple-element.29), channel_id=1, source_target_pairs={{0,1},{1,0},{2,3},{3,2},{4,5},{5,4},{6,7},{7,6},{8,9},{9,8},{10,11... | collective-permute-start | bytes 1597448 | tf_op jit(solution)/shard_map/ppermute | solution.py:586
  14.6 0.0 collective-permute-done.rest_1_
  14.6 3.2 %collective-permute-start.1 = (bf16[272,512]{1,0:T(8,128)(2,1)S(1)}, bf16[272,512]{1,0:T(8,128)(2,1)S(1)}, u32[]{:S(2)}, u32[]{:S(2)}) collective-permute-start(bf16[272,512]{1,0:T(8,128)(2,1)S(1)} %collective-permute-done.rest_1_), channel_id=1, source_target_pairs={{0,2},{1,3},{2,4},{3,5},{4,6},{5,7},{8,10},{9,11},{10,12},{11,13},... | collective-permute-start | bytes 835592 | tf_op jit(solution)/shard_map/ppermute | solution.py:582
  17.8 8.1 %delta_local.3 = (bf16[1040,256]{1,0:T(8,128)(2,1)}, bf16[256,1024]{1,0:T(8,128)(2,1)}, f32[256,1024]{1,0:T(8,128)}) custom-call(s32[1]{0:T(128)} %bitcast.half_ref.core_ref, s32[1,256]{1,0:T(1,128)} %bitcast.13, bf16[256,1024]{1,0:T(8,128)(2,1)} %q_ref.5, bf16[256,1024]{1,0:T(8,128)(2,1)} %k_ref.3, bf16[256,2048]{1,0:T(8,128)(2,1)} %v_ref.3, ...), custom_call_target="tpu_custom_call" | custom-call | flops 6000000000 | bytes 3145728 | tf_op jit(solution)/shard_map/delta_local/pallas_call | solution.py:282
  25.9 0.0 collective-permute-done.1.rest_2_
  25.9 0.1 select_bitcast_fusion.1
  26.0 0.0 copy-start.2
  26.0 0.1 pad_maximum_fusion
  26.0 0.5 collective-permute-start.4
  26.5 0.0 collective-permute-done.2.other_ref
  26.5 0.5 copy-done.2
  27.0 0.3 compose.1
  27.3 2.0 %collective-permute-start.3 = (bf16[1040,128]{1,0:T(8,128)(2,1)S(1)}, bf16[1040,128]{1,0:T(8,128)(2,1)S(1)}, u32[]{:S(2)}, u32[]{:S(2)}) collective-permute-start(bf16[1040,128]{1,0:T(8,128)(2,1)S(1)} %get-tuple-element.33.add_ref), channel_id=1, source_target_pairs={{0,2},{1,3},{2,4},{3,5},{4,6},{5,7},{8,10},{9,11},{10,12},{11,13},... | collective-permute-start | bytes 798728 | tf_op jit(solution)/shard_map/ppermute | solution.py:582
  29.3 0.0 collective-permute-done.4.rest_3_
  29.3 0.1 broadcast_in_dim.2.freq_ref
  29.4 0.9 %window.1 = (bf16[256,1280]{1,0:T(8,128)(2,1)S(1)}, bf16[1280,256]{1,0:T(8,128)(2,1)S(1)}, f32[1,1280]{1,0:T(1,128)S(1)}, f32[256,128]{1,0:T(8,128)S(1)}, f32[256,128]{1,0:T(8,128)S(1)}) custom-call(f32[32,128]{1,0:T(8,128)S(1)} %broadcast_in_dim.2.freq_ref, bf16[272,512]{1,0:T(8,128)(2,1)S(1)} %copy-done.1, ...), custom_call_target="tpu_custom_call" | custom-call | flops 100000000 | bytes 1048576 | tf_op jit(solution)/shard_map/window/pallas_call | solution.py:381
  30.3 6.4 %collective-permute-done.3.state_ref = bf16[1040,128]{1,0:T(8,128)(2,1)S(1)} collective-permute-done((bf16[1040,128]{1,0:T(8,128)(2,1)S(1)}, bf16[1040,128]{1,0:T(8,128)(2,1)S(1)}, u32[]{:S(2)}, u32[]{:S(2)}) %collective-permute-start.3) | collective-permute-done | bytes 266272 | tf_op jit(solution)/shard_map/ppermute | solution.py:582
  36.8 0.2 relay.1
  37.0 2.1 %collective-permute-start.5 = (bf16[1040,128]{1,0:T(8,128)(2,1)S(1)}, bf16[1040,128]{1,0:T(8,128)(2,1)S(1)}, u32[]{:S(2)}, u32[]{:S(2)}) collective-permute-start(bf16[1040,128]{1,0:T(8,128)(2,1)S(1)} %relay.1), channel_id=1, source_target_pairs={{0,2},{1,3},{2,4},{3,5},{4,6},{5,7},{8,10},{9,11},{10,12},{11,13},... | collective-permute-start | bytes 798728 | tf_op jit(solution)/shard_map/ppermute | solution.py:582
  39.1 0.0 copy-start.3
  39.1 3.9 %attention.2.rest_0_ = bf16[256,2048]{1,0:T(8,128)(2,1)} custom-call(f32[1,1280]{1,0:T(1,128)S(1)} %get-tuple-element.41.ids_ref, f32[256,128]{1,0:T(8,128)S(1)} %get-tuple-element.42.cos_ref, f32[256,128]{1,0:T(8,128)S(1)} %get-tuple-element.43.sin_ref, bf16[256,1280]{1,0:T(8,128)(2,1)S(1)} %get-tuple-element.44.kt_ref, ...), custom_call_target="tpu_custom_call" | custom-call | flops 5000000000 | bytes 3145728 | tf_op jit(solution)/shard_map/attention/pallas_call | solution.py:567
  43.0 2.5 %collective-permute-done.5.state_ref = bf16[1040,128]{1,0:T(8,128)(2,1)S(1)} collective-permute-done((bf16[1040,128]{1,0:T(8,128)(2,1)S(1)}, bf16[1040,128]{1,0:T(8,128)(2,1)S(1)}, u32[]{:S(2)}, u32[]{:S(2)}) %collective-permute-start.5) | collective-permute-done | bytes 266272 | tf_op jit(solution)/shard_map/ppermute | solution.py:582
  45.5 0.4 arrive.1
  45.9 2.3 %collective-permute-start.6 = (bf16[1024,128]{1,0:T(8,128)(2,1)S(1)}, bf16[1024,128]{1,0:T(8,128)(2,1)S(1)}, u32[]{:S(2)}, u32[]{:S(2)}) collective-permute-start(bf16[1024,128]{1,0:T(8,128)(2,1)S(1)} %get-tuple-element.52), channel_id=1, source_target_pairs={{0,1},{1,0},{2,3},{3,2},{4,5},{5,4},{6,7},{7,6},{8,9},{9,8},{10,11... | collective-permute-start | bytes 786440 | tf_op jit(solution)/shard_map/ppermute | solution.py:586
  48.1 0.6 %copy-done.7 = f32[128]{0:T(128)S(1)} copy-done((f32[128]{0:T(128)S(1)}, f32[128]{0:T(128)}, u32[]{:S(2)}) %copy-start.7) | copy-done | bytes 536
  48.8 1.8 %delta_out.2.rest_0_ = bf16[256,2048]{1,0:T(8,128)(2,1)} custom-call(s32[1]{0:T(128)} %bitcast.half_ref.core_ref, bf16[256,1024]{1,0:T(8,128)(2,1)S(1)} %copy-done.5, f32[256,1024]{1,0:T(8,128)S(1)} %copy-done.3, bf16[1024,128]{1,0:T(8,128)(2,1)S(1)} %get-tuple-element.55.state_ref, bf16[256,2048]{1,0:T(8,128)(2,1)S(1)} %copy-done, f32[1,128]{1,0:T(1,128)S(1)} %bitcast.9), custom_call_target="tpu_custom_call" | custom-call | flops 100000000 | bytes 3145728 | tf_op jit(solution)/shard_map/delta_out/pallas_call | solution.py:430
  50.5 3.9 %attention.3 = bf16[256,2048]{1,0:T(8,128)(2,1)} custom-call(f32[1,1280]{1,0:T(1,128)S(1)} %get-tuple-element.41.ids_ref, f32[256,128]{1,0:T(8,128)S(1)} %get-tuple-element.42.cos_ref, f32[256,128]{1,0:T(8,128)S(1)} %get-tuple-element.43.sin_ref, bf16[256,1280]{1,0:T(8,128)(2,1)S(1)} %get-tuple-element.44.kt_ref, ...), custom_call_target="tpu_custom_call", output_to_operand_aliasing={{}: (7, {})} | custom-call | flops 5000000000 | bytes 3145728 | tf_op jit(solution)/shard_map/attention/pallas_call | solution.py:567
  54.4 0.0 collective-permute-done.6.state_ref
  54.4 1.8 %delta_out.3 = bf16[256,2048]{1,0:T(8,128)(2,1)} custom-call(s32[1]{0:T(128)S(6)} %sub.3.half_ref, bf16[256,1024]{1,0:T(8,128)(2,1)S(1)} %copy-done.6, f32[256,1024]{1,0:T(8,128)S(1)} %copy-done.4, bf16[1024,128]{1,0:T(8,128)(2,1)S(1)} %collective-permute-done.6.state_ref, bf16[256,2048]{1,0:T(8,128)(2,1)S(1)} %copy-done, ...), custom_call_target="tpu_custom_call", output_to_operand_aliasing={{}: (6, {})} | custom-call | flops 100000000 | bytes 3145728 | tf_op jit(solution)/shard_map/delta_out/pallas_call | solution.py:430
  (17 shorter events, 0.0 us)
Async XLA Ops:
  2.4 12.2 %collective-permute-start = (bf16[272,512]{1,0:T(8,128)(2,1)}, bf16[272,512]{1,0:T(8,128)(2,1)S(1)}, u32[]{:S(2)}, u32[]{:S(2)}) collective-permute-start(bf16[272,512]{1,0:T(8,128)(2,1)} %pack.1.rest_0_), channel_id=1, source_target_pairs={{0,2},{1,3},{2,4},{3,5},{4,6},{5,7},{8,10},{9,11},{10,12},{11,13},... | collective-permute-start | bytes 835592 | tf_op jit(solution)/shard_map/ppermute | solution.py:582
  13.6 12.3 %copy-start.1 = (bf16[272,512]{1,0:T(8,128)(2,1)S(1)}, bf16[272,512]{1,0:T(8,128)(2,1)}, u32[]{:S(2)}) copy-start(bf16[272,512]{1,0:T(8,128)(2,1)} %pack.1.rest_0_) | copy-start | bytes 835588
  13.6 12.9 %collective-permute-start.2 = (bf16[1040,256]{1,0:T(8,128)(2,1)}, bf16[1040,256]{1,0:T(8,128)(2,1)S(1)}, u32[]{:S(2)}, u32[]{:S(2)}) collective-permute-start(bf16[1040,256]{1,0:T(8,128)(2,1)} %get-tuple-element.29), channel_id=1, source_target_pairs={{0,1},{1,0},{2,3},{3,2},{4,5},{5,4},{6,7},{7,6},{8,9},{9,8},{10,11... | collective-permute-start | bytes 1597448 | tf_op jit(solution)/shard_map/ppermute | solution.py:586
  14.6 11.3 %collective-permute-start.1 = (bf16[272,512]{1,0:T(8,128)(2,1)S(1)}, bf16[272,512]{1,0:T(8,128)(2,1)S(1)}, u32[]{:S(2)}, u32[]{:S(2)}) collective-permute-start(bf16[272,512]{1,0:T(8,128)(2,1)S(1)} %collective-permute-done.rest_1_), channel_id=1, source_target_pairs={{0,2},{1,3},{2,4},{3,5},{4,6},{5,7},{8,10},{9,11},{10,12},{11,13},... | collective-permute-start | bytes 835592 | tf_op jit(solution)/shard_map/ppermute | solution.py:582
  26.0 1.0 %copy-start.2 = (bf16[1040,256]{1,0:T(8,128)(2,1)S(1)}, bf16[1040,256]{1,0:T(8,128)(2,1)}, u32[]{:S(2)}) copy-start(bf16[1040,256]{1,0:T(8,128)(2,1)} %get-tuple-element.32.mine_ref) | copy-start | bytes 1597444
  26.0 3.3 %collective-permute-start.4 = (bf16[2,272,512]{2,1,0:T(8,128)(2,1)S(1)}, bf16[2,272,512]{2,1,0:T(8,128)(2,1)S(1)}, u32[]{:S(2)}, u32[]{:S(2)}) collective-permute-start(bf16[2,272,512]{2,1,0:T(8,128)(2,1)S(1)} %pad_maximum_fusion), channel_id=1, source_target_pairs={{0,1},{1,0},{2,3},{3,2},{4,5},{5,4},{6,7},{7,6},{8,9},{9,8},{10,11... | collective-permute-start | bytes 1671176 | tf_op jit(solution)/shard_map/ppermute | solution.py:586
  27.3 9.4 %collective-permute-start.3 = (bf16[1040,128]{1,0:T(8,128)(2,1)S(1)}, bf16[1040,128]{1,0:T(8,128)(2,1)S(1)}, u32[]{:S(2)}, u32[]{:S(2)}) collective-permute-start(bf16[1040,128]{1,0:T(8,128)(2,1)S(1)} %get-tuple-element.33.add_ref), channel_id=1, source_target_pairs={{0,2},{1,3},{2,4},{3,5},{4,6},{5,7},{8,10},{9,11},{10,12},{11,13},... | collective-permute-start | bytes 798728 | tf_op jit(solution)/shard_map/ppermute | solution.py:582
  29.4 9.7 %copy-start.8 = (bf16[256,2048]{1,0:T(8,128)(2,1)S(1)}, bf16[256,2048]{1,0:T(8,128)(2,1)}, u32[]{:S(2)}) copy-start(bf16[256,2048]{1,0:T(8,128)(2,1)} %q_ref.7) | copy-start | bytes 3145732
  29.4 9.7 %copy-start.9 = (bf16[256,2048]{1,0:T(8,128)(2,1)S(1)}, bf16[256,2048]{1,0:T(8,128)(2,1)}, u32[]{:S(2)}) copy-start(bf16[256,2048]{1,0:T(8,128)(2,1)} %gate_ref.5) | copy-start | bytes 3145732
  37.0 8.5 %collective-permute-start.5 = (bf16[1040,128]{1,0:T(8,128)(2,1)S(1)}, bf16[1040,128]{1,0:T(8,128)(2,1)S(1)}, u32[]{:S(2)}, u32[]{:S(2)}) collective-permute-start(bf16[1040,128]{1,0:T(8,128)(2,1)S(1)} %relay.1), channel_id=1, source_target_pairs={{0,2},{1,3},{2,4},{3,5},{4,6},{5,7},{8,10},{9,11},{10,12},{11,13},... | collective-permute-start | bytes 798728 | tf_op jit(solution)/shard_map/ppermute | solution.py:582
  39.1 9.0 %copy-start.3 = (f32[256,1024]{1,0:T(8,128)S(1)}, f32[256,1024]{1,0:T(8,128)}, u32[]{:S(2)}) copy-start(f32[256,1024]{1,0:T(8,128)} %get-tuple-element.54.inner_ref) | copy-start | bytes 3145732
  39.1 9.0 %copy-start.5 = (bf16[256,1024]{1,0:T(8,128)(2,1)S(1)}, bf16[256,1024]{1,0:T(8,128)(2,1)}, u32[]{:S(2)}) copy-start(bf16[256,1024]{1,0:T(8,128)(2,1)} %get-tuple-element.53.reach_ref) | copy-start | bytes 1572868
  43.0 5.1 %copy-start = (bf16[256,2048]{1,0:T(8,128)(2,1)S(1)}, bf16[256,2048]{1,0:T(8,128)(2,1)}, u32[]{:S(2)}) copy-start(bf16[256,2048]{1,0:T(8,128)(2,1)} %gate_ref.7) | copy-start | bytes 3145732
  45.9 8.5 %collective-permute-start.6 = (bf16[1024,128]{1,0:T(8,128)(2,1)S(1)}, bf16[1024,128]{1,0:T(8,128)(2,1)S(1)}, u32[]{:S(2)}, u32[]{:S(2)}) collective-permute-start(bf16[1024,128]{1,0:T(8,128)(2,1)S(1)} %get-tuple-element.52), channel_id=1, source_target_pairs={{0,1},{1,0},{2,3},{3,2},{4,5},{5,4},{6,7},{7,6},{8,9},{9,8},{10,11... | collective-permute-start | bytes 786440 | tf_op jit(solution)/shard_map/ppermute | solution.py:586
  48.1 0.7 %copy-start.7 = (f32[128]{0:T(128)S(1)}, f32[128]{0:T(128)}, u32[]{:S(2)}) copy-start(f32[128]{0:T(128)} %param.23) | copy-start | bytes 1540
  50.5 3.9 %copy-start.4 = (f32[256,1024]{1,0:T(8,128)S(1)}, f32[256,1024]{1,0:T(8,128)}, u32[]{:S(2)}) copy-start(f32[256,1024]{1,0:T(8,128)} %get-tuple-element.50.inner_ref) | copy-start | bytes 3145732
  50.5 3.9 %copy-start.6 = (bf16[256,1024]{1,0:T(8,128)(2,1)S(1)}, bf16[256,1024]{1,0:T(8,128)(2,1)}, u32[]{:S(2)}) copy-start(bf16[256,1024]{1,0:T(8,128)(2,1)} %get-tuple-element.49.reach_ref) | copy-start | bytes 1572868

commit v6 on v5

--- a/solution.py
+++ b/solution.py
@@ -44,6 +44,7 @@
 MERGES = 3
 STRIP = 32
 FINE = 16
+DONE = object()
 
 
 def odd_rows(m, b):
@@ -158,9 +159,9 @@
         1.0,
         0.0,
     )
-    work = []
     strips = [slice(i, i + STRIP) for i in range(0, rows, STRIP)]
-    for kk in range(KEYS_PER_STEP):
+
+    def elementwise(kk, pair):
         cols = slice(kk * DK, (kk + 1) * DK)
         k_raw = k_ref[:, cols]
         q_raw = q_ref[:, cols]
@@ -169,12 +170,12 @@
         ktb = kt.astype(bf16)
         upper = dot(jnp.concatenate([k_raw[:TILE], q_raw[:TILE]], axis=0), ktb[:, :TILE])
         lower = dot(jnp.concatenate([k_raw[TILE:], q_raw[TILE:]], axis=0), ktb)
-        pair = [
+        pair += [
             dict(h=2 * kk + j, d=[], p=[], right=[], scaled=[],
                  cr=crow_ref[pl.ds(step * heads + 2 * kk + j, 1), :])
             for j in range(2)
         ]
-        work += pair
+        yield
         for at in strips:
             raw, start = (upper, at.start) if at.start < TILE else (lower, at.start - TILE)
             wide = slice(0, raw.shape[1])
@@ -206,6 +207,7 @@
                 if at.stop == rows:
                     w["last"] = entry[STRIP - 1 :]
                     w["kd"] = (kt * (rk_row * span[STRIP - 1 :])).astype(bf16)
+            yield
         top = TILE // STRIP
         for w in pair:
             d11 = jnp.concatenate(w["d"][:top], axis=0)
@@ -215,43 +217,73 @@
             w["p11"] = jnp.concatenate(w["p"][:top], axis=0)
             w["p2"] = jnp.concatenate(w["p"][top:], axis=0)
             w["right"] = jnp.concatenate(w["right"], axis=0)
-    mats = [m for w in work for m in w["d"]]
-    inverses = block_inverses(mats)
-    mats = [m.astype(bf16) for m in mats]
-    zeros = jnp.zeros((TILE // 2, TILE), bf16)
-    for level in range(MERGES):
-        b = BLOCK << level
-        keep = level_ref[level]
-        picked = [odd_rows(m, b) * keep for m in mats]
-        ys = [(p.astype(f32) + dot(p, x)).astype(bf16) for p, x in zip(picked, inverses)]
-        odds = [odd_rows(x, b) for x in inverses]
-        odds = [
-            x + (y.astype(f32) + dot(x, interleave(zeros, y, b))).astype(bf16)
-            for x, y in zip(odds, ys)
-        ]
-        inverses = [interleave(even_rows(x, b), o, b) for x, o in zip(inverses, odds)]
-    for i, w in enumerate(work):
-        x1, x2 = inverses[2 * i], inverses[2 * i + 1]
-        h = w["h"]
-        r1 = w["right"][:TILE]
-        u1 = add_strips(r1, dot(x1, r1))
-        after = dot(jnp.concatenate([w["d21"], w["p11"]], axis=0), u1)
-        r2 = add_strips(w["right"][TILE:], after[:TILE])
-        u2 = add_strips(r2, dot(x2, r2))
-        u = jnp.concatenate([u1, u2], axis=0)
-        last = dot(jnp.concatenate([w["p2"], w["kd"]], axis=0), u)
-        for at, scaled in zip(strips, w["scaled"]):
-            pu = after[TILE + at.start :] if at.start < TILE else last[at.start - TILE :]
-            pu = pu[:STRIP]
-            reach_ref[at, h * DK : (h + 1) * DK] = (scaled.astype(f32) - pu[:, :DK]).astype(bf16)
-            inner_ref[at, h * DV : (h + 1) * DV] = pu[:, DK:].astype(inner_ref.dtype)
-        base = pl.multiple_of((step * heads + h) * DK, DK)
-        for start in range(0, DK, STRIP):
-            ma = last[TILE + start : TILE + start + STRIP]
-            kept = w["last"] * eye[start : start + STRIP]
-            map_add_ref[pl.ds(base + start, STRIP), :] = jnp.concatenate(
-                [kept - ma[:, :DK], ma[:, DK:]], axis=1
-            ).astype(bf16)
+        yield
+
+    def invert(pair):
+        mats = [m for w in pair for m in w["d"]]
+        inverses = block_inverses(mats)
+        yield
+        mats = [m.astype(bf16) for m in mats]
+        zeros = jnp.zeros((TILE // 2, TILE), bf16)
+        for level in range(MERGES):
+            b = BLOCK << level
+            keep = level_ref[level]
+            picked = [odd_rows(m, b) * keep for m in mats]
+            ys = [(p.astype(f32) + dot(p, x)).astype(bf16) for p, x in zip(picked, inverses)]
+            yield
+            odds = [odd_rows(x, b) for x in inverses]
+            odds = [
+                x + (y.astype(f32) + dot(x, interleave(zeros, y, b))).astype(bf16)
+                for x, y in zip(odds, ys)
+            ]
+            inverses = [interleave(even_rows(x, b), o, b) for x, o in zip(inverses, odds)]
+            yield
+        for i, w in enumerate(pair):
+            w["x"] = inverses[2 * i : 2 * i + 2]
+
+    def finish(pair):
+        for w in pair:
+            w["u1"] = add_strips(w["right"][:TILE], dot(w["x"][0], w["right"][:TILE]))
+        yield
+        for w in pair:
+            w["after"] = dot(jnp.concatenate([w["d21"], w["p11"]], axis=0), w["u1"])
+        yield
+        for w in pair:
+            r2 = add_strips(w["right"][TILE:], w["after"][:TILE])
+            w["u"] = jnp.concatenate([w["u1"], add_strips(r2, dot(w["x"][1], r2))], axis=0)
+        yield
+        for w in pair:
+            w["end"] = dot(jnp.concatenate([w["p2"], w["kd"]], axis=0), w["u"])
+        yield
+        for w in pair:
+            h, after, last = w["h"], w["after"], w["end"]
+            for at, scaled in zip(strips, w["scaled"]):
+                pu = after[TILE + at.start :] if at.start < TILE else last[at.start - TILE :]
+                pu = pu[:STRIP]
+                reach_ref[at, h * DK : (h + 1) * DK] = (
+                    scaled.astype(f32) - pu[:, :DK]
+                ).astype(bf16)
+                inner_ref[at, h * DV : (h + 1) * DV] = pu[:, DK:].astype(inner_ref.dtype)
+            base = pl.multiple_of((step * heads + h) * DK, DK)
+            for start in range(0, DK, STRIP):
+                ma = last[TILE + start : TILE + start + STRIP]
+                kept = w["last"] * eye[start : start + STRIP]
+                map_add_ref[pl.ds(base + start, STRIP), :] = jnp.concatenate(
+                    [kept - ma[:, :DK], ma[:, DK:]], axis=1
+                ).astype(bf16)
+            yield
+
+    pairs = [[] for _ in range(KEYS_PER_STEP)]
+    for slot in range(KEYS_PER_STEP + 2):
+        phases = []
+        if slot < KEYS_PER_STEP:
+            phases.append(elementwise(slot, pairs[slot]))
+        if 0 <= slot - 1 < KEYS_PER_STEP:
+            phases.append(invert(pairs[slot - 1]))
+        if 0 <= slot - 2:
+            phases.append(finish(pairs[slot - 2]))
+        while phases:
+            phases = [p for p in phases if next(p, DONE) is not DONE]
 
 
 def add_strips(a, b):
@@ -638,7 +670,7 @@
     for _ in range(hops - 1):
         same.append(up_chip(same[-1], ranks))
     keep_ma, keep_reach, keep_inner = local(keep_half, 60)
-    same, keep_ma = lax.optimization_barrier((same, keep_ma))
+    same, keep_ma, other_ma = lax.optimization_barrier((same, keep_ma, other_ma))
     chain = [own, *same]
     other = swap_cores(
         jnp.stack([jnp.where(odd, chain[i + 1], chain[i]) for i in range(hops)]), ranks
@@ -670,21 +702,21 @@
         *same,
         other,
     )
-    state, window_arrays = lax.optimization_barrier((state, window_arrays))
-    for _ in range(hops - 1):
-        (leaving,) = small_call(relay_kernel, "relay", [state_like], chip_map, chip_add, state)
-        state = up_chip(leaving, ranks)
     kt, v_all, window_ids, cosine, sine = window_arrays
     window_arrays = (window_ids, cosine, sine, kt, v_all)
     attn_mixed = attention_half(0, window_arrays, attn_query, attn_gate)
     state, attn_mixed = lax.optimization_barrier((state, attn_mixed))
+    for _ in range(hops - 1):
+        (leaving,) = small_call(relay_kernel, "relay", [state_like], chip_map, chip_add, state)
+        state = up_chip(leaving, ranks)
+    attn_mixed = attention_half(1, window_arrays, attn_query, attn_gate, attn_mixed)
+    state, attn_mixed = lax.optimization_barrier((state, attn_mixed))
 
     final_like = jax.ShapeDtypeStruct((tall - BLOCK, DV), bf16)
     keep_state, pass_state = small_call(
         arrive_kernel, "arrive", [final_like] * 2, keep_half, keep_ma, other_ma, state, scalars=1
     )
     give_state = swap_cores(pass_state, ranks)
-    attn_mixed = attention_half(1, window_arrays, attn_query, attn_gate, attn_mixed)
 
     gain = norm_gain.reshape(1, DV)
     delta_mixed = delta_out(keep_half, keep_reach, keep_inner, keep_state, delta_gate, gain)

time: 56.5 us -> 52.1 us (0.922)
  waiting for transfers between devices: 8.94 us -> 4.75 us
  Pallas kernels: 31 us -> 30.2 us
    ppermute x4, waiting for transfers between devices: 8.93 us -> 4.74 us  [up_chip(): return lax.ppermute(value, 'ctx', [(i, i + 2) for i in range(ranks - 2)])]
    pallas_call x2, Pallas kernels: 16.2 us -> 15.4 us  [delta_local(): pl.pallas_call(delta_local_kernel, grid_spec=pltpu.PrefetchScalarGridSpec...]
  transfers between devices with their start and end apart: 7 -> 7, of which waited for: 2 -> 2; matrix products, arithmetic and copies ran while one was open for 0% -> 0% of each run, Pallas kernels for 48% -> 50%
where the time goes in v6:
time: 52.1 us; the launch traced here: 51.7 us
  Pallas kernels  30.2 us (58%)
  starting transfers between devices  14.7 us (28%)
  waiting for transfers between devices  4.75 us (9%)
  local copies, waits for them, and re-layouts  1.2 us (2%)
  between operations  0.79 us (2%)
    pallas_call x2, Pallas kernels, delta_local(): pl.pallas_call(delta_local_kernel, grid_spec=pltpu.PrefetchScalarGridSpec...  15.4 us
    ppermute x4, starting transfers between devices, up_chip(): return lax.ppermute(value, 'ctx', [(i, i + 2) for i in range(ranks - 2)])  11 us
    pallas_call x2, Pallas kernels, attention_half(): pl.pallas_call(attention_kernel, grid=(steps,), in_specs=in_specs, out_sp...  7.66 us
    ppermute x4, waiting for transfers between devices, up_chip(): return lax.ppermute(value, 'ctx', [(i, i + 2) for i in range(ranks - 2)])  4.74 us
    ppermute x3, starting transfers between devices, swap_cores(): return lax.ppermute(value, 'ctx', [(i, i ^ 1) for i in range(ranks)])  3.73 us
    pallas_call x5, Pallas kernels, small_call(): pl.pallas_call(kernel, in_specs=[SMEM] * scalars + [VMEM] * (len(args) -...  3.56 us
    pallas_call x2, Pallas kernels, delta_out(): pl.pallas_call(delta_out_kernel, grid_spec=pltpu.PrefetchScalarGridSpec(n...  3.54 us
    unnamed x20, local copies, waits for them, and re-layouts  1.13 us
  transfers between devices with their start and end apart: 7, of which 2 were waited for; matrix products, arithmetic and copies ran while one was open for 0% of the time, Pallas kernels for 50%

profile of v6, /device:TPU:9, one launch (start us, length us, event | category | flops | bytes accessed | tf_op | source)
XLA Modules:
  0.0 51.7 jit_solution(12037277493175521843)
XLA Ops:
  0.6 1.7 %pack.1.rest_0_ = bf16[272,512]{1,0:T(8,128)(2,1)} custom-call(s32[1,256]{1,0:T(1,128)} %bitcast.11, bf16[256,256]{1,0:T(8,128)(2,1)} %key_ref.1, bf16[256,256]{1,0:T(8,128)(2,1)} %value_ref.1), custom_call_target="tpu_custom_call" | custom-call | flops 100000000 | bytes 1048576 | tf_op jit(solution)/shard_map/pack/pallas_call | solution.py:413
  2.4 3.2 %collective-permute-start = (bf16[272,512]{1,0:T(8,128)(2,1)}, bf16[272,512]{1,0:T(8,128)(2,1)S(1)}, u32[]{:S(2)}, u32[]{:S(2)}) collective-permute-start(bf16[272,512]{1,0:T(8,128)(2,1)} %pack.1.rest_0_), channel_id=1, source_target_pairs={{0,2},{1,3},{2,4},{3,5},{4,6},{5,7},{8,10},{9,11},{10,12},{11,13},... | collective-permute-start | bytes 835592 | tf_op jit(solution)/shard_map/ppermute | solution.py:614
  5.6 7.7 %delta_local.2 = (bf16[1040,256]{1,0:T(8,128)(2,1)}, bf16[256,1024]{1,0:T(8,128)(2,1)}, f32[256,1024]{1,0:T(8,128)}) custom-call(s32[1]{0:T(128)S(6)} %sub.3.half_ref, s32[1,256]{1,0:T(1,128)} %bitcast.12, bf16[256,1024]{1,0:T(8,128)(2,1)} %q_ref.5, bf16[256,1024]{1,0:T(8,128)(2,1)} %k_ref.3, bf16[256,2048]{1,0:T(8,128)(2,1)} %v_ref.3, f32[16,256]{1,0:T(8,128)} %bitcast.14, ...), custom_call_target="tpu_custom_call" | custom-call | flops 6000000000 | bytes 3145728 | tf_op jit(solution)/shard_map/delta_local/pallas_call | solution.py:314
  13.3 1.0 %collective-permute-start.2 = (bf16[1040,256]{1,0:T(8,128)(2,1)}, bf16[1040,256]{1,0:T(8,128)(2,1)S(1)}, u32[]{:S(2)}, u32[]{:S(2)}) collective-permute-start(bf16[1040,256]{1,0:T(8,128)(2,1)} %get-tuple-element.26), channel_id=1, source_target_pairs={{0,1},{1,0},{2,3},{3,2},{4,5},{5,4},{6,7},{7,6},{8,9},{9,8},{10,11... | collective-permute-start | bytes 1597448 | tf_op jit(solution)/shard_map/ppermute | solution.py:618
  14.2 0.0 collective-permute-done.rest_1_
  14.2 3.2 %collective-permute-start.1 = (bf16[272,512]{1,0:T(8,128)(2,1)S(1)}, bf16[272,512]{1,0:T(8,128)(2,1)S(1)}, u32[]{:S(2)}, u32[]{:S(2)}) collective-permute-start(bf16[272,512]{1,0:T(8,128)(2,1)S(1)} %collective-permute-done.rest_1_), channel_id=1, source_target_pairs={{0,2},{1,3},{2,4},{3,5},{4,6},{5,7},{8,10},{9,11},{10,12},{11,13},... | collective-permute-start | bytes 835592 | tf_op jit(solution)/shard_map/ppermute | solution.py:614
  17.4 7.7 %delta_local.3 = (bf16[1040,256]{1,0:T(8,128)(2,1)}, bf16[256,1024]{1,0:T(8,128)(2,1)}, f32[256,1024]{1,0:T(8,128)}) custom-call(s32[1]{0:T(128)} %bitcast.half_ref.core_ref, s32[1,256]{1,0:T(1,128)} %bitcast.13, bf16[256,1024]{1,0:T(8,128)(2,1)} %q_ref.5, bf16[256,1024]{1,0:T(8,128)(2,1)} %k_ref.3, bf16[256,2048]{1,0:T(8,128)(2,1)} %v_ref.3, ...), custom_call_target="tpu_custom_call" | custom-call | flops 6000000000 | bytes 3145728 | tf_op jit(solution)/shard_map/delta_local/pallas_call | solution.py:314
  25.2 0.0 collective-permute-done.2.other_ref
  25.2 0.0 collective-permute-done.1.rest_2_
  25.2 0.1 select_bitcast_fusion.1
  25.2 0.1 pad_maximum_fusion
  25.3 0.5 collective-permute-start.4
  25.8 0.5 copy-done.2
  26.3 0.3 compose.1
  26.6 2.7 %collective-permute-start.3 = (bf16[1040,128]{1,0:T(8,128)(2,1)S(1)}, bf16[1040,128]{1,0:T(8,128)(2,1)S(1)}, u32[]{:S(2)}, u32[]{:S(2)}) collective-permute-start(bf16[1040,128]{1,0:T(8,128)(2,1)S(1)} %get-tuple-element.32.add_ref), channel_id=1, source_target_pairs={{0,2},{1,3},{2,4},{3,5},{4,6},{5,7},{8,10},{9,11},{10,12},{11,13},... | collective-permute-start | bytes 798728 | tf_op jit(solution)/shard_map/ppermute | solution.py:614
  29.3 0.0 collective-permute-done.4.rest_3_
  29.3 0.1 broadcast_in_dim.2.freq_ref
  29.4 0.9 %window.1 = (bf16[256,1280]{1,0:T(8,128)(2,1)S(1)}, bf16[1280,256]{1,0:T(8,128)(2,1)S(1)}, f32[1,1280]{1,0:T(1,128)S(1)}, f32[256,128]{1,0:T(8,128)S(1)}, f32[256,128]{1,0:T(8,128)S(1)}) custom-call(f32[32,128]{1,0:T(8,128)S(1)} %broadcast_in_dim.2.freq_ref, bf16[272,512]{1,0:T(8,128)(2,1)S(1)} %copy-done.1, ...), custom_call_target="tpu_custom_call" | custom-call | flops 100000000 | bytes 1048576 | tf_op jit(solution)/shard_map/window/pallas_call | solution.py:413
  30.3 0.0 copy-done.8
  30.3 3.8 %attention.2.rest_0_ = bf16[256,2048]{1,0:T(8,128)(2,1)} custom-call(f32[1,1280]{1,0:T(1,128)S(1)} %get-tuple-element.35.ids_ref, f32[256,128]{1,0:T(8,128)S(1)} %get-tuple-element.36.cos_ref, f32[256,128]{1,0:T(8,128)S(1)} %get-tuple-element.37.sin_ref, bf16[256,1280]{1,0:T(8,128)(2,1)S(1)} %get-tuple-element.38.kt_ref, ...), custom_call_target="tpu_custom_call" | custom-call | flops 5000000000 | bytes 3145728 | tf_op jit(solution)/shard_map/attention/pallas_call | solution.py:599
  34.1 2.0 %collective-permute-done.3.state_ref = bf16[1040,128]{1,0:T(8,128)(2,1)S(1)} collective-permute-done((bf16[1040,128]{1,0:T(8,128)(2,1)S(1)}, bf16[1040,128]{1,0:T(8,128)(2,1)S(1)}, u32[]{:S(2)}, u32[]{:S(2)}) %collective-permute-start.3) | collective-permute-done | bytes 266272 | tf_op jit(solution)/shard_map/ppermute | solution.py:614
  36.2 0.2 relay.1
  36.4 1.9 %collective-permute-start.5 = (bf16[1040,128]{1,0:T(8,128)(2,1)S(1)}, bf16[1040,128]{1,0:T(8,128)(2,1)S(1)}, u32[]{:S(2)}, u32[]{:S(2)}) collective-permute-start(bf16[1040,128]{1,0:T(8,128)(2,1)S(1)} %relay.1), channel_id=1, source_target_pairs={{0,2},{1,3},{2,4},{3,5},{4,6},{5,7},{8,10},{9,11},{10,12},{11,13},... | collective-permute-start | bytes 798728 | tf_op jit(solution)/shard_map/ppermute | solution.py:614
  38.3 0.0 copy-start.3
  38.3 3.8 %attention.3 = bf16[256,2048]{1,0:T(8,128)(2,1)} custom-call(f32[1,1280]{1,0:T(1,128)S(1)} %get-tuple-element.35.ids_ref, f32[256,128]{1,0:T(8,128)S(1)} %get-tuple-element.36.cos_ref, f32[256,128]{1,0:T(8,128)S(1)} %get-tuple-element.37.sin_ref, bf16[256,1280]{1,0:T(8,128)(2,1)S(1)} %get-tuple-element.38.kt_ref, ...), custom_call_target="tpu_custom_call", output_to_operand_aliasing={{}: (7, {})} | custom-call | flops 5000000000 | bytes 3145728 | tf_op jit(solution)/shard_map/attention/pallas_call | solution.py:599
  42.2 2.7 %collective-permute-done.5.state_ref = bf16[1040,128]{1,0:T(8,128)(2,1)S(1)} collective-permute-done((bf16[1040,128]{1,0:T(8,128)(2,1)S(1)}, bf16[1040,128]{1,0:T(8,128)(2,1)S(1)}, u32[]{:S(2)}, u32[]{:S(2)}) %collective-permute-start.5) | collective-permute-done | bytes 266272 | tf_op jit(solution)/shard_map/ppermute | solution.py:614
  44.9 0.4 arrive.1
  45.3 2.3 %collective-permute-start.6 = (bf16[1024,128]{1,0:T(8,128)(2,1)S(1)}, bf16[1024,128]{1,0:T(8,128)(2,1)S(1)}, u32[]{:S(2)}, u32[]{:S(2)}) collective-permute-start(bf16[1024,128]{1,0:T(8,128)(2,1)S(1)} %get-tuple-element.46), channel_id=1, source_target_pairs={{0,1},{1,0},{2,3},{3,2},{4,5},{5,4},{6,7},{7,6},{8,9},{9,8},{10,11... | collective-permute-start | bytes 786440 | tf_op jit(solution)/shard_map/ppermute | solution.py:618
  47.5 0.6 %copy-done.7 = f32[128]{0:T(128)S(1)} copy-done((f32[128]{0:T(128)S(1)}, f32[128]{0:T(128)}, u32[]{:S(2)}) %copy-start.7) | copy-done | bytes 536
  48.2 1.8 %delta_out.2.rest_0_ = bf16[256,2048]{1,0:T(8,128)(2,1)} custom-call(s32[1]{0:T(128)} %bitcast.half_ref.core_ref, bf16[256,1024]{1,0:T(8,128)(2,1)S(1)} %copy-done.5, f32[256,1024]{1,0:T(8,128)S(1)} %copy-done.3, bf16[1024,128]{1,0:T(8,128)(2,1)S(1)} %get-tuple-element.49.state_ref, bf16[256,2048]{1,0:T(8,128)(2,1)S(1)} %copy-done, f32[1,128]{1,0:T(1,128)S(1)} %bitcast.9), custom_call_target="tpu_custom_call" | custom-call | flops 100000000 | bytes 3145728 | tf_op jit(solution)/shard_map/delta_out/pallas_call | solution.py:462
  49.9 0.0 collective-permute-done.6.state_ref
  50.0 1.8 %delta_out.3 = bf16[256,2048]{1,0:T(8,128)(2,1)} custom-call(s32[1]{0:T(128)S(6)} %sub.3.half_ref, bf16[256,1024]{1,0:T(8,128)(2,1)S(1)} %copy-done.6, f32[256,1024]{1,0:T(8,128)S(1)} %copy-done.4, bf16[1024,128]{1,0:T(8,128)(2,1)S(1)} %collective-permute-done.6.state_ref, bf16[256,2048]{1,0:T(8,128)(2,1)S(1)} %copy-done, ...), custom_call_target="tpu_custom_call", output_to_operand_aliasing={{}: (6, {})} | custom-call | flops 100000000 | bytes 3145728 | tf_op jit(solution)/shard_map/delta_out/pallas_call | solution.py:462
  (17 shorter events, 0.0 us)
Async XLA Ops:
  2.4 11.9 %collective-permute-start = (bf16[272,512]{1,0:T(8,128)(2,1)}, bf16[272,512]{1,0:T(8,128)(2,1)S(1)}, u32[]{:S(2)}, u32[]{:S(2)}) collective-permute-start(bf16[272,512]{1,0:T(8,128)(2,1)} %pack.1.rest_0_), channel_id=1, source_target_pairs={{0,2},{1,3},{2,4},{3,5},{4,6},{5,7},{8,10},{9,11},{10,12},{11,13},... | collective-permute-start | bytes 835592 | tf_op jit(solution)/shard_map/ppermute | solution.py:614
  13.3 11.9 %copy-start.1 = (bf16[272,512]{1,0:T(8,128)(2,1)S(1)}, bf16[272,512]{1,0:T(8,128)(2,1)}, u32[]{:S(2)}) copy-start(bf16[272,512]{1,0:T(8,128)(2,1)} %pack.1.rest_0_) | copy-start | bytes 835588
  13.3 11.9 %collective-permute-start.2 = (bf16[1040,256]{1,0:T(8,128)(2,1)}, bf16[1040,256]{1,0:T(8,128)(2,1)S(1)}, u32[]{:S(2)}, u32[]{:S(2)}) collective-permute-start(bf16[1040,256]{1,0:T(8,128)(2,1)} %get-tuple-element.26), channel_id=1, source_target_pairs={{0,1},{1,0},{2,3},{3,2},{4,5},{5,4},{6,7},{7,6},{8,9},{9,8},{10,11... | collective-permute-start | bytes 1597448 | tf_op jit(solution)/shard_map/ppermute | solution.py:618
  14.2 10.9 %collective-permute-start.1 = (bf16[272,512]{1,0:T(8,128)(2,1)S(1)}, bf16[272,512]{1,0:T(8,128)(2,1)S(1)}, u32[]{:S(2)}, u32[]{:S(2)}) collective-permute-start(bf16[272,512]{1,0:T(8,128)(2,1)S(1)} %collective-permute-done.rest_1_), channel_id=1, source_target_pairs={{0,2},{1,3},{2,4},{3,5},{4,6},{5,7},{8,10},{9,11},{10,12},{11,13},... | collective-permute-start | bytes 835592 | tf_op jit(solution)/shard_map/ppermute | solution.py:614
  25.2 1.0 %copy-start.2 = (bf16[1040,256]{1,0:T(8,128)(2,1)S(1)}, bf16[1040,256]{1,0:T(8,128)(2,1)}, u32[]{:S(2)}) copy-start(bf16[1040,256]{1,0:T(8,128)(2,1)} %get-tuple-element.29.mine_ref) | copy-start | bytes 1597444
  25.3 4.0 %collective-permute-start.4 = (bf16[2,272,512]{2,1,0:T(8,128)(2,1)S(1)}, bf16[2,272,512]{2,1,0:T(8,128)(2,1)S(1)}, u32[]{:S(2)}, u32[]{:S(2)}) collective-permute-start(bf16[2,272,512]{2,1,0:T(8,128)(2,1)S(1)} %pad_maximum_fusion), channel_id=1, source_target_pairs={{0,1},{1,0},{2,3},{3,2},{4,5},{5,4},{6,7},{7,6},{8,9},{9,8},{10,11... | collective-permute-start | bytes 1671176 | tf_op jit(solution)/shard_map/ppermute | solution.py:618
  26.3 4.0 %copy-start.8 = (bf16[256,2048]{1,0:T(8,128)(2,1)S(1)}, bf16[256,2048]{1,0:T(8,128)(2,1)}, u32[]{:S(2)}) copy-start(bf16[256,2048]{1,0:T(8,128)(2,1)} %q_ref.7) | copy-start | bytes 3145732
  26.3 4.0 %copy-start.9 = (bf16[256,2048]{1,0:T(8,128)(2,1)S(1)}, bf16[256,2048]{1,0:T(8,128)(2,1)}, u32[]{:S(2)}) copy-start(bf16[256,2048]{1,0:T(8,128)(2,1)} %gate_ref.5) | copy-start | bytes 3145732
  26.6 9.6 %collective-permute-start.3 = (bf16[1040,128]{1,0:T(8,128)(2,1)S(1)}, bf16[1040,128]{1,0:T(8,128)(2,1)S(1)}, u32[]{:S(2)}, u32[]{:S(2)}) collective-permute-start(bf16[1040,128]{1,0:T(8,128)(2,1)S(1)} %get-tuple-element.32.add_ref), channel_id=1, source_target_pairs={{0,2},{1,3},{2,4},{3,5},{4,6},{5,7},{8,10},{9,11},{10,12},{11,13},... | collective-permute-start | bytes 798728 | tf_op jit(solution)/shard_map/ppermute | solution.py:614
  36.4 8.5 %collective-permute-start.5 = (bf16[1040,128]{1,0:T(8,128)(2,1)S(1)}, bf16[1040,128]{1,0:T(8,128)(2,1)S(1)}, u32[]{:S(2)}, u32[]{:S(2)}) collective-permute-start(bf16[1040,128]{1,0:T(8,128)(2,1)S(1)} %relay.1), channel_id=1, source_target_pairs={{0,2},{1,3},{2,4},{3,5},{4,6},{5,7},{8,10},{9,11},{10,12},{11,13},... | collective-permute-start | bytes 798728 | tf_op jit(solution)/shard_map/ppermute | solution.py:614
  38.3 9.2 %copy-start.3 = (f32[256,1024]{1,0:T(8,128)S(1)}, f32[256,1024]{1,0:T(8,128)}, u32[]{:S(2)}) copy-start(f32[256,1024]{1,0:T(8,128)} %get-tuple-element.48.inner_ref) | copy-start | bytes 3145732
  38.3 9.2 %copy-start.5 = (bf16[256,1024]{1,0:T(8,128)(2,1)S(1)}, bf16[256,1024]{1,0:T(8,128)(2,1)}, u32[]{:S(2)}) copy-start(bf16[256,1024]{1,0:T(8,128)(2,1)} %get-tuple-element.47.reach_ref) | copy-start | bytes 1572868
  42.2 5.4 %copy-start = (bf16[256,2048]{1,0:T(8,128)(2,1)S(1)}, bf16[256,2048]{1,0:T(8,128)(2,1)}, u32[]{:S(2)}) copy-start(bf16[256,2048]{1,0:T(8,128)(2,1)} %gate_ref.7) | copy-start | bytes 3145732
  45.3 4.7 %collective-permute-start.6 = (bf16[1024,128]{1,0:T(8,128)(2,1)S(1)}, bf16[1024,128]{1,0:T(8,128)(2,1)S(1)}, u32[]{:S(2)}, u32[]{:S(2)}) collective-permute-start(bf16[1024,128]{1,0:T(8,128)(2,1)S(1)} %get-tuple-element.46), channel_id=1, source_target_pairs={{0,1},{1,0},{2,3},{3,2},{4,5},{5,4},{6,7},{7,6},{8,9},{9,8},{10,11... | collective-permute-start | bytes 786440 | tf_op jit(solution)/shard_map/ppermute | solution.py:618
  47.5 0.7 %copy-start.7 = (f32[128]{0:T(128)S(1)}, f32[128]{0:T(128)}, u32[]{:S(2)}) copy-start(f32[128]{0:T(128)} %param.23) | copy-start | bytes 1540
  48.2 1.8 %copy-start.4 = (f32[256,1024]{1,0:T(8,128)S(1)}, f32[256,1024]{1,0:T(8,128)}, u32[]{:S(2)}) copy-start(f32[256,1024]{1,0:T(8,128)} %get-tuple-element.44.inner_ref) | copy-start | bytes 3145732
  48.2 1.8 %copy-start.6 = (bf16[256,1024]{1,0:T(8,128)(2,1)S(1)}, bf16[256,1024]{1,0:T(8,128)(2,1)}, u32[]{:S(2)}) copy-start(bf16[256,1024]{1,0:T(8,128)(2,1)} %get-tuple-element.43.reach_ref) | copy-start | bytes 1572868

commit v7 on v6

--- a/solution.py
+++ b/solution.py
@@ -17,7 +17,6 @@
 MASKED = -1e30
 EPS = 1e-6
 TILE = 128
-KEYS_PER_STEP = 4
 MIB = 1024 * 1024
 
 f32 = jnp.float32
@@ -94,116 +93,106 @@
     return out
 
 
+def setup(half_ref, seg_ref, decay_ref, n, mask_ref, crow_ref, ccol_ref, first_ref, beta_ref=None):
+    rows = seg_ref.shape[1]
+    seg_row = seg_ref[...].astype(f32) + 1.0
+    seg_col = jnp.transpose(jnp.broadcast_to(seg_row, (TILE, rows)))
+    seg_cols = jnp.concatenate([seg_col] * (rows // TILE), axis=1)
+    r = lax.broadcasted_iota(jnp.int32, (rows, rows), 0)
+    c = lax.broadcasted_iota(jnp.int32, (rows, rows), 1)
+    mask_ref[...] = jnp.where((seg_cols == seg_row) & (r >= c), 0.0, MASKED)
+    first_ref[...] = jnp.where(seg_col == seg_row[:, :1], 1.0, 0.0)
+    base = pl.multiple_of(half_ref[0] * n, n)
+    decay = decay_ref[pl.ds(base, n), :] * LOG2E
+    high = decay.astype(bf16)
+    rest = decay - high.astype(f32)
+    middle = rest.astype(bf16)
+    parts = [high, middle, (rest - middle.astype(f32)).astype(bf16)]
+    parts = jnp.concatenate([p.astype(f32) for p in parts], axis=0).astype(bf16)
+    sums = dot(parts, jnp.where(r <= c, 1.0, 0.0).astype(bf16))
+    cumulative = sums[:n] + sums[n : 2 * n] + sums[2 * n :]
+    crow_ref[...] = cumulative
+    beta = jnp.zeros((n, rows), f32) if beta_ref is None else beta_ref[pl.ds(base, n), :]
+    fill = jnp.zeros((TILE - 2 * n, rows), f32)
+    ccol_ref[...] = jnp.transpose(jnp.concatenate([cumulative, beta, fill], axis=0))
+    return seg_row
+
+
+def column(ref, at, lane, width):
+    one = jnp.broadcast_to(ref[at, lane : lane + 1], (STRIP, TILE))
+    return one if width == TILE else jnp.concatenate([one] * (width // TILE), axis=1)
+
+
+def pipeline(phases, count):
+    for slot in range(count + len(phases) - 1):
+        running = [
+            phase(slot - i) for i, phase in enumerate(phases) if 0 <= slot - i < count
+        ]
+        while running:
+            running = [p for p in running if next(p, DONE) is not DONE]
+
+
 def delta_local_kernel(
     half_ref,
     seg_ref,
-    q_ref,
     k_ref,
     v_ref,
     beta_ref,
     decay_ref,
     map_add_ref,
-    reach_ref,
-    inner_ref,
+    solved_ref,
     mask_ref,
     level_ref,
     crow_ref,
     ccol_ref,
     first_ref,
 ):
-    rows = q_ref.shape[0]
-    step = pl.program_id(0)
-    heads = 2 * KEYS_PER_STEP
-
-    @pl.when(step == 0)
-    def _():
-        seg_row = seg_ref[...].astype(f32) + 1.0
-        seg_col = jnp.transpose(jnp.broadcast_to(seg_row, (TILE, rows)))
-        seg_cols = jnp.concatenate([seg_col] * (rows // TILE), axis=1)
-        r = lax.broadcasted_iota(jnp.int32, (rows, rows), 0)
-        c = lax.broadcasted_iota(jnp.int32, (rows, rows), 1)
-        mask_ref[...] = jnp.where((seg_cols == seg_row) & (r >= c), 0.0, MASKED)
-        first_ref[...] = jnp.where(seg_col == seg_row[:, :1], 1.0, 0.0)
-        r = lax.broadcasted_iota(jnp.int32, (TILE, TILE), 0)
-        c = lax.broadcasted_iota(jnp.int32, (TILE, TILE), 1)
-        for level in range(MERGES):
-            b = BLOCK << level
-            sibling = jnp.where(r // b == c // b + 1, 1.0, 0.0)
-            level_ref[level] = odd_rows(sibling, b).astype(bf16)
-        n = map_add_ref.shape[0] // DK
-        base = pl.multiple_of(half_ref[0] * n, n)
-        decay = decay_ref[pl.ds(base, n), :] * LOG2E
-        high = decay.astype(bf16)
-        rest = decay - high.astype(f32)
-        middle = rest.astype(bf16)
-        parts = [high, middle, (rest - middle.astype(f32)).astype(bf16)]
-        parts = jnp.concatenate([p.astype(f32) for p in parts], axis=0).astype(bf16)
-        r = lax.broadcasted_iota(jnp.int32, (rows, rows), 0)
-        c = lax.broadcasted_iota(jnp.int32, (rows, rows), 1)
-        sums = dot(parts, jnp.where(r <= c, 1.0, 0.0).astype(bf16))
-        cumulative = sums[:n] + sums[n : 2 * n] + sums[2 * n :]
-        crow_ref[...] = cumulative
-        fill = jnp.zeros((TILE - 2 * n, rows), f32)
-        both = jnp.concatenate([cumulative, beta_ref[pl.ds(base, n), :], fill], axis=0)
-        ccol_ref[...] = jnp.transpose(both)
-        end = map_add_ref.shape[0] - BLOCK
-        map_add_ref[end:, :] = jnp.broadcast_to(seg_row, (BLOCK, rows)).astype(bf16)
-
-    shift = lax.rem(TILE - step * heads, TILE)
-    columns = pltpu.roll(ccol_ref[...], shift, 1)
-    n = map_add_ref.shape[0] // DK
-    first = first_ref[...]
-    eye = jnp.where(
-        lax.broadcasted_iota(jnp.int32, (TILE, TILE), 0)
-        == lax.broadcasted_iota(jnp.int32, (TILE, TILE), 1),
-        1.0,
-        0.0,
-    )
+    rows = k_ref.shape[0]
+    n = v_ref.shape[1] // DV
+    seg_row = setup(
+        half_ref, seg_ref, decay_ref, n, mask_ref, crow_ref, ccol_ref, first_ref, beta_ref
+    )
+    map_add_ref[n * DK :, :] = jnp.broadcast_to(seg_row, (BLOCK, rows)).astype(bf16)
+    r = lax.broadcasted_iota(jnp.int32, (TILE, TILE), 0)
+    c = lax.broadcasted_iota(jnp.int32, (TILE, TILE), 1)
+    eye = jnp.where(r == c, 1.0, 0.0)
+    for level in range(MERGES):
+        b = BLOCK << level
+        sibling = jnp.where(r // b == c // b + 1, 1.0, 0.0)
+        level_ref[level] = odd_rows(sibling, b).astype(bf16)
     strips = [slice(i, i + STRIP) for i in range(0, rows, STRIP)]
-
-    def elementwise(kk, pair):
-        cols = slice(kk * DK, (kk + 1) * DK)
-        k_raw = k_ref[:, cols]
-        q_raw = q_ref[:, cols]
+    pairs = [
+        [dict(h=2 * kk + j, d=[], right=[]) for j in range(2)] for kk in range(n // 2)
+    ]
+
+    def elementwise(kk):
+        pair = pairs[kk]
+        k_raw = k_ref[:, kk * DK : (kk + 1) * DK]
         kt = jnp.transpose(k_raw.astype(f32))
         rk_row = lax.rsqrt(jnp.sum(kt * kt, axis=0, keepdims=True) + EPS)
         ktb = kt.astype(bf16)
-        upper = dot(jnp.concatenate([k_raw[:TILE], q_raw[:TILE]], axis=0), ktb[:, :TILE])
-        lower = dot(jnp.concatenate([k_raw[TILE:], q_raw[TILE:]], axis=0), ktb)
-        pair += [
-            dict(h=2 * kk + j, d=[], p=[], right=[], scaled=[],
-                 cr=crow_ref[pl.ds(step * heads + 2 * kk + j, 1), :])
-            for j in range(2)
-        ]
+        upper = dot(k_raw[:TILE], ktb[:, :TILE])
+        lower = dot(k_raw[TILE:], ktb)
         yield
         for at in strips:
             raw, start = (upper, at.start) if at.start < TILE else (lower, at.start - TILE)
-            wide = slice(0, raw.shape[1])
+            width = raw.shape[1]
             kf = k_raw[at].astype(f32)
-            qf = q_raw[at].astype(f32)
             rk = lax.rsqrt(jnp.sum(kf * kf, axis=1, keepdims=True) + EPS)
-            rq = lax.rsqrt(jnp.sum(qf * qf, axis=1, keepdims=True) + EPS) * DK**-0.5
             kn = kf * rk
-            qn = qf * rq
-            gram = raw[start : start + STRIP] * rk_row[:, wide] * -rk
-            probe = raw[TILE + start : TILE + start + STRIP] * rk_row[:, wide] * rq
+            gram = raw[start : start + STRIP] * rk_row[:, :width] * -rk
             for w in pair:
                 h = w["h"]
-                cc = jnp.broadcast_to(columns[at, h : h + 1], (STRIP, TILE))
-                bt = jnp.broadcast_to(columns[at, n + h : n + h + 1], (STRIP, TILE))
-                ccw, btw = cc, bt
-                if raw.shape[1] > TILE:
-                    ccw = jnp.concatenate([cc, cc], axis=1)
-                    btw = jnp.concatenate([bt, bt], axis=1)
-                span = jnp.exp2(ccw - w["cr"][:, wide] + mask_ref[at, wide])
-                w["d"].append(span * btw * gram)
-                w["p"].append((span * probe).astype(bf16))
-                entry = jnp.exp2(cc) * first[at]
+                cc = column(ccol_ref, at, h, width)
+                bt = column(ccol_ref, at, n + h, width)
+                span = jnp.exp2(cc - crow_ref[h : h + 1, :width] + mask_ref[at, :width])
+                w["d"].append(span * bt * gram)
+                cc, bt = cc[:, :TILE], bt[:, :TILE]
+                entry = jnp.exp2(cc) * first_ref[at]
                 value = v_ref[at, h * DV : (h + 1) * DV].astype(f32)
                 w["right"].append(
                     jnp.concatenate([bt * entry * kn, bt * value], axis=1).astype(bf16)
                 )
-                w["scaled"].append((entry * qn).astype(bf16))
                 if at.stop == rows:
                     w["last"] = entry[STRIP - 1 :]
                     w["kd"] = (kt * (rk_row * span[STRIP - 1 :])).astype(bf16)
@@ -214,12 +203,11 @@
             d2 = jnp.concatenate(w["d"][top:], axis=0)
             w["d"] = [d11, d2[:, TILE:]]
             w["d21"] = d2[:, :TILE].astype(bf16)
-            w["p11"] = jnp.concatenate(w["p"][:top], axis=0)
-            w["p2"] = jnp.concatenate(w["p"][top:], axis=0)
             w["right"] = jnp.concatenate(w["right"], axis=0)
         yield
 
-    def invert(pair):
+    def invert(kk):
+        pair = pairs[kk]
         mats = [m for w in pair for m in w["d"]]
         inverses = block_inverses(mats)
         yield
@@ -241,49 +229,31 @@
         for i, w in enumerate(pair):
             w["x"] = inverses[2 * i : 2 * i + 2]
 
-    def finish(pair):
+    def finish(kk):
+        pair = pairs[kk]
         for w in pair:
             w["u1"] = add_strips(w["right"][:TILE], dot(w["x"][0], w["right"][:TILE]))
         yield
         for w in pair:
-            w["after"] = dot(jnp.concatenate([w["d21"], w["p11"]], axis=0), w["u1"])
+            w["r2"] = add_strips(w["right"][TILE:], dot(w["d21"], w["u1"]))
         yield
         for w in pair:
-            r2 = add_strips(w["right"][TILE:], w["after"][:TILE])
-            w["u"] = jnp.concatenate([w["u1"], add_strips(r2, dot(w["x"][1], r2))], axis=0)
+            u2 = add_strips(w["r2"], dot(w["x"][1], w["r2"]))
+            w["u"] = jnp.concatenate([w["u1"], u2], axis=0)
+            solved_ref[w["h"] * rows : (w["h"] + 1) * rows, :] = w["u"]
         yield
         for w in pair:
-            w["end"] = dot(jnp.concatenate([w["p2"], w["kd"]], axis=0), w["u"])
-        yield
-        for w in pair:
-            h, after, last = w["h"], w["after"], w["end"]
-            for at, scaled in zip(strips, w["scaled"]):
-                pu = after[TILE + at.start :] if at.start < TILE else last[at.start - TILE :]
-                pu = pu[:STRIP]
-                reach_ref[at, h * DK : (h + 1) * DK] = (
-                    scaled.astype(f32) - pu[:, :DK]
-                ).astype(bf16)
-                inner_ref[at, h * DV : (h + 1) * DV] = pu[:, DK:].astype(inner_ref.dtype)
-            base = pl.multiple_of((step * heads + h) * DK, DK)
+            h = w["h"]
+            ma = dot(w["kd"], w["u"])
             for start in range(0, DK, STRIP):
-                ma = last[TILE + start : TILE + start + STRIP]
+                part = ma[start : start + STRIP]
                 kept = w["last"] * eye[start : start + STRIP]
-                map_add_ref[pl.ds(base + start, STRIP), :] = jnp.concatenate(
-                    [kept - ma[:, :DK], ma[:, DK:]], axis=1
+                map_add_ref[h * DK + start : h * DK + start + STRIP, :] = jnp.concatenate(
+                    [kept - part[:, :DK], part[:, DK:]], axis=1
                 ).astype(bf16)
             yield
 
-    pairs = [[] for _ in range(KEYS_PER_STEP)]
-    for slot in range(KEYS_PER_STEP + 2):
-        phases = []
-        if slot < KEYS_PER_STEP:
-            phases.append(elementwise(slot, pairs[slot]))
-        if 0 <= slot - 1 < KEYS_PER_STEP:
-            phases.append(invert(pairs[slot - 1]))
-        if 0 <= slot - 2:
-            phases.append(finish(pairs[slot - 2]))
-        while phases:
-            phases = [p for p in phases if next(p, DONE) is not DONE]
+    pipeline([elementwise, invert, finish], n // 2)
 
 
 def add_strips(a, b):
@@ -296,56 +266,148 @@
     )
 
 
-def delta_local(half, mib, seg_row, query, key, value, beta, decay):
-    rows = query.shape[0]
-    heads = 2 * KEYS_PER_STEP
-    n = value.shape[1] // DV // 2
-    steps = n // heads
-    kw = KEYS_PER_STEP * DK
-    vw = heads * DV
-    tall = n * DK + BLOCK
-
+def delta_reach_kernel(
+    half_ref,
+    seg_ref,
+    q_ref,
+    k_ref,
+    decay_ref,
+    solved_ref,
+    reach_ref,
+    inner_ref,
+    mask_ref,
+    crow_ref,
+    ccol_ref,
+    first_ref,
+):
+    rows = k_ref.shape[0]
+    n = reach_ref.shape[1] // DK
+    setup(half_ref, seg_ref, decay_ref, n, mask_ref, crow_ref, ccol_ref, first_ref)
+    strips = [slice(i, i + STRIP) for i in range(0, rows, STRIP)]
+    pairs = [
+        [dict(h=2 * kk + j, p=[], scaled=[]) for j in range(2)] for kk in range(n // 2)
+    ]
+
+    def elementwise(kk):
+        pair = pairs[kk]
+        cols = slice(kk * DK, (kk + 1) * DK)
+        k_raw = k_ref[:, cols]
+        q_raw = q_ref[:, cols]
+        kt = jnp.transpose(k_raw.astype(f32))
+        rk_row = lax.rsqrt(jnp.sum(kt * kt, axis=0, keepdims=True) + EPS)
+        ktb = kt.astype(bf16)
+        upper = dot(q_raw[:TILE], ktb[:, :TILE])
+        lower = dot(q_raw[TILE:], ktb)
+        yield
+        for at in strips:
+            raw, start = (upper, at.start) if at.start < TILE else (lower, at.start - TILE)
+            width = raw.shape[1]
+            qf = q_raw[at].astype(f32)
+            rq = lax.rsqrt(jnp.sum(qf * qf, axis=1, keepdims=True) + EPS) * DK**-0.5
+            qn = qf * rq
+            probe = raw[start : start + STRIP] * rk_row[:, :width] * rq
+            for w in pair:
+                h = w["h"]
+                cc = column(ccol_ref, at, h, width)
+                span = jnp.exp2(cc - crow_ref[h : h + 1, :width] + mask_ref[at, :width])
+                w["p"].append((span * probe).astype(bf16))
+                entry = jnp.exp2(cc[:, :TILE]) * first_ref[at]
+                w["scaled"].append((entry * qn).astype(bf16))
+            yield
+
+    def finish(kk):
+        top = TILE // STRIP
+        for w in pairs[kk]:
+            h = w["h"]
+            u = solved_ref[h * rows : (h + 1) * rows, :]
+            upper = dot(jnp.concatenate(w["p"][:top], axis=0), u[:TILE])
+            lower = dot(jnp.concatenate(w["p"][top:], axis=0), u)
+            for at, scaled in zip(strips, w["scaled"]):
+                pu = upper[at.start :] if at.start < TILE else lower[at.start - TILE :]
+                pu = pu[:STRIP]
+                reach_ref[at, h * DK : (h + 1) * DK] = (
+                    scaled.astype(f32) - pu[:, :DK]
+                ).astype(bf16)
+                inner_ref[at, h * DV : (h + 1) * DV] = pu[:, DK:]
+            yield
+
+    pipeline([elementwise, finish], n // 2)
+
+
+def half_call(kernel, name, mib, half, operands, outs, scratch):
     def at_half(i, s):
-        return (0, s[0] * steps + i)
-
-    def whole(i, s):
+        return (0, s[0])
+
+    def at_zero(i, s):
         return (0, 0)
 
+    specs = []
+    args = []
+    for a in operands:
+        if isinstance(a, tuple):
+            (a,) = a
+            specs.append(pl.BlockSpec((a.shape[0], a.shape[1] // 2), at_half))
+        else:
+            specs.append(pl.BlockSpec(a.shape, at_zero))
+        args.append(a)
     return pl.pallas_call(
-        delta_local_kernel,
+        kernel,
         grid_spec=pltpu.PrefetchScalarGridSpec(
             num_scalar_prefetch=1,
-            grid=(steps,),
-            in_specs=[
-                pl.BlockSpec((1, rows), whole),
-                pl.BlockSpec((rows, kw), at_half),
-                pl.BlockSpec((rows, kw), at_half),
-                pl.BlockSpec((rows, vw), at_half),
-                pl.BlockSpec(beta.shape, whole),
-                pl.BlockSpec(decay.shape, whole),
-            ],
-            out_specs=[
-                pl.BlockSpec((tall, DK + DV), whole),
-                pl.BlockSpec((rows, heads * DK), lambda i, s: (0, i)),
-                pl.BlockSpec((rows, vw), lambda i, s: (0, i)),
-            ],
-            scratch_shapes=[
-                pltpu.VMEM((rows, rows), f32),
-                pltpu.VMEM((MERGES, TILE // 2, TILE), bf16),
-                pltpu.VMEM((n, rows), f32),
-                pltpu.VMEM((rows, TILE), f32),
-                pltpu.VMEM((rows, TILE), f32),
-            ],
+            grid=(1,),
+            in_specs=specs,
+            out_specs=[pl.BlockSpec(o.shape, at_zero) for o in outs],
+            scratch_shapes=scratch,
         ),
-        out_shape=[
-            jax.ShapeDtypeStruct((tall, DK + DV), bf16),
+        out_shape=outs,
+        compiler_params=params(mib),
+        cost_estimate=cost(4 * 10**9, 3 * 2**20),
+        name=name,
+    )(half, *args)
+
+
+def setup_scratch(rows, n):
+    return [
+        pltpu.VMEM((rows, rows), f32),
+        pltpu.VMEM((n, rows), f32),
+        pltpu.VMEM((rows, TILE), f32),
+        pltpu.VMEM((rows, TILE), f32),
+    ]
+
+
+def delta_local(half, mib, seg_row, key, value, beta, decay):
+    rows = key.shape[0]
+    n = value.shape[1] // DV // 2
+    mask, *others = setup_scratch(rows, n)
+    return half_call(
+        delta_local_kernel,
+        "delta_local",
+        mib,
+        half,
+        [seg_row, (key,), (value,), beta, decay],
+        [
+            jax.ShapeDtypeStruct((n * DK + BLOCK, DK + DV), bf16),
+            jax.ShapeDtypeStruct((n * rows, DK + DV), bf16),
+        ],
+        [mask, pltpu.VMEM((MERGES, TILE // 2, TILE), bf16), *others],
+    )
+
+
+def delta_reach(half, seg_row, query, key, decay, solved):
+    rows = key.shape[0]
+    n = solved.shape[0] // rows
+    return half_call(
+        delta_reach_kernel,
+        "delta_reach",
+        20,
+        half,
+        [seg_row, (query,), (key,), decay, solved],
+        [
             jax.ShapeDtypeStruct((rows, n * DK), bf16),
             jax.ShapeDtypeStruct((rows, n * DV), f32),
         ],
-        compiler_params=params(mib),
-        cost_estimate=cost(6 * 10**9, 3 * 2**20),
-        name="delta_local",
-    )(half, seg_row, query, key, value, beta, decay)
+        setup_scratch(rows, n),
+    )
 
 
 def ids_of(ref):
@@ -654,22 +716,25 @@
 
     keep_half = core.reshape(1).astype(jnp.int32)
     give_half = 1 - keep_half
+    decay_rows = delta_decay.T
     local = partial(
         delta_local,
         seg_row=ids,
-        query=delta_query,
         key=delta_key,
         value=update_rule_payload,
         beta=delta_beta.T,
-        decay=delta_decay.T,
-    )
-    give_ma, give_reach, give_inner = local(give_half, 60)
+        decay=decay_rows,
+    )
+    reach = partial(
+        delta_reach, seg_row=ids, query=delta_query, key=delta_key, decay=decay_rows
+    )
+    give_ma, give_solved = local(give_half, 60)
     other_ma = swap_cores(give_ma, ranks)
     nearest, give_ma = lax.optimization_barrier((nearest, give_ma))
     same = [nearest]
     for _ in range(hops - 1):
         same.append(up_chip(same[-1], ranks))
-    keep_ma, keep_reach, keep_inner = local(keep_half, 60)
+    keep_ma, keep_solved = local(keep_half, 60)
     same, keep_ma, other_ma = lax.optimization_barrier((same, keep_ma, other_ma))
     chain = [own, *same]
     other = swap_cores(
@@ -705,12 +770,17 @@
     kt, v_all, window_ids, cosine, sine = window_arrays
     window_arrays = (window_ids, cosine, sine, kt, v_all)
     attn_mixed = attention_half(0, window_arrays, attn_query, attn_gate)
-    state, attn_mixed = lax.optimization_barrier((state, attn_mixed))
+    give_solved, chip_add = lax.optimization_barrier((give_solved, chip_add))
+    give_rows = reach(give_half, solved=give_solved)
+    state, attn_mixed, give_rows = lax.optimization_barrier((state, attn_mixed, give_rows))
+    leaving = chip_add
     for _ in range(hops - 1):
         (leaving,) = small_call(relay_kernel, "relay", [state_like], chip_map, chip_add, state)
         state = up_chip(leaving, ranks)
     attn_mixed = attention_half(1, window_arrays, attn_query, attn_gate, attn_mixed)
-    state, attn_mixed = lax.optimization_barrier((state, attn_mixed))
+    keep_solved, leaving = lax.optimization_barrier((keep_solved, leaving))
+    keep_rows = reach(keep_half, solved=keep_solved)
+    state, attn_mixed, keep_rows = lax.optimization_barrier((state, attn_mixed, keep_rows))
 
     final_like = jax.ShapeDtypeStruct((tall - BLOCK, DV), bf16)
     keep_state, pass_state = small_call(
@@ -719,9 +789,9 @@
     give_state = swap_cores(pass_state, ranks)
 
     gain = norm_gain.reshape(1, DV)
-    delta_mixed = delta_out(keep_half, keep_reach, keep_inner, keep_state, delta_gate, gain)
+    delta_mixed = delta_out(keep_half, *keep_rows, keep_state, delta_gate, gain)
     delta_mixed = delta_out(
-        give_half, give_reach, give_inner, give_state, delta_gate, gain, delta_mixed
+        give_half, *give_rows, give_state, delta_gate, gain, delta_mixed
     )
     return (attn_mixed, delta_mixed)
 

time: 52.1 us -> 51.4 us (0.987)
  waiting for transfers between devices: 4.75 us -> 1.12 us
  Pallas kernels: 30.2 us -> 31.9 us
  starting transfers between devices: 14.7 us -> 15.6 us
    ppermute x4, waiting for transfers between devices: 4.74 us -> 1.11 us  [up_chip(): return lax.ppermute(value, 'ctx', [(i, i + 2) for i in range(ranks - 2)])]
    pallas_call x2 -> x4, Pallas kernels: 15.4 us -> 17.2 us  [half_call(): pl.pallas_call(kernel, grid_spec=pltpu.PrefetchScalarGridSpec(num_scalar_...]
    ppermute x4, starting transfers between devices: 11 us -> 11.9 us  [up_chip(): return lax.ppermute(value, 'ctx', [(i, i + 2) for i in range(ranks - 2)])]
    unnamed x20 -> x24, local copies, waits for them, and re-layouts: 1.13 us -> 1.29 us
  transfers between devices with their start and end apart: 7 -> 7, of which waited for: 2 -> 1; matrix products, arithmetic and copies ran while one was open for 0% -> 0% of each run, Pallas kernels for 50% -> 55%
where the time goes in v7:
time: 51.4 us; the launch traced here: 51 us
  Pallas kernels  31.9 us (62%)
  starting transfers between devices  15.6 us (30%)
  local copies, waits for them, and re-layouts  1.36 us (3%)
  waiting for transfers between devices  1.12 us (2%)
  between operations  0.85 us (2%)
    pallas_call x4, Pallas kernels, half_call(): pl.pallas_call(kernel, grid_spec=pltpu.PrefetchScalarGridSpec(num_scalar_...  17.2 us
    ppermute x4, starting transfers between devices, up_chip(): return lax.ppermute(value, 'ctx', [(i, i + 2) for i in range(ranks - 2)])  11.9 us
    pallas_call x2, Pallas kernels, attention_half(): pl.pallas_call(attention_kernel, grid=(steps,), in_specs=in_specs, out_sp...  7.65 us
    ppermute x3, starting transfers between devices, swap_cores(): return lax.ppermute(value, 'ctx', [(i, i ^ 1) for i in range(ranks)])  3.69 us
    pallas_call x5, Pallas kernels, small_call(): pl.pallas_call(kernel, in_specs=[SMEM] * scalars + [VMEM] * (len(args) -...  3.58 us
    pallas_call x2, Pallas kernels, delta_out(): pl.pallas_call(delta_out_kernel, grid_spec=pltpu.PrefetchScalarGridSpec(n...  3.51 us
    unnamed x24, local copies, waits for them, and re-layouts  1.29 us
    ppermute x4, waiting for transfers between devices, up_chip(): return lax.ppermute(value, 'ctx', [(i, i + 2) for i in range(ranks - 2)])  1.11 us
  transfers between devices with their start and end apart: 7, of which 1 were waited for; matrix products, arithmetic and copies ran while one was open for 0% of the time, Pallas kernels for 55%

profile of v7, /device:TPU:9, one launch (start us, length us, event | category | flops | bytes accessed | tf_op | source)
XLA Modules:
  0.0 51.0 jit_solution(7088871953179854732)
XLA Ops:
  0.6 1.7 %pack.1.rest_0_ = bf16[272,512]{1,0:T(8,128)(2,1)} custom-call(s32[1,256]{1,0:T(1,128)} %bitcast.11, bf16[256,256]{1,0:T(8,128)(2,1)} %key_ref.1, bf16[256,256]{1,0:T(8,128)(2,1)} %value_ref.1), custom_call_target="tpu_custom_call" | custom-call | flops 100000000 | bytes 1048576 | tf_op jit(solution)/shard_map/pack/pallas_call | solution.py:475
  2.4 3.2 %collective-permute-start = (bf16[272,512]{1,0:T(8,128)(2,1)}, bf16[272,512]{1,0:T(8,128)(2,1)S(1)}, u32[]{:S(2)}, u32[]{:S(2)}) collective-permute-start(bf16[272,512]{1,0:T(8,128)(2,1)} %pack.1.rest_0_), channel_id=1, source_target_pairs={{0,2},{1,3},{2,4},{3,5},{4,6},{5,7},{8,10},{9,11},{10,12},{11,13},... | collective-permute-start | bytes 835592 | tf_op jit(solution)/shard_map/ppermute | solution.py:676
  5.6 7.1 %delta_local.2 = (bf16[1040,256]{1,0:T(8,128)(2,1)}, bf16[2048,256]{1,0:T(8,128)(2,1)}) custom-call(s32[1]{0:T(128)S(6)} %sub.3.half_ref, s32[1,256]{1,0:T(1,128)} %bitcast.12, bf16[256,1024]{1,0:T(8,128)(2,1)} %k_ref.7, bf16[256,2048]{1,0:T(8,128)(2,1)} %v_ref.3, f32[16,256]{1,0:T(8,128)} %bitcast.20, f32[16,256]{1,0:T(8,128)} %bitcast.16), custom_call_target="tpu_custom_call" | custom-call | flops 4000000000 | bytes 3145728 | tf_op jit(solution)/shard_map/delta_local/pallas_call | solution.py:353
  12.7 1.0 %collective-permute-start.2 = (bf16[1040,256]{1,0:T(8,128)(2,1)}, bf16[1040,256]{1,0:T(8,128)(2,1)S(1)}, u32[]{:S(2)}, u32[]{:S(2)}) collective-permute-start(bf16[1040,256]{1,0:T(8,128)(2,1)} %get-tuple-element.35), channel_id=1, source_target_pairs={{0,1},{1,0},{2,3},{3,2},{4,5},{5,4},{6,7},{7,6},{8,9},{9,8},{10,11... | collective-permute-start | bytes 1597448 | tf_op jit(solution)/shard_map/ppermute | solution.py:680
  13.6 3.3 %collective-permute-start.1 = (bf16[272,512]{1,0:T(8,128)(2,1)S(1)}, bf16[272,512]{1,0:T(8,128)(2,1)S(1)}, u32[]{:S(2)}, u32[]{:S(2)}) collective-permute-start(bf16[272,512]{1,0:T(8,128)(2,1)S(1)} %collective-permute-done.rest_1_), channel_id=1, source_target_pairs={{0,2},{1,3},{2,4},{3,5},{4,6},{5,7},{8,10},{9,11},{10,12},{11,13},... | collective-permute-start | bytes 835592 | tf_op jit(solution)/shard_map/ppermute | solution.py:676
  17.0 7.1 %delta_local.3 = (bf16[1040,256]{1,0:T(8,128)(2,1)}, bf16[2048,256]{1,0:T(8,128)(2,1)}) custom-call(s32[1]{0:T(128)} %bitcast.half_ref.core_ref, s32[1,256]{1,0:T(1,128)} %bitcast.13, bf16[256,1024]{1,0:T(8,128)(2,1)} %k_ref.7, bf16[256,2048]{1,0:T(8,128)(2,1)} %v_ref.3, f32[16,256]{1,0:T(8,128)} %bitcast.21, f32[16,256]{1,0:T(8,128)} %bitcast.17), custom_call_target="tpu_custom_call" | custom-call | flops 4000000000 | bytes 3145728 | tf_op jit(solution)/shard_map/delta_local/pallas_call | solution.py:353
  24.1 0.0 copy-start.11
  24.2 0.1 select_bitcast_fusion.1
  24.2 0.1 pad_maximum_fusion
  24.3 0.6 %collective-permute-start.4 = (bf16[2,272,512]{2,1,0:T(8,128)(2,1)S(1)}, bf16[2,272,512]{2,1,0:T(8,128)(2,1)S(1)}, u32[]{:S(2)}, u32[]{:S(2)}) collective-permute-start(bf16[2,272,512]{2,1,0:T(8,128)(2,1)S(1)} %pad_maximum_fusion), channel_id=1, source_target_pairs={{0,1},{1,0},{2,3},{3,2},{4,5},{5,4},{6,7},{7,6},{8,9},{9,8},{10,11... | collective-permute-start | bytes 1671176 | tf_op jit(solution)/shard_map/ppermute | solution.py:680
  24.9 0.4 copy-done.2
  25.3 0.3 compose.1
  25.7 0.0 copy-start.4
  25.7 3.2 %collective-permute-start.3 = (bf16[1040,128]{1,0:T(8,128)(2,1)S(1)}, bf16[1040,128]{1,0:T(8,128)(2,1)S(1)}, u32[]{:S(2)}, u32[]{:S(2)}) collective-permute-start(bf16[1040,128]{1,0:T(8,128)(2,1)S(1)} %get-tuple-element.43.add_ref), channel_id=1, source_target_pairs={{0,2},{1,3},{2,4},{3,5},{4,6},{5,7},{8,10},{9,11},{10,12},{11,13},... | collective-permute-start | bytes 798728 | tf_op jit(solution)/shard_map/ppermute | solution.py:676
  28.9 0.0 copy-start.6
  28.9 1.4 %delta_reach.2 = (bf16[256,1024]{1,0:T(8,128)(2,1)S(1)}, f32[256,1024]{1,0:T(8,128)S(1)}) custom-call(s32[1]{0:T(128)S(6)} %sub.3.half_ref, s32[1,256]{1,0:T(1,128)S(1)} %bitcast.14, bf16[256,1024]{1,0:T(8,128)(2,1)S(1)} %copy-done.7, bf16[256,1024]{1,0:T(8,128)(2,1)S(1)} %copy-done.8, f32[16,256]{1,0:T(8,128)S(1)} %bitcast.18, bf16[2048,256]{1,0:T(8,128)(2,1)S(1)} %copy-done.11), custom_call_target="tpu_custom_call" | custom-call | flops 4000000000 | bytes 3145728 | tf_op jit(solution)/shard_map/delta_reach/pallas_call | solution.py:353
  30.4 0.0 copy-start.5
  30.4 0.1 broadcast_in_dim.2.freq_ref
  30.5 0.9 %window.1 = (bf16[256,1280]{1,0:T(8,128)(2,1)S(1)}, bf16[1280,256]{1,0:T(8,128)(2,1)S(1)}, f32[1,1280]{1,0:T(1,128)S(1)}, f32[256,128]{1,0:T(8,128)S(1)}, f32[256,128]{1,0:T(8,128)S(1)}) custom-call(f32[32,128]{1,0:T(8,128)S(1)} %broadcast_in_dim.2.freq_ref, bf16[272,512]{1,0:T(8,128)(2,1)S(1)} %copy-done.1, ...), custom_call_target="tpu_custom_call" | custom-call | flops 100000000 | bytes 1048576 | tf_op jit(solution)/shard_map/window/pallas_call | solution.py:475
  31.4 0.2 copy-done.5
  31.6 3.8 %attention.2.rest_0_ = bf16[256,2048]{1,0:T(8,128)(2,1)} custom-call(f32[1,1280]{1,0:T(1,128)S(1)} %get-tuple-element.46.ids_ref, f32[256,128]{1,0:T(8,128)S(1)} %get-tuple-element.47.cos_ref, f32[256,128]{1,0:T(8,128)S(1)} %get-tuple-element.48.sin_ref, bf16[256,1280]{1,0:T(8,128)(2,1)S(1)} %get-tuple-element.49.kt_ref, ...), custom_call_target="tpu_custom_call" | custom-call | flops 5000000000 | bytes 3145728 | tf_op jit(solution)/shard_map/attention/pallas_call | solution.py:661
  35.4 0.2 relay.1
  35.7 2.2 %collective-permute-start.5 = (bf16[1040,128]{1,0:T(8,128)(2,1)S(1)}, bf16[1040,128]{1,0:T(8,128)(2,1)S(1)}, u32[]{:S(2)}, u32[]{:S(2)}) collective-permute-start(bf16[1040,128]{1,0:T(8,128)(2,1)S(1)} %relay.1), channel_id=1, source_target_pairs={{0,2},{1,3},{2,4},{3,5},{4,6},{5,7},{8,10},{9,11},{10,12},{11,13},... | collective-permute-start | bytes 798728 | tf_op jit(solution)/shard_map/ppermute | solution.py:676
  37.9 3.8 %attention.3 = bf16[256,2048]{1,0:T(8,128)(2,1)} custom-call(f32[1,1280]{1,0:T(1,128)S(1)} %get-tuple-element.46.ids_ref, f32[256,128]{1,0:T(8,128)S(1)} %get-tuple-element.47.cos_ref, f32[256,128]{1,0:T(8,128)S(1)} %get-tuple-element.48.sin_ref, bf16[256,1280]{1,0:T(8,128)(2,1)S(1)} %get-tuple-element.49.kt_ref, ...), custom_call_target="tpu_custom_call", output_to_operand_aliasing={{}: (7, {})} | custom-call | flops 5000000000 | bytes 3145728 | tf_op jit(solution)/shard_map/attention/pallas_call | solution.py:661
  41.8 1.5 %delta_reach.3 = (bf16[256,1024]{1,0:T(8,128)(2,1)S(1)}, f32[256,1024]{1,0:T(8,128)S(1)}) custom-call(s32[1]{0:T(128)} %bitcast.half_ref.core_ref, s32[1,256]{1,0:T(1,128)S(1)} %bitcast.15, bf16[256,1024]{1,0:T(8,128)(2,1)S(1)} %copy-done.7, bf16[256,1024]{1,0:T(8,128)(2,1)S(1)} %copy-done.8, f32[16,256]{1,0:T(8,128)S(1)} %bitcast.19, ...), custom_call_target="tpu_custom_call" | custom-call | flops 4000000000 | bytes 3145728 | tf_op jit(solution)/shard_map/delta_reach/pallas_call | solution.py:353
  43.2 0.0 copy-start
  43.2 1.1 %collective-permute-done.5.state_ref = bf16[1040,128]{1,0:T(8,128)(2,1)S(1)} collective-permute-done((bf16[1040,128]{1,0:T(8,128)(2,1)S(1)}, bf16[1040,128]{1,0:T(8,128)(2,1)S(1)}, u32[]{:S(2)}, u32[]{:S(2)}) %collective-permute-start.5) | collective-permute-done | bytes 266272 | tf_op jit(solution)/shard_map/ppermute | solution.py:676
  44.3 0.4 arrive.1
  44.7 2.1 %collective-permute-start.6 = (bf16[1024,128]{1,0:T(8,128)(2,1)S(1)}, bf16[1024,128]{1,0:T(8,128)(2,1)S(1)}, u32[]{:S(2)}, u32[]{:S(2)}) collective-permute-start(bf16[1024,128]{1,0:T(8,128)(2,1)S(1)} %get-tuple-element.64), channel_id=1, source_target_pairs={{0,1},{1,0},{2,3},{3,2},{4,5},{5,4},{6,7},{7,6},{8,9},{9,8},{10,11... | collective-permute-start | bytes 786440 | tf_op jit(solution)/shard_map/ppermute | solution.py:680
  46.8 0.7 %copy-done.3 = f32[128]{0:T(128)S(1)} copy-done((f32[128]{0:T(128)S(1)}, f32[128]{0:T(128)}, u32[]{:S(2)}) %copy-start.3) | copy-done | bytes 536
  47.4 1.8 %delta_out.2.rest_0_ = bf16[256,2048]{1,0:T(8,128)(2,1)} custom-call(s32[1]{0:T(128)} %bitcast.half_ref.core_ref, bf16[256,1024]{1,0:T(8,128)(2,1)S(1)} %get-tuple-element.65.reach_ref, f32[256,1024]{1,0:T(8,128)S(1)} %get-tuple-element.66.inner_ref, bf16[1024,128]{1,0:T(8,128)(2,1)S(1)} %get-tuple-element.67.state_ref, bf16[256,2048]{1,0:T(8,128)(2,1)S(1)} %copy-done, ...), custom_call_target="tpu_custom_call" | custom-call | flops 100000000 | bytes 3145728 | tf_op jit(solution)/shard_map/delta_out/pallas_call | solution.py:524
  49.2 1.8 %delta_out.3 = bf16[256,2048]{1,0:T(8,128)(2,1)} custom-call(s32[1]{0:T(128)S(6)} %sub.3.half_ref, bf16[256,1024]{1,0:T(8,128)(2,1)S(1)} %get-tuple-element.61.reach_ref, f32[256,1024]{1,0:T(8,128)S(1)} %get-tuple-element.62.inner_ref, bf16[1024,128]{1,0:T(8,128)(2,1)S(1)} %collective-permute-done.6.state_ref, ...), custom_call_target="tpu_custom_call", output_to_operand_aliasing={{}: (6, {})} | custom-call | flops 100000000 | bytes 3145728 | tf_op jit(solution)/shard_map/delta_out/pallas_call | solution.py:524
  (23 shorter events, 0.1 us)
Async XLA Ops:
  2.4 11.3 %collective-permute-start = (bf16[272,512]{1,0:T(8,128)(2,1)}, bf16[272,512]{1,0:T(8,128)(2,1)S(1)}, u32[]{:S(2)}, u32[]{:S(2)}) collective-permute-start(bf16[272,512]{1,0:T(8,128)(2,1)} %pack.1.rest_0_), channel_id=1, source_target_pairs={{0,2},{1,3},{2,4},{3,5},{4,6},{5,7},{8,10},{9,11},{10,12},{11,13},... | collective-permute-start | bytes 835592 | tf_op jit(solution)/shard_map/ppermute | solution.py:676
  12.7 11.4 %collective-permute-start.2 = (bf16[1040,256]{1,0:T(8,128)(2,1)}, bf16[1040,256]{1,0:T(8,128)(2,1)S(1)}, u32[]{:S(2)}, u32[]{:S(2)}) collective-permute-start(bf16[1040,256]{1,0:T(8,128)(2,1)} %get-tuple-element.35), channel_id=1, source_target_pairs={{0,1},{1,0},{2,3},{3,2},{4,5},{5,4},{6,7},{7,6},{8,9},{9,8},{10,11... | collective-permute-start | bytes 1597448 | tf_op jit(solution)/shard_map/ppermute | solution.py:680
  13.6 10.5 %copy-start.1 = (bf16[272,512]{1,0:T(8,128)(2,1)S(1)}, bf16[272,512]{1,0:T(8,128)(2,1)}, u32[]{:S(2)}) copy-start(bf16[272,512]{1,0:T(8,128)(2,1)} %pack.1.rest_0_) | copy-start | bytes 835588
  13.6 10.5 %collective-permute-start.1 = (bf16[272,512]{1,0:T(8,128)(2,1)S(1)}, bf16[272,512]{1,0:T(8,128)(2,1)S(1)}, u32[]{:S(2)}, u32[]{:S(2)}) collective-permute-start(bf16[272,512]{1,0:T(8,128)(2,1)S(1)} %collective-permute-done.rest_1_), channel_id=1, source_target_pairs={{0,2},{1,3},{2,4},{3,5},{4,6},{5,7},{8,10},{9,11},{10,12},{11,13},... | collective-permute-start | bytes 835592 | tf_op jit(solution)/shard_map/ppermute | solution.py:676
  24.1 4.7 %copy-start.11 = (bf16[2048,256]{1,0:T(8,128)(2,1)S(1)}, bf16[2048,256]{1,0:T(8,128)(2,1)}, u32[]{:S(2)}) copy-start(bf16[2048,256]{1,0:T(8,128)(2,1)} %get-tuple-element.51.solved_ref) | copy-start | bytes 3145732
  24.2 1.1 %copy-start.2 = (bf16[1040,256]{1,0:T(8,128)(2,1)S(1)}, bf16[1040,256]{1,0:T(8,128)(2,1)}, u32[]{:S(2)}) copy-start(bf16[1040,256]{1,0:T(8,128)(2,1)} %get-tuple-element.38.mine_ref) | copy-start | bytes 1597444
  24.3 6.1 %collective-permute-start.4 = (bf16[2,272,512]{2,1,0:T(8,128)(2,1)S(1)}, bf16[2,272,512]{2,1,0:T(8,128)(2,1)S(1)}, u32[]{:S(2)}, u32[]{:S(2)}) collective-permute-start(bf16[2,272,512]{2,1,0:T(8,128)(2,1)S(1)} %pad_maximum_fusion), channel_id=1, source_target_pairs={{0,1},{1,0},{2,3},{3,2},{4,5},{5,4},{6,7},{7,6},{8,9},{9,8},{10,11... | collective-permute-start | bytes 1671176 | tf_op jit(solution)/shard_map/ppermute | solution.py:680
  25.3 3.5 %copy-start.7 = (bf16[256,1024]{1,0:T(8,128)(2,1)S(1)}, bf16[256,1024]{1,0:T(8,128)(2,1)}, u32[]{:S(2)}) copy-start(bf16[256,1024]{1,0:T(8,128)(2,1)} %q_ref.7) | copy-start | bytes 1572868
  25.3 3.5 %copy-start.8 = (bf16[256,1024]{1,0:T(8,128)(2,1)S(1)}, bf16[256,1024]{1,0:T(8,128)(2,1)}, u32[]{:S(2)}) copy-start(bf16[256,1024]{1,0:T(8,128)(2,1)} %k_ref.7) | copy-start | bytes 1572868
  25.3 3.5 %copy-start.9 = (f32[256,16]{0,1:T(8,128)S(1)}, f32[256,16]{0,1:T(8,128)}, u32[]{:S(2)}) copy-start(f32[256,16]{0,1:T(8,128)} %param.21) | copy-start | bytes 49156
  25.7 3.2 %copy-start.4 = (s32[256]{0:T(256)S(1)}, s32[256]{0:T(256)}, u32[]{:S(2)}) copy-start(s32[256]{0:T(256)} %param.12) | copy-start | bytes 3076
  25.7 9.7 %collective-permute-start.3 = (bf16[1040,128]{1,0:T(8,128)(2,1)S(1)}, bf16[1040,128]{1,0:T(8,128)(2,1)S(1)}, u32[]{:S(2)}, u32[]{:S(2)}) collective-permute-start(bf16[1040,128]{1,0:T(8,128)(2,1)S(1)} %get-tuple-element.43.add_ref), channel_id=1, source_target_pairs={{0,2},{1,3},{2,4},{3,5},{4,6},{5,7},{8,10},{9,11},{10,12},{11,13},... | collective-permute-start | bytes 798728 | tf_op jit(solution)/shard_map/ppermute | solution.py:676
  28.9 2.5 %copy-start.6 = (bf16[256,2048]{1,0:T(8,128)(2,1)S(1)}, bf16[256,2048]{1,0:T(8,128)(2,1)}, u32[]{:S(2)}) copy-start(bf16[256,2048]{1,0:T(8,128)(2,1)} %gate_ref.5) | copy-start | bytes 3145732
  30.4 1.2 %copy-start.5 = (bf16[256,2048]{1,0:T(8,128)(2,1)S(1)}, bf16[256,2048]{1,0:T(8,128)(2,1)}, u32[]{:S(2)}) copy-start(bf16[256,2048]{1,0:T(8,128)(2,1)} %q_ref.6) | copy-start | bytes 3145732
  35.7 8.7 %collective-permute-start.5 = (bf16[1040,128]{1,0:T(8,128)(2,1)S(1)}, bf16[1040,128]{1,0:T(8,128)(2,1)S(1)}, u32[]{:S(2)}, u32[]{:S(2)}) collective-permute-start(bf16[1040,128]{1,0:T(8,128)(2,1)S(1)} %relay.1), channel_id=1, source_target_pairs={{0,2},{1,3},{2,4},{3,5},{4,6},{5,7},{8,10},{9,11},{10,12},{11,13},... | collective-permute-start | bytes 798728 | tf_op jit(solution)/shard_map/ppermute | solution.py:676
  37.9 3.8 %copy-start.10 = (bf16[2048,256]{1,0:T(8,128)(2,1)S(1)}, bf16[2048,256]{1,0:T(8,128)(2,1)}, u32[]{:S(2)}) copy-start(bf16[2048,256]{1,0:T(8,128)(2,1)} %get-tuple-element.57.solved_ref) | copy-start | bytes 3145732
  43.2 3.6 %copy-start = (bf16[256,2048]{1,0:T(8,128)(2,1)S(1)}, bf16[256,2048]{1,0:T(8,128)(2,1)}, u32[]{:S(2)}) copy-start(bf16[256,2048]{1,0:T(8,128)(2,1)} %gate_ref.7) | copy-start | bytes 3145732
  44.7 4.5 %collective-permute-start.6 = (bf16[1024,128]{1,0:T(8,128)(2,1)S(1)}, bf16[1024,128]{1,0:T(8,128)(2,1)S(1)}, u32[]{:S(2)}, u32[]{:S(2)}) collective-permute-start(bf16[1024,128]{1,0:T(8,128)(2,1)S(1)} %get-tuple-element.64), channel_id=1, source_target_pairs={{0,1},{1,0},{2,3},{3,2},{4,5},{5,4},{6,7},{7,6},{8,9},{9,8},{10,11... | collective-permute-start | bytes 786440 | tf_op jit(solution)/shard_map/ppermute | solution.py:680
  46.8 0.7 %copy-start.3 = (f32[128]{0:T(128)S(1)}, f32[128]{0:T(128)}, u32[]{:S(2)}) copy-start(f32[128]{0:T(128)} %param.23) | copy-start | bytes 1540

commit v8 on v7

--- a/solution.py
+++ b/solution.py
@@ -61,30 +61,45 @@
     return jnp.concatenate([m[i : i + b] for i in range(0, TILE, 2 * b)], axis=0)
 
 
-def block_inverses(mats):
+def fold(m):
     row = lax.broadcasted_iota(jnp.int32, (BLOCK, TILE), 0)
     lane = lax.broadcasted_iota(jnp.int32, (BLOCK, TILE), 1)
+    group = lane // BLOCK
+    z = jnp.where(group == 0, m[:BLOCK], 0.0)
+    for r in range(1, TILE // BLOCK):
+        z = jnp.where(group == r, m[r * BLOCK : (r + 1) * BLOCK], z)
+    return jnp.where(row > lax.rem(lane, BLOCK), z, 0.0).astype(bf16)
+
+
+def fill_spread(spread_ref):
+    row = lax.broadcasted_iota(jnp.int32, (TILE, TILE), 0)
+    lane = lax.broadcasted_iota(jnp.int32, (TILE, TILE), 1)
+    base = row - lane // BLOCK * BLOCK
+    for k in range(BLOCK - 1):
+        spread_ref[:, k * TILE : (k + 1) * TILE] = jnp.where(base == k, 1.0, 0.0).astype(bf16)
+
+
+def block_inverses(folded, spread_ref):
+    row = lax.broadcasted_iota(jnp.int32, (BLOCK, TILE), 0)
+    lane = lax.broadcasted_iota(jnp.int32, (BLOCK, TILE), 1)
+    group = lane // BLOCK
     within = lax.rem(lane, BLOCK)
-    group = lane // BLOCK
-    folded = []
-    for m in mats:
-        z = jnp.where(group == 0, m[:BLOCK], 0.0)
-        for r in range(1, TILE // BLOCK):
-            z = jnp.where(group == r, m[r * BLOCK : (r + 1) * BLOCK], z)
-        folded.append(jnp.where(row > within, z, 0.0))
-    xs = [jnp.where(row == within, 1.0, 0.0)] * len(mats)
-    small = 8
+    spread = dot(jnp.concatenate(folded, axis=0), spread_ref[...])
+    unit = jnp.where(row == within, 1.0, 0.0)
+    small = BLOCK // 2
+    out = []
+    tops = [unit[:small]] * len(folded)
+    lows = [unit[small:]] * len(folded)
     for k in range(BLOCK - 1):
-        low = 0 if k < small - 1 else small
-        at = (group * BLOCK + k)[low:]
-        for i, z in enumerate(folded):
-            spread = jnp.take_along_axis(z[low:], at, axis=1, mode="promise_in_bounds")
-            x = xs[i]
-            new = x[low:] + spread * x[k : k + 1]
-            xs[i] = new if low == 0 else jnp.concatenate([x[:low], new], axis=0)
-    out = []
-    for x in xs:
-        x = jnp.where(row > within, x, 0.0)
+        at = slice(k * TILE, (k + 1) * TILE)
+        for i in range(len(folded)):
+            rows = spread[i * BLOCK : (i + 1) * BLOCK, at]
+            source = tops[i][k : k + 1] if k < small else lows[i][k - small : k - small + 1]
+            if k < small - 1:
+                tops[i] = tops[i] + rows[:small] * source
+            lows[i] = lows[i] + rows[small:] * source
+    for top, low in zip(tops, lows):
+        x = jnp.where(row > within, jnp.concatenate([top, low], axis=0), 0.0)
         out.append(
             jnp.concatenate(
                 [jnp.where(group == r, x, 0.0) for r in range(TILE // BLOCK)], axis=0
@@ -143,12 +158,14 @@
     solved_ref,
     mask_ref,
     level_ref,
+    spread_ref,
     crow_ref,
     ccol_ref,
     first_ref,
 ):
     rows = k_ref.shape[0]
     n = v_ref.shape[1] // DV
+    fill_spread(spread_ref)
     seg_row = setup(
         half_ref, seg_ref, decay_ref, n, mask_ref, crow_ref, ccol_ref, first_ref, beta_ref
     )
@@ -201,32 +218,30 @@
         for w in pair:
             d11 = jnp.concatenate(w["d"][:top], axis=0)
             d2 = jnp.concatenate(w["d"][top:], axis=0)
-            w["d"] = [d11, d2[:, TILE:]]
+            blocks = [d11, d2[:, TILE:]]
+            w["folded"] = [fold(m) for m in blocks]
+            w["d"] = [m.astype(bf16) for m in blocks]
             w["d21"] = d2[:, :TILE].astype(bf16)
             w["right"] = jnp.concatenate(w["right"], axis=0)
         yield
 
-    def invert(kk):
-        pair = pairs[kk]
-        mats = [m for w in pair for m in w["d"]]
-        inverses = block_inverses(mats)
-        yield
-        mats = [m.astype(bf16) for m in mats]
+    def invert():
+        work = [w for pair in pairs for w in pair]
+        mats = [m for w in work for m in w["d"]]
+        inverses = block_inverses([z for w in work for z in w["folded"]], spread_ref)
         zeros = jnp.zeros((TILE // 2, TILE), bf16)
         for level in range(MERGES):
             b = BLOCK << level
             keep = level_ref[level]
             picked = [odd_rows(m, b) * keep for m in mats]
             ys = [(p.astype(f32) + dot(p, x)).astype(bf16) for p, x in zip(picked, inverses)]
-            yield
             odds = [odd_rows(x, b) for x in inverses]
             odds = [
                 x + (y.astype(f32) + dot(x, interleave(zeros, y, b))).astype(bf16)
                 for x, y in zip(odds, ys)
             ]
             inverses = [interleave(even_rows(x, b), o, b) for x, o in zip(inverses, odds)]
-            yield
-        for i, w in enumerate(pair):
+        for i, w in enumerate(work):
             w["x"] = inverses[2 * i : 2 * i + 2]
 
     def finish(kk):
@@ -253,7 +268,9 @@
                 ).astype(bf16)
             yield
 
-    pipeline([elementwise, invert, finish], n // 2)
+    pipeline([elementwise], n // 2)
+    invert()
+    pipeline([finish], n // 2)
 
 
 def add_strips(a, b):
@@ -389,7 +406,12 @@
             jax.ShapeDtypeStruct((n * DK + BLOCK, DK + DV), bf16),
             jax.ShapeDtypeStruct((n * rows, DK + DV), bf16),
         ],
-        [mask, pltpu.VMEM((MERGES, TILE // 2, TILE), bf16), *others],
+        [
+            mask,
+            pltpu.VMEM((MERGES, TILE // 2, TILE), bf16),
+            pltpu.VMEM((TILE, (BLOCK - 1) * TILE), bf16),
+            *others,
+        ],
     )
 
 

time: 51.4 us -> 51.4 us (level)
  no operation moved by 1% of the time
where the time goes in v8:
time: 51.4 us; the launch traced here: 51 us
  Pallas kernels  31.9 us (62%)
  starting transfers between devices  15.6 us (30%)
  local copies, waits for them, and re-layouts  1.37 us (3%)
  waiting for transfers between devices  1.13 us (2%)
  between operations  0.85 us (2%)
    pallas_call x4, Pallas kernels, half_call(): pl.pallas_call(kernel, grid_spec=pltpu.PrefetchScalarGridSpec(num_scalar_...  17.2 us
    ppermute x4, starting transfers between devices, up_chip(): return lax.ppermute(value, 'ctx', [(i, i + 2) for i in range(ranks - 2)])  11.9 us
    pallas_call x2, Pallas kernels, attention_half(): pl.pallas_call(attention_kernel, grid=(steps,), in_specs=in_specs, out_sp...  7.65 us
    ppermute x3, starting transfers between devices, swap_cores(): return lax.ppermute(value, 'ctx', [(i, i ^ 1) for i in range(ranks)])  3.67 us
    pallas_call x5, Pallas kernels, small_call(): pl.pallas_call(kernel, in_specs=[SMEM] * scalars + [VMEM] * (len(args) -...  3.58 us
    pallas_call x2, Pallas kernels, delta_out(): pl.pallas_call(delta_out_kernel, grid_spec=pltpu.PrefetchScalarGridSpec(n...  3.51 us
    unnamed x24, local copies, waits for them, and re-layouts  1.3 us
    ppermute x4, waiting for transfers between devices, up_chip(): return lax.ppermute(value, 'ctx', [(i, i + 2) for i in range(ranks - 2)])  1.12 us
  transfers between devices with their start and end apart: 7, of which 1 were waited for; matrix products, arithmetic and copies ran while one was open for 0% of the time, Pallas kernels for 55%

profile of v8, /device:TPU:9, one launch (start us, length us, event | category | flops | bytes accessed | tf_op | source)
XLA Modules:
  0.0 51.0 jit_solution(4873326079374397208)
XLA Ops:
  0.6 1.7 %pack.1.rest_0_ = bf16[272,512]{1,0:T(8,128)(2,1)} custom-call(s32[1,256]{1,0:T(1,128)} %bitcast.11, bf16[256,256]{1,0:T(8,128)(2,1)} %key_ref.1, bf16[256,256]{1,0:T(8,128)(2,1)} %value_ref.1), custom_call_target="tpu_custom_call" | custom-call | flops 100000000 | bytes 1048576 | tf_op jit(solution)/shard_map/pack/pallas_call | solution.py:497
  2.4 3.2 %collective-permute-start = (bf16[272,512]{1,0:T(8,128)(2,1)}, bf16[272,512]{1,0:T(8,128)(2,1)S(1)}, u32[]{:S(2)}, u32[]{:S(2)}) collective-permute-start(bf16[272,512]{1,0:T(8,128)(2,1)} %pack.1.rest_0_), channel_id=1, source_target_pairs={{0,2},{1,3},{2,4},{3,5},{4,6},{5,7},{8,10},{9,11},{10,12},{11,13},... | collective-permute-start | bytes 835592 | tf_op jit(solution)/shard_map/ppermute | solution.py:698
  5.6 7.1 %delta_local.2 = (bf16[1040,256]{1,0:T(8,128)(2,1)}, bf16[2048,256]{1,0:T(8,128)(2,1)}) custom-call(s32[1]{0:T(128)S(6)} %sub.3.half_ref, s32[1,256]{1,0:T(1,128)} %bitcast.12, bf16[256,1024]{1,0:T(8,128)(2,1)} %k_ref.7, bf16[256,2048]{1,0:T(8,128)(2,1)} %v_ref.3, f32[16,256]{1,0:T(8,128)} %bitcast.20, f32[16,256]{1,0:T(8,128)} %bitcast.16), custom_call_target="tpu_custom_call" | custom-call | flops 4000000000 | bytes 3145728 | tf_op jit(solution)/shard_map/delta_local/pallas_call | solution.py:370
  12.7 1.0 %collective-permute-start.2 = (bf16[1040,256]{1,0:T(8,128)(2,1)}, bf16[1040,256]{1,0:T(8,128)(2,1)S(1)}, u32[]{:S(2)}, u32[]{:S(2)}) collective-permute-start(bf16[1040,256]{1,0:T(8,128)(2,1)} %get-tuple-element.35), channel_id=1, source_target_pairs={{0,1},{1,0},{2,3},{3,2},{4,5},{5,4},{6,7},{7,6},{8,9},{9,8},{10,11... | collective-permute-start | bytes 1597448 | tf_op jit(solution)/shard_map/ppermute | solution.py:702
  13.7 3.3 %collective-permute-start.1 = (bf16[272,512]{1,0:T(8,128)(2,1)S(1)}, bf16[272,512]{1,0:T(8,128)(2,1)S(1)}, u32[]{:S(2)}, u32[]{:S(2)}) collective-permute-start(bf16[272,512]{1,0:T(8,128)(2,1)S(1)} %collective-permute-done.rest_1_), channel_id=1, source_target_pairs={{0,2},{1,3},{2,4},{3,5},{4,6},{5,7},{8,10},{9,11},{10,12},{11,13},... | collective-permute-start | bytes 835592 | tf_op jit(solution)/shard_map/ppermute | solution.py:698
  17.0 7.2 %delta_local.3 = (bf16[1040,256]{1,0:T(8,128)(2,1)}, bf16[2048,256]{1,0:T(8,128)(2,1)}) custom-call(s32[1]{0:T(128)} %bitcast.half_ref.core_ref, s32[1,256]{1,0:T(1,128)} %bitcast.13, bf16[256,1024]{1,0:T(8,128)(2,1)} %k_ref.7, bf16[256,2048]{1,0:T(8,128)(2,1)} %v_ref.3, f32[16,256]{1,0:T(8,128)} %bitcast.21, f32[16,256]{1,0:T(8,128)} %bitcast.17), custom_call_target="tpu_custom_call" | custom-call | flops 4000000000 | bytes 3145728 | tf_op jit(solution)/shard_map/delta_local/pallas_call | solution.py:370
  24.2 0.0 copy-start.11
  24.2 0.1 select_bitcast_fusion.1
  24.2 0.1 pad_maximum_fusion
  24.3 0.6 %collective-permute-start.4 = (bf16[2,272,512]{2,1,0:T(8,128)(2,1)S(1)}, bf16[2,272,512]{2,1,0:T(8,128)(2,1)S(1)}, u32[]{:S(2)}, u32[]{:S(2)}) collective-permute-start(bf16[2,272,512]{2,1,0:T(8,128)(2,1)S(1)} %pad_maximum_fusion), channel_id=1, source_target_pairs={{0,1},{1,0},{2,3},{3,2},{4,5},{5,4},{6,7},{7,6},{8,9},{9,8},{10,11... | collective-permute-start | bytes 1671176 | tf_op jit(solution)/shard_map/ppermute | solution.py:702
  25.0 0.4 copy-done.2
  25.4 0.3 compose.1
  25.7 0.0 copy-start.4
  25.7 3.2 %collective-permute-start.3 = (bf16[1040,128]{1,0:T(8,128)(2,1)S(1)}, bf16[1040,128]{1,0:T(8,128)(2,1)S(1)}, u32[]{:S(2)}, u32[]{:S(2)}) collective-permute-start(bf16[1040,128]{1,0:T(8,128)(2,1)S(1)} %get-tuple-element.43.add_ref), channel_id=1, source_target_pairs={{0,2},{1,3},{2,4},{3,5},{4,6},{5,7},{8,10},{9,11},{10,12},{11,13},... | collective-permute-start | bytes 798728 | tf_op jit(solution)/shard_map/ppermute | solution.py:698
  28.9 0.0 copy-start.6
  28.9 1.5 %delta_reach.2 = (bf16[256,1024]{1,0:T(8,128)(2,1)S(1)}, f32[256,1024]{1,0:T(8,128)S(1)}) custom-call(s32[1]{0:T(128)S(6)} %sub.3.half_ref, s32[1,256]{1,0:T(1,128)S(1)} %bitcast.14, bf16[256,1024]{1,0:T(8,128)(2,1)S(1)} %copy-done.7, bf16[256,1024]{1,0:T(8,128)(2,1)S(1)} %copy-done.8, f32[16,256]{1,0:T(8,128)S(1)} %bitcast.18, bf16[2048,256]{1,0:T(8,128)(2,1)S(1)} %copy-done.11), custom_call_target="tpu_custom_call" | custom-call | flops 4000000000 | bytes 3145728 | tf_op jit(solution)/shard_map/delta_reach/pallas_call | solution.py:370
  30.4 0.0 copy-start.5
  30.4 0.1 broadcast_in_dim.2.freq_ref
  30.5 0.9 %window.1 = (bf16[256,1280]{1,0:T(8,128)(2,1)S(1)}, bf16[1280,256]{1,0:T(8,128)(2,1)S(1)}, f32[1,1280]{1,0:T(1,128)S(1)}, f32[256,128]{1,0:T(8,128)S(1)}, f32[256,128]{1,0:T(8,128)S(1)}) custom-call(f32[32,128]{1,0:T(8,128)S(1)} %broadcast_in_dim.2.freq_ref, bf16[272,512]{1,0:T(8,128)(2,1)S(1)} %copy-done.1, ...), custom_call_target="tpu_custom_call" | custom-call | flops 100000000 | bytes 1048576 | tf_op jit(solution)/shard_map/window/pallas_call | solution.py:497
  31.4 0.2 copy-done.5
  31.6 3.8 %attention.2.rest_0_ = bf16[256,2048]{1,0:T(8,128)(2,1)} custom-call(f32[1,1280]{1,0:T(1,128)S(1)} %get-tuple-element.46.ids_ref, f32[256,128]{1,0:T(8,128)S(1)} %get-tuple-element.47.cos_ref, f32[256,128]{1,0:T(8,128)S(1)} %get-tuple-element.48.sin_ref, bf16[256,1280]{1,0:T(8,128)(2,1)S(1)} %get-tuple-element.49.kt_ref, ...), custom_call_target="tpu_custom_call" | custom-call | flops 5000000000 | bytes 3145728 | tf_op jit(solution)/shard_map/attention/pallas_call | solution.py:683
  35.4 0.2 relay.1
  35.7 2.2 %collective-permute-start.5 = (bf16[1040,128]{1,0:T(8,128)(2,1)S(1)}, bf16[1040,128]{1,0:T(8,128)(2,1)S(1)}, u32[]{:S(2)}, u32[]{:S(2)}) collective-permute-start(bf16[1040,128]{1,0:T(8,128)(2,1)S(1)} %relay.1), channel_id=1, source_target_pairs={{0,2},{1,3},{2,4},{3,5},{4,6},{5,7},{8,10},{9,11},{10,12},{11,13},... | collective-permute-start | bytes 798728 | tf_op jit(solution)/shard_map/ppermute | solution.py:698
  37.9 3.8 %attention.3 = bf16[256,2048]{1,0:T(8,128)(2,1)} custom-call(f32[1,1280]{1,0:T(1,128)S(1)} %get-tuple-element.46.ids_ref, f32[256,128]{1,0:T(8,128)S(1)} %get-tuple-element.47.cos_ref, f32[256,128]{1,0:T(8,128)S(1)} %get-tuple-element.48.sin_ref, bf16[256,1280]{1,0:T(8,128)(2,1)S(1)} %get-tuple-element.49.kt_ref, ...), custom_call_target="tpu_custom_call", output_to_operand_aliasing={{}: (7, {})} | custom-call | flops 5000000000 | bytes 3145728 | tf_op jit(solution)/shard_map/attention/pallas_call | solution.py:683
  41.8 1.5 %delta_reach.3 = (bf16[256,1024]{1,0:T(8,128)(2,1)S(1)}, f32[256,1024]{1,0:T(8,128)S(1)}) custom-call(s32[1]{0:T(128)} %bitcast.half_ref.core_ref, s32[1,256]{1,0:T(1,128)S(1)} %bitcast.15, bf16[256,1024]{1,0:T(8,128)(2,1)S(1)} %copy-done.7, bf16[256,1024]{1,0:T(8,128)(2,1)S(1)} %copy-done.8, f32[16,256]{1,0:T(8,128)S(1)} %bitcast.19, ...), custom_call_target="tpu_custom_call" | custom-call | flops 4000000000 | bytes 3145728 | tf_op jit(solution)/shard_map/delta_reach/pallas_call | solution.py:370
  43.2 0.0 copy-start
  43.2 1.1 %collective-permute-done.5.state_ref = bf16[1040,128]{1,0:T(8,128)(2,1)S(1)} collective-permute-done((bf16[1040,128]{1,0:T(8,128)(2,1)S(1)}, bf16[1040,128]{1,0:T(8,128)(2,1)S(1)}, u32[]{:S(2)}, u32[]{:S(2)}) %collective-permute-start.5) | collective-permute-done | bytes 266272 | tf_op jit(solution)/shard_map/ppermute | solution.py:698
  44.4 0.4 arrive.1
  44.7 2.1 %collective-permute-start.6 = (bf16[1024,128]{1,0:T(8,128)(2,1)S(1)}, bf16[1024,128]{1,0:T(8,128)(2,1)S(1)}, u32[]{:S(2)}, u32[]{:S(2)}) collective-permute-start(bf16[1024,128]{1,0:T(8,128)(2,1)S(1)} %get-tuple-element.64), channel_id=1, source_target_pairs={{0,1},{1,0},{2,3},{3,2},{4,5},{5,4},{6,7},{7,6},{8,9},{9,8},{10,11... | collective-permute-start | bytes 786440 | tf_op jit(solution)/shard_map/ppermute | solution.py:702
  46.8 0.7 %copy-done.3 = f32[128]{0:T(128)S(1)} copy-done((f32[128]{0:T(128)S(1)}, f32[128]{0:T(128)}, u32[]{:S(2)}) %copy-start.3) | copy-done | bytes 536
  47.5 1.8 %delta_out.2.rest_0_ = bf16[256,2048]{1,0:T(8,128)(2,1)} custom-call(s32[1]{0:T(128)} %bitcast.half_ref.core_ref, bf16[256,1024]{1,0:T(8,128)(2,1)S(1)} %get-tuple-element.65.reach_ref, f32[256,1024]{1,0:T(8,128)S(1)} %get-tuple-element.66.inner_ref, bf16[1024,128]{1,0:T(8,128)(2,1)S(1)} %get-tuple-element.67.state_ref, bf16[256,2048]{1,0:T(8,128)(2,1)S(1)} %copy-done, ...), custom_call_target="tpu_custom_call" | custom-call | flops 100000000 | bytes 3145728 | tf_op jit(solution)/shard_map/delta_out/pallas_call | solution.py:546
  49.2 1.8 %delta_out.3 = bf16[256,2048]{1,0:T(8,128)(2,1)} custom-call(s32[1]{0:T(128)S(6)} %sub.3.half_ref, bf16[256,1024]{1,0:T(8,128)(2,1)S(1)} %get-tuple-element.61.reach_ref, f32[256,1024]{1,0:T(8,128)S(1)} %get-tuple-element.62.inner_ref, bf16[1024,128]{1,0:T(8,128)(2,1)S(1)} %collective-permute-done.6.state_ref, ...), custom_call_target="tpu_custom_call", output_to_operand_aliasing={{}: (6, {})} | custom-call | flops 100000000 | bytes 3145728 | tf_op jit(solution)/shard_map/delta_out/pallas_call | solution.py:546
  (23 shorter events, 0.1 us)
Async XLA Ops:
  2.4 11.3 %collective-permute-start = (bf16[272,512]{1,0:T(8,128)(2,1)}, bf16[272,512]{1,0:T(8,128)(2,1)S(1)}, u32[]{:S(2)}, u32[]{:S(2)}) collective-permute-start(bf16[272,512]{1,0:T(8,128)(2,1)} %pack.1.rest_0_), channel_id=1, source_target_pairs={{0,2},{1,3},{2,4},{3,5},{4,6},{5,7},{8,10},{9,11},{10,12},{11,13},... | collective-permute-start | bytes 835592 | tf_op jit(solution)/shard_map/ppermute | solution.py:698
  12.7 11.4 %collective-permute-start.2 = (bf16[1040,256]{1,0:T(8,128)(2,1)}, bf16[1040,256]{1,0:T(8,128)(2,1)S(1)}, u32[]{:S(2)}, u32[]{:S(2)}) collective-permute-start(bf16[1040,256]{1,0:T(8,128)(2,1)} %get-tuple-element.35), channel_id=1, source_target_pairs={{0,1},{1,0},{2,3},{3,2},{4,5},{5,4},{6,7},{7,6},{8,9},{9,8},{10,11... | collective-permute-start | bytes 1597448 | tf_op jit(solution)/shard_map/ppermute | solution.py:702
  13.7 10.5 %copy-start.1 = (bf16[272,512]{1,0:T(8,128)(2,1)S(1)}, bf16[272,512]{1,0:T(8,128)(2,1)}, u32[]{:S(2)}) copy-start(bf16[272,512]{1,0:T(8,128)(2,1)} %pack.1.rest_0_) | copy-start | bytes 835588
  13.7 10.5 %collective-permute-start.1 = (bf16[272,512]{1,0:T(8,128)(2,1)S(1)}, bf16[272,512]{1,0:T(8,128)(2,1)S(1)}, u32[]{:S(2)}, u32[]{:S(2)}) collective-permute-start(bf16[272,512]{1,0:T(8,128)(2,1)S(1)} %collective-permute-done.rest_1_), channel_id=1, source_target_pairs={{0,2},{1,3},{2,4},{3,5},{4,6},{5,7},{8,10},{9,11},{10,12},{11,13},... | collective-permute-start | bytes 835592 | tf_op jit(solution)/shard_map/ppermute | solution.py:698
  24.2 4.7 %copy-start.11 = (bf16[2048,256]{1,0:T(8,128)(2,1)S(1)}, bf16[2048,256]{1,0:T(8,128)(2,1)}, u32[]{:S(2)}) copy-start(bf16[2048,256]{1,0:T(8,128)(2,1)} %get-tuple-element.51.solved_ref) | copy-start | bytes 3145732
  24.2 1.1 %copy-start.2 = (bf16[1040,256]{1,0:T(8,128)(2,1)S(1)}, bf16[1040,256]{1,0:T(8,128)(2,1)}, u32[]{:S(2)}) copy-start(bf16[1040,256]{1,0:T(8,128)(2,1)} %get-tuple-element.38.mine_ref) | copy-start | bytes 1597444
  24.3 6.1 %collective-permute-start.4 = (bf16[2,272,512]{2,1,0:T(8,128)(2,1)S(1)}, bf16[2,272,512]{2,1,0:T(8,128)(2,1)S(1)}, u32[]{:S(2)}, u32[]{:S(2)}) collective-permute-start(bf16[2,272,512]{2,1,0:T(8,128)(2,1)S(1)} %pad_maximum_fusion), channel_id=1, source_target_pairs={{0,1},{1,0},{2,3},{3,2},{4,5},{5,4},{6,7},{7,6},{8,9},{9,8},{10,11... | collective-permute-start | bytes 1671176 | tf_op jit(solution)/shard_map/ppermute | solution.py:702
  25.4 3.5 %copy-start.7 = (bf16[256,1024]{1,0:T(8,128)(2,1)S(1)}, bf16[256,1024]{1,0:T(8,128)(2,1)}, u32[]{:S(2)}) copy-start(bf16[256,1024]{1,0:T(8,128)(2,1)} %q_ref.7) | copy-start | bytes 1572868
  25.4 3.5 %copy-start.8 = (bf16[256,1024]{1,0:T(8,128)(2,1)S(1)}, bf16[256,1024]{1,0:T(8,128)(2,1)}, u32[]{:S(2)}) copy-start(bf16[256,1024]{1,0:T(8,128)(2,1)} %k_ref.7) | copy-start | bytes 1572868
  25.4 3.5 %copy-start.9 = (f32[256,16]{0,1:T(8,128)S(1)}, f32[256,16]{0,1:T(8,128)}, u32[]{:S(2)}) copy-start(f32[256,16]{0,1:T(8,128)} %param.21) | copy-start | bytes 49156
  25.7 3.2 %copy-start.4 = (s32[256]{0:T(256)S(1)}, s32[256]{0:T(256)}, u32[]{:S(2)}) copy-start(s32[256]{0:T(256)} %param.12) | copy-start | bytes 3076
  25.7 9.7 %collective-permute-start.3 = (bf16[1040,128]{1,0:T(8,128)(2,1)S(1)}, bf16[1040,128]{1,0:T(8,128)(2,1)S(1)}, u32[]{:S(2)}, u32[]{:S(2)}) collective-permute-start(bf16[1040,128]{1,0:T(8,128)(2,1)S(1)} %get-tuple-element.43.add_ref), channel_id=1, source_target_pairs={{0,2},{1,3},{2,4},{3,5},{4,6},{5,7},{8,10},{9,11},{10,12},{11,13},... | collective-permute-start | bytes 798728 | tf_op jit(solution)/shard_map/ppermute | solution.py:698
  28.9 2.5 %copy-start.6 = (bf16[256,2048]{1,0:T(8,128)(2,1)S(1)}, bf16[256,2048]{1,0:T(8,128)(2,1)}, u32[]{:S(2)}) copy-start(bf16[256,2048]{1,0:T(8,128)(2,1)} %gate_ref.5) | copy-start | bytes 3145732
  30.4 1.2 %copy-start.5 = (bf16[256,2048]{1,0:T(8,128)(2,1)S(1)}, bf16[256,2048]{1,0:T(8,128)(2,1)}, u32[]{:S(2)}) copy-start(bf16[256,2048]{1,0:T(8,128)(2,1)} %q_ref.6) | copy-start | bytes 3145732
  35.7 8.7 %collective-permute-start.5 = (bf16[1040,128]{1,0:T(8,128)(2,1)S(1)}, bf16[1040,128]{1,0:T(8,128)(2,1)S(1)}, u32[]{:S(2)}, u32[]{:S(2)}) collective-permute-start(bf16[1040,128]{1,0:T(8,128)(2,1)S(1)} %relay.1), channel_id=1, source_target_pairs={{0,2},{1,3},{2,4},{3,5},{4,6},{5,7},{8,10},{9,11},{10,12},{11,13},... | collective-permute-start | bytes 798728 | tf_op jit(solution)/shard_map/ppermute | solution.py:698
  37.9 3.8 %copy-start.10 = (bf16[2048,256]{1,0:T(8,128)(2,1)S(1)}, bf16[2048,256]{1,0:T(8,128)(2,1)}, u32[]{:S(2)}) copy-start(bf16[2048,256]{1,0:T(8,128)(2,1)} %get-tuple-element.57.solved_ref) | copy-start | bytes 3145732
  43.2 3.6 %copy-start = (bf16[256,2048]{1,0:T(8,128)(2,1)S(1)}, bf16[256,2048]{1,0:T(8,128)(2,1)}, u32[]{:S(2)}) copy-start(bf16[256,2048]{1,0:T(8,128)(2,1)} %gate_ref.7) | copy-start | bytes 3145732
  44.7 4.5 %collective-permute-start.6 = (bf16[1024,128]{1,0:T(8,128)(2,1)S(1)}, bf16[1024,128]{1,0:T(8,128)(2,1)S(1)}, u32[]{:S(2)}, u32[]{:S(2)}) collective-permute-start(bf16[1024,128]{1,0:T(8,128)(2,1)S(1)} %get-tuple-element.64), channel_id=1, source_target_pairs={{0,1},{1,0},{2,3},{3,2},{4,5},{5,4},{6,7},{7,6},{8,9},{9,8},{10,11... | collective-permute-start | bytes 786440 | tf_op jit(solution)/shard_map/ppermute | solution.py:702
  46.8 0.7 %copy-start.3 = (f32[128]{0:T(128)S(1)}, f32[128]{0:T(128)}, u32[]{:S(2)}) copy-start(f32[128]{0:T(128)} %param.23) | copy-start | bytes 1540

commit v9 on v8

--- a/solution.py
+++ b/solution.py
@@ -150,26 +150,56 @@
 def delta_local_kernel(
     half_ref,
     seg_ref,
-    k_ref,
-    v_ref,
+    k_hbm,
+    v_hbm,
     beta_ref,
     decay_ref,
-    map_add_ref,
-    solved_ref,
+    map_add_hbm,
+    solved_hbm,
     mask_ref,
     level_ref,
     spread_ref,
+    k_ref,
+    v_ref,
+    map_add_ref,
+    solved_ref,
+    in_sem,
+    out_sem,
     crow_ref,
     ccol_ref,
     first_ref,
 ):
     rows = k_ref.shape[0]
     n = v_ref.shape[1] // DV
+    arriving = []
+    for kk in range(n // 2):
+        for i, (source, target, width) in enumerate(
+            [(k_hbm, k_ref, DK), (v_hbm, v_ref, 2 * DV)]
+        ):
+            at = pl.multiple_of(half_ref[0] * (width * n // 2) + kk * width, width)
+            arriving.append(
+                pltpu.make_async_copy(
+                    source.at[:, pl.ds(at, width)],
+                    target.at[:, pl.ds(kk * width, width)],
+                    in_sem.at[2 * kk + i],
+                )
+            )
+            arriving[-1].start()
+    leaving = []
+
+    def send(source, target, at, size):
+        part = pl.ds(at, size)
+        leaving.append(
+            pltpu.make_async_copy(source.at[part], target.at[part], out_sem.at[len(leaving)])
+        )
+        leaving[-1].start()
+
     fill_spread(spread_ref)
     seg_row = setup(
         half_ref, seg_ref, decay_ref, n, mask_ref, crow_ref, ccol_ref, first_ref, beta_ref
     )
     map_add_ref[n * DK :, :] = jnp.broadcast_to(seg_row, (BLOCK, rows)).astype(bf16)
+    send(map_add_ref, map_add_hbm, n * DK, BLOCK)
     r = lax.broadcasted_iota(jnp.int32, (TILE, TILE), 0)
     c = lax.broadcasted_iota(jnp.int32, (TILE, TILE), 1)
     eye = jnp.where(r == c, 1.0, 0.0)
@@ -184,6 +214,8 @@
 
     def elementwise(kk):
         pair = pairs[kk]
+        arriving[2 * kk].wait()
+        arriving[2 * kk + 1].wait()
         k_raw = k_ref[:, kk * DK : (kk + 1) * DK]
         kt = jnp.transpose(k_raw.astype(f32))
         rk_row = lax.rsqrt(jnp.sum(kt * kt, axis=0, keepdims=True) + EPS)
@@ -256,6 +288,7 @@
             u2 = add_strips(w["r2"], dot(w["x"][1], w["r2"]))
             w["u"] = jnp.concatenate([w["u1"], u2], axis=0)
             solved_ref[w["h"] * rows : (w["h"] + 1) * rows, :] = w["u"]
+            send(solved_ref, solved_hbm, w["h"] * rows, rows)
         yield
         for w in pair:
             h = w["h"]
@@ -266,11 +299,14 @@
                 map_add_ref[h * DK + start : h * DK + start + STRIP, :] = jnp.concatenate(
                     [kept - part[:, :DK], part[:, DK:]], axis=1
                 ).astype(bf16)
+            send(map_add_ref, map_add_hbm, h * DK, DK)
             yield
 
     pipeline([elementwise], n // 2)
     invert()
     pipeline([finish], n // 2)
+    for copy in leaving:
+        copy.wait()
 
 
 def add_strips(a, b):
@@ -290,8 +326,11 @@
     k_ref,
     decay_ref,
     solved_ref,
+    gate_ref,
+    gain_ref,
     reach_ref,
     inner_ref,
+    factor_ref,
     mask_ref,
     crow_ref,
     ccol_ref,
@@ -330,6 +369,9 @@
                 w["p"].append((span * probe).astype(bf16))
                 entry = jnp.exp2(cc[:, :TILE]) * first_ref[at]
                 w["scaled"].append((entry * qn).astype(bf16))
+                cols = slice(h * DV, (h + 1) * DV)
+                gate = gate_ref[at, cols].astype(f32)
+                factor_ref[at, cols] = gate * sigmoid(gate) * gain_ref[...]
             yield
 
     def finish(kk):
@@ -351,7 +393,7 @@
     pipeline([elementwise, finish], n // 2)
 
 
-def half_call(kernel, name, mib, half, operands, outs, scratch):
+def half_call(kernel, name, mib, half, operands, outs, scratch, hbm=False):
     def at_half(i, s):
         return (0, s[0])
 
@@ -363,7 +405,10 @@
     for a in operands:
         if isinstance(a, tuple):
             (a,) = a
-            specs.append(pl.BlockSpec((a.shape[0], a.shape[1] // 2), at_half))
+            if hbm:
+                specs.append(pl.BlockSpec(memory_space=pl.ANY))
+            else:
+                specs.append(pl.BlockSpec((a.shape[0], a.shape[1] // 2), at_half))
         else:
             specs.append(pl.BlockSpec(a.shape, at_zero))
         args.append(a)
@@ -373,7 +418,10 @@
             num_scalar_prefetch=1,
             grid=(1,),
             in_specs=specs,
-            out_specs=[pl.BlockSpec(o.shape, at_zero) for o in outs],
+            out_specs=[
+                pl.BlockSpec(memory_space=pl.ANY) if hbm else pl.BlockSpec(o.shape, at_zero)
+                for o in outs
+            ],
             scratch_shapes=scratch,
         ),
         out_shape=outs,
@@ -410,12 +458,19 @@
             mask,
             pltpu.VMEM((MERGES, TILE // 2, TILE), bf16),
             pltpu.VMEM((TILE, (BLOCK - 1) * TILE), bf16),
+            pltpu.VMEM((rows, n // 2 * DK), bf16),
+            pltpu.VMEM((rows, n * DV), bf16),
+            pltpu.VMEM((n * DK + BLOCK, DK + DV), bf16),
+            pltpu.VMEM((n * rows, DK + DV), bf16),
+            pltpu.SemaphoreType.DMA((n,)),
+            pltpu.SemaphoreType.DMA((2 * n + 1,)),
             *others,
         ],
-    )
-
-
-def delta_reach(half, seg_row, query, key, decay, solved):
+        hbm=True,
+    )
+
+
+def delta_reach(half, seg_row, query, key, decay, gate, gain, solved):
     rows = key.shape[0]
     n = solved.shape[0] // rows
     return half_call(
@@ -423,9 +478,10 @@
         "delta_reach",
         20,
         half,
-        [seg_row, (query,), (key,), decay, solved],
+        [seg_row, (query,), (key,), decay, solved, (gate,), gain],
         [
             jax.ShapeDtypeStruct((rows, n * DK), bf16),
+            jax.ShapeDtypeStruct((rows, n * DV), f32),
             jax.ShapeDtypeStruct((rows, n * DV), f32),
         ],
         setup_scratch(rows, n),
@@ -505,53 +561,50 @@
     )(*args)
 
 
-def delta_out_kernel(half_ref, reach_ref, inner_ref, state_ref, gate_ref, gain_ref, *rest):
-    out_ref = rest[-1]
-    gain = gain_ref[...]
-    for h in range(state_ref.shape[0] // DK):
+def delta_out_kernel(half_ref, reach_ref, inner_ref, factor_ref, state_ref, *rest):
+    out_hbm, out_ref, sem = rest[-3:]
+    n = state_ref.shape[0] // DK
+    width = 2 * DV
+    copies = []
+    for h in range(n):
         cols = slice(h * DV, (h + 1) * DV)
-        state = state_ref[h * DK : (h + 1) * DK]
-        carried = dot(reach_ref[:, cols], state)
+        carried = dot(reach_ref[:, cols], state_ref[h * DK : (h + 1) * DK])
         for i in range(0, carried.shape[0], STRIP):
             at = slice(i, i + STRIP)
-            out = inner_ref[at, cols].astype(f32) + carried[at]
+            out = inner_ref[at, cols] + carried[at]
             spread = lax.rsqrt(jnp.mean(out * out, axis=1, keepdims=True) + EPS)
-            gate = gate_ref[at, cols].astype(f32)
-            gate = gate * sigmoid(gate)
-            out_ref[at, cols] = (out * spread * gain * gate).astype(bf16)
-
-
-def delta_out(half, reach, inner, state, gate, gain, partial_out=None):
+            out_ref[at, cols] = (out * spread * factor_ref[at, cols]).astype(bf16)
+        if h % 2 == 1:
+            start = (h - 1) * DV
+            target = pl.multiple_of(half_ref[0] * (n * DV) + start, width)
+            copies.append(
+                pltpu.make_async_copy(
+                    out_ref.at[:, pl.ds(start, width)],
+                    out_hbm.at[:, pl.ds(target, width)],
+                    sem.at[h // 2],
+                )
+            )
+            copies[-1].start()
+    for copy in copies:
+        copy.wait()
+
+
+def delta_out(half, reach, inner, factor, state, partial_out=None):
     rows = reach.shape[0]
     n = state.shape[0] // DK
-    heads = 4
-    steps = n // heads
-
-    def at_half(i, s):
-        return (0, s[0] * steps + i)
-
-    in_specs = [
-        pl.BlockSpec((rows, heads * DK), lambda i, s: (0, i)),
-        pl.BlockSpec((rows, heads * DV), lambda i, s: (0, i)),
-        pl.BlockSpec((heads * DK, DV), lambda i, s: (i, 0)),
-        pl.BlockSpec((rows, heads * DV), at_half),
-        pl.BlockSpec((1, DV), lambda i, s: (0, 0)),
-    ]
-    args = [half, reach, inner, state, gate, gain]
+    in_specs = [SMEM] + [VMEM] * 4
+    args = [half, reach, inner, factor, state]
     aliases = {}
     if partial_out is not None:
+        aliases = {len(args): 0}
         in_specs.append(pl.BlockSpec(memory_space=pl.ANY))
         args.append(partial_out)
-        aliases = {6: 0}
     return pl.pallas_call(
         delta_out_kernel,
-        grid_spec=pltpu.PrefetchScalarGridSpec(
-            num_scalar_prefetch=1,
-            grid=(steps,),
-            in_specs=in_specs,
-            out_specs=pl.BlockSpec((rows, heads * DV), at_half),
-        ),
-        out_shape=jax.ShapeDtypeStruct(gate.shape, bf16),
+        in_specs=in_specs,
+        out_specs=pl.BlockSpec(memory_space=pl.ANY),
+        out_shape=jax.ShapeDtypeStruct((rows, 2 * n * DV), bf16),
+        scratch_shapes=[pltpu.VMEM((rows, n * DV), bf16), pltpu.SemaphoreType.DMA((n // 2,))],
         input_output_aliases=aliases,
         compiler_params=params(),
         cost_estimate=cost(10**8, 3 * 2**20),
@@ -567,13 +620,40 @@
     return order[::-1]
 
 
-def pack_kernel(seg_ref, key_ref, value_ref, out_ref):
-    rows = key_ref.shape[0]
-    ids = seg_ref[...].astype(f32) + 1.0
-    out_ref[:rows, :HEAD_WIDTH] = key_ref[...]
-    out_ref[:rows, HEAD_WIDTH:] = value_ref[...]
-    out_ref[rows:, :rows] = jnp.broadcast_to(ids, (BLOCK, rows)).astype(bf16)
-    out_ref[rows:, rows:] = jnp.zeros((BLOCK, 2 * HEAD_WIDTH - rows), bf16)
+def pack_kernel(seg_ref, key_hbm, value_hbm, out_hbm, ids_ref, sem):
+    rows = seg_ref.shape[1]
+    body = out_hbm.at[pl.ds(0, rows)]
+    copies = [
+        pltpu.make_async_copy(key_hbm, body.at[:, pl.ds(0, HEAD_WIDTH)], sem.at[0]),
+        pltpu.make_async_copy(value_hbm, body.at[:, pl.ds(HEAD_WIDTH, HEAD_WIDTH)], sem.at[1]),
+        pltpu.make_async_copy(ids_ref, out_hbm.at[pl.ds(rows, BLOCK)], sem.at[2]),
+    ]
+    copies[0].start()
+    copies[1].start()
+    ids = jnp.broadcast_to(seg_ref[...].astype(f32) + 1.0, (BLOCK, rows))
+    unused = jnp.zeros((BLOCK, 2 * HEAD_WIDTH - rows), f32)
+    ids_ref[...] = jnp.concatenate([ids, unused], axis=1).astype(bf16)
+    copies[2].start()
+    for copy in copies:
+        copy.wait()
+
+
+def pack(ids, keys, values):
+    rows = keys.shape[0]
+    free = pl.BlockSpec(memory_space=pl.ANY)
+    return pl.pallas_call(
+        pack_kernel,
+        in_specs=[VMEM, free, free],
+        out_specs=free,
+        out_shape=jax.ShapeDtypeStruct((rows + BLOCK, 2 * HEAD_WIDTH), bf16),
+        scratch_shapes=[
+            pltpu.VMEM((BLOCK, 2 * HEAD_WIDTH), bf16),
+            pltpu.SemaphoreType.DMA((3,)),
+        ],
+        compiler_params=params(60),
+        cost_estimate=cost(10**6, 2**19),
+        name="pack",
+    )(ids, keys, values)
 
 
 def window_kernel(freq_ref, *rest):
@@ -725,15 +805,7 @@
 
     ids = segment_ids.reshape(1, rows)
 
-    (own,) = small_call(
-        pack_kernel,
-        "pack",
-        [jax.ShapeDtypeStruct((rows + BLOCK, 2 * HEAD_WIDTH), bf16)],
-        ids,
-        attention_keys,
-        attention_values,
-        mib=60,
-    )
+    own = pack(ids, attention_keys, attention_values)
     nearest = up_chip(own, ranks)
 
     keep_half = core.reshape(1).astype(jnp.int32)
@@ -748,7 +820,13 @@
         decay=decay_rows,
     )
     reach = partial(
-        delta_reach, seg_row=ids, query=delta_query, key=delta_key, decay=decay_rows
+        delta_reach,
+        seg_row=ids,
+        query=delta_query,
+        key=delta_key,
+        decay=decay_rows,
+        gate=delta_gate,
+        gain=norm_gain.reshape(1, DV),
     )
     give_ma, give_solved = local(give_half, 60)
     other_ma = swap_cores(give_ma, ranks)
@@ -799,8 +877,8 @@
     for _ in range(hops - 1):
         (leaving,) = small_call(relay_kernel, "relay", [state_like], chip_map, chip_add, state)
         state = up_chip(leaving, ranks)
+    attn_mixed, keep_solved, leaving = lax.optimization_barrier((attn_mixed, keep_solved, leaving))
     attn_mixed = attention_half(1, window_arrays, attn_query, attn_gate, attn_mixed)
-    keep_solved, leaving = lax.optimization_barrier((keep_solved, leaving))
     keep_rows = reach(keep_half, solved=keep_solved)
     state, attn_mixed, keep_rows = lax.optimization_barrier((state, attn_mixed, keep_rows))
 
@@ -810,11 +888,8 @@
     )
     give_state = swap_cores(pass_state, ranks)
 
-    gain = norm_gain.reshape(1, DV)
-    delta_mixed = delta_out(keep_half, *keep_rows, keep_state, delta_gate, gain)
-    delta_mixed = delta_out(
-        give_half, *give_rows, give_state, delta_gate, gain, delta_mixed
-    )
+    delta_mixed = delta_out(keep_half, *keep_rows, keep_state)
+    delta_mixed = delta_out(give_half, *give_rows, give_state, delta_mixed)
     return (attn_mixed, delta_mixed)
 
 

time: 51.4 us -> 60 us (1.17); the launches traced: 51 us -> 59 us
  Pallas kernels: 31.9 us -> 40.6 us
  starting transfers between devices: 15.6 us -> 14.4 us
    pallas_call x2 -> x3, Pallas kernels: 3.51 us -> 12.2 us  [the longest x1 9.75 us: pack(): pl.pallas_call(pack_kernel, in_specs=[VMEM, free, free], out_specs=free,...]
    pallas_call x4, Pallas kernels: 17.2 us -> 19 us  [half_call(): pl.pallas_call(kernel, grid_spec=pltpu.PrefetchScalarGridSpec(num_scalar_...]
    pallas_call x5 -> x4, Pallas kernels: 3.58 us -> 1.84 us  [small_call(): pl.pallas_call(kernel, in_specs=[SMEM] * scalars + [VMEM] * (len(args) -...]
    ppermute x4, starting transfers between devices: 11.9 us -> 10.9 us  [up_chip(): return lax.ppermute(value, 'ctx', [(i, i + 2) for i in range(ranks - 2)])]
  transfers between devices with their start and end apart: 7 -> 7, of which waited for: 1 -> 1; matrix products, arithmetic and copies ran while one was open for 0% -> 0% of each run, Pallas kernels for 55% -> 49%
where the time goes in v9:
time: 60 us; the launch traced here: 59 us
  Pallas kernels  40.6 us (68%)
  starting transfers between devices  14.4 us (24%)
  local copies, waits for them, and re-layouts  1.54 us (3%)
  waiting for transfers between devices  1.23 us (2%)
  between operations  1.07 us (2%)
    pallas_call x4, Pallas kernels, half_call(): pl.pallas_call(kernel, grid_spec=pltpu.PrefetchScalarGridSpec(num_scalar_...  19 us
    ppermute x4, starting transfers between devices, up_chip(): return lax.ppermute(value, 'ctx', [(i, i + 2) for i in range(ranks - 2)])  10.9 us
    pallas_call x1, Pallas kernels, pack(): pl.pallas_call(pack_kernel, in_specs=[VMEM, free, free], out_specs=free,...  9.75 us
    pallas_call x2, Pallas kernels, attention_half(): pl.pallas_call(attention_kernel, grid=(steps,), in_specs=in_specs, out_sp...  7.65 us
    ppermute x3, starting transfers between devices, swap_cores(): return lax.ppermute(value, 'ctx', [(i, i ^ 1) for i in range(ranks)])  3.52 us
    pallas_call x2, Pallas kernels, delta_out(): pl.pallas_call(delta_out_kernel, in_specs=in_specs, out_specs=pl.BlockSpe...  2.41 us
    pallas_call x4, Pallas kernels, small_call(): pl.pallas_call(kernel, in_specs=[SMEM] * scalars + [VMEM] * (len(args) -...  1.84 us
    unnamed x24, local copies, waits for them, and re-layouts  1.47 us
  transfers between devices with their start and end apart: 7, of which 1 were waited for; matrix products, arithmetic and copies ran while one was open for 0% of the time, Pallas kernels for 49%

profile of v9, /device:TPU:9, one launch (start us, length us, event | category | flops | bytes accessed | tf_op | source)
XLA Modules:
  0.0 59.0 jit_solution(10086466214120134961)
XLA Ops:
  0.6 9.8 %pack.1.rest_0_ = bf16[272,512]{1,0:T(8,128)(2,1)} custom-call(s32[1,256]{1,0:T(1,128)} %bitcast.9, bf16[256,256]{1,0:T(8,128)(2,1)} %key_hbm.1, bf16[256,256]{1,0:T(8,128)(2,1)} %value_hbm.1), custom_call_target="tpu_custom_call" | custom-call | flops 1000000 | bytes 524288 | tf_op jit(solution)/shard_map/pack/pallas_call | solution.py:644
  10.4 3.2 %collective-permute-start = (bf16[272,512]{1,0:T(8,128)(2,1)}, bf16[272,512]{1,0:T(8,128)(2,1)S(1)}, u32[]{:S(2)}, u32[]{:S(2)}) collective-permute-start(bf16[272,512]{1,0:T(8,128)(2,1)} %pack.1.rest_0_), channel_id=1, source_target_pairs={{0,2},{1,3},{2,4},{3,5},{4,6},{5,7},{8,10},{9,11},{10,12},{11,13},... | collective-permute-start | bytes 835592 | tf_op jit(solution)/shard_map/ppermute | solution.py:778
  13.6 7.7 %delta_local.2 = (bf16[1040,256]{1,0:T(8,128)(2,1)}, bf16[2048,256]{1,0:T(8,128)(2,1)}) custom-call(s32[1]{0:T(128)S(6)} %sub.3.half_ref, s32[1,256]{1,0:T(1,128)} %bitcast.10, bf16[256,1024]{1,0:T(8,128)(2,1)} %k_ref.3, bf16[256,2048]{1,0:T(8,128)(2,1)} %v_hbm.3, f32[16,256]{1,0:T(8,128)} %bitcast.20, f32[16,256]{1,0:T(8,128)} %bitcast.14), custom_call_target="tpu_custom_call" | custom-call | flops 4000000000 | bytes 3145728 | tf_op jit(solution)/shard_map/delta_local/pallas_call | solution.py:415
  21.4 1.0 %collective-permute-start.2 = (bf16[1040,256]{1,0:T(8,128)(2,1)}, bf16[1040,256]{1,0:T(8,128)(2,1)S(1)}, u32[]{:S(2)}, u32[]{:S(2)}) collective-permute-start(bf16[1040,256]{1,0:T(8,128)(2,1)} %get-tuple-element.40), channel_id=1, source_target_pairs={{0,1},{1,0},{2,3},{3,2},{4,5},{5,4},{6,7},{7,6},{8,9},{9,8},{10,11... | collective-permute-start | bytes 1597448 | tf_op jit(solution)/shard_map/ppermute | solution.py:782
  22.4 3.3 %collective-permute-start.1 = (bf16[272,512]{1,0:T(8,128)(2,1)S(1)}, bf16[272,512]{1,0:T(8,128)(2,1)S(1)}, u32[]{:S(2)}, u32[]{:S(2)}) collective-permute-start(bf16[272,512]{1,0:T(8,128)(2,1)S(1)} %collective-permute-done.rest_1_), channel_id=1, source_target_pairs={{0,2},{1,3},{2,4},{3,5},{4,6},{5,7},{8,10},{9,11},{10,12},{11,13},... | collective-permute-start | bytes 835592 | tf_op jit(solution)/shard_map/ppermute | solution.py:778
  25.7 0.0 copy-start.11
  25.7 7.8 %delta_local.3 = (bf16[1040,256]{1,0:T(8,128)(2,1)}, bf16[2048,256]{1,0:T(8,128)(2,1)}) custom-call(s32[1]{0:T(128)} %bitcast.half_ref.core_ref, s32[1,256]{1,0:T(1,128)} %bitcast.11, bf16[256,1024]{1,0:T(8,128)(2,1)} %k_ref.3, bf16[256,2048]{1,0:T(8,128)(2,1)} %v_hbm.3, f32[16,256]{1,0:T(8,128)} %bitcast.21, f32[16,256]{1,0:T(8,128)} %bitcast.15), custom_call_target="tpu_custom_call" | custom-call | flops 4000000000 | bytes 3145728 | tf_op jit(solution)/shard_map/delta_local/pallas_call | solution.py:415
  33.6 0.0 copy-start.7
  33.6 0.1 select_bitcast_fusion.1
  33.7 0.0 copy-start.5
  33.7 0.1 pad_maximum_fusion
  33.7 0.4 collective-permute-start.4
  34.1 0.6 %copy-done.1 = bf16[1040,256]{1,0:T(8,128)(2,1)S(1)} copy-done((bf16[1040,256]{1,0:T(8,128)(2,1)S(1)}, bf16[1040,256]{1,0:T(8,128)(2,1)}, u32[]{:S(2)}) %copy-start.1) | copy-done | bytes 532504
  34.8 0.3 compose.1
  35.1 2.4 %collective-permute-start.3 = (bf16[1040,128]{1,0:T(8,128)(2,1)S(1)}, bf16[1040,128]{1,0:T(8,128)(2,1)S(1)}, u32[]{:S(2)}, u32[]{:S(2)}) collective-permute-start(bf16[1040,128]{1,0:T(8,128)(2,1)S(1)} %get-tuple-element.48.add_ref), channel_id=1, source_target_pairs={{0,2},{1,3},{2,4},{3,5},{4,6},{5,7},{8,10},{9,11},{10,12},{11,13},... | collective-permute-start | bytes 798728 | tf_op jit(solution)/shard_map/ppermute | solution.py:778
  37.5 0.0 copy-start.9
  37.6 0.6 %copy-done.2 = s32[256]{0:T(256)S(1)} copy-done((s32[256]{0:T(256)S(1)}, s32[256]{0:T(256)}, u32[]{:S(2)}) %copy-start.2) | copy-done | bytes 1048
  38.2 1.7 %delta_reach.2 = (bf16[256,1024]{1,0:T(8,128)(2,1)S(1)}, f32[256,1024]{1,0:T(8,128)S(1)}, f32[256,1024]{1,0:T(8,128)S(1)}) custom-call(s32[1]{0:T(128)S(6)} %sub.3.half_ref, s32[1,256]{1,0:T(1,128)S(1)} %bitcast.12, bf16[256,1024]{1,0:T(8,128)(2,1)S(1)} %copy-done.6, bf16[256,1024]{1,0:T(8,128)(2,1)S(1)} %copy-done.7, f32[16,256]{1,0:T(8,128)S(1)} %bitcast.16, ...), custom_call_target="tpu_custom_call" | custom-call | flops 4000000000 | bytes 3145728 | tf_op jit(solution)/shard_map/delta_reach/pallas_call | solution.py:415
  39.9 0.0 copy-start.3
  40.0 0.1 broadcast_in_dim.2.freq_ref
  40.0 0.9 %window.1 = (bf16[256,1280]{1,0:T(8,128)(2,1)S(1)}, bf16[1280,256]{1,0:T(8,128)(2,1)S(1)}, f32[1,1280]{1,0:T(1,128)S(1)}, f32[256,128]{1,0:T(8,128)S(1)}, f32[256,128]{1,0:T(8,128)S(1)}) custom-call(f32[32,128]{1,0:T(8,128)S(1)} %broadcast_in_dim.2.freq_ref, bf16[272,512]{1,0:T(8,128)(2,1)S(1)} %copy-done, ...), custom_call_target="tpu_custom_call" | custom-call | flops 100000000 | bytes 1048576 | tf_op jit(solution)/shard_map/window/pallas_call | solution.py:553
  41.0 0.2 copy-done.3
  41.2 3.8 %attention.2.rest_0_ = bf16[256,2048]{1,0:T(8,128)(2,1)} custom-call(f32[1,1280]{1,0:T(1,128)S(1)} %get-tuple-element.51.ids_ref, f32[256,128]{1,0:T(8,128)S(1)} %get-tuple-element.52.cos_ref, f32[256,128]{1,0:T(8,128)S(1)} %get-tuple-element.53.sin_ref, bf16[256,1280]{1,0:T(8,128)(2,1)S(1)} %get-tuple-element.54.kt_ref, ...), custom_call_target="tpu_custom_call" | custom-call | flops 5000000000 | bytes 3145728 | tf_op jit(solution)/shard_map/attention/pallas_call | solution.py:763
  45.0 0.2 relay.1
  45.2 1.9 %collective-permute-start.5 = (bf16[1040,128]{1,0:T(8,128)(2,1)S(1)}, bf16[1040,128]{1,0:T(8,128)(2,1)S(1)}, u32[]{:S(2)}, u32[]{:S(2)}) collective-permute-start(bf16[1040,128]{1,0:T(8,128)(2,1)S(1)} %relay.1), channel_id=1, source_target_pairs={{0,2},{1,3},{2,4},{3,5},{4,6},{5,7},{8,10},{9,11},{10,12},{11,13},... | collective-permute-start | bytes 798728 | tf_op jit(solution)/shard_map/ppermute | solution.py:778
  47.2 3.8 %attention.3 = bf16[256,2048]{1,0:T(8,128)(2,1)} custom-call(f32[1,1280]{1,0:T(1,128)S(1)} %get-tuple-element.51.ids_ref, f32[256,128]{1,0:T(8,128)S(1)} %get-tuple-element.52.cos_ref, f32[256,128]{1,0:T(8,128)S(1)} %get-tuple-element.53.sin_ref, bf16[256,1280]{1,0:T(8,128)(2,1)S(1)} %get-tuple-element.54.kt_ref, ...), custom_call_target="tpu_custom_call", output_to_operand_aliasing={{}: (7, {})} | custom-call | flops 5000000000 | bytes 3145728 | tf_op jit(solution)/shard_map/attention/pallas_call | solution.py:763
  51.0 1.7 %delta_reach.3 = (bf16[256,1024]{1,0:T(8,128)(2,1)S(1)}, f32[256,1024]{1,0:T(8,128)S(1)}, f32[256,1024]{1,0:T(8,128)S(1)}) custom-call(s32[1]{0:T(128)} %bitcast.half_ref.core_ref, s32[1,256]{1,0:T(1,128)S(1)} %bitcast.13, bf16[256,1024]{1,0:T(8,128)(2,1)S(1)} %copy-done.6, bf16[256,1024]{1,0:T(8,128)(2,1)S(1)} %copy-done.7, f32[16,256]{1,0:T(8,128)S(1)} %bitcast.17, ...), custom_call_target="tpu_custom_call" | custom-call | flops 4000000000 | bytes 3145728 | tf_op jit(solution)/shard_map/delta_reach/pallas_call | solution.py:415
  52.7 1.2 %collective-permute-done.5.state_ref = bf16[1040,128]{1,0:T(8,128)(2,1)S(1)} collective-permute-done((bf16[1040,128]{1,0:T(8,128)(2,1)S(1)}, bf16[1040,128]{1,0:T(8,128)(2,1)S(1)}, u32[]{:S(2)}, u32[]{:S(2)}) %collective-permute-start.5) | collective-permute-done | bytes 266272 | tf_op jit(solution)/shard_map/ppermute | solution.py:778
  53.9 0.4 arrive.1
  54.3 2.1 %collective-permute-start.6 = (bf16[1024,128]{1,0:T(8,128)(2,1)S(1)}, bf16[1024,128]{1,0:T(8,128)(2,1)S(1)}, u32[]{:S(2)}, u32[]{:S(2)}) collective-permute-start(bf16[1024,128]{1,0:T(8,128)(2,1)S(1)} %get-tuple-element.73), channel_id=1, source_target_pairs={{0,1},{1,0},{2,3},{3,2},{4,5},{5,4},{6,7},{7,6},{8,9},{9,8},{10,11... | collective-permute-start | bytes 786440 | tf_op jit(solution)/shard_map/ppermute | solution.py:782
  56.4 1.2 %delta_out.2.rest_0_ = bf16[256,2048]{1,0:T(8,128)(2,1)} custom-call(s32[1]{0:T(128)} %bitcast.half_ref.core_ref, bf16[256,1024]{1,0:T(8,128)(2,1)S(1)} %get-tuple-element.74.reach_ref, f32[256,1024]{1,0:T(8,128)S(1)} %get-tuple-element.75.inner_ref, f32[256,1024]{1,0:T(8,128)S(1)} %get-tuple-element.76.factor_ref, ...), custom_call_target="tpu_custom_call" | custom-call | flops 100000000 | bytes 3145728 | tf_op jit(solution)/shard_map/delta_out/pallas_call | solution.py:602
  57.6 1.2 %delta_out.3 = bf16[256,2048]{1,0:T(8,128)(2,1)} custom-call(s32[1]{0:T(128)S(6)} %sub.3.half_ref, bf16[256,1024]{1,0:T(8,128)(2,1)S(1)} %get-tuple-element.69.reach_ref, f32[256,1024]{1,0:T(8,128)S(1)} %get-tuple-element.70.inner_ref, f32[256,1024]{1,0:T(8,128)S(1)} %get-tuple-element.71.factor_ref, ...), custom_call_target="tpu_custom_call", output_to_operand_aliasing={{}: (5, {})} | custom-call | flops 100000000 | bytes 3145728 | tf_op jit(solution)/shard_map/delta_out/pallas_call | solution.py:602
  (23 shorter events, 0.1 us)
Async XLA Ops:
  10.4 12.0 %collective-permute-start = (bf16[272,512]{1,0:T(8,128)(2,1)}, bf16[272,512]{1,0:T(8,128)(2,1)S(1)}, u32[]{:S(2)}, u32[]{:S(2)}) collective-permute-start(bf16[272,512]{1,0:T(8,128)(2,1)} %pack.1.rest_0_), channel_id=1, source_target_pairs={{0,2},{1,3},{2,4},{3,5},{4,6},{5,7},{8,10},{9,11},{10,12},{11,13},... | collective-permute-start | bytes 835592 | tf_op jit(solution)/shard_map/ppermute | solution.py:778
  21.4 12.2 %collective-permute-start.2 = (bf16[1040,256]{1,0:T(8,128)(2,1)}, bf16[1040,256]{1,0:T(8,128)(2,1)S(1)}, u32[]{:S(2)}, u32[]{:S(2)}) collective-permute-start(bf16[1040,256]{1,0:T(8,128)(2,1)} %get-tuple-element.40), channel_id=1, source_target_pairs={{0,1},{1,0},{2,3},{3,2},{4,5},{5,4},{6,7},{7,6},{8,9},{9,8},{10,11... | collective-permute-start | bytes 1597448 | tf_op jit(solution)/shard_map/ppermute | solution.py:782
  22.4 11.2 %copy-start = (bf16[272,512]{1,0:T(8,128)(2,1)S(1)}, bf16[272,512]{1,0:T(8,128)(2,1)}, u32[]{:S(2)}) copy-start(bf16[272,512]{1,0:T(8,128)(2,1)} %pack.1.rest_0_) | copy-start | bytes 835588
  22.4 11.2 %collective-permute-start.1 = (bf16[272,512]{1,0:T(8,128)(2,1)S(1)}, bf16[272,512]{1,0:T(8,128)(2,1)S(1)}, u32[]{:S(2)}, u32[]{:S(2)}) collective-permute-start(bf16[272,512]{1,0:T(8,128)(2,1)S(1)} %collective-permute-done.rest_1_), channel_id=1, source_target_pairs={{0,2},{1,3},{2,4},{3,5},{4,6},{5,7},{8,10},{9,11},{10,12},{11,13},... | collective-permute-start | bytes 835592 | tf_op jit(solution)/shard_map/ppermute | solution.py:778
  25.7 11.8 %copy-start.11 = (bf16[2048,256]{1,0:T(8,128)(2,1)S(1)}, bf16[2048,256]{1,0:T(8,128)(2,1)}, u32[]{:S(2)}) copy-start(bf16[2048,256]{1,0:T(8,128)(2,1)} %get-tuple-element.56.solved_ref) | copy-start | bytes 3145732
  33.6 4.0 %copy-start.7 = (bf16[256,1024]{1,0:T(8,128)(2,1)S(1)}, bf16[256,1024]{1,0:T(8,128)(2,1)}, u32[]{:S(2)}) copy-start(bf16[256,1024]{1,0:T(8,128)(2,1)} %k_ref.3) | copy-start | bytes 1572868
  33.7 1.1 %copy-start.1 = (bf16[1040,256]{1,0:T(8,128)(2,1)S(1)}, bf16[1040,256]{1,0:T(8,128)(2,1)}, u32[]{:S(2)}) copy-start(bf16[1040,256]{1,0:T(8,128)(2,1)} %get-tuple-element.43.mine_ref) | copy-start | bytes 1597444
  33.7 3.9 %copy-start.5 = (bf16[256,2048]{1,0:T(8,128)(2,1)S(1)}, bf16[256,2048]{1,0:T(8,128)(2,1)}, u32[]{:S(2)}) copy-start(bf16[256,2048]{1,0:T(8,128)(2,1)} %gate_ref.7) | copy-start | bytes 3145732
  33.7 6.2 %collective-permute-start.4 = (bf16[2,272,512]{2,1,0:T(8,128)(2,1)S(1)}, bf16[2,272,512]{2,1,0:T(8,128)(2,1)S(1)}, u32[]{:S(2)}, u32[]{:S(2)}) collective-permute-start(bf16[2,272,512]{2,1,0:T(8,128)(2,1)S(1)} %pad_maximum_fusion), channel_id=1, source_target_pairs={{0,1},{1,0},{2,3},{3,2},{4,5},{5,4},{6,7},{7,6},{8,9},{9,8},{10,11... | collective-permute-start | bytes 1671176 | tf_op jit(solution)/shard_map/ppermute | solution.py:782
  34.8 2.8 %copy-start.6 = (bf16[256,1024]{1,0:T(8,128)(2,1)S(1)}, bf16[256,1024]{1,0:T(8,128)(2,1)}, u32[]{:S(2)}) copy-start(bf16[256,1024]{1,0:T(8,128)(2,1)} %q_ref.7) | copy-start | bytes 1572868
  34.8 2.8 %copy-start.8 = (f32[256,16]{0,1:T(8,128)S(1)}, f32[256,16]{0,1:T(8,128)}, u32[]{:S(2)}) copy-start(f32[256,16]{0,1:T(8,128)} %param.21) | copy-start | bytes 49156
  35.1 9.9 %collective-permute-start.3 = (bf16[1040,128]{1,0:T(8,128)(2,1)S(1)}, bf16[1040,128]{1,0:T(8,128)(2,1)S(1)}, u32[]{:S(2)}, u32[]{:S(2)}) collective-permute-start(bf16[1040,128]{1,0:T(8,128)(2,1)S(1)} %get-tuple-element.48.add_ref), channel_id=1, source_target_pairs={{0,2},{1,3},{2,4},{3,5},{4,6},{5,7},{8,10},{9,11},{10,12},{11,13},... | collective-permute-start | bytes 798728 | tf_op jit(solution)/shard_map/ppermute | solution.py:778
  37.5 0.7 %copy-start.2 = (s32[256]{0:T(256)S(1)}, s32[256]{0:T(256)}, u32[]{:S(2)}) copy-start(s32[256]{0:T(256)} %param.12) | copy-start | bytes 3076
  37.5 0.7 %copy-start.9 = (f32[128]{0:T(128)S(1)}, f32[128]{0:T(128)}, u32[]{:S(2)}) copy-start(f32[128]{0:T(128)} %param.23) | copy-start | bytes 1540
  38.2 2.8 %copy-start.4 = (bf16[256,2048]{1,0:T(8,128)(2,1)S(1)}, bf16[256,2048]{1,0:T(8,128)(2,1)}, u32[]{:S(2)}) copy-start(bf16[256,2048]{1,0:T(8,128)(2,1)} %gate_ref.6) | copy-start | bytes 3145732
  39.9 1.2 %copy-start.3 = (bf16[256,2048]{1,0:T(8,128)(2,1)S(1)}, bf16[256,2048]{1,0:T(8,128)(2,1)}, u32[]{:S(2)}) copy-start(bf16[256,2048]{1,0:T(8,128)(2,1)} %q_ref.6) | copy-start | bytes 3145732
  45.2 8.7 %collective-permute-start.5 = (bf16[1040,128]{1,0:T(8,128)(2,1)S(1)}, bf16[1040,128]{1,0:T(8,128)(2,1)S(1)}, u32[]{:S(2)}, u32[]{:S(2)}) collective-permute-start(bf16[1040,128]{1,0:T(8,128)(2,1)S(1)} %relay.1), channel_id=1, source_target_pairs={{0,2},{1,3},{2,4},{3,5},{4,6},{5,7},{8,10},{9,11},{10,12},{11,13},... | collective-permute-start | bytes 798728 | tf_op jit(solution)/shard_map/ppermute | solution.py:778
  47.2 3.8 %copy-start.10 = (bf16[2048,256]{1,0:T(8,128)(2,1)S(1)}, bf16[2048,256]{1,0:T(8,128)(2,1)}, u32[]{:S(2)}) copy-start(bf16[2048,256]{1,0:T(8,128)(2,1)} %get-tuple-element.64.solved_ref) | copy-start | bytes 3145732
  54.3 3.3 %collective-permute-start.6 = (bf16[1024,128]{1,0:T(8,128)(2,1)S(1)}, bf16[1024,128]{1,0:T(8,128)(2,1)S(1)}, u32[]{:S(2)}, u32[]{:S(2)}) collective-permute-start(bf16[1024,128]{1,0:T(8,128)(2,1)S(1)} %get-tuple-element.73), channel_id=1, source_target_pairs={{0,1},{1,0},{2,3},{3,2},{4,5},{5,4},{6,7},{7,6},{8,9},{9,8},{10,11... | collective-permute-start | bytes 786440 | tf_op jit(solution)/shard_map/ppermute | solution.py:782

commit v10 on v8

--- a/solution.py
+++ b/solution.py
@@ -290,8 +290,11 @@
     k_ref,
     decay_ref,
     solved_ref,
+    gate_ref,
+    gain_ref,
     reach_ref,
     inner_ref,
+    factor_ref,
     mask_ref,
     crow_ref,
     ccol_ref,
@@ -330,6 +333,9 @@
                 w["p"].append((span * probe).astype(bf16))
                 entry = jnp.exp2(cc[:, :TILE]) * first_ref[at]
                 w["scaled"].append((entry * qn).astype(bf16))
+                cols = slice(h * DV, (h + 1) * DV)
+                gate = gate_ref[at, cols].astype(f32)
+                factor_ref[at, cols] = gate * sigmoid(gate) * gain_ref[...]
             yield
 
     def finish(kk):
@@ -415,7 +421,7 @@
     )
 
 
-def delta_reach(half, seg_row, query, key, decay, solved):
+def delta_reach(half, seg_row, query, key, decay, gate, gain, solved):
     rows = key.shape[0]
     n = solved.shape[0] // rows
     return half_call(
@@ -423,9 +429,10 @@
         "delta_reach",
         20,
         half,
-        [seg_row, (query,), (key,), decay, solved],
+        [seg_row, (query,), (key,), decay, solved, (gate,), gain],
         [
             jax.ShapeDtypeStruct((rows, n * DK), bf16),
+            jax.ShapeDtypeStruct((rows, n * DV), f32),
             jax.ShapeDtypeStruct((rows, n * DV), f32),
         ],
         setup_scratch(rows, n),
@@ -505,53 +512,50 @@
     )(*args)
 
 
-def delta_out_kernel(half_ref, reach_ref, inner_ref, state_ref, gate_ref, gain_ref, *rest):
-    out_ref = rest[-1]
-    gain = gain_ref[...]
-    for h in range(state_ref.shape[0] // DK):
+def delta_out_kernel(half_ref, reach_ref, inner_ref, factor_ref, state_ref, *rest):
+    out_hbm, out_ref, sem = rest[-3:]
+    n = state_ref.shape[0] // DK
+    width = 2 * DV
+    copies = []
+    for h in range(n):
         cols = slice(h * DV, (h + 1) * DV)
-        state = state_ref[h * DK : (h + 1) * DK]
-        carried = dot(reach_ref[:, cols], state)
+        carried = dot(reach_ref[:, cols], state_ref[h * DK : (h + 1) * DK])
         for i in range(0, carried.shape[0], STRIP):
             at = slice(i, i + STRIP)
-            out = inner_ref[at, cols].astype(f32) + carried[at]
+            out = inner_ref[at, cols] + carried[at]
             spread = lax.rsqrt(jnp.mean(out * out, axis=1, keepdims=True) + EPS)
-            gate = gate_ref[at, cols].astype(f32)
-            gate = gate * sigmoid(gate)
-            out_ref[at, cols] = (out * spread * gain * gate).astype(bf16)
-
-
-def delta_out(half, reach, inner, state, gate, gain, partial_out=None):
+            out_ref[at, cols] = (out * spread * factor_ref[at, cols]).astype(bf16)
+        if h % 2 == 1:
+            start = (h - 1) * DV
+            target = pl.multiple_of(half_ref[0] * (n * DV) + start, width)
+            copies.append(
+                pltpu.make_async_copy(
+                    out_ref.at[:, pl.ds(start, width)],
+                    out_hbm.at[:, pl.ds(target, width)],
+                    sem.at[h // 2],
+                )
+            )
+            copies[-1].start()
+    for copy in copies:
+        copy.wait()
+
+
+def delta_out(half, reach, inner, factor, state, partial_out=None):
     rows = reach.shape[0]
     n = state.shape[0] // DK
-    heads = 4
-    steps = n // heads
-
-    def at_half(i, s):
-        return (0, s[0] * steps + i)
-
-    in_specs = [
-        pl.BlockSpec((rows, heads * DK), lambda i, s: (0, i)),
-        pl.BlockSpec((rows, heads * DV), lambda i, s: (0, i)),
-        pl.BlockSpec((heads * DK, DV), lambda i, s: (i, 0)),
-        pl.BlockSpec((rows, heads * DV), at_half),
-        pl.BlockSpec((1, DV), lambda i, s: (0, 0)),
-    ]
-    args = [half, reach, inner, state, gate, gain]
+    in_specs = [SMEM] + [VMEM] * 4
+    args = [half, reach, inner, factor, state]
     aliases = {}
     if partial_out is not None:
+        aliases = {len(args): 0}
         in_specs.append(pl.BlockSpec(memory_space=pl.ANY))
         args.append(partial_out)
-        aliases = {6: 0}
     return pl.pallas_call(
         delta_out_kernel,
-        grid_spec=pltpu.PrefetchScalarGridSpec(
-            num_scalar_prefetch=1,
-            grid=(steps,),
-            in_specs=in_specs,
-            out_specs=pl.BlockSpec((rows, heads * DV), at_half),
-        ),
-        out_shape=jax.ShapeDtypeStruct(gate.shape, bf16),
+        in_specs=in_specs,
+        out_specs=pl.BlockSpec(memory_space=pl.ANY),
+        out_shape=jax.ShapeDtypeStruct((rows, 2 * n * DV), bf16),
+        scratch_shapes=[pltpu.VMEM((rows, n * DV), bf16), pltpu.SemaphoreType.DMA((n // 2,))],
         input_output_aliases=aliases,
         compiler_params=params(),
         cost_estimate=cost(10**8, 3 * 2**20),
@@ -748,15 +752,21 @@
         decay=decay_rows,
     )
     reach = partial(
-        delta_reach, seg_row=ids, query=delta_query, key=delta_key, decay=decay_rows
-    )
-    give_ma, give_solved = local(give_half, 60)
+        delta_reach,
+        seg_row=ids,
+        query=delta_query,
+        key=delta_key,
+        decay=decay_rows,
+        gate=delta_gate,
+        gain=norm_gain.reshape(1, DV),
+    )
+    give_ma, give_solved = local(give_half, 20)
     other_ma = swap_cores(give_ma, ranks)
     nearest, give_ma = lax.optimization_barrier((nearest, give_ma))
     same = [nearest]
     for _ in range(hops - 1):
         same.append(up_chip(same[-1], ranks))
-    keep_ma, keep_solved = local(keep_half, 60)
+    keep_ma, keep_solved = local(keep_half, 20)
     same, keep_ma, other_ma = lax.optimization_barrier((same, keep_ma, other_ma))
     chain = [own, *same]
     other = swap_cores(
@@ -799,8 +809,8 @@
     for _ in range(hops - 1):
         (leaving,) = small_call(relay_kernel, "relay", [state_like], chip_map, chip_add, state)
         state = up_chip(leaving, ranks)
+    attn_mixed, keep_solved, leaving = lax.optimization_barrier((attn_mixed, keep_solved, leaving))
     attn_mixed = attention_half(1, window_arrays, attn_query, attn_gate, attn_mixed)
-    keep_solved, leaving = lax.optimization_barrier((keep_solved, leaving))
     keep_rows = reach(keep_half, solved=keep_solved)
     state, attn_mixed, keep_rows = lax.optimization_barrier((state, attn_mixed, keep_rows))
 
@@ -810,11 +820,8 @@
     )
     give_state = swap_cores(pass_state, ranks)
 
-    gain = norm_gain.reshape(1, DV)
-    delta_mixed = delta_out(keep_half, *keep_rows, keep_state, delta_gate, gain)
-    delta_mixed = delta_out(
-        give_half, *give_rows, give_state, delta_gate, gain, delta_mixed
-    )
+    delta_mixed = delta_out(keep_half, *keep_rows, keep_state)
+    delta_mixed = delta_out(give_half, *give_rows, give_state, delta_mixed)
     return (attn_mixed, delta_mixed)
 
 

time: 51.4 us -> 51.5 us (level)
  Pallas kernels: 31.9 us -> 27 us
  waiting for transfers between devices: 1.13 us -> 3.7 us
  local copies, waits for them, and re-layouts: 1.37 us -> 3.8 us
    pallas_call x4, Pallas kernels: 17.2 us -> 13.4 us  [half_call(): pl.pallas_call(kernel, grid_spec=pltpu.PrefetchScalarGridSpec(num_scalar_...]
    ppermute x4, waiting for transfers between devices: 1.12 us -> 3.7 us  [up_chip(): return lax.ppermute(value, 'ctx', [(i, i + 2) for i in range(ranks - 2)])]
    unnamed x24 -> x28, local copies, waits for them, and re-layouts: 1.3 us -> 3.73 us
    pallas_call x2, Pallas kernels: 3.51 us -> 2.41 us  [delta_out(): pl.pallas_call(delta_out_kernel, in_specs=in_specs, out_specs=pl.BlockSpe...]
  transfers between devices with their start and end apart: 7 -> 7, of which waited for: 1 -> 2; matrix products, arithmetic and copies ran while one was open for 0% -> 0% of each run, Pallas kernels for 55% -> 46%
where the time goes in v10:
time: 51.5 us; the launch traced here: 50.9 us
  Pallas kernels  27 us (52%)
  starting transfers between devices  15.2 us (30%)
  local copies, waits for them, and re-layouts  3.8 us (7%)
  waiting for transfers between devices  3.7 us (7%)
  between operations  1.04 us (2%)
    pallas_call x4, Pallas kernels, half_call(): pl.pallas_call(kernel, grid_spec=pltpu.PrefetchScalarGridSpec(num_scalar_...  13.4 us
    ppermute x4, starting transfers between devices, up_chip(): return lax.ppermute(value, 'ctx', [(i, i + 2) for i in range(ranks - 2)])  12 us
    pallas_call x2, Pallas kernels, attention_half(): pl.pallas_call(attention_kernel, grid=(steps,), in_specs=in_specs, out_sp...  7.65 us
    unnamed x28, local copies, waits for them, and re-layouts  3.73 us
    ppermute x4, waiting for transfers between devices, up_chip(): return lax.ppermute(value, 'ctx', [(i, i + 2) for i in range(ranks - 2)])  3.7 us
    pallas_call x5, Pallas kernels, small_call(): pl.pallas_call(kernel, in_specs=[SMEM] * scalars + [VMEM] * (len(args) -...  3.62 us
    ppermute x3, starting transfers between devices, swap_cores(): return lax.ppermute(value, 'ctx', [(i, i ^ 1) for i in range(ranks)])  3.17 us
    pallas_call x2, Pallas kernels, delta_out(): pl.pallas_call(delta_out_kernel, in_specs=in_specs, out_specs=pl.BlockSpe...  2.41 us
  transfers between devices with their start and end apart: 7, of which 2 were waited for; matrix products, arithmetic and copies ran while one was open for 0% of the time, Pallas kernels for 46%

profile of v10, /device:TPU:9, one launch (start us, length us, event | category | flops | bytes accessed | tf_op | source)
XLA Modules:
  0.0 50.9 jit_solution(11557792622510728693)
XLA Ops:
  0.6 1.8 %pack.1.rest_0_ = bf16[272,512]{1,0:T(8,128)(2,1)} custom-call(s32[1,256]{1,0:T(1,128)} %bitcast.9, bf16[256,256]{1,0:T(8,128)(2,1)} %key_ref.1, bf16[256,256]{1,0:T(8,128)(2,1)} %value_ref.1), custom_call_target="tpu_custom_call" | custom-call | flops 100000000 | bytes 1048576 | tf_op jit(solution)/shard_map/pack/pallas_call | solution.py:504
  2.4 3.2 %collective-permute-start = (bf16[272,512]{1,0:T(8,128)(2,1)}, bf16[272,512]{1,0:T(8,128)(2,1)S(1)}, u32[]{:S(2)}, u32[]{:S(2)}) collective-permute-start(bf16[272,512]{1,0:T(8,128)(2,1)} %pack.1.rest_0_), channel_id=1, source_target_pairs={{0,2},{1,3},{2,4},{3,5},{4,6},{5,7},{8,10},{9,11},{10,12},{11,13},... | collective-permute-start | bytes 835592 | tf_op jit(solution)/shard_map/ppermute | solution.py:702
  5.6 0.0 copy-start.10
  5.7 0.7 %copy-done.10 = f32[256,16]{0,1:T(8,128)S(1)} copy-done((f32[256,16]{0,1:T(8,128)S(1)}, f32[256,16]{0,1:T(8,128)}, u32[]{:S(2)}) %copy-start.10) | copy-done | bytes 16408
  6.3 0.0 copy-done.9
  6.4 1.2 %copy-done.2 = bf16[256,2048]{1,0:T(8,128)(2,1)S(1)} copy-done((bf16[256,2048]{1,0:T(8,128)(2,1)S(1)}, bf16[256,2048]{1,0:T(8,128)(2,1)}, u32[]{:S(2)}) %copy-start.2) | copy-done | bytes 1048600
  7.6 5.0 %delta_local.2 = (bf16[1040,256]{1,0:T(8,128)(2,1)S(1)}, bf16[2048,256]{1,0:T(8,128)(2,1)S(1)}) custom-call(s32[1]{0:T(128)S(6)} %sub.3.half_ref, s32[1,256]{1,0:T(1,128)S(1)} %bitcast.10, bf16[256,1024]{1,0:T(8,128)(2,1)S(1)} %copy-done.8, bf16[256,2048]{1,0:T(8,128)(2,1)S(1)} %copy-done.2, f32[16,256]{1,0:T(8,128)S(1)} %bitcast.14, f32[16,256]{1,0:T(8,128)S(1)} %bitcast.16), custom_call_target="tpu_custom_call" | custom-call | flops 4000000000 | bytes 3145728 | tf_op jit(solution)/shard_map/delta_local/pallas_call | solution.py:376
  12.6 1.0 %copy-done.12 = bf16[2048,256]{1,0:T(8,128)(2,1)} copy-done((bf16[2048,256]{1,0:T(8,128)(2,1)}, bf16[2048,256]{1,0:T(8,128)(2,1)S(1)}, u32[]{:S(2)}) %copy-start.12) | copy-done | bytes 1048600
  13.6 1.0 %collective-permute-start.2 = (bf16[1040,256]{1,0:T(8,128)(2,1)S(1)}, bf16[1040,256]{1,0:T(8,128)(2,1)S(1)}, u32[]{:S(2)}, u32[]{:S(2)}) collective-permute-start(bf16[1040,256]{1,0:T(8,128)(2,1)S(1)} %get-tuple-element.40), channel_id=1, source_target_pairs={{0,1},{1,0},{2,3},{3,2},{4,5},{5,4},{6,7},{7,6},{8,9},{9,8},{10,11... | collective-permute-start | bytes 1597448 | tf_op jit(solution)/shard_map/ppermute | solution.py:706
  14.5 3.3 %collective-permute-start.1 = (bf16[272,512]{1,0:T(8,128)(2,1)S(1)}, bf16[272,512]{1,0:T(8,128)(2,1)S(1)}, u32[]{:S(2)}, u32[]{:S(2)}) collective-permute-start(bf16[272,512]{1,0:T(8,128)(2,1)S(1)} %collective-permute-done.rest_1_), channel_id=1, source_target_pairs={{0,2},{1,3},{2,4},{3,5},{4,6},{5,7},{8,10},{9,11},{10,12},{11,13},... | collective-permute-start | bytes 835592 | tf_op jit(solution)/shard_map/ppermute | solution.py:702
  17.9 5.0 %delta_local.3 = (bf16[1040,256]{1,0:T(8,128)(2,1)S(1)}, bf16[2048,256]{1,0:T(8,128)(2,1)S(1)}) custom-call(s32[1]{0:T(128)} %bitcast.half_ref.core_ref, s32[1,256]{1,0:T(1,128)S(1)} %bitcast.11, bf16[256,1024]{1,0:T(8,128)(2,1)S(1)} %copy-done.8, bf16[256,2048]{1,0:T(8,128)(2,1)S(1)} %copy-done.3, f32[16,256]{1,0:T(8,128)S(1)} %bitcast.15, ...), custom_call_target="tpu_custom_call" | custom-call | flops 4000000000 | bytes 3145728 | tf_op jit(solution)/shard_map/delta_local/pallas_call | solution.py:376
  22.9 1.9 %collective-permute-done.1.rest_2_ = bf16[272,512]{1,0:T(8,128)(2,1)S(1)} collective-permute-done((bf16[272,512]{1,0:T(8,128)(2,1)S(1)}, bf16[272,512]{1,0:T(8,128)(2,1)S(1)}, u32[]{:S(2)}, u32[]{:S(2)}) %collective-permute-start.1) | collective-permute-done | bytes 278560 | tf_op jit(solution)/shard_map/ppermute | solution.py:702
  24.8 0.1 select_bitcast_fusion.1
  24.9 0.1 pad_maximum_fusion
  25.0 0.9 %collective-permute-start.4 = (bf16[2,272,512]{2,1,0:T(8,128)(2,1)S(1)}, bf16[2,272,512]{2,1,0:T(8,128)(2,1)S(1)}, u32[]{:S(2)}, u32[]{:S(2)}) collective-permute-start(bf16[2,272,512]{2,1,0:T(8,128)(2,1)S(1)} %pad_maximum_fusion), channel_id=1, source_target_pairs={{0,1},{1,0},{2,3},{3,2},{4,5},{5,4},{6,7},{7,6},{8,9},{9,8},{10,11... | collective-permute-start | bytes 1671176 | tf_op jit(solution)/shard_map/ppermute | solution.py:706
  25.8 0.3 compose.1
  26.2 3.4 %collective-permute-start.3 = (bf16[1040,128]{1,0:T(8,128)(2,1)S(1)}, bf16[1040,128]{1,0:T(8,128)(2,1)S(1)}, u32[]{:S(2)}, u32[]{:S(2)}) collective-permute-start(bf16[1040,128]{1,0:T(8,128)(2,1)S(1)} %get-tuple-element.48.add_ref), channel_id=1, source_target_pairs={{0,2},{1,3},{2,4},{3,5},{4,6},{5,7},{8,10},{9,11},{10,12},{11,13},... | collective-permute-start | bytes 798728 | tf_op jit(solution)/shard_map/ppermute | solution.py:702
  29.6 0.6 %copy-done.11 = f32[128]{0:T(128)S(1)} copy-done((f32[128]{0:T(128)S(1)}, f32[128]{0:T(128)}, u32[]{:S(2)}) %copy-start.11) | copy-done | bytes 536
  30.2 1.7 %delta_reach.2 = (bf16[256,1024]{1,0:T(8,128)(2,1)S(1)}, f32[256,1024]{1,0:T(8,128)S(1)}, f32[256,1024]{1,0:T(8,128)S(1)}) custom-call(s32[1]{0:T(128)S(6)} %sub.3.half_ref, s32[1,256]{1,0:T(1,128)S(1)} %bitcast.12, bf16[256,1024]{1,0:T(8,128)(2,1)S(1)} %copy-done.7, bf16[256,1024]{1,0:T(8,128)(2,1)S(1)} %copy-done.8, f32[16,256]{1,0:T(8,128)S(1)} %bitcast.18, ...), custom_call_target="tpu_custom_call" | custom-call | flops 4000000000 | bytes 3145728 | tf_op jit(solution)/shard_map/delta_reach/pallas_call | solution.py:376
  31.9 0.1 broadcast_in_dim.2.freq_ref
  32.0 0.9 %window.1 = (bf16[256,1280]{1,0:T(8,128)(2,1)S(1)}, bf16[1280,256]{1,0:T(8,128)(2,1)S(1)}, f32[1,1280]{1,0:T(1,128)S(1)}, f32[256,128]{1,0:T(8,128)S(1)}, f32[256,128]{1,0:T(8,128)S(1)}) custom-call(f32[32,128]{1,0:T(8,128)S(1)} %broadcast_in_dim.2.freq_ref, bf16[272,512]{1,0:T(8,128)(2,1)S(1)} %copy-done, ...), custom_call_target="tpu_custom_call" | custom-call | flops 100000000 | bytes 1048576 | tf_op jit(solution)/shard_map/window/pallas_call | solution.py:504
  32.9 0.2 copy-done.4
  33.1 3.8 %attention.2.rest_0_ = bf16[256,2048]{1,0:T(8,128)(2,1)} custom-call(f32[1,1280]{1,0:T(1,128)S(1)} %get-tuple-element.51.ids_ref, f32[256,128]{1,0:T(8,128)S(1)} %get-tuple-element.52.cos_ref, f32[256,128]{1,0:T(8,128)S(1)} %get-tuple-element.53.sin_ref, bf16[256,1280]{1,0:T(8,128)(2,1)S(1)} %get-tuple-element.54.kt_ref, ...), custom_call_target="tpu_custom_call" | custom-call | flops 5000000000 | bytes 3145728 | tf_op jit(solution)/shard_map/attention/pallas_call | solution.py:687
  37.0 0.2 relay.1
  37.2 2.1 %collective-permute-start.5 = (bf16[1040,128]{1,0:T(8,128)(2,1)S(1)}, bf16[1040,128]{1,0:T(8,128)(2,1)S(1)}, u32[]{:S(2)}, u32[]{:S(2)}) collective-permute-start(bf16[1040,128]{1,0:T(8,128)(2,1)S(1)} %relay.1), channel_id=1, source_target_pairs={{0,2},{1,3},{2,4},{3,5},{4,6},{5,7},{8,10},{9,11},{10,12},{11,13},... | collective-permute-start | bytes 798728 | tf_op jit(solution)/shard_map/ppermute | solution.py:702
  39.3 3.8 %attention.3 = bf16[256,2048]{1,0:T(8,128)(2,1)} custom-call(f32[1,1280]{1,0:T(1,128)S(1)} %get-tuple-element.51.ids_ref, f32[256,128]{1,0:T(8,128)S(1)} %get-tuple-element.52.cos_ref, f32[256,128]{1,0:T(8,128)S(1)} %get-tuple-element.53.sin_ref, bf16[256,1280]{1,0:T(8,128)(2,1)S(1)} %get-tuple-element.54.kt_ref, ...), custom_call_target="tpu_custom_call", output_to_operand_aliasing={{}: (7, {})} | custom-call | flops 5000000000 | bytes 3145728 | tf_op jit(solution)/shard_map/attention/pallas_call | solution.py:687
  43.2 1.7 %delta_reach.3 = (bf16[256,1024]{1,0:T(8,128)(2,1)S(1)}, f32[256,1024]{1,0:T(8,128)S(1)}, f32[256,1024]{1,0:T(8,128)S(1)}) custom-call(s32[1]{0:T(128)} %bitcast.half_ref.core_ref, s32[1,256]{1,0:T(1,128)S(1)} %bitcast.13, bf16[256,1024]{1,0:T(8,128)(2,1)S(1)} %copy-done.7, bf16[256,1024]{1,0:T(8,128)(2,1)S(1)} %copy-done.8, f32[16,256]{1,0:T(8,128)S(1)} %bitcast.19, ...), custom_call_target="tpu_custom_call" | custom-call | flops 4000000000 | bytes 3145728 | tf_op jit(solution)/shard_map/delta_reach/pallas_call | solution.py:376
  44.8 1.8 %collective-permute-done.5.state_ref = bf16[1040,128]{1,0:T(8,128)(2,1)S(1)} collective-permute-done((bf16[1040,128]{1,0:T(8,128)(2,1)S(1)}, bf16[1040,128]{1,0:T(8,128)(2,1)S(1)}, u32[]{:S(2)}, u32[]{:S(2)}) %collective-permute-start.5) | collective-permute-done | bytes 266272 | tf_op jit(solution)/shard_map/ppermute | solution.py:702
  46.6 0.4 arrive.1
  47.0 1.3 %collective-permute-start.6 = (bf16[1024,128]{1,0:T(8,128)(2,1)S(1)}, bf16[1024,128]{1,0:T(8,128)(2,1)S(1)}, u32[]{:S(2)}, u32[]{:S(2)}) collective-permute-start(bf16[1024,128]{1,0:T(8,128)(2,1)S(1)} %get-tuple-element.73), channel_id=1, source_target_pairs={{0,1},{1,0},{2,3},{3,2},{4,5},{5,4},{6,7},{7,6},{8,9},{9,8},{10,11... | collective-permute-start | bytes 786440 | tf_op jit(solution)/shard_map/ppermute | solution.py:706
  48.3 1.2 %delta_out.2.rest_0_ = bf16[256,2048]{1,0:T(8,128)(2,1)} custom-call(s32[1]{0:T(128)} %bitcast.half_ref.core_ref, bf16[256,1024]{1,0:T(8,128)(2,1)S(1)} %get-tuple-element.74.reach_ref, f32[256,1024]{1,0:T(8,128)S(1)} %get-tuple-element.75.inner_ref, f32[256,1024]{1,0:T(8,128)S(1)} %get-tuple-element.76.factor_ref, ...), custom_call_target="tpu_custom_call" | custom-call | flops 100000000 | bytes 3145728 | tf_op jit(solution)/shard_map/delta_out/pallas_call | solution.py:553
  49.6 1.2 %delta_out.3 = bf16[256,2048]{1,0:T(8,128)(2,1)} custom-call(s32[1]{0:T(128)S(6)} %sub.3.half_ref, bf16[256,1024]{1,0:T(8,128)(2,1)S(1)} %get-tuple-element.69.reach_ref, f32[256,1024]{1,0:T(8,128)S(1)} %get-tuple-element.70.inner_ref, f32[256,1024]{1,0:T(8,128)S(1)} %get-tuple-element.71.factor_ref, ...), custom_call_target="tpu_custom_call", output_to_operand_aliasing={{}: (5, {})} | custom-call | flops 100000000 | bytes 3145728 | tf_op jit(solution)/shard_map/delta_out/pallas_call | solution.py:553
  (27 shorter events, 0.1 us)
Async XLA Ops:
  0.6 5.0 %copy-start.8 = (bf16[256,1024]{1,0:T(8,128)(2,1)S(1)}, bf16[256,1024]{1,0:T(8,128)(2,1)}, u32[]{:S(2)}) copy-start(bf16[256,1024]{1,0:T(8,128)(2,1)} %k_ref.7) | copy-start | bytes 1572868
  2.4 12.1 %collective-permute-start = (bf16[272,512]{1,0:T(8,128)(2,1)}, bf16[272,512]{1,0:T(8,128)(2,1)S(1)}, u32[]{:S(2)}, u32[]{:S(2)}) collective-permute-start(bf16[272,512]{1,0:T(8,128)(2,1)} %pack.1.rest_0_), channel_id=1, source_target_pairs={{0,2},{1,3},{2,4},{3,5},{4,6},{5,7},{8,10},{9,11},{10,12},{11,13},... | collective-permute-start | bytes 835592 | tf_op jit(solution)/shard_map/ppermute | solution.py:702
  5.6 0.7 %copy-start.10 = (f32[256,16]{0,1:T(8,128)S(1)}, f32[256,16]{0,1:T(8,128)}, u32[]{:S(2)}) copy-start(f32[256,16]{0,1:T(8,128)} %param.21) | copy-start | bytes 49156
  5.6 0.7 %copy-start.9 = (f32[256,16]{0,1:T(8,128)S(1)}, f32[256,16]{0,1:T(8,128)}, u32[]{:S(2)}) copy-start(f32[256,16]{0,1:T(8,128)} %param.20) | copy-start | bytes 49156
  5.6 0.7 %copy-start.1 = (s32[256]{0:T(256)S(1)}, s32[256]{0:T(256)}, u32[]{:S(2)}) copy-start(s32[256]{0:T(256)} %param.12) | copy-start | bytes 3076
  6.4 1.2 %copy-start.2 = (bf16[256,2048]{1,0:T(8,128)(2,1)S(1)}, bf16[256,2048]{1,0:T(8,128)(2,1)}, u32[]{:S(2)}) copy-start(bf16[256,2048]{1,0:T(8,128)(2,1)} %v_ref.3) | copy-start | bytes 3145732
  7.6 10.3 %copy-start.3 = (bf16[256,2048]{1,0:T(8,128)(2,1)S(1)}, bf16[256,2048]{1,0:T(8,128)(2,1)}, u32[]{:S(2)}) copy-start(bf16[256,2048]{1,0:T(8,128)(2,1)} %v_ref.3) | copy-start | bytes 3145732
  12.6 1.0 %copy-start.12 = (bf16[2048,256]{1,0:T(8,128)(2,1)}, bf16[2048,256]{1,0:T(8,128)(2,1)S(1)}, u32[]{:S(2)}) copy-start(bf16[2048,256]{1,0:T(8,128)(2,1)S(1)} %get-tuple-element.56.solved_ref) | copy-start | bytes 3145732
  13.6 9.3 %collective-permute-start.2 = (bf16[1040,256]{1,0:T(8,128)(2,1)S(1)}, bf16[1040,256]{1,0:T(8,128)(2,1)S(1)}, u32[]{:S(2)}, u32[]{:S(2)}) collective-permute-start(bf16[1040,256]{1,0:T(8,128)(2,1)S(1)} %get-tuple-element.40), channel_id=1, source_target_pairs={{0,1},{1,0},{2,3},{3,2},{4,5},{5,4},{6,7},{7,6},{8,9},{9,8},{10,11... | collective-permute-start | bytes 1597448 | tf_op jit(solution)/shard_map/ppermute | solution.py:706
  14.5 10.3 %copy-start = (bf16[272,512]{1,0:T(8,128)(2,1)S(1)}, bf16[272,512]{1,0:T(8,128)(2,1)}, u32[]{:S(2)}) copy-start(bf16[272,512]{1,0:T(8,128)(2,1)} %pack.1.rest_0_) | copy-start | bytes 835588
  14.5 10.3 %collective-permute-start.1 = (bf16[272,512]{1,0:T(8,128)(2,1)S(1)}, bf16[272,512]{1,0:T(8,128)(2,1)S(1)}, u32[]{:S(2)}, u32[]{:S(2)}) collective-permute-start(bf16[272,512]{1,0:T(8,128)(2,1)S(1)} %collective-permute-done.rest_1_), channel_id=1, source_target_pairs={{0,2},{1,3},{2,4},{3,5},{4,6},{5,7},{8,10},{9,11},{10,12},{11,13},... | collective-permute-start | bytes 835592 | tf_op jit(solution)/shard_map/ppermute | solution.py:702
  24.8 4.7 %copy-start.13 = (bf16[2048,256]{1,0:T(8,128)(2,1)S(1)}, bf16[2048,256]{1,0:T(8,128)(2,1)}, u32[]{:S(2)}) copy-start(bf16[2048,256]{1,0:T(8,128)(2,1)} %copy-done.12) | copy-start | bytes 3145732
  24.9 4.7 %copy-start.6 = (bf16[256,2048]{1,0:T(8,128)(2,1)S(1)}, bf16[256,2048]{1,0:T(8,128)(2,1)}, u32[]{:S(2)}) copy-start(bf16[256,2048]{1,0:T(8,128)(2,1)} %gate_ref.7) | copy-start | bytes 3145732
  25.0 7.0 %collective-permute-start.4 = (bf16[2,272,512]{2,1,0:T(8,128)(2,1)S(1)}, bf16[2,272,512]{2,1,0:T(8,128)(2,1)S(1)}, u32[]{:S(2)}, u32[]{:S(2)}) collective-permute-start(bf16[2,272,512]{2,1,0:T(8,128)(2,1)S(1)} %pad_maximum_fusion), channel_id=1, source_target_pairs={{0,1},{1,0},{2,3},{3,2},{4,5},{5,4},{6,7},{7,6},{8,9},{9,8},{10,11... | collective-permute-start | bytes 1671176 | tf_op jit(solution)/shard_map/ppermute | solution.py:706
  25.8 3.8 %copy-start.7 = (bf16[256,1024]{1,0:T(8,128)(2,1)S(1)}, bf16[256,1024]{1,0:T(8,128)(2,1)}, u32[]{:S(2)}) copy-start(bf16[256,1024]{1,0:T(8,128)(2,1)} %q_ref.7) | copy-start | bytes 1572868
  26.2 10.8 %collective-permute-start.3 = (bf16[1040,128]{1,0:T(8,128)(2,1)S(1)}, bf16[1040,128]{1,0:T(8,128)(2,1)S(1)}, u32[]{:S(2)}, u32[]{:S(2)}) collective-permute-start(bf16[1040,128]{1,0:T(8,128)(2,1)S(1)} %get-tuple-element.48.add_ref), channel_id=1, source_target_pairs={{0,2},{1,3},{2,4},{3,5},{4,6},{5,7},{8,10},{9,11},{10,12},{11,13},... | collective-permute-start | bytes 798728 | tf_op jit(solution)/shard_map/ppermute | solution.py:702
  29.6 0.7 %copy-start.11 = (f32[128]{0:T(128)S(1)}, f32[128]{0:T(128)}, u32[]{:S(2)}) copy-start(f32[128]{0:T(128)} %param.23) | copy-start | bytes 1540
  30.2 2.7 %copy-start.5 = (bf16[256,2048]{1,0:T(8,128)(2,1)S(1)}, bf16[256,2048]{1,0:T(8,128)(2,1)}, u32[]{:S(2)}) copy-start(bf16[256,2048]{1,0:T(8,128)(2,1)} %gate_ref.6) | copy-start | bytes 3145732
  31.9 1.2 %copy-start.4 = (bf16[256,2048]{1,0:T(8,128)(2,1)S(1)}, bf16[256,2048]{1,0:T(8,128)(2,1)}, u32[]{:S(2)}) copy-start(bf16[256,2048]{1,0:T(8,128)(2,1)} %q_ref.6) | copy-start | bytes 3145732
  37.2 9.4 %collective-permute-start.5 = (bf16[1040,128]{1,0:T(8,128)(2,1)S(1)}, bf16[1040,128]{1,0:T(8,128)(2,1)S(1)}, u32[]{:S(2)}, u32[]{:S(2)}) collective-permute-start(bf16[1040,128]{1,0:T(8,128)(2,1)S(1)} %relay.1), channel_id=1, source_target_pairs={{0,2},{1,3},{2,4},{3,5},{4,6},{5,7},{8,10},{9,11},{10,12},{11,13},... | collective-permute-start | bytes 798728 | tf_op jit(solution)/shard_map/ppermute | solution.py:702
  47.0 2.6 %collective-permute-start.6 = (bf16[1024,128]{1,0:T(8,128)(2,1)S(1)}, bf16[1024,128]{1,0:T(8,128)(2,1)S(1)}, u32[]{:S(2)}, u32[]{:S(2)}) collective-permute-start(bf16[1024,128]{1,0:T(8,128)(2,1)S(1)} %get-tuple-element.73), channel_id=1, source_target_pairs={{0,1},{1,0},{2,3},{3,2},{4,5},{5,4},{6,7},{7,6},{8,9},{9,8},{10,11... | collective-permute-start | bytes 786440 | tf_op jit(solution)/shard_map/ppermute | solution.py:706

commit v11 on v10

--- a/solution.py
+++ b/solution.py
@@ -36,7 +36,9 @@
 
 
 def cost(flops, nbytes, exps=0):
-    return pl.CostEstimate(flops=flops, bytes_accessed=nbytes, transcendentals=exps)
+    return pl.CostEstimate(
+        flops=flops // 10**4, bytes_accessed=nbytes // 10**4, transcendentals=exps // 10**4
+    )
 
 
 BLOCK = 16
@@ -767,11 +769,7 @@
     for _ in range(hops - 1):
         same.append(up_chip(same[-1], ranks))
     keep_ma, keep_solved = local(keep_half, 20)
-    same, keep_ma, other_ma = lax.optimization_barrier((same, keep_ma, other_ma))
-    chain = [own, *same]
-    other = swap_cores(
-        jnp.stack([jnp.where(odd, chain[i + 1], chain[i]) for i in range(hops)]), ranks
-    )
+    keep_ma, other_ma = lax.optimization_barrier((keep_ma, other_ma))
 
     tall = keep_ma.shape[0]
     state_like = jax.ShapeDtypeStruct((tall, DV), bf16)
@@ -779,6 +777,16 @@
         compose_kernel, "compose", [state_like] * 2, keep_half, keep_ma, other_ma, scalars=1
     )
     state = up_chip(chip_add, ranks)
+    give_solved, keep_solved, _ = lax.optimization_barrier((give_solved, keep_solved, chip_add))
+    give_rows = reach(give_half, solved=give_solved)
+    same, keep_solved, give_rows = lax.optimization_barrier((same, keep_solved, give_rows))
+    chain = [own, *same]
+    other = swap_cores(
+        jnp.stack([jnp.where(odd, chain[i + 1], chain[i]) for i in range(hops)]), ranks
+    )
+
+    keep_rows = reach(keep_half, solved=keep_solved)
+    other, keep_rows = lax.optimization_barrier((other, keep_rows))
 
     window = (2 * hops + 1) * rows
     index = jnp.arange(ROTARY_ENTRIES // 2).astype(f32)
@@ -802,17 +810,14 @@
     kt, v_all, window_ids, cosine, sine = window_arrays
     window_arrays = (window_ids, cosine, sine, kt, v_all)
     attn_mixed = attention_half(0, window_arrays, attn_query, attn_gate)
-    give_solved, chip_add = lax.optimization_barrier((give_solved, chip_add))
-    give_rows = reach(give_half, solved=give_solved)
-    state, attn_mixed, give_rows = lax.optimization_barrier((state, attn_mixed, give_rows))
+    state, attn_mixed = lax.optimization_barrier((state, attn_mixed))
     leaving = chip_add
     for _ in range(hops - 1):
         (leaving,) = small_call(relay_kernel, "relay", [state_like], chip_map, chip_add, state)
         state = up_chip(leaving, ranks)
-    attn_mixed, keep_solved, leaving = lax.optimization_barrier((attn_mixed, keep_solved, leaving))
+    attn_mixed, leaving = lax.optimization_barrier((attn_mixed, leaving))
     attn_mixed = attention_half(1, window_arrays, attn_query, attn_gate, attn_mixed)
-    keep_rows = reach(keep_half, solved=keep_solved)
-    state, attn_mixed, keep_rows = lax.optimization_barrier((state, attn_mixed, keep_rows))
+    state, attn_mixed = lax.optimization_barrier((state, attn_mixed))
 
     final_like = jax.ShapeDtypeStruct((tall - BLOCK, DV), bf16)
     keep_state, pass_state = small_call(

time: 51.5 us -> 53.3 us (1.035)
  local copies, waits for them, and re-layouts: 3.8 us -> 6.08 us
  starting transfers between devices: 15.2 us -> 14 us
  Pallas kernels: 27 us -> 27.8 us
    unnamed x28 -> x30, local copies, waits for them, and re-layouts: 3.73 us -> 6.01 us
    ppermute x4, starting transfers between devices: 12 us -> 10.5 us  [up_chip(): return lax.ppermute(value, 'ctx', [(i, i + 2) for i in range(ranks - 2)])]
    pallas_call x4, Pallas kernels: 13.4 us -> 14.1 us  [half_call(): pl.pallas_call(kernel, grid_spec=pltpu.PrefetchScalarGridSpec(num_scalar_...]
where the time goes in v11:
time: 53.3 us; the launch traced here: 52.7 us
  Pallas kernels  27.8 us (52%)
  starting transfers between devices  14 us (26%)
  local copies, waits for them, and re-layouts  6.08 us (11%)
  waiting for transfers between devices  3.65 us (7%)
  between operations  1.05 us (2%)
    pallas_call x4, Pallas kernels, half_call(): pl.pallas_call(kernel, grid_spec=pltpu.PrefetchScalarGridSpec(num_scalar_...  14.1 us
    ppermute x4, starting transfers between devices, up_chip(): return lax.ppermute(value, 'ctx', [(i, i + 2) for i in range(ranks - 2)])  10.5 us
    pallas_call x2, Pallas kernels, attention_half(): pl.pallas_call(attention_kernel, grid=(steps,), in_specs=in_specs, out_sp...  7.69 us
    unnamed x30, local copies, waits for them, and re-layouts  6.01 us
    ppermute x4, waiting for transfers between devices, up_chip(): return lax.ppermute(value, 'ctx', [(i, i + 2) for i in range(ranks - 2)])  3.64 us
    pallas_call x5, Pallas kernels, small_call(): pl.pallas_call(kernel, in_specs=[SMEM] * scalars + [VMEM] * (len(args) -...  3.62 us
    ppermute x3, starting transfers between devices, swap_cores(): return lax.ppermute(value, 'ctx', [(i, i ^ 1) for i in range(ranks)])  3.46 us
    pallas_call x2, Pallas kernels, delta_out(): pl.pallas_call(delta_out_kernel, in_specs=in_specs, out_specs=pl.BlockSpe...  2.41 us
  transfers between devices with their start and end apart: 7, of which 2 were waited for; matrix products, arithmetic and copies ran while one was open for 0% of the time, Pallas kernels for 46%

profile of v11, /device:TPU:9, one launch (start us, length us, event | category | flops | bytes accessed | tf_op | source)
XLA Modules:
  0.0 52.7 jit_solution(1364906362222268973)
XLA Ops:
  0.7 1.8 %pack.1.rest_0_ = bf16[272,512]{1,0:T(8,128)(2,1)} custom-call(s32[1,256]{1,0:T(1,128)} %bitcast.15, bf16[256,256]{1,0:T(8,128)(2,1)} %key_ref.1, bf16[256,256]{1,0:T(8,128)(2,1)} %value_ref.1), custom_call_target="tpu_custom_call" | custom-call | flops 10000 | bytes 104 | tf_op jit(solution)/shard_map/pack/pallas_call | solution.py:506
  2.4 3.2 %collective-permute-start.2 = (bf16[272,512]{1,0:T(8,128)(2,1)}, bf16[272,512]{1,0:T(8,128)(2,1)S(1)}, u32[]{:S(2)}, u32[]{:S(2)}) collective-permute-start(bf16[272,512]{1,0:T(8,128)(2,1)} %pack.1.rest_0_), channel_id=1, source_target_pairs={{0,2},{1,3},{2,4},{3,5},{4,6},{5,7},{8,10},{9,11},{10,12},{11,13},... | collective-permute-start | bytes 835592 | tf_op jit(solution)/shard_map/ppermute | solution.py:704
  5.7 0.7 %copy-done.11 = f32[256,16]{0,1:T(8,128)S(1)} copy-done((f32[256,16]{0,1:T(8,128)S(1)}, f32[256,16]{0,1:T(8,128)}, u32[]{:S(2)}) %copy-start.11) | copy-done | bytes 16408
  6.4 1.2 %copy-done.1 = bf16[256,2048]{1,0:T(8,128)(2,1)S(1)} copy-done((bf16[256,2048]{1,0:T(8,128)(2,1)S(1)}, bf16[256,2048]{1,0:T(8,128)(2,1)}, u32[]{:S(2)}) %copy-start.1) | copy-done | bytes 1048600
  7.6 5.8 %delta_local.3 = (bf16[1040,256]{1,0:T(8,128)(2,1)}, bf16[2048,256]{1,0:T(8,128)(2,1)S(1)}) custom-call(s32[1]{0:T(128)S(6)} %sub.3.half_ref, s32[1,256]{1,0:T(1,128)S(1)} %bitcast.16, bf16[256,1024]{1,0:T(8,128)(2,1)S(1)} %copy-done, bf16[256,2048]{1,0:T(8,128)(2,1)S(1)} %copy-done.1, f32[16,256]{1,0:T(8,128)S(1)} %bitcast.13, f32[16,256]{1,0:T(8,128)S(1)} %bitcast.9), custom_call_target="tpu_custom_call" | custom-call | flops 400000 | bytes 314 | tf_op jit(solution)/shard_map/delta_local/pallas_call | solution.py:378
  13.4 1.0 %copy-done.9 = bf16[2048,256]{1,0:T(8,128)(2,1)} copy-done((bf16[2048,256]{1,0:T(8,128)(2,1)}, bf16[2048,256]{1,0:T(8,128)(2,1)S(1)}, u32[]{:S(2)}) %copy-start.9) | copy-done | bytes 1048600
  14.4 1.0 %collective-permute-start = (bf16[1040,256]{1,0:T(8,128)(2,1)}, bf16[1040,256]{1,0:T(8,128)(2,1)S(1)}, u32[]{:S(2)}, u32[]{:S(2)}) collective-permute-start(bf16[1040,256]{1,0:T(8,128)(2,1)} %get-tuple-element.42), channel_id=1, source_target_pairs={{0,1},{1,0},{2,3},{3,2},{4,5},{5,4},{6,7},{7,6},{8,9},{9,8},{10,11... | collective-permute-start | bytes 1597448 | tf_op jit(solution)/shard_map/ppermute | solution.py:708
  15.3 3.2 %collective-permute-start.3 = (bf16[272,512]{1,0:T(8,128)(2,1)S(1)}, bf16[272,512]{1,0:T(8,128)(2,1)S(1)}, u32[]{:S(2)}, u32[]{:S(2)}) collective-permute-start(bf16[272,512]{1,0:T(8,128)(2,1)S(1)} %collective-permute-done.2.rest_1_), channel_id=1, source_target_pairs={{0,2},{1,3},{2,4},{3,5},{4,6},{5,7},{8,10},{9,11},{10,12},{11,13},... | collective-permute-start | bytes 835592 | tf_op jit(solution)/shard_map/ppermute | solution.py:704
  18.5 5.0 %delta_local.2 = (bf16[1040,256]{1,0:T(8,128)(2,1)S(1)}, bf16[2048,256]{1,0:T(8,128)(2,1)S(1)}) custom-call(s32[1]{0:T(128)} %bitcast.half_ref.core_ref, s32[1,256]{1,0:T(1,128)S(1)} %bitcast.17, bf16[256,1024]{1,0:T(8,128)(2,1)S(1)} %copy-done, bf16[256,2048]{1,0:T(8,128)(2,1)S(1)} %copy-done.1, f32[16,256]{1,0:T(8,128)S(1)} %bitcast.14, f32[16,256]{1,0:T(8,128)S(1)} %bitcast.10), custom_call_target="tpu_custom_call" | custom-call | flops 400000 | bytes 314 | tf_op jit(solution)/shard_map/delta_local/pallas_call | solution.py:378
  23.6 1.0 %copy-done.7 = bf16[2048,256]{1,0:T(8,128)(2,1)} copy-done((bf16[2048,256]{1,0:T(8,128)(2,1)}, bf16[2048,256]{1,0:T(8,128)(2,1)S(1)}, u32[]{:S(2)}) %copy-start.7) | copy-done | bytes 1048600
  24.5 0.3 compose.1
  24.9 0.7 %copy-done.6 = bf16[256,1024]{1,0:T(8,128)(2,1)S(1)} copy-done((bf16[256,1024]{1,0:T(8,128)(2,1)S(1)}, bf16[256,1024]{1,0:T(8,128)(2,1)}, u32[]{:S(2)}) %copy-start.6) | copy-done | bytes 524312
  25.6 1.2 %copy-done.10 = bf16[2048,256]{1,0:T(8,128)(2,1)S(1)} copy-done((bf16[2048,256]{1,0:T(8,128)(2,1)S(1)}, bf16[2048,256]{1,0:T(8,128)(2,1)}, u32[]{:S(2)}) %copy-start.10) | copy-done | bytes 1048600
  26.8 1.7 %delta_reach.2 = (bf16[256,1024]{1,0:T(8,128)(2,1)S(1)}, f32[256,1024]{1,0:T(8,128)S(1)}, f32[256,1024]{1,0:T(8,128)S(1)}) custom-call(s32[1]{0:T(128)S(6)} %sub.3.half_ref, s32[1,256]{1,0:T(1,128)S(1)} %bitcast.18, bf16[256,1024]{1,0:T(8,128)(2,1)S(1)} %copy-done.6, bf16[256,1024]{1,0:T(8,128)(2,1)S(1)} %copy-done, f32[16,256]{1,0:T(8,128)S(1)} %bitcast.11, ...), custom_call_target="tpu_custom_call" | custom-call | flops 400000 | bytes 314 | tf_op jit(solution)/shard_map/delta_reach/pallas_call | solution.py:378
  28.5 0.1 select_bitcast_fusion.1
  28.5 0.1 pad_maximum_fusion
  28.6 0.5 collective-permute-start.4
  29.1 2.1 %collective-permute-start.1 = (bf16[1040,128]{1,0:T(8,128)(2,1)S(1)}, bf16[1040,128]{1,0:T(8,128)(2,1)S(1)}, u32[]{:S(2)}, u32[]{:S(2)}) collective-permute-start(bf16[1040,128]{1,0:T(8,128)(2,1)S(1)} %get-tuple-element.46.add_ref), channel_id=1, source_target_pairs={{0,2},{1,3},{2,4},{3,5},{4,6},{5,7},{8,10},{9,11},{10,12},{11,13},... | collective-permute-start | bytes 798728 | tf_op jit(solution)/shard_map/ppermute | solution.py:704
  31.2 1.7 %delta_reach.3 = (bf16[256,1024]{1,0:T(8,128)(2,1)S(1)}, f32[256,1024]{1,0:T(8,128)S(1)}, f32[256,1024]{1,0:T(8,128)S(1)}) custom-call(s32[1]{0:T(128)} %bitcast.half_ref.core_ref, s32[1,256]{1,0:T(1,128)S(1)} %bitcast.19, bf16[256,1024]{1,0:T(8,128)(2,1)S(1)} %copy-done.6, bf16[256,1024]{1,0:T(8,128)(2,1)S(1)} %copy-done, f32[16,256]{1,0:T(8,128)S(1)} %bitcast.12, ...), custom_call_target="tpu_custom_call" | custom-call | flops 400000 | bytes 314 | tf_op jit(solution)/shard_map/delta_reach/pallas_call | solution.py:378
  32.9 0.1 broadcast_in_dim.2.freq_ref
  33.0 0.9 %window.1 = (bf16[256,1280]{1,0:T(8,128)(2,1)S(1)}, bf16[1280,256]{1,0:T(8,128)(2,1)S(1)}, f32[1,1280]{1,0:T(1,128)S(1)}, f32[256,128]{1,0:T(8,128)S(1)}, f32[256,128]{1,0:T(8,128)S(1)}) custom-call(f32[32,128]{1,0:T(8,128)S(1)} %broadcast_in_dim.2.freq_ref, bf16[272,512]{1,0:T(8,128)(2,1)S(1)} %copy-done.5, ...), custom_call_target="tpu_custom_call" | custom-call | flops 10000 | bytes 104 | tf_op jit(solution)/shard_map/window/pallas_call | solution.py:506
  33.9 0.2 copy-done.3
  34.1 3.8 %attention.2.rest_0_ = bf16[256,2048]{1,0:T(8,128)(2,1)} custom-call(f32[1,1280]{1,0:T(1,128)S(1)} %get-tuple-element.62.ids_ref, f32[256,128]{1,0:T(8,128)S(1)} %get-tuple-element.63.cos_ref, f32[256,128]{1,0:T(8,128)S(1)} %get-tuple-element.64.sin_ref, bf16[256,1280]{1,0:T(8,128)(2,1)S(1)} %get-tuple-element.65.kt_ref, ...), custom_call_target="tpu_custom_call" | custom-call | flops 500000 | bytes 314 | tf_op jit(solution)/shard_map/attention/pallas_call | solution.py:689
  38.0 0.8 %collective-permute-done.1.state_ref = bf16[1040,128]{1,0:T(8,128)(2,1)S(1)} collective-permute-done((bf16[1040,128]{1,0:T(8,128)(2,1)S(1)}, bf16[1040,128]{1,0:T(8,128)(2,1)S(1)}, u32[]{:S(2)}, u32[]{:S(2)}) %collective-permute-start.1) | collective-permute-done | bytes 266272 | tf_op jit(solution)/shard_map/ppermute | solution.py:704
  38.8 0.2 relay.1
  39.0 2.1 %collective-permute-start.5 = (bf16[1040,128]{1,0:T(8,128)(2,1)S(1)}, bf16[1040,128]{1,0:T(8,128)(2,1)S(1)}, u32[]{:S(2)}, u32[]{:S(2)}) collective-permute-start(bf16[1040,128]{1,0:T(8,128)(2,1)S(1)} %relay.1), channel_id=1, source_target_pairs={{0,2},{1,3},{2,4},{3,5},{4,6},{5,7},{8,10},{9,11},{10,12},{11,13},... | collective-permute-start | bytes 798728 | tf_op jit(solution)/shard_map/ppermute | solution.py:704
  41.1 3.8 %attention.3 = bf16[256,2048]{1,0:T(8,128)(2,1)} custom-call(f32[1,1280]{1,0:T(1,128)S(1)} %get-tuple-element.62.ids_ref, f32[256,128]{1,0:T(8,128)S(1)} %get-tuple-element.63.cos_ref, f32[256,128]{1,0:T(8,128)S(1)} %get-tuple-element.64.sin_ref, bf16[256,1280]{1,0:T(8,128)(2,1)S(1)} %get-tuple-element.65.kt_ref, ...), custom_call_target="tpu_custom_call", output_to_operand_aliasing={{}: (7, {})} | custom-call | flops 500000 | bytes 314 | tf_op jit(solution)/shard_map/attention/pallas_call | solution.py:689
  45.0 2.8 %collective-permute-done.5.state_ref = bf16[1040,128]{1,0:T(8,128)(2,1)S(1)} collective-permute-done((bf16[1040,128]{1,0:T(8,128)(2,1)S(1)}, bf16[1040,128]{1,0:T(8,128)(2,1)S(1)}, u32[]{:S(2)}, u32[]{:S(2)}) %collective-permute-start.5) | collective-permute-done | bytes 266272 | tf_op jit(solution)/shard_map/ppermute | solution.py:704
  47.8 0.4 arrive.1
  48.2 2.0 %collective-permute-start.6 = (bf16[1024,128]{1,0:T(8,128)(2,1)S(1)}, bf16[1024,128]{1,0:T(8,128)(2,1)S(1)}, u32[]{:S(2)}, u32[]{:S(2)}) collective-permute-start(bf16[1024,128]{1,0:T(8,128)(2,1)S(1)} %get-tuple-element.75), channel_id=1, source_target_pairs={{0,1},{1,0},{2,3},{3,2},{4,5},{5,4},{6,7},{7,6},{8,9},{9,8},{10,11... | collective-permute-start | bytes 786440 | tf_op jit(solution)/shard_map/ppermute | solution.py:708
  50.2 1.2 %delta_out.2.rest_0_ = bf16[256,2048]{1,0:T(8,128)(2,1)} custom-call(s32[1]{0:T(128)} %bitcast.half_ref.core_ref, bf16[256,1024]{1,0:T(8,128)(2,1)S(1)} %get-tuple-element.76.reach_ref, f32[256,1024]{1,0:T(8,128)S(1)} %get-tuple-element.77.inner_ref, f32[256,1024]{1,0:T(8,128)S(1)} %get-tuple-element.78.factor_ref, ...), custom_call_target="tpu_custom_call" | custom-call | flops 10000 | bytes 314 | tf_op jit(solution)/shard_map/delta_out/pallas_call | solution.py:555
  51.4 1.2 %delta_out.3 = bf16[256,2048]{1,0:T(8,128)(2,1)} custom-call(s32[1]{0:T(128)S(6)} %sub.3.half_ref, bf16[256,1024]{1,0:T(8,128)(2,1)S(1)} %get-tuple-element.71.reach_ref, f32[256,1024]{1,0:T(8,128)S(1)} %get-tuple-element.72.inner_ref, f32[256,1024]{1,0:T(8,128)S(1)} %get-tuple-element.73.factor_ref, ...), custom_call_target="tpu_custom_call", output_to_operand_aliasing={{}: (5, {})} | custom-call | flops 10000 | bytes 314 | tf_op jit(solution)/shard_map/delta_out/pallas_call | solution.py:555
  (29 shorter events, 0.1 us)
Async XLA Ops:
  0.6 5.0 %copy-start = (bf16[256,1024]{1,0:T(8,128)(2,1)S(1)}, bf16[256,1024]{1,0:T(8,128)(2,1)}, u32[]{:S(2)}) copy-start(bf16[256,1024]{1,0:T(8,128)(2,1)} %k_ref.7) | copy-start | bytes 1572868
  0.6 5.0 %copy-start.13 = (s32[256]{0:T(256)S(1)}, s32[256]{0:T(256)}, u32[]{:S(2)}) copy-start(s32[256]{0:T(256)} %param.12) | copy-start | bytes 3076
  2.4 12.9 %collective-permute-start.2 = (bf16[272,512]{1,0:T(8,128)(2,1)}, bf16[272,512]{1,0:T(8,128)(2,1)S(1)}, u32[]{:S(2)}, u32[]{:S(2)}) collective-permute-start(bf16[272,512]{1,0:T(8,128)(2,1)} %pack.1.rest_0_), channel_id=1, source_target_pairs={{0,2},{1,3},{2,4},{3,5},{4,6},{5,7},{8,10},{9,11},{10,12},{11,13},... | collective-permute-start | bytes 835592 | tf_op jit(solution)/shard_map/ppermute | solution.py:704
  5.6 0.7 %copy-start.11 = (f32[256,16]{0,1:T(8,128)S(1)}, f32[256,16]{0,1:T(8,128)}, u32[]{:S(2)}) copy-start(f32[256,16]{0,1:T(8,128)} %param.21) | copy-start | bytes 49156
  5.6 0.7 %copy-start.12 = (f32[256,16]{0,1:T(8,128)S(1)}, f32[256,16]{0,1:T(8,128)}, u32[]{:S(2)}) copy-start(f32[256,16]{0,1:T(8,128)} %param.20) | copy-start | bytes 49156
  6.4 1.2 %copy-start.1 = (bf16[256,2048]{1,0:T(8,128)(2,1)S(1)}, bf16[256,2048]{1,0:T(8,128)(2,1)}, u32[]{:S(2)}) copy-start(bf16[256,2048]{1,0:T(8,128)(2,1)} %v_ref.3) | copy-start | bytes 3145732
  13.4 1.0 %copy-start.9 = (bf16[2048,256]{1,0:T(8,128)(2,1)}, bf16[2048,256]{1,0:T(8,128)(2,1)S(1)}, u32[]{:S(2)}) copy-start(bf16[2048,256]{1,0:T(8,128)(2,1)S(1)} %get-tuple-element.51.solved_ref) | copy-start | bytes 3145732
  14.4 10.5 %copy-start.2 = (bf16[256,2048]{1,0:T(8,128)(2,1)S(1)}, bf16[256,2048]{1,0:T(8,128)(2,1)}, u32[]{:S(2)}) copy-start(bf16[256,2048]{1,0:T(8,128)(2,1)} %gate_ref.5) | copy-start | bytes 3145732
  14.4 10.2 %collective-permute-start = (bf16[1040,256]{1,0:T(8,128)(2,1)}, bf16[1040,256]{1,0:T(8,128)(2,1)S(1)}, u32[]{:S(2)}, u32[]{:S(2)}) collective-permute-start(bf16[1040,256]{1,0:T(8,128)(2,1)} %get-tuple-element.42), channel_id=1, source_target_pairs={{0,1},{1,0},{2,3},{3,2},{4,5},{5,4},{6,7},{7,6},{8,9},{9,8},{10,11... | collective-permute-start | bytes 1597448 | tf_op jit(solution)/shard_map/ppermute | solution.py:708
  15.3 13.1 %collective-permute-start.3 = (bf16[272,512]{1,0:T(8,128)(2,1)S(1)}, bf16[272,512]{1,0:T(8,128)(2,1)S(1)}, u32[]{:S(2)}, u32[]{:S(2)}) collective-permute-start(bf16[272,512]{1,0:T(8,128)(2,1)S(1)} %collective-permute-done.2.rest_1_), channel_id=1, source_target_pairs={{0,2},{1,3},{2,4},{3,5},{4,6},{5,7},{8,10},{9,11},{10,12},{11,13},... | collective-permute-start | bytes 835592 | tf_op jit(solution)/shard_map/ppermute | solution.py:704
  23.5 1.0 %copy-start.7 = (bf16[2048,256]{1,0:T(8,128)(2,1)}, bf16[2048,256]{1,0:T(8,128)(2,1)S(1)}, u32[]{:S(2)}) copy-start(bf16[2048,256]{1,0:T(8,128)(2,1)S(1)} %get-tuple-element.57.solved_ref) | copy-start | bytes 3145732
  24.5 1.0 %copy-start.6 = (bf16[256,1024]{1,0:T(8,128)(2,1)S(1)}, bf16[256,1024]{1,0:T(8,128)(2,1)}, u32[]{:S(2)}) copy-start(bf16[256,1024]{1,0:T(8,128)(2,1)} %q_ref.5) | copy-start | bytes 1572868
  24.8 0.7 %copy-start.14 = (f32[128]{0:T(128)S(1)}, f32[128]{0:T(128)}, u32[]{:S(2)}) copy-start(f32[128]{0:T(128)} %param.23) | copy-start | bytes 1540
  25.6 1.2 %copy-start.10 = (bf16[2048,256]{1,0:T(8,128)(2,1)S(1)}, bf16[2048,256]{1,0:T(8,128)(2,1)}, u32[]{:S(2)}) copy-start(bf16[2048,256]{1,0:T(8,128)(2,1)} %copy-done.9) | copy-start | bytes 3145732
  26.8 1.7 %copy-start.5 = (bf16[272,512]{1,0:T(8,128)(2,1)S(1)}, bf16[272,512]{1,0:T(8,128)(2,1)}, u32[]{:S(2)}) copy-start(bf16[272,512]{1,0:T(8,128)(2,1)} %pack.1.rest_0_) | copy-start | bytes 835588
  28.5 2.7 %copy-start.8 = (bf16[2048,256]{1,0:T(8,128)(2,1)S(1)}, bf16[2048,256]{1,0:T(8,128)(2,1)}, u32[]{:S(2)}) copy-start(bf16[2048,256]{1,0:T(8,128)(2,1)} %copy-done.7) | copy-start | bytes 3145732
  28.6 4.3 %collective-permute-start.4 = (bf16[2,272,512]{2,1,0:T(8,128)(2,1)S(1)}, bf16[2,272,512]{2,1,0:T(8,128)(2,1)S(1)}, u32[]{:S(2)}, u32[]{:S(2)}) collective-permute-start(bf16[2,272,512]{2,1,0:T(8,128)(2,1)S(1)} %pad_maximum_fusion), channel_id=1, source_target_pairs={{0,1},{1,0},{2,3},{3,2},{4,5},{5,4},{6,7},{7,6},{8,9},{9,8},{10,11... | collective-permute-start | bytes 1671176 | tf_op jit(solution)/shard_map/ppermute | solution.py:708
  29.1 9.7 %collective-permute-start.1 = (bf16[1040,128]{1,0:T(8,128)(2,1)S(1)}, bf16[1040,128]{1,0:T(8,128)(2,1)S(1)}, u32[]{:S(2)}, u32[]{:S(2)}) collective-permute-start(bf16[1040,128]{1,0:T(8,128)(2,1)S(1)} %get-tuple-element.46.add_ref), channel_id=1, source_target_pairs={{0,2},{1,3},{2,4},{3,5},{4,6},{5,7},{8,10},{9,11},{10,12},{11,13},... | collective-permute-start | bytes 798728 | tf_op jit(solution)/shard_map/ppermute | solution.py:704
  31.2 2.7 %copy-start.4 = (bf16[256,2048]{1,0:T(8,128)(2,1)S(1)}, bf16[256,2048]{1,0:T(8,128)(2,1)}, u32[]{:S(2)}) copy-start(bf16[256,2048]{1,0:T(8,128)(2,1)} %gate_ref.7) | copy-start | bytes 3145732
  32.9 1.2 %copy-start.3 = (bf16[256,2048]{1,0:T(8,128)(2,1)S(1)}, bf16[256,2048]{1,0:T(8,128)(2,1)}, u32[]{:S(2)}) copy-start(bf16[256,2048]{1,0:T(8,128)(2,1)} %q_ref.7) | copy-start | bytes 3145732
  39.0 8.8 %collective-permute-start.5 = (bf16[1040,128]{1,0:T(8,128)(2,1)S(1)}, bf16[1040,128]{1,0:T(8,128)(2,1)S(1)}, u32[]{:S(2)}, u32[]{:S(2)}) collective-permute-start(bf16[1040,128]{1,0:T(8,128)(2,1)S(1)} %relay.1), channel_id=1, source_target_pairs={{0,2},{1,3},{2,4},{3,5},{4,6},{5,7},{8,10},{9,11},{10,12},{11,13},... | collective-permute-start | bytes 798728 | tf_op jit(solution)/shard_map/ppermute | solution.py:704
  48.2 3.2 %collective-permute-start.6 = (bf16[1024,128]{1,0:T(8,128)(2,1)S(1)}, bf16[1024,128]{1,0:T(8,128)(2,1)S(1)}, u32[]{:S(2)}, u32[]{:S(2)}) collective-permute-start(bf16[1024,128]{1,0:T(8,128)(2,1)S(1)} %get-tuple-element.75), channel_id=1, source_target_pairs={{0,1},{1,0},{2,3},{3,2},{4,5},{5,4},{6,7},{7,6},{8,9},{9,8},{10,11... | collective-permute-start | bytes 786440 | tf_op jit(solution)/shard_map/ppermute | solution.py:708

commit v12 on v10

--- a/solution.py
+++ b/solution.py
@@ -357,7 +357,7 @@
     pipeline([elementwise, finish], n // 2)
 
 
-def half_call(kernel, name, mib, half, operands, outs, scratch):
+def half_call(kernel, name, mib, flops, half, operands, outs, scratch):
     def at_half(i, s):
         return (0, s[0])
 
@@ -384,7 +384,7 @@
         ),
         out_shape=outs,
         compiler_params=params(mib),
-        cost_estimate=cost(4 * 10**9, 3 * 2**20),
+        cost_estimate=cost(flops, 2**14),
         name=name,
     )(half, *args)
 
@@ -406,6 +406,7 @@
         delta_local_kernel,
         "delta_local",
         mib,
+        8 * 10**9,
         half,
         [seg_row, (key,), (value,), beta, decay],
         [
@@ -428,6 +429,7 @@
         delta_reach_kernel,
         "delta_reach",
         20,
+        10**6,
         half,
         [seg_row, (query,), (key,), decay, solved, (gate,), gain],
         [
@@ -767,7 +769,11 @@
     for _ in range(hops - 1):
         same.append(up_chip(same[-1], ranks))
     keep_ma, keep_solved = local(keep_half, 20)
-    same, keep_ma, other_ma = lax.optimization_barrier((same, keep_ma, other_ma))
+    give_solved, keep_ma = lax.optimization_barrier((give_solved, keep_ma))
+    give_rows = reach(give_half, solved=give_solved)
+    same, keep_ma, other_ma, give_rows = lax.optimization_barrier(
+        (same, keep_ma, other_ma, give_rows)
+    )
     chain = [own, *same]
     other = swap_cores(
         jnp.stack([jnp.where(odd, chain[i + 1], chain[i]) for i in range(hops)]), ranks
@@ -802,17 +808,16 @@
     kt, v_all, window_ids, cosine, sine = window_arrays
     window_arrays = (window_ids, cosine, sine, kt, v_all)
     attn_mixed = attention_half(0, window_arrays, attn_query, attn_gate)
-    give_solved, chip_add = lax.optimization_barrier((give_solved, chip_add))
-    give_rows = reach(give_half, solved=give_solved)
-    state, attn_mixed, give_rows = lax.optimization_barrier((state, attn_mixed, give_rows))
+    keep_solved, chip_add = lax.optimization_barrier((keep_solved, chip_add))
+    keep_rows = reach(keep_half, solved=keep_solved)
+    state, attn_mixed, keep_rows = lax.optimization_barrier((state, attn_mixed, keep_rows))
     leaving = chip_add
     for _ in range(hops - 1):
         (leaving,) = small_call(relay_kernel, "relay", [state_like], chip_map, chip_add, state)
         state = up_chip(leaving, ranks)
-    attn_mixed, keep_solved, leaving = lax.optimization_barrier((attn_mixed, keep_solved, leaving))
+    attn_mixed, leaving = lax.optimization_barrier((attn_mixed, leaving))
     attn_mixed = attention_half(1, window_arrays, attn_query, attn_gate, attn_mixed)
-    keep_rows = reach(keep_half, solved=keep_solved)
-    state, attn_mixed, keep_rows = lax.optimization_barrier((state, attn_mixed, keep_rows))
+    state, attn_mixed = lax.optimization_barrier((state, attn_mixed))
 
     final_like = jax.ShapeDtypeStruct((tall - BLOCK, DV), bf16)
     keep_state, pass_state = small_call(

time: 51.5 us -> 53.9 us (1.047)
  local copies, waits for them, and re-layouts: 3.8 us -> 5.83 us
  Pallas kernels: 27 us -> 28.9 us
  starting transfers between devices: 15.2 us -> 13.4 us
  other arithmetic: 0.13 us -> 1.08 us
  waiting for transfers between devices: 3.7 us -> 3.1 us
    unnamed x28 -> x30, local copies, waits for them, and re-layouts: 3.73 us -> 5.76 us
    ppermute x4, starting transfers between devices: 12 us -> 10.4 us  [up_chip(): return lax.ppermute(value, 'ctx', [(i, i + 2) for i in range(ranks - 2)])]
    pallas_call x5, Pallas kernels: 3.62 us -> 4.69 us  [small_call(): pl.pallas_call(kernel, in_specs=[SMEM] * scalars + [VMEM] * (len(args) -...]
    another operation x2, other arithmetic: 0.12 us -> 1.08 us  [per_device(): jnp.stack([jnp.where(odd, chain[i + 1], chain[i]) for i in range(hops)])]
    pallas_call x4, Pallas kernels: 13.4 us -> 14.1 us  [half_call(): pl.pallas_call(kernel, grid_spec=pltpu.PrefetchScalarGridSpec(num_scalar_...]
    ppermute x4, waiting for transfers between devices: 3.7 us -> 3.09 us  [up_chip(): return lax.ppermute(value, 'ctx', [(i, i + 2) for i in range(ranks - 2)])]
  transfers between devices with their start and end apart: 7 -> 7, of which waited for: 2 -> 1; matrix products, arithmetic and copies ran while one was open for 0% -> 0% of each run, Pallas kernels for 46% -> 47%
where the time goes in v12:
time: 53.9 us; the launch traced here: 53.4 us
  Pallas kernels  28.9 us (54%)
  starting transfers between devices  13.4 us (25%)
  local copies, waits for them, and re-layouts  5.83 us (11%)
  waiting for transfers between devices  3.1 us (6%)
  other arithmetic  1.08 us (2%)
  between operations  1.06 us (2%)
    pallas_call x4, Pallas kernels, half_call(): pl.pallas_call(kernel, grid_spec=pltpu.PrefetchScalarGridSpec(num_scalar_...  14.1 us
    ppermute x4, starting transfers between devices, up_chip(): return lax.ppermute(value, 'ctx', [(i, i + 2) for i in range(ranks - 2)])  10.4 us
    pallas_call x2, Pallas kernels, attention_half(): pl.pallas_call(attention_kernel, grid=(steps,), in_specs=in_specs, out_sp...  7.65 us
    unnamed x30, local copies, waits for them, and re-layouts  5.76 us
    pallas_call x5, Pallas kernels, small_call(): pl.pallas_call(kernel, in_specs=[SMEM] * scalars + [VMEM] * (len(args) -...  4.69 us
    ppermute x4, waiting for transfers between devices, up_chip(): return lax.ppermute(value, 'ctx', [(i, i + 2) for i in range(ranks - 2)])  3.09 us
    ppermute x3, starting transfers between devices, swap_cores(): return lax.ppermute(value, 'ctx', [(i, i ^ 1) for i in range(ranks)])  2.95 us
    pallas_call x2, Pallas kernels, delta_out(): pl.pallas_call(delta_out_kernel, in_specs=in_specs, out_specs=pl.BlockSpe...  2.47 us
  transfers between devices with their start and end apart: 7, of which 1 were waited for; matrix products, arithmetic and copies ran while one was open for 0% of the time, Pallas kernels for 47%

profile of v12, /device:TPU:9, one launch (start us, length us, event | category | flops | bytes accessed | tf_op | source)
XLA Modules:
  0.0 53.4 jit_solution(10064427572630693141)
XLA Ops:
  0.6 1.8 %pack.1.rest_0_ = bf16[272,512]{1,0:T(8,128)(2,1)} custom-call(s32[1,256]{1,0:T(1,128)} %bitcast.13, bf16[256,256]{1,0:T(8,128)(2,1)} %key_ref.1, bf16[256,256]{1,0:T(8,128)(2,1)} %value_ref.1), custom_call_target="tpu_custom_call" | custom-call | flops 100000000 | bytes 1048576 | tf_op jit(solution)/shard_map/pack/pallas_call | solution.py:506
  2.4 3.2 %collective-permute-start = (bf16[272,512]{1,0:T(8,128)(2,1)}, bf16[272,512]{1,0:T(8,128)(2,1)S(1)}, u32[]{:S(2)}, u32[]{:S(2)}) collective-permute-start(bf16[272,512]{1,0:T(8,128)(2,1)} %pack.1.rest_0_), channel_id=1, source_target_pairs={{0,2},{1,3},{2,4},{3,5},{4,6},{5,7},{8,10},{9,11},{10,12},{11,13},... | collective-permute-start | bytes 835592 | tf_op jit(solution)/shard_map/ppermute | solution.py:704
  5.6 0.0 copy-start.14
  5.7 0.7 %copy-done.14 = f32[256,16]{0,1:T(8,128)S(1)} copy-done((f32[256,16]{0,1:T(8,128)S(1)}, f32[256,16]{0,1:T(8,128)}, u32[]{:S(2)}) %copy-start.14) | copy-done | bytes 16408
  6.3 0.0 copy-done.8
  6.4 1.2 %copy-done.11 = bf16[256,2048]{1,0:T(8,128)(2,1)S(1)} copy-done((bf16[256,2048]{1,0:T(8,128)(2,1)S(1)}, bf16[256,2048]{1,0:T(8,128)(2,1)}, u32[]{:S(2)}) %copy-start.11) | copy-done | bytes 1048600
  7.6 5.8 %delta_local.2 = (bf16[1040,256]{1,0:T(8,128)(2,1)}, bf16[2048,256]{1,0:T(8,128)(2,1)S(1)}) custom-call(s32[1]{0:T(128)S(6)} %sub.3.half_ref, s32[1,256]{1,0:T(1,128)S(1)} %bitcast.14, bf16[256,1024]{1,0:T(8,128)(2,1)S(1)} %copy-done.3, bf16[256,2048]{1,0:T(8,128)(2,1)S(1)} %copy-done.11, f32[16,256]{1,0:T(8,128)S(1)} %bitcast.20, f32[16,256]{1,0:T(8,128)S(1)} %bitcast.9), custom_call_target="tpu_custom_call" | custom-call | flops 8000000000 | bytes 16384 | tf_op jit(solution)/shard_map/delta_local/pallas_call | solution.py:376
  13.4 1.0 %copy-done.6 = bf16[2048,256]{1,0:T(8,128)(2,1)} copy-done((bf16[2048,256]{1,0:T(8,128)(2,1)}, bf16[2048,256]{1,0:T(8,128)(2,1)S(1)}, u32[]{:S(2)}) %copy-start.6) | copy-done | bytes 1048600
  14.4 1.0 %collective-permute-start.2 = (bf16[1040,256]{1,0:T(8,128)(2,1)}, bf16[1040,256]{1,0:T(8,128)(2,1)S(1)}, u32[]{:S(2)}, u32[]{:S(2)}) collective-permute-start(bf16[1040,256]{1,0:T(8,128)(2,1)} %get-tuple-element.41), channel_id=1, source_target_pairs={{0,1},{1,0},{2,3},{3,2},{4,5},{5,4},{6,7},{7,6},{8,9},{9,8},{10,11... | collective-permute-start | bytes 1597448 | tf_op jit(solution)/shard_map/ppermute | solution.py:708
  15.3 3.2 %collective-permute-start.1 = (bf16[272,512]{1,0:T(8,128)(2,1)S(1)}, bf16[272,512]{1,0:T(8,128)(2,1)}, u32[]{:S(2)}, u32[]{:S(2)}) collective-permute-start(bf16[272,512]{1,0:T(8,128)(2,1)S(1)} %collective-permute-done.rest_1_), channel_id=1, source_target_pairs={{0,2},{1,3},{2,4},{3,5},{4,6},{5,7},{8,10},{9,11},{10,12},{11,13},... | collective-permute-start | bytes 835592 | tf_op jit(solution)/shard_map/ppermute | solution.py:704
  18.5 5.0 %delta_local.3 = (bf16[1040,256]{1,0:T(8,128)(2,1)S(1)}, bf16[2048,256]{1,0:T(8,128)(2,1)S(1)}) custom-call(s32[1]{0:T(128)} %bitcast.half_ref.core_ref, s32[1,256]{1,0:T(1,128)S(1)} %bitcast.15, bf16[256,1024]{1,0:T(8,128)(2,1)S(1)} %copy-done.3, bf16[256,2048]{1,0:T(8,128)(2,1)S(1)} %copy-done.11, f32[16,256]{1,0:T(8,128)S(1)} %bitcast.21, ...), custom_call_target="tpu_custom_call" | custom-call | flops 8000000000 | bytes 16384 | tf_op jit(solution)/shard_map/delta_local/pallas_call | solution.py:376
  23.5 1.0 %copy-done.4 = bf16[2048,256]{1,0:T(8,128)(2,1)} copy-done((bf16[2048,256]{1,0:T(8,128)(2,1)}, bf16[2048,256]{1,0:T(8,128)(2,1)S(1)}, u32[]{:S(2)}) %copy-start.4) | copy-done | bytes 1048600
  24.5 0.6 %copy-done.10 = f32[128]{0:T(128)S(1)} copy-done((f32[128]{0:T(128)S(1)}, f32[128]{0:T(128)}, u32[]{:S(2)}) %copy-start.10) | copy-done | bytes 536
  25.2 1.2 %copy-done.7 = bf16[2048,256]{1,0:T(8,128)(2,1)S(1)} copy-done((bf16[2048,256]{1,0:T(8,128)(2,1)S(1)}, bf16[2048,256]{1,0:T(8,128)(2,1)}, u32[]{:S(2)}) %copy-start.7) | copy-done | bytes 1048600
  26.4 1.7 %delta_reach.2 = (bf16[256,1024]{1,0:T(8,128)(2,1)S(1)}, f32[256,1024]{1,0:T(8,128)S(1)}, f32[256,1024]{1,0:T(8,128)S(1)}) custom-call(s32[1]{0:T(128)S(6)} %sub.3.half_ref, s32[1,256]{1,0:T(1,128)S(1)} %bitcast.16, bf16[256,1024]{1,0:T(8,128)(2,1)S(1)} %copy-done.2, bf16[256,1024]{1,0:T(8,128)(2,1)S(1)} %copy-done.3, f32[16,256]{1,0:T(8,128)S(1)} %bitcast.11, ...), custom_call_target="tpu_custom_call" | custom-call | flops 1000000 | bytes 16384 | tf_op jit(solution)/shard_map/delta_reach/pallas_call | solution.py:376
  28.1 1.0 %select_bitcast_fusion.1 = (bf16[1,272,512]{2,1,0:T(8,128)(2,1)S(1)}, bf16[1,272,512]{2,1,0:T(8,128)(2,1)S(1)}) fusion(bf16[272,512]{1,0:T(8,128)(2,1)S(1)} %collective-permute-done.rest_1_, bf16[272,512]{1,0:T(8,128)(2,1)S(1)} %copy-done.1, pred[]{:T(512)S(6)} %eq.5, bf16[272,512]{1,0:T(8,128)(2,1)} %collective-permute-done.1.rest_2_), kind=kLoop, calls=%fused_computation.2 | loop fusion | flops 278528 | bytes 1392641 | tf_op jit(solution)/shard_map/stack | solution.py:779
  29.1 0.1 pad_maximum_fusion
  29.2 0.1 collective-permute-start.4
  29.3 0.3 compose.1
  29.6 2.1 %collective-permute-start.3 = (bf16[1040,128]{1,0:T(8,128)(2,1)S(1)}, bf16[1040,128]{1,0:T(8,128)(2,1)S(1)}, u32[]{:S(2)}, u32[]{:S(2)}) collective-permute-start(bf16[1040,128]{1,0:T(8,128)(2,1)S(1)} %get-tuple-element.55.add_ref), channel_id=1, source_target_pairs={{0,2},{1,3},{2,4},{3,5},{4,6},{5,7},{8,10},{9,11},{10,12},{11,13},... | collective-permute-start | bytes 798728 | tf_op jit(solution)/shard_map/ppermute | solution.py:704
  31.7 1.7 %delta_reach.3 = (bf16[256,1024]{1,0:T(8,128)(2,1)S(1)}, f32[256,1024]{1,0:T(8,128)S(1)}, f32[256,1024]{1,0:T(8,128)S(1)}) custom-call(s32[1]{0:T(128)} %bitcast.half_ref.core_ref, s32[1,256]{1,0:T(1,128)S(1)} %bitcast.17, bf16[256,1024]{1,0:T(8,128)(2,1)S(1)} %copy-done.2, bf16[256,1024]{1,0:T(8,128)(2,1)S(1)} %copy-done.3, f32[16,256]{1,0:T(8,128)S(1)} %bitcast.12, ...), custom_call_target="tpu_custom_call" | custom-call | flops 1000000 | bytes 16384 | tf_op jit(solution)/shard_map/delta_reach/pallas_call | solution.py:376
  33.4 0.1 broadcast_in_dim.2.freq_ref
  33.5 2.0 %window.1 = (bf16[256,1280]{1,0:T(8,128)(2,1)S(1)}, bf16[1280,256]{1,0:T(8,128)(2,1)S(1)}, f32[1,1280]{1,0:T(1,128)S(1)}, f32[256,128]{1,0:T(8,128)S(1)}, f32[256,128]{1,0:T(8,128)S(1)}) custom-call(f32[32,128]{1,0:T(8,128)S(1)} %broadcast_in_dim.2.freq_ref, bf16[272,512]{1,0:T(8,128)(2,1)S(1)} %copy-done.1, ...), custom_call_target="tpu_custom_call" | custom-call | flops 100000000 | bytes 1048576 | tf_op jit(solution)/shard_map/window/pallas_call | solution.py:506
  35.5 3.8 %attention.2.rest_0_ = bf16[256,2048]{1,0:T(8,128)(2,1)} custom-call(f32[1,1280]{1,0:T(1,128)S(1)} %get-tuple-element.58.ids_ref, f32[256,128]{1,0:T(8,128)S(1)} %get-tuple-element.59.cos_ref, f32[256,128]{1,0:T(8,128)S(1)} %get-tuple-element.60.sin_ref, bf16[256,1280]{1,0:T(8,128)(2,1)S(1)} %get-tuple-element.61.kt_ref, ...), custom_call_target="tpu_custom_call" | custom-call | flops 5000000000 | bytes 3145728 | tf_op jit(solution)/shard_map/attention/pallas_call | solution.py:689
  39.3 0.2 relay.1
  39.6 1.9 %collective-permute-start.5 = (bf16[1040,128]{1,0:T(8,128)(2,1)S(1)}, bf16[1040,128]{1,0:T(8,128)(2,1)S(1)}, u32[]{:S(2)}, u32[]{:S(2)}) collective-permute-start(bf16[1040,128]{1,0:T(8,128)(2,1)S(1)} %relay.1), channel_id=1, source_target_pairs={{0,2},{1,3},{2,4},{3,5},{4,6},{5,7},{8,10},{9,11},{10,12},{11,13},... | collective-permute-start | bytes 798728 | tf_op jit(solution)/shard_map/ppermute | solution.py:704
  41.5 3.8 %attention.3 = bf16[256,2048]{1,0:T(8,128)(2,1)} custom-call(f32[1,1280]{1,0:T(1,128)S(1)} %get-tuple-element.58.ids_ref, f32[256,128]{1,0:T(8,128)S(1)} %get-tuple-element.59.cos_ref, f32[256,128]{1,0:T(8,128)S(1)} %get-tuple-element.60.sin_ref, bf16[256,1280]{1,0:T(8,128)(2,1)S(1)} %get-tuple-element.61.kt_ref, ...), custom_call_target="tpu_custom_call", output_to_operand_aliasing={{}: (7, {})} | custom-call | flops 5000000000 | bytes 3145728 | tf_op jit(solution)/shard_map/attention/pallas_call | solution.py:689
  45.3 3.1 %collective-permute-done.5.state_ref = bf16[1040,128]{1,0:T(8,128)(2,1)S(1)} collective-permute-done((bf16[1040,128]{1,0:T(8,128)(2,1)S(1)}, bf16[1040,128]{1,0:T(8,128)(2,1)S(1)}, u32[]{:S(2)}, u32[]{:S(2)}) %collective-permute-start.5) | collective-permute-done | bytes 266272 | tf_op jit(solution)/shard_map/ppermute | solution.py:704
  48.4 0.4 arrive.1
  48.8 1.9 %collective-permute-start.6 = (bf16[1024,128]{1,0:T(8,128)(2,1)S(1)}, bf16[1024,128]{1,0:T(8,128)(2,1)S(1)}, u32[]{:S(2)}, u32[]{:S(2)}) collective-permute-start(bf16[1024,128]{1,0:T(8,128)(2,1)S(1)} %get-tuple-element.75), channel_id=1, source_target_pairs={{0,1},{1,0},{2,3},{3,2},{4,5},{5,4},{6,7},{7,6},{8,9},{9,8},{10,11... | collective-permute-start | bytes 786440 | tf_op jit(solution)/shard_map/ppermute | solution.py:708
  50.7 1.2 %delta_out.2.rest_0_ = bf16[256,2048]{1,0:T(8,128)(2,1)} custom-call(s32[1]{0:T(128)} %bitcast.half_ref.core_ref, bf16[256,1024]{1,0:T(8,128)(2,1)S(1)} %get-tuple-element.76.reach_ref, f32[256,1024]{1,0:T(8,128)S(1)} %get-tuple-element.77.inner_ref, f32[256,1024]{1,0:T(8,128)S(1)} %get-tuple-element.78.factor_ref, ...), custom_call_target="tpu_custom_call" | custom-call | flops 100000000 | bytes 3145728 | tf_op jit(solution)/shard_map/delta_out/pallas_call | solution.py:555
  52.0 1.2 %delta_out.3 = bf16[256,2048]{1,0:T(8,128)(2,1)} custom-call(s32[1]{0:T(128)S(6)} %sub.3.half_ref, bf16[256,1024]{1,0:T(8,128)(2,1)S(1)} %get-tuple-element.71.reach_ref, f32[256,1024]{1,0:T(8,128)S(1)} %get-tuple-element.72.inner_ref, f32[256,1024]{1,0:T(8,128)S(1)} %get-tuple-element.73.factor_ref, ...), custom_call_target="tpu_custom_call", output_to_operand_aliasing={{}: (5, {})} | custom-call | flops 100000000 | bytes 3145728 | tf_op jit(solution)/shard_map/delta_out/pallas_call | solution.py:555
  (29 shorter events, 0.1 us)
Async XLA Ops:
  0.6 5.0 %copy-start.3 = (bf16[256,1024]{1,0:T(8,128)(2,1)S(1)}, bf16[256,1024]{1,0:T(8,128)(2,1)}, u32[]{:S(2)}) copy-start(bf16[256,1024]{1,0:T(8,128)(2,1)} %k_ref.7) | copy-start | bytes 1572868
  2.4 12.9 %collective-permute-start = (bf16[272,512]{1,0:T(8,128)(2,1)}, bf16[272,512]{1,0:T(8,128)(2,1)S(1)}, u32[]{:S(2)}, u32[]{:S(2)}) collective-permute-start(bf16[272,512]{1,0:T(8,128)(2,1)} %pack.1.rest_0_), channel_id=1, source_target_pairs={{0,2},{1,3},{2,4},{3,5},{4,6},{5,7},{8,10},{9,11},{10,12},{11,13},... | collective-permute-start | bytes 835592 | tf_op jit(solution)/shard_map/ppermute | solution.py:704
  5.6 0.7 %copy-start.14 = (f32[256,16]{0,1:T(8,128)S(1)}, f32[256,16]{0,1:T(8,128)}, u32[]{:S(2)}) copy-start(f32[256,16]{0,1:T(8,128)} %param.20) | copy-start | bytes 49156
  5.6 0.7 %copy-start.8 = (f32[256,16]{0,1:T(8,128)S(1)}, f32[256,16]{0,1:T(8,128)}, u32[]{:S(2)}) copy-start(f32[256,16]{0,1:T(8,128)} %param.21) | copy-start | bytes 49156
  5.7 0.7 %copy-start.9 = (s32[256]{0:T(256)S(1)}, s32[256]{0:T(256)}, u32[]{:S(2)}) copy-start(s32[256]{0:T(256)} %param.12) | copy-start | bytes 3076
  6.4 1.2 %copy-start.11 = (bf16[256,2048]{1,0:T(8,128)(2,1)S(1)}, bf16[256,2048]{1,0:T(8,128)(2,1)}, u32[]{:S(2)}) copy-start(bf16[256,2048]{1,0:T(8,128)(2,1)} %v_ref.3) | copy-start | bytes 3145732
  13.4 1.0 %copy-start.6 = (bf16[2048,256]{1,0:T(8,128)(2,1)}, bf16[2048,256]{1,0:T(8,128)(2,1)S(1)}, u32[]{:S(2)}) copy-start(bf16[2048,256]{1,0:T(8,128)(2,1)S(1)} %get-tuple-element.46.solved_ref) | copy-start | bytes 3145732
  14.4 10.2 %copy-start = (bf16[256,2048]{1,0:T(8,128)(2,1)S(1)}, bf16[256,2048]{1,0:T(8,128)(2,1)}, u32[]{:S(2)}) copy-start(bf16[256,2048]{1,0:T(8,128)(2,1)} %gate_ref.6) | copy-start | bytes 3145732
  14.4 10.2 %copy-start.2 = (bf16[256,1024]{1,0:T(8,128)(2,1)S(1)}, bf16[256,1024]{1,0:T(8,128)(2,1)}, u32[]{:S(2)}) copy-start(bf16[256,1024]{1,0:T(8,128)(2,1)} %q_ref.6) | copy-start | bytes 1572868
  14.4 13.7 %collective-permute-start.2 = (bf16[1040,256]{1,0:T(8,128)(2,1)}, bf16[1040,256]{1,0:T(8,128)(2,1)S(1)}, u32[]{:S(2)}, u32[]{:S(2)}) collective-permute-start(bf16[1040,256]{1,0:T(8,128)(2,1)} %get-tuple-element.41), channel_id=1, source_target_pairs={{0,1},{1,0},{2,3},{3,2},{4,5},{5,4},{6,7},{7,6},{8,9},{9,8},{10,11... | collective-permute-start | bytes 1597448 | tf_op jit(solution)/shard_map/ppermute | solution.py:708
  15.3 12.7 %collective-permute-start.1 = (bf16[272,512]{1,0:T(8,128)(2,1)S(1)}, bf16[272,512]{1,0:T(8,128)(2,1)}, u32[]{:S(2)}, u32[]{:S(2)}) collective-permute-start(bf16[272,512]{1,0:T(8,128)(2,1)S(1)} %collective-permute-done.rest_1_), channel_id=1, source_target_pairs={{0,2},{1,3},{2,4},{3,5},{4,6},{5,7},{8,10},{9,11},{10,12},{11,13},... | collective-permute-start | bytes 835592 | tf_op jit(solution)/shard_map/ppermute | solution.py:704
  23.5 1.0 %copy-start.4 = (bf16[2048,256]{1,0:T(8,128)(2,1)}, bf16[2048,256]{1,0:T(8,128)(2,1)S(1)}, u32[]{:S(2)}) copy-start(bf16[2048,256]{1,0:T(8,128)(2,1)S(1)} %get-tuple-element.63.solved_ref) | copy-start | bytes 3145732
  24.5 0.7 %copy-start.10 = (f32[128]{0:T(128)S(1)}, f32[128]{0:T(128)}, u32[]{:S(2)}) copy-start(f32[128]{0:T(128)} %param.23) | copy-start | bytes 1540
  25.2 1.2 %copy-start.7 = (bf16[2048,256]{1,0:T(8,128)(2,1)S(1)}, bf16[2048,256]{1,0:T(8,128)(2,1)}, u32[]{:S(2)}) copy-start(bf16[2048,256]{1,0:T(8,128)(2,1)} %copy-done.6) | copy-start | bytes 3145732
  26.4 1.7 %copy-start.1 = (bf16[272,512]{1,0:T(8,128)(2,1)S(1)}, bf16[272,512]{1,0:T(8,128)(2,1)}, u32[]{:S(2)}) copy-start(bf16[272,512]{1,0:T(8,128)(2,1)} %pack.1.rest_0_) | copy-start | bytes 835588
  29.1 2.6 %copy-start.5 = (bf16[2048,256]{1,0:T(8,128)(2,1)S(1)}, bf16[2048,256]{1,0:T(8,128)(2,1)}, u32[]{:S(2)}) copy-start(bf16[2048,256]{1,0:T(8,128)(2,1)} %copy-done.4) | copy-start | bytes 3145732
  29.2 4.3 %collective-permute-start.4 = (bf16[2,272,512]{2,1,0:T(8,128)(2,1)S(1)}, bf16[2,272,512]{2,1,0:T(8,128)(2,1)S(1)}, u32[]{:S(2)}, u32[]{:S(2)}) collective-permute-start(bf16[2,272,512]{2,1,0:T(8,128)(2,1)S(1)} %pad_maximum_fusion), channel_id=1, source_target_pairs={{0,1},{1,0},{2,3},{3,2},{4,5},{5,4},{6,7},{7,6},{8,9},{9,8},{10,11... | collective-permute-start | bytes 1671176 | tf_op jit(solution)/shard_map/ppermute | solution.py:708
  29.6 9.7 %collective-permute-start.3 = (bf16[1040,128]{1,0:T(8,128)(2,1)S(1)}, bf16[1040,128]{1,0:T(8,128)(2,1)S(1)}, u32[]{:S(2)}, u32[]{:S(2)}) collective-permute-start(bf16[1040,128]{1,0:T(8,128)(2,1)S(1)} %get-tuple-element.55.add_ref), channel_id=1, source_target_pairs={{0,2},{1,3},{2,4},{3,5},{4,6},{5,7},{8,10},{9,11},{10,12},{11,13},... | collective-permute-start | bytes 798728 | tf_op jit(solution)/shard_map/ppermute | solution.py:704
  31.7 3.8 %copy-start.13 = (bf16[256,2048]{1,0:T(8,128)(2,1)S(1)}, bf16[256,2048]{1,0:T(8,128)(2,1)}, u32[]{:S(2)}) copy-start(bf16[256,2048]{1,0:T(8,128)(2,1)} %gate_ref.7) | copy-start | bytes 3145732
  33.4 2.1 %copy-start.12 = (bf16[256,2048]{1,0:T(8,128)(2,1)S(1)}, bf16[256,2048]{1,0:T(8,128)(2,1)}, u32[]{:S(2)}) copy-start(bf16[256,2048]{1,0:T(8,128)(2,1)} %q_ref.7) | copy-start | bytes 3145732
  39.6 8.8 %collective-permute-start.5 = (bf16[1040,128]{1,0:T(8,128)(2,1)S(1)}, bf16[1040,128]{1,0:T(8,128)(2,1)S(1)}, u32[]{:S(2)}, u32[]{:S(2)}) collective-permute-start(bf16[1040,128]{1,0:T(8,128)(2,1)S(1)} %relay.1), channel_id=1, source_target_pairs={{0,2},{1,3},{2,4},{3,5},{4,6},{5,7},{8,10},{9,11},{10,12},{11,13},... | collective-permute-start | bytes 798728 | tf_op jit(solution)/shard_map/ppermute | solution.py:704
  48.8 3.2 %collective-permute-start.6 = (bf16[1024,128]{1,0:T(8,128)(2,1)S(1)}, bf16[1024,128]{1,0:T(8,128)(2,1)S(1)}, u32[]{:S(2)}, u32[]{:S(2)}) collective-permute-start(bf16[1024,128]{1,0:T(8,128)(2,1)S(1)} %get-tuple-element.75), channel_id=1, source_target_pairs={{0,1},{1,0},{2,3},{3,2},{4,5},{5,4},{6,7},{7,6},{8,9},{9,8},{10,11... | collective-permute-start | bytes 786440 | tf_op jit(solution)/shard_map/ppermute | solution.py:708

commit v13 on v10

--- a/solution.py
+++ b/solution.py
@@ -760,13 +760,13 @@
         gate=delta_gate,
         gain=norm_gain.reshape(1, DV),
     )
-    give_ma, give_solved = local(give_half, 20)
+    give_ma, give_solved = local(give_half, 60)
     other_ma = swap_cores(give_ma, ranks)
     nearest, give_ma = lax.optimization_barrier((nearest, give_ma))
     same = [nearest]
     for _ in range(hops - 1):
         same.append(up_chip(same[-1], ranks))
-    keep_ma, keep_solved = local(keep_half, 20)
+    keep_ma, keep_solved = local(keep_half, 60)
     same, keep_ma, other_ma = lax.optimization_barrier((same, keep_ma, other_ma))
     chain = [own, *same]
     other = swap_cores(

time: 51.5 us -> 51.1 us (level)
  Pallas kernels: 27 us -> 31.4 us
  waiting for transfers between devices: 3.7 us -> 1.25 us
  local copies, waits for them, and re-layouts: 3.8 us -> 1.38 us
    pallas_call x4, Pallas kernels: 13.4 us -> 17.7 us  [half_call(): pl.pallas_call(kernel, grid_spec=pltpu.PrefetchScalarGridSpec(num_scalar_...]
    ppermute x4, waiting for transfers between devices: 3.7 us -> 1.24 us  [up_chip(): return lax.ppermute(value, 'ctx', [(i, i + 2) for i in range(ranks - 2)])]
    unnamed x28 -> x24, local copies, waits for them, and re-layouts: 3.73 us -> 1.31 us
    ppermute x4, starting transfers between devices: 12 us -> 11.5 us  [up_chip(): return lax.ppermute(value, 'ctx', [(i, i + 2) for i in range(ranks - 2)])]
  transfers between devices with their start and end apart: 7 -> 7, of which waited for: 2 -> 1; matrix products, arithmetic and copies ran while one was open for 0% -> 0% of each run, Pallas kernels for 46% -> 55%
where the time goes in v13:
time: 51.1 us; the launch traced here: 50.3 us
  Pallas kernels  31.4 us (61%)
  starting transfers between devices  15.1 us (30%)
  local copies, waits for them, and re-layouts  1.38 us (3%)
  waiting for transfers between devices  1.25 us (2%)
  between operations  1.04 us (2%)
    pallas_call x4, Pallas kernels, half_call(): pl.pallas_call(kernel, grid_spec=pltpu.PrefetchScalarGridSpec(num_scalar_...  17.7 us
    ppermute x4, starting transfers between devices, up_chip(): return lax.ppermute(value, 'ctx', [(i, i + 2) for i in range(ranks - 2)])  11.5 us
    pallas_call x2, Pallas kernels, attention_half(): pl.pallas_call(attention_kernel, grid=(steps,), in_specs=in_specs, out_sp...  7.65 us
    ppermute x3, starting transfers between devices, swap_cores(): return lax.ppermute(value, 'ctx', [(i, i ^ 1) for i in range(ranks)])  3.59 us
    pallas_call x5, Pallas kernels, small_call(): pl.pallas_call(kernel, in_specs=[SMEM] * scalars + [VMEM] * (len(args) -...  3.58 us
    pallas_call x2, Pallas kernels, delta_out(): pl.pallas_call(delta_out_kernel, in_specs=in_specs, out_specs=pl.BlockSpe...  2.41 us
    unnamed x24, local copies, waits for them, and re-layouts  1.31 us
    ppermute x4, waiting for transfers between devices, up_chip(): return lax.ppermute(value, 'ctx', [(i, i + 2) for i in range(ranks - 2)])  1.24 us
  transfers between devices with their start and end apart: 7, of which 1 were waited for; matrix products, arithmetic and copies ran while one was open for 0% of the time, Pallas kernels for 55%

profile of v13, /device:TPU:9, one launch (start us, length us, event | category | flops | bytes accessed | tf_op | source)
XLA Modules:
  0.0 50.3 jit_solution(17246033690609457067)
XLA Ops:
  0.6 1.7 %pack.1.rest_0_ = bf16[272,512]{1,0:T(8,128)(2,1)} custom-call(s32[1,256]{1,0:T(1,128)} %bitcast.9, bf16[256,256]{1,0:T(8,128)(2,1)} %key_ref.1, bf16[256,256]{1,0:T(8,128)(2,1)} %value_ref.1), custom_call_target="tpu_custom_call" | custom-call | flops 100000000 | bytes 1048576 | tf_op jit(solution)/shard_map/pack/pallas_call | solution.py:504
  2.4 3.2 %collective-permute-start = (bf16[272,512]{1,0:T(8,128)(2,1)}, bf16[272,512]{1,0:T(8,128)(2,1)S(1)}, u32[]{:S(2)}, u32[]{:S(2)}) collective-permute-start(bf16[272,512]{1,0:T(8,128)(2,1)} %pack.1.rest_0_), channel_id=1, source_target_pairs={{0,2},{1,3},{2,4},{3,5},{4,6},{5,7},{8,10},{9,11},{10,12},{11,13},... | collective-permute-start | bytes 835592 | tf_op jit(solution)/shard_map/ppermute | solution.py:702
  5.6 7.1 %delta_local.2 = (bf16[1040,256]{1,0:T(8,128)(2,1)}, bf16[2048,256]{1,0:T(8,128)(2,1)}) custom-call(s32[1]{0:T(128)S(6)} %sub.3.half_ref, s32[1,256]{1,0:T(1,128)} %bitcast.10, bf16[256,1024]{1,0:T(8,128)(2,1)} %k_ref.7, bf16[256,2048]{1,0:T(8,128)(2,1)} %v_ref.3, f32[16,256]{1,0:T(8,128)} %bitcast.20, f32[16,256]{1,0:T(8,128)} %bitcast.14), custom_call_target="tpu_custom_call" | custom-call | flops 4000000000 | bytes 3145728 | tf_op jit(solution)/shard_map/delta_local/pallas_call | solution.py:376
  12.7 1.0 %collective-permute-start.2 = (bf16[1040,256]{1,0:T(8,128)(2,1)}, bf16[1040,256]{1,0:T(8,128)(2,1)S(1)}, u32[]{:S(2)}, u32[]{:S(2)}) collective-permute-start(bf16[1040,256]{1,0:T(8,128)(2,1)} %get-tuple-element.40), channel_id=1, source_target_pairs={{0,1},{1,0},{2,3},{3,2},{4,5},{5,4},{6,7},{7,6},{8,9},{9,8},{10,11... | collective-permute-start | bytes 1597448 | tf_op jit(solution)/shard_map/ppermute | solution.py:706
  13.7 3.3 %collective-permute-start.1 = (bf16[272,512]{1,0:T(8,128)(2,1)S(1)}, bf16[272,512]{1,0:T(8,128)(2,1)S(1)}, u32[]{:S(2)}, u32[]{:S(2)}) collective-permute-start(bf16[272,512]{1,0:T(8,128)(2,1)S(1)} %collective-permute-done.rest_1_), channel_id=1, source_target_pairs={{0,2},{1,3},{2,4},{3,5},{4,6},{5,7},{8,10},{9,11},{10,12},{11,13},... | collective-permute-start | bytes 835592 | tf_op jit(solution)/shard_map/ppermute | solution.py:702
  17.0 0.0 copy-start.11
  17.0 7.2 %delta_local.3 = (bf16[1040,256]{1,0:T(8,128)(2,1)}, bf16[2048,256]{1,0:T(8,128)(2,1)}) custom-call(s32[1]{0:T(128)} %bitcast.half_ref.core_ref, s32[1,256]{1,0:T(1,128)} %bitcast.11, bf16[256,1024]{1,0:T(8,128)(2,1)} %k_ref.7, bf16[256,2048]{1,0:T(8,128)(2,1)} %v_ref.3, f32[16,256]{1,0:T(8,128)} %bitcast.21, f32[16,256]{1,0:T(8,128)} %bitcast.15), custom_call_target="tpu_custom_call" | custom-call | flops 4000000000 | bytes 3145728 | tf_op jit(solution)/shard_map/delta_local/pallas_call | solution.py:376
  24.3 0.0 copy-start.7
  24.3 0.1 select_bitcast_fusion.1
  24.3 0.0 copy-start.5
  24.4 0.1 pad_maximum_fusion
  24.4 0.5 %collective-permute-start.4 = (bf16[2,272,512]{2,1,0:T(8,128)(2,1)S(1)}, bf16[2,272,512]{2,1,0:T(8,128)(2,1)S(1)}, u32[]{:S(2)}, u32[]{:S(2)}) collective-permute-start(bf16[2,272,512]{2,1,0:T(8,128)(2,1)S(1)} %pad_maximum_fusion), channel_id=1, source_target_pairs={{0,1},{1,0},{2,3},{3,2},{4,5},{5,4},{6,7},{7,6},{8,9},{9,8},{10,11... | collective-permute-start | bytes 1671176 | tf_op jit(solution)/shard_map/ppermute | solution.py:706
  25.0 0.5 copy-done.1
  25.4 0.3 compose.1
  25.8 3.1 %collective-permute-start.3 = (bf16[1040,128]{1,0:T(8,128)(2,1)S(1)}, bf16[1040,128]{1,0:T(8,128)(2,1)S(1)}, u32[]{:S(2)}, u32[]{:S(2)}) collective-permute-start(bf16[1040,128]{1,0:T(8,128)(2,1)S(1)} %get-tuple-element.48.add_ref), channel_id=1, source_target_pairs={{0,2},{1,3},{2,4},{3,5},{4,6},{5,7},{8,10},{9,11},{10,12},{11,13},... | collective-permute-start | bytes 798728 | tf_op jit(solution)/shard_map/ppermute | solution.py:702
  28.8 0.0 copy-start.2
  28.9 0.6 %copy-done.2 = s32[256]{0:T(256)S(1)} copy-done((s32[256]{0:T(256)S(1)}, s32[256]{0:T(256)}, u32[]{:S(2)}) %copy-start.2) | copy-done | bytes 1048
  29.5 1.7 %delta_reach.2 = (bf16[256,1024]{1,0:T(8,128)(2,1)S(1)}, f32[256,1024]{1,0:T(8,128)S(1)}, f32[256,1024]{1,0:T(8,128)S(1)}) custom-call(s32[1]{0:T(128)S(6)} %sub.3.half_ref, s32[1,256]{1,0:T(1,128)S(1)} %bitcast.12, bf16[256,1024]{1,0:T(8,128)(2,1)S(1)} %copy-done.6, bf16[256,1024]{1,0:T(8,128)(2,1)S(1)} %copy-done.7, f32[16,256]{1,0:T(8,128)S(1)} %bitcast.16, ...), custom_call_target="tpu_custom_call" | custom-call | flops 4000000000 | bytes 3145728 | tf_op jit(solution)/shard_map/delta_reach/pallas_call | solution.py:376
  31.2 0.0 copy-start.3
  31.3 0.1 broadcast_in_dim.2.freq_ref
  31.3 0.9 %window.1 = (bf16[256,1280]{1,0:T(8,128)(2,1)S(1)}, bf16[1280,256]{1,0:T(8,128)(2,1)S(1)}, f32[1,1280]{1,0:T(1,128)S(1)}, f32[256,128]{1,0:T(8,128)S(1)}, f32[256,128]{1,0:T(8,128)S(1)}) custom-call(f32[32,128]{1,0:T(8,128)S(1)} %broadcast_in_dim.2.freq_ref, bf16[272,512]{1,0:T(8,128)(2,1)S(1)} %copy-done, ...), custom_call_target="tpu_custom_call" | custom-call | flops 100000000 | bytes 1048576 | tf_op jit(solution)/shard_map/window/pallas_call | solution.py:504
  32.3 0.2 copy-done.3
  32.5 3.8 %attention.2.rest_0_ = bf16[256,2048]{1,0:T(8,128)(2,1)} custom-call(f32[1,1280]{1,0:T(1,128)S(1)} %get-tuple-element.51.ids_ref, f32[256,128]{1,0:T(8,128)S(1)} %get-tuple-element.52.cos_ref, f32[256,128]{1,0:T(8,128)S(1)} %get-tuple-element.53.sin_ref, bf16[256,1280]{1,0:T(8,128)(2,1)S(1)} %get-tuple-element.54.kt_ref, ...), custom_call_target="tpu_custom_call" | custom-call | flops 5000000000 | bytes 3145728 | tf_op jit(solution)/shard_map/attention/pallas_call | solution.py:687
  36.3 0.2 relay.1
  36.5 1.9 %collective-permute-start.5 = (bf16[1040,128]{1,0:T(8,128)(2,1)S(1)}, bf16[1040,128]{1,0:T(8,128)(2,1)S(1)}, u32[]{:S(2)}, u32[]{:S(2)}) collective-permute-start(bf16[1040,128]{1,0:T(8,128)(2,1)S(1)} %relay.1), channel_id=1, source_target_pairs={{0,2},{1,3},{2,4},{3,5},{4,6},{5,7},{8,10},{9,11},{10,12},{11,13},... | collective-permute-start | bytes 798728 | tf_op jit(solution)/shard_map/ppermute | solution.py:702
  38.5 3.8 %attention.3 = bf16[256,2048]{1,0:T(8,128)(2,1)} custom-call(f32[1,1280]{1,0:T(1,128)S(1)} %get-tuple-element.51.ids_ref, f32[256,128]{1,0:T(8,128)S(1)} %get-tuple-element.52.cos_ref, f32[256,128]{1,0:T(8,128)S(1)} %get-tuple-element.53.sin_ref, bf16[256,1280]{1,0:T(8,128)(2,1)S(1)} %get-tuple-element.54.kt_ref, ...), custom_call_target="tpu_custom_call", output_to_operand_aliasing={{}: (7, {})} | custom-call | flops 5000000000 | bytes 3145728 | tf_op jit(solution)/shard_map/attention/pallas_call | solution.py:687
  42.3 1.7 %delta_reach.3 = (bf16[256,1024]{1,0:T(8,128)(2,1)S(1)}, f32[256,1024]{1,0:T(8,128)S(1)}, f32[256,1024]{1,0:T(8,128)S(1)}) custom-call(s32[1]{0:T(128)} %bitcast.half_ref.core_ref, s32[1,256]{1,0:T(1,128)S(1)} %bitcast.13, bf16[256,1024]{1,0:T(8,128)(2,1)S(1)} %copy-done.6, bf16[256,1024]{1,0:T(8,128)(2,1)S(1)} %copy-done.7, f32[16,256]{1,0:T(8,128)S(1)} %bitcast.17, ...), custom_call_target="tpu_custom_call" | custom-call | flops 4000000000 | bytes 3145728 | tf_op jit(solution)/shard_map/delta_reach/pallas_call | solution.py:376
  44.0 1.2 %collective-permute-done.5.state_ref = bf16[1040,128]{1,0:T(8,128)(2,1)S(1)} collective-permute-done((bf16[1040,128]{1,0:T(8,128)(2,1)S(1)}, bf16[1040,128]{1,0:T(8,128)(2,1)S(1)}, u32[]{:S(2)}, u32[]{:S(2)}) %collective-permute-start.5) | collective-permute-done | bytes 266272 | tf_op jit(solution)/shard_map/ppermute | solution.py:702
  45.2 0.4 arrive.1
  45.6 2.1 %collective-permute-start.6 = (bf16[1024,128]{1,0:T(8,128)(2,1)S(1)}, bf16[1024,128]{1,0:T(8,128)(2,1)S(1)}, u32[]{:S(2)}, u32[]{:S(2)}) collective-permute-start(bf16[1024,128]{1,0:T(8,128)(2,1)S(1)} %get-tuple-element.73), channel_id=1, source_target_pairs={{0,1},{1,0},{2,3},{3,2},{4,5},{5,4},{6,7},{7,6},{8,9},{9,8},{10,11... | collective-permute-start | bytes 786440 | tf_op jit(solution)/shard_map/ppermute | solution.py:706
  47.7 1.2 %delta_out.2.rest_0_ = bf16[256,2048]{1,0:T(8,128)(2,1)} custom-call(s32[1]{0:T(128)} %bitcast.half_ref.core_ref, bf16[256,1024]{1,0:T(8,128)(2,1)S(1)} %get-tuple-element.74.reach_ref, f32[256,1024]{1,0:T(8,128)S(1)} %get-tuple-element.75.inner_ref, f32[256,1024]{1,0:T(8,128)S(1)} %get-tuple-element.76.factor_ref, ...), custom_call_target="tpu_custom_call" | custom-call | flops 100000000 | bytes 3145728 | tf_op jit(solution)/shard_map/delta_out/pallas_call | solution.py:553
  48.9 1.2 %delta_out.3 = bf16[256,2048]{1,0:T(8,128)(2,1)} custom-call(s32[1]{0:T(128)S(6)} %sub.3.half_ref, bf16[256,1024]{1,0:T(8,128)(2,1)S(1)} %get-tuple-element.69.reach_ref, f32[256,1024]{1,0:T(8,128)S(1)} %get-tuple-element.70.inner_ref, f32[256,1024]{1,0:T(8,128)S(1)} %get-tuple-element.71.factor_ref, ...), custom_call_target="tpu_custom_call", output_to_operand_aliasing={{}: (5, {})} | custom-call | flops 100000000 | bytes 3145728 | tf_op jit(solution)/shard_map/delta_out/pallas_call | solution.py:553
  (23 shorter events, 0.1 us)
Async XLA Ops:
  2.4 11.3 %collective-permute-start = (bf16[272,512]{1,0:T(8,128)(2,1)}, bf16[272,512]{1,0:T(8,128)(2,1)S(1)}, u32[]{:S(2)}, u32[]{:S(2)}) collective-permute-start(bf16[272,512]{1,0:T(8,128)(2,1)} %pack.1.rest_0_), channel_id=1, source_target_pairs={{0,2},{1,3},{2,4},{3,5},{4,6},{5,7},{8,10},{9,11},{10,12},{11,13},... | collective-permute-start | bytes 835592 | tf_op jit(solution)/shard_map/ppermute | solution.py:702
  12.7 11.5 %collective-permute-start.2 = (bf16[1040,256]{1,0:T(8,128)(2,1)}, bf16[1040,256]{1,0:T(8,128)(2,1)S(1)}, u32[]{:S(2)}, u32[]{:S(2)}) collective-permute-start(bf16[1040,256]{1,0:T(8,128)(2,1)} %get-tuple-element.40), channel_id=1, source_target_pairs={{0,1},{1,0},{2,3},{3,2},{4,5},{5,4},{6,7},{7,6},{8,9},{9,8},{10,11... | collective-permute-start | bytes 1597448 | tf_op jit(solution)/shard_map/ppermute | solution.py:706
  13.7 10.6 %copy-start = (bf16[272,512]{1,0:T(8,128)(2,1)S(1)}, bf16[272,512]{1,0:T(8,128)(2,1)}, u32[]{:S(2)}) copy-start(bf16[272,512]{1,0:T(8,128)(2,1)} %pack.1.rest_0_) | copy-start | bytes 835588
  13.7 10.6 %collective-permute-start.1 = (bf16[272,512]{1,0:T(8,128)(2,1)S(1)}, bf16[272,512]{1,0:T(8,128)(2,1)S(1)}, u32[]{:S(2)}, u32[]{:S(2)}) collective-permute-start(bf16[272,512]{1,0:T(8,128)(2,1)S(1)} %collective-permute-done.rest_1_), channel_id=1, source_target_pairs={{0,2},{1,3},{2,4},{3,5},{4,6},{5,7},{8,10},{9,11},{10,12},{11,13},... | collective-permute-start | bytes 835592 | tf_op jit(solution)/shard_map/ppermute | solution.py:702
  17.0 11.9 %copy-start.11 = (bf16[2048,256]{1,0:T(8,128)(2,1)S(1)}, bf16[2048,256]{1,0:T(8,128)(2,1)}, u32[]{:S(2)}) copy-start(bf16[2048,256]{1,0:T(8,128)(2,1)} %get-tuple-element.56.solved_ref) | copy-start | bytes 3145732
  24.3 4.6 %copy-start.7 = (bf16[256,1024]{1,0:T(8,128)(2,1)S(1)}, bf16[256,1024]{1,0:T(8,128)(2,1)}, u32[]{:S(2)}) copy-start(bf16[256,1024]{1,0:T(8,128)(2,1)} %k_ref.7) | copy-start | bytes 1572868
  24.3 1.1 %copy-start.1 = (bf16[1040,256]{1,0:T(8,128)(2,1)S(1)}, bf16[1040,256]{1,0:T(8,128)(2,1)}, u32[]{:S(2)}) copy-start(bf16[1040,256]{1,0:T(8,128)(2,1)} %get-tuple-element.43.mine_ref) | copy-start | bytes 1597444
  24.3 4.5 %copy-start.5 = (bf16[256,2048]{1,0:T(8,128)(2,1)S(1)}, bf16[256,2048]{1,0:T(8,128)(2,1)}, u32[]{:S(2)}) copy-start(bf16[256,2048]{1,0:T(8,128)(2,1)} %gate_ref.7) | copy-start | bytes 3145732
  24.4 6.8 %collective-permute-start.4 = (bf16[2,272,512]{2,1,0:T(8,128)(2,1)S(1)}, bf16[2,272,512]{2,1,0:T(8,128)(2,1)S(1)}, u32[]{:S(2)}, u32[]{:S(2)}) collective-permute-start(bf16[2,272,512]{2,1,0:T(8,128)(2,1)S(1)} %pad_maximum_fusion), channel_id=1, source_target_pairs={{0,1},{1,0},{2,3},{3,2},{4,5},{5,4},{6,7},{7,6},{8,9},{9,8},{10,11... | collective-permute-start | bytes 1671176 | tf_op jit(solution)/shard_map/ppermute | solution.py:706
  25.4 3.4 %copy-start.6 = (bf16[256,1024]{1,0:T(8,128)(2,1)S(1)}, bf16[256,1024]{1,0:T(8,128)(2,1)}, u32[]{:S(2)}) copy-start(bf16[256,1024]{1,0:T(8,128)(2,1)} %q_ref.7) | copy-start | bytes 1572868
  25.4 3.5 %copy-start.8 = (f32[256,16]{0,1:T(8,128)S(1)}, f32[256,16]{0,1:T(8,128)}, u32[]{:S(2)}) copy-start(f32[256,16]{0,1:T(8,128)} %param.21) | copy-start | bytes 49156
  25.8 10.5 %collective-permute-start.3 = (bf16[1040,128]{1,0:T(8,128)(2,1)S(1)}, bf16[1040,128]{1,0:T(8,128)(2,1)S(1)}, u32[]{:S(2)}, u32[]{:S(2)}) collective-permute-start(bf16[1040,128]{1,0:T(8,128)(2,1)S(1)} %get-tuple-element.48.add_ref), channel_id=1, source_target_pairs={{0,2},{1,3},{2,4},{3,5},{4,6},{5,7},{8,10},{9,11},{10,12},{11,13},... | collective-permute-start | bytes 798728 | tf_op jit(solution)/shard_map/ppermute | solution.py:702
  28.8 0.7 %copy-start.2 = (s32[256]{0:T(256)S(1)}, s32[256]{0:T(256)}, u32[]{:S(2)}) copy-start(s32[256]{0:T(256)} %param.12) | copy-start | bytes 3076
  28.8 0.7 %copy-start.9 = (f32[128]{0:T(128)S(1)}, f32[128]{0:T(128)}, u32[]{:S(2)}) copy-start(f32[128]{0:T(128)} %param.23) | copy-start | bytes 1540
  29.5 2.8 %copy-start.4 = (bf16[256,2048]{1,0:T(8,128)(2,1)S(1)}, bf16[256,2048]{1,0:T(8,128)(2,1)}, u32[]{:S(2)}) copy-start(bf16[256,2048]{1,0:T(8,128)(2,1)} %gate_ref.6) | copy-start | bytes 3145732
  31.2 1.2 %copy-start.3 = (bf16[256,2048]{1,0:T(8,128)(2,1)S(1)}, bf16[256,2048]{1,0:T(8,128)(2,1)}, u32[]{:S(2)}) copy-start(bf16[256,2048]{1,0:T(8,128)(2,1)} %q_ref.6) | copy-start | bytes 3145732
  36.5 8.7 %collective-permute-start.5 = (bf16[1040,128]{1,0:T(8,128)(2,1)S(1)}, bf16[1040,128]{1,0:T(8,128)(2,1)S(1)}, u32[]{:S(2)}, u32[]{:S(2)}) collective-permute-start(bf16[1040,128]{1,0:T(8,128)(2,1)S(1)} %relay.1), channel_id=1, source_target_pairs={{0,2},{1,3},{2,4},{3,5},{4,6},{5,7},{8,10},{9,11},{10,12},{11,13},... | collective-permute-start | bytes 798728 | tf_op jit(solution)/shard_map/ppermute | solution.py:702
  38.5 3.8 %copy-start.10 = (bf16[2048,256]{1,0:T(8,128)(2,1)S(1)}, bf16[2048,256]{1,0:T(8,128)(2,1)}, u32[]{:S(2)}) copy-start(bf16[2048,256]{1,0:T(8,128)(2,1)} %get-tuple-element.64.solved_ref) | copy-start | bytes 3145732
  45.6 3.3 %collective-permute-start.6 = (bf16[1024,128]{1,0:T(8,128)(2,1)S(1)}, bf16[1024,128]{1,0:T(8,128)(2,1)S(1)}, u32[]{:S(2)}, u32[]{:S(2)}) collective-permute-start(bf16[1024,128]{1,0:T(8,128)(2,1)S(1)} %get-tuple-element.73), channel_id=1, source_target_pairs={{0,1},{1,0},{2,3},{3,2},{4,5},{5,4},{6,7},{7,6},{8,9},{9,8},{10,11... | collective-permute-start | bytes 786440 | tf_op jit(solution)/shard_map/ppermute | solution.py:706
